TPU v7x, 32 devices: a whole 2x2x4 slice. The times are simulated.
32 devices in a mesh: section: 2 (over core), dp: 16 (over z, y, x).
Axes of the slice: x: 2, y: 2, z: 4, core: 2. Of those that a mesh axis runs over, the one named last changes fastest.
Arguments:
- tokens: bfloat16 [16384, 768], P('dp'), may hold values from -6 to 6
- heights: int32 [64], P('dp'), may hold values from 1 to 15, as said below
- out_grad: bfloat16 [16384, 768], P('dp'), may hold values from -6 to 6
- w_query: bfloat16 [2, 768, 768], P('section', 'dp'), may hold values from -0.21875 to 0.21875
- w_key: bfloat16 [2, 768, 768], P('section', 'dp'), may hold values from -0.21875 to 0.21875
- w_value: bfloat16 [2, 768, 768], P('section', 'dp'), may hold values from -0.21875 to 0.21875
- w_out: bfloat16 [2, 768, 768], P('section', 'dp'), may hold values from -0.875 to 0.875
- w_gate: bfloat16 [2, 768, 2048], P('section', 'dp'), may hold values from -0.21875 to 0.21875
- w_up: bfloat16 [2, 768, 2048], P('section', 'dp'), may hold values from -0.21875 to 0.21875
- w_down: bfloat16 [2, 2048, 768], P('section', 'dp'), may hold values from -0.125 to 0.125
- gain_attn: bfloat16 [2, 768], P('section', 'dp'), may hold values from 0.5 to 1.5
- gain_ffn: bfloat16 [2, 768], P('section', 'dp'), may hold values from 0.5 to 1.5
Outputs:
- activations: bfloat16 [2, 16384, 768], P('section', 'dp')
- input_grads: bfloat16 [2, 16384, 768], P('section', 'dp')
- grad_query: float32 [2, 768, 768], P('section', 'dp')
- grad_key: float32 [2, 768, 768], P('section', 'dp')
- grad_value: float32 [2, 768, 768], P('section', 'dp')
- grad_out: float32 [2, 768, 768], P('section', 'dp')
- grad_gate: float32 [2, 768, 2048], P('section', 'dp')
- grad_up: float32 [2, 768, 2048], P('section', 'dp')
- grad_down: float32 [2, 2048, 768], P('section', 'dp')
- grad_gain_attn: float32 [2, 768], P('section', 'dp')
- grad_gain_ffn: float32 [2, 768], P('section', 'dp')
Inputs may be any that keep to these rules, and one draw needn't show every extreme that they name: `heights`: rows of each cropped image; in every draw some image has 15 rows and some has 1.
All inputs are finite; a program needn't handle non-finite values.
Results may differ from a plain program's by a relative error of at most 0.02.
Values may be sent and summed in bfloat16 or wider, within the bound.
No kernel may reach another device: no remote copies, remote signals or barrier semaphores. Data moves between devices by JAX's collectives and lax.ppermute only.
A program may use at most 256 MiB of HBM per device.

v0:
```python
import jax
import jax.numpy as jnp
from jax import lax
from jax.sharding import PartitionSpec as P

D = 768
HEADS = 12
HEAD_DIM = 64
WIDE = 16
SLOT = 256
MICRO = 2


EPS = 1e-05
SCALE = 0.125


def shifted(value, axis, steps):
    count = lax.axis_size(axis)
    initial, last = (max(0, -steps), min(count, count - steps))
    return lax.ppermute(value, axis, [(source, source + steps) for source in range(initial, last)])


def rope_tables(slot_len):
    position = jnp.arange(slot_len)
    index = jnp.maximum(position - 1, 0)
    started = (position > 0).astype(jnp.float32)
    row_pos = (index // WIDE).astype(jnp.float32) * started
    col_pos = (index % WIDE).astype(jnp.float32) * started
    quarter = HEAD_DIM // 4
    freq = 10000.0 ** (-jnp.arange(quarter).astype(jnp.float32) / quarter)
    row_angle = row_pos[:, None] * freq[None, :]
    col_angle = col_pos[:, None] * freq[None, :]
    angle = jnp.stack([row_angle, row_angle, col_angle, col_angle], axis=1).reshape(
        slot_len, 1, HEAD_DIM
    )
    angle = jnp.tile(angle, (1, HEADS, 1)).reshape(slot_len, HEADS * HEAD_DIM)
    return (jnp.cos(angle), jnp.sin(angle))


def rotate(values):
    leading = values.shape[:-1]
    pieces = values.reshape(leading + (values.shape[-1] // HEAD_DIM, 4, HEAD_DIM // 4))
    turned = jnp.stack(
        [-pieces[..., 1, :], pieces[..., 0, :], -pieces[..., 3, :], pieces[..., 2, :]], axis=-2
    )
    return turned.reshape(values.shape)


def apply_rope(values, cosine, sine_table):
    return values * cosine + rotate(values) * sine_table


def rope_back(values, cosine, sine_table):
    return values * cosine - rotate(values * sine_table)


def rms_scale(values):
    return lax.rsqrt(jnp.mean(values * values, axis=-1, keepdims=True) + EPS)


def project(left, weight):
    return jnp.einsum("bsd,de->bse", left, weight, preferred_element_type=jnp.float32)


def project_back(grad_left, weight):
    return jnp.einsum("bse,de->bsd", grad_left, weight, preferred_element_type=jnp.float32)


def weight_grad(left, grad_right):
    return jnp.einsum("bsd,bse->de", left, grad_right, preferred_element_type=jnp.float32)


def norm_back(grad_normed, values, scale_row, gain):
    scaled = grad_normed * gain
    return scale_row * scaled - values * scale_row**3 * jnp.mean(
        scaled * values, axis=-1, keepdims=True
    )


def heads_view(values):
    return values.reshape(values.shape[0], values.shape[1], HEADS, HEAD_DIM)


def layer_parts(inputs, lengths, weights, tables):
    w_q, w_k, w_v, w_o, w_g, w_u, w_d, gain_one, gain_two = weights
    cosine, sine_table = tables
    batch_size, slot_len, model_width = inputs.shape
    position = jnp.arange(slot_len)
    limit_len = WIDE * lengths + 1
    valid_rows = (position[None, :] < limit_len[:, None]).astype(jnp.float32)[:, :, None]
    causal = position[None, :] <= position[:, None]
    attn_mask = (
        causal[None, None, :, :] & (position[None, :] < limit_len[:, None])[:, None, None, :]
    )
    scale_one = rms_scale(inputs)
    normed = (inputs * scale_one * gain_one.astype(jnp.float32)).astype(jnp.bfloat16)
    query_rot = apply_rope(project(normed, w_q), cosine, sine_table).astype(jnp.bfloat16)
    key_rot = apply_rope(project(normed, w_k), cosine, sine_table).astype(jnp.bfloat16)
    value_low = project(normed, w_v).astype(jnp.bfloat16)
    scores = (
        jnp.einsum(
            "bqhd,bkhd->bhqk",
            heads_view(query_rot),
            heads_view(key_rot),
            preferred_element_type=jnp.float32,
        )
        * SCALE
    )
    scores = jnp.where(attn_mask, scores, -1e30)
    probs_full = jax.nn.softmax(scores, axis=-1)
    probs_low = probs_full.astype(jnp.bfloat16)
    mixed_low = jnp.einsum(
        "bhqk,bkhd->bqhd", probs_low, heads_view(value_low), preferred_element_type=jnp.float32
    ).reshape(batch_size, slot_len, model_width)
    mixed_low = mixed_low.astype(jnp.bfloat16)
    middle = inputs + project(mixed_low, w_o)
    scale_two = rms_scale(middle)
    normed_two = (middle * scale_two * gain_two.astype(jnp.float32)).astype(jnp.bfloat16)
    gate_raw = project(normed_two, w_g)
    up_raw = project(normed_two, w_u)
    hidden_low = (jax.nn.silu(gate_raw) * up_raw).astype(jnp.bfloat16)
    result = valid_rows * (middle + project(hidden_low, w_d))
    return (
        result,
        valid_rows,
        scale_one,
        normed,
        query_rot,
        key_rot,
        value_low,
        probs_full,
        probs_low,
        mixed_low,
        middle,
        scale_two,
        normed_two,
        gate_raw,
        up_raw,
        hidden_low,
    )


def layer_back(inputs, lengths, weights, tables, grad_result):
    w_q, w_k, w_v, w_o, w_g, w_u, w_d, gain_one, gain_two = weights
    cosine, sine_table = tables
    (
        result,
        valid_rows,
        scale_one,
        normed,
        query_rot,
        key_rot,
        value_low,
        probs_full,
        probs_low,
        mixed_low,
        middle,
        scale_two,
        normed_two,
        gate_raw,
        up_raw,
        hidden_low,
    ) = layer_parts(inputs, lengths, weights, tables)
    batch_size, slot_len, model_width = inputs.shape
    grad_valid = valid_rows * grad_result
    grad_ffn = grad_valid.astype(jnp.bfloat16)
    grad_w_down = weight_grad(hidden_low, grad_ffn)
    grad_hidden = project_back(grad_ffn, w_d)
    sigmoid_gate = jax.nn.sigmoid(gate_raw)
    swish_gate = gate_raw * sigmoid_gate
    grad_gate = (
        grad_hidden * up_raw * (sigmoid_gate * (1.0 + gate_raw * (1.0 - sigmoid_gate)))
    ).astype(jnp.bfloat16)
    grad_up = (grad_hidden * swish_gate).astype(jnp.bfloat16)
    grad_w_gate = weight_grad(normed_two, grad_gate)
    grad_w_up = weight_grad(normed_two, grad_up)
    grad_normed_two = project_back(grad_gate, w_g) + project_back(grad_up, w_u)
    grad_gain_two = jnp.sum(grad_normed_two * middle * scale_two, axis=(0, 1))
    grad_middle = grad_valid + norm_back(
        grad_normed_two, middle, scale_two, gain_two.astype(jnp.float32)
    )
    grad_branch = grad_middle.astype(jnp.bfloat16)
    grad_w_out = weight_grad(mixed_low, grad_branch)
    grad_mixed = project_back(grad_branch, w_o).astype(jnp.bfloat16)
    grad_probs = jnp.einsum(
        "bqhd,bkhd->bhqk",
        heads_view(grad_mixed),
        heads_view(value_low),
        preferred_element_type=jnp.float32,
    )
    grad_scores = probs_full * (
        grad_probs - jnp.sum(probs_full * grad_probs, axis=-1, keepdims=True)
    )
    grad_scores = grad_scores.astype(jnp.bfloat16)
    grad_qrot = (
        jnp.einsum(
            "bhqk,bkhd->bqhd", grad_scores, heads_view(key_rot), preferred_element_type=jnp.float32
        ).reshape(batch_size, slot_len, model_width)
        * SCALE
    )
    grad_krot = (
        jnp.einsum(
            "bhqk,bqhd->bkhd",
            grad_scores,
            heads_view(query_rot),
            preferred_element_type=jnp.float32,
        ).reshape(batch_size, slot_len, model_width)
        * SCALE
    )
    grad_query = rope_back(grad_qrot, cosine, sine_table).astype(jnp.bfloat16)
    grad_key = rope_back(grad_krot, cosine, sine_table).astype(jnp.bfloat16)
    grad_value = jnp.einsum(
        "bhqk,bqhd->bkhd", probs_low, heads_view(grad_mixed), preferred_element_type=jnp.float32
    ).reshape(batch_size, slot_len, model_width)
    grad_value = grad_value.astype(jnp.bfloat16)
    grad_w_query = weight_grad(normed, grad_query)
    grad_w_key = weight_grad(normed, grad_key)
    grad_w_value = weight_grad(normed, grad_value)
    grad_normed = (
        project_back(grad_query, w_q) + project_back(grad_key, w_k) + project_back(grad_value, w_v)
    )
    grad_gain_one = jnp.sum(grad_normed * inputs * scale_one, axis=(0, 1))
    grad_inputs = grad_middle + norm_back(
        grad_normed, inputs, scale_one, gain_one.astype(jnp.float32)
    )
    grads = (
        grad_w_query,
        grad_w_key,
        grad_w_value,
        grad_w_out,
        grad_w_gate,
        grad_w_up,
        grad_w_down,
        grad_gain_one,
        grad_gain_two,
    )
    return (grad_inputs.astype(jnp.bfloat16), grads)


def on_device(
    tokens,
    heights,
    out_grad,
    w_query,
    w_key,
    w_value,
    w_out,
    w_gate,
    w_up,
    w_down,
    gain_attn,
    gain_ffn,
):
    section_id = lax.axis_index("section")
    dp_count = lax.axis_size("dp")
    sharded = (w_query, w_key, w_value, w_out, w_gate, w_up, w_down, gain_attn, gain_ffn)
    gathered = (
        lax.all_gather(sharded[0], "dp", axis=1, tiled=True),
        lax.all_gather(sharded[1], "dp", axis=1, tiled=True),
        lax.all_gather(sharded[2], "dp", axis=1, tiled=True),
        lax.all_gather(sharded[3], "dp", axis=1, tiled=True),
        lax.all_gather(sharded[4], "dp", axis=1, tiled=True),
        lax.all_gather(sharded[5], "dp", axis=1, tiled=True),
        lax.all_gather(sharded[6], "dp", axis=1, tiled=True),
        lax.all_gather(sharded[7], "dp", axis=1, tiled=True),
        lax.all_gather(sharded[8], "dp", axis=1, tiled=True),
    )
    weights = tuple((weight[0] for weight in gathered))
    images = heights.shape[0]
    per_micro = images // MICRO
    tables = rope_tables(SLOT)
    token_blocks = tokens.reshape(MICRO, per_micro, SLOT, D)
    length_blocks = heights.reshape(MICRO, per_micro)
    cotangent_blocks = out_grad.reshape(MICRO, per_micro, SLOT, D)
    received = jnp.zeros((per_micro, SLOT, D), jnp.bfloat16)
    inputs_kept = []
    outputs_kept = []
    for moment in range(MICRO + 1):
        micro_id = jnp.clip(moment - section_id, 0, MICRO - 1)
        own_rows = token_blocks[min(moment, MICRO - 1)]
        layer_in = jnp.where(section_id == 0, own_rows, received)
        lengths = lax.dynamic_index_in_dim(length_blocks, micro_id, 0, keepdims=False)
        result = layer_parts(layer_in.astype(jnp.float32), lengths, weights, tables)[0]
        result_low = result.astype(jnp.bfloat16)
        inputs_kept.append(layer_in)
        outputs_kept.append(result_low)
        if moment < MICRO:
            received = shifted(result_low, "section", 1)
    activations = jnp.stack(
        [
            jnp.where(section_id == 0, outputs_kept[micro_no], outputs_kept[micro_no + 1])
            for micro_no in range(MICRO)
        ]
    )
    totals = tuple((jnp.zeros(weight.shape, jnp.float32) for weight in weights))
    shards = tuple(
        (
            jnp.zeros((1, weight.shape[0] // dp_count) + weight.shape[1:], jnp.float32)
            for weight in weights
        )
    )
    back_received = jnp.zeros((per_micro, SLOT, D), jnp.bfloat16)
    grads_kept = []
    for moment in range(MICRO + 1):
        micro_raw = moment - (1 - section_id)
        is_live = (micro_raw >= 0) & (micro_raw < MICRO)
        micro_id = jnp.clip(micro_raw, 0, MICRO - 1)
        own_grad = cotangent_blocks[min(moment, MICRO - 1)]
        grad_result = jnp.where(section_id == 1, own_grad, back_received).astype(jnp.float32)
        layer_in = jnp.where(
            section_id == 0, inputs_kept[max(moment - 1, 0)], inputs_kept[min(moment + 1, MICRO)]
        )
        lengths = lax.dynamic_index_in_dim(length_blocks, micro_id, 0, keepdims=False)
        grad_inputs, grads = layer_back(
            layer_in.astype(jnp.float32), lengths, weights, tables, grad_result
        )
        live_grads = tuple((jnp.where(is_live, piece, 0.0) for piece in grads))
        totals = tuple((held + added for held, added in zip(totals, live_grads)))
        grads_kept.append(grad_inputs)
        if moment < MICRO:
            back_received = shifted(grad_inputs, "section", -1)
    shards = lax.psum_scatter(
        tuple((total[None] for total in totals)), "dp", scatter_dimension=1, tiled=True
    )
    input_grads = jnp.stack(
        [
            jnp.where(section_id == 0, grads_kept[micro_no + 1], grads_kept[micro_no])
            for micro_no in range(MICRO)
        ]
    )
    rows_dev = MICRO * per_micro * SLOT
    return (
        activations.reshape(1, rows_dev, D),
        input_grads.reshape(1, rows_dev, D),
        shards[0],
        shards[1],
        shards[2],
        shards[3],
        shards[4],
        shards[5],
        shards[6],
        shards[7],
        shards[8],
    )


def solution(mesh):
    in_specs = (
        P("dp", None),
        P("dp"),
        P("dp", None),
        P("section", "dp", None),
        P("section", "dp", None),
        P("section", "dp", None),
        P("section", "dp", None),
        P("section", "dp", None),
        P("section", "dp", None),
        P("section", "dp", None),
        P("section", "dp"),
        P("section", "dp"),
    )
    out_specs = (
        P("section", "dp", None),
        P("section", "dp", None),
        P("section", "dp", None),
        P("section", "dp", None),
        P("section", "dp", None),
        P("section", "dp", None),
        P("section", "dp", None),
        P("section", "dp", None),
        P("section", "dp", None),
        P("section", "dp"),
        P("section", "dp"),
    )
    return jax.shard_map(
        on_device, mesh=mesh, in_specs=in_specs, out_specs=out_specs, check_vma=False
    )
```

profile of v0, /device:TPU:1, one launch (start us, length us, event | category | flops | bytes accessed | tf_op | source)
XLA Modules:
  0.0 2107.0 jit_solution(15239131618581608521)
XLA Ops:
  18.1 35.8 %all-reduce.2 = (bf16[768]{0:T(1024)(128)(2,1)S(1)}, bf16[768]{0:T(1024)(128)(2,1)S(1)}) all-reduce(bf16[768]{0:T(1024)(128)(2,1)S(1)} %dynamic-update-slice, bf16[768]{0:T(1024)(128)(2,1)S(1)} %dynamic-update-slice.1), channel_id=1, replica_groups=mesh['section'=2,'dp'=16] {'dp'}, use_global_device_ids=true, to_apply=%add | all-reduce | flops 1536 | bytes 6144
  58.4 9.2 all-gather.8.cloned.1.call-done
  72.9 52.6 %all-gather.12.cloned.1.call-done = bf16[1,768,768]{2,1,0:T(8,128)(2,1)} async-done(((bf16[1,48,768]{2,1,0:T(8,128)(2,1)}), bf16[1,768,768]{2,1,0:T(8,128)(2,1)}) %all-gather.12.cloned.1.call-update) | async-done | bytes 1179664 | tf_op jit(solution)/shard_map/all_gather | solution.py:260
  137.7 45.7 %all-gather.10.cloned.1.call-done = bf16[1,768,768]{2,1,0:T(8,128)(2,1)} async-done(((bf16[1,48,768]{2,1,0:T(8,128)(2,1)}), bf16[1,768,768]{2,1,0:T(8,128)(2,1)}) %all-gather.10.cloned.1.call-update) | async-done | bytes 1179664 | tf_op jit(solution)/shard_map/all_gather | solution.py:259
  195.6 4.3 add_convert_fusion.10
  203.4 6.3 fusion.399
  209.6 4.4 fusion.204
  214.0 27.0 %all-gather.14.cloned.1.call-done = bf16[1,768,768]{2,1,0:T(8,128)(2,1)} async-done(((bf16[1,48,768]{2,1,0:T(8,128)(2,1)}), bf16[1,768,768]{2,1,0:T(8,128)(2,1)}) %all-gather.14.cloned.1.call-update) | async-done | bytes 1179664 | tf_op jit(solution)/shard_map/all_gather | solution.py:262
  241.0 3.5 multiply_reduce_fusion.14
  244.5 66.5 %all-gather.16.cloned.1.call-done = bf16[1,768,2048]{2,1,0:T(8,128)(2,1)} async-done(((bf16[1,48,2048]{2,1,0:T(8,128)(2,1)}), bf16[1,768,2048]{2,1,0:T(8,128)(2,1)}) %all-gather.16.cloned.1.call-update) | async-done | bytes 3145744 | tf_op jit(solution)/shard_map/all_gather | solution.py:263
  311.0 6.3 fusion.67
  317.3 63.0 %all-gather.20.cloned.1.call-done = bf16[1,2048,768]{2,1,0:T(8,128)(2,1)} async-done(((bf16[1,128,768]{2,1,0:T(8,128)(2,1)}), bf16[1,2048,768]{2,1,0:T(8,128)(2,1)}) %all-gather.20.cloned.1.call-update) | async-done | bytes 3145744 | tf_op jit(solution)/shard_map/all_gather | solution.py:265
  380.3 69.4 %all-gather.18.cloned.1.call-done = bf16[1,768,2048]{2,1,0:T(8,128)(2,1)} async-done(((bf16[1,48,2048]{2,1,0:T(8,128)(2,1)}), bf16[1,768,2048]{2,1,0:T(8,128)(2,1)}) %all-gather.18.cloned.1.call-update) | async-done | bytes 3145744 | tf_op jit(solution)/shard_map/all_gather | solution.py:264
  449.8 9.2 multiply_convert_fusion.26
  467.7 3.8 fusion.28
  502.8 4.5 add_convert_fusion.8
  510.8 6.3 fusion.400
  517.1 3.5 fusion.203
  522.6 4.1 fusion.65
  526.7 9.7 multiply_convert_fusion.24
  575.3 3.5 fusion.250
  587.8 3.5 fusion.232
  613.3 3.7 fusion.226
  626.0 3.3 fusion.240
  638.4 12.4 add_convert_fusion
  654.9 5.9 fusion.402
  660.8 3.8 fusion.184
  675.9 6.8 fusion.403
  682.7 3.7 fusion.196
  693.1 5.0 fusion.404
  698.1 3.8 fusion.190
  710.3 4.8 multiply_convert_fusion.11
  722.9 4.0 fusion.187
  727.0 6.9 multiply_reduce_fusion.2
  733.9 4.3 multiply_convert_fusion.2
  749.7 4.6 collective-permute-start.2
  775.2 4.2 fusion.193
  779.5 6.8 multiply_reduce_fusion.1
  786.3 4.3 multiply_convert_fusion.1
  825.7 5.1 fusion.199
  830.9 6.8 multiply_reduce_fusion
  837.7 4.3 multiply_convert_fusion
  848.9 9.8 fusion.144
  858.7 3.6 fusion.383
  873.7 5.1 fusion.100
  898.2 3.8 fusion.411
  904.0 5.2 fusion.13
  909.5 3.8 fusion.413
  915.2 5.3 fusion.10
  921.1 6.2 fusion.102
  931.5 4.9 fusion.7
  946.3 6.3 fusion.401
  952.6 3.6 fusion.202
  958.1 3.9 fusion.63
  962.0 9.6 fusion.270
  976.7 14.1 reduce-scatter.28.cloned.1.call-done
  992.1 124.7 %reduce-scatter.30.cloned.1.call-done = f32[48,1]{1,0:T(8,128)} async-done(((f32[768,1]{1,0:T(8,128)}), f32[48,1]{1,0:T(8,128)}) %reduce-scatter.30.cloned.1.call-update) | async-done | bytes 208
  1118.2 130.7 %reduce-scatter.14.cloned.1.call-done = f32[1,48,768]{2,1,0:T(8,128)} async-done(((f32[1,768,768]{2,1,0:T(8,128)}), f32[1,48,768]{2,1,0:T(8,128)}) %reduce-scatter.14.cloned.1.call-update) | async-done | bytes 147472 | tf_op jit(solution)/shard_map/reduce_scatter | solution.py:323
  1248.9 132.9 %reduce-scatter.16.cloned.1.call-done = f32[1,48,768]{2,1,0:T(8,128)} async-done(((f32[1,768,768]{2,1,0:T(8,128)}), f32[1,48,768]{2,1,0:T(8,128)}) %reduce-scatter.16.cloned.1.call-update) | async-done | bytes 147472 | tf_op jit(solution)/shard_map/reduce_scatter | solution.py:323
  1381.8 132.1 %reduce-scatter.18.cloned.1.call-done = f32[1,48,768]{2,1,0:T(8,128)} async-done(((f32[1,768,768]{2,1,0:T(8,128)}), f32[1,48,768]{2,1,0:T(8,128)}) %reduce-scatter.18.cloned.1.call-update) | async-done | bytes 147472 | tf_op jit(solution)/shard_map/reduce_scatter | solution.py:323
  1513.9 133.1 %reduce-scatter.20.cloned.1.call-done = f32[1,48,768]{2,1,0:T(8,128)} async-done(((f32[1,768,768]{2,1,0:T(8,128)}), f32[1,48,768]{2,1,0:T(8,128)}) %reduce-scatter.20.cloned.1.call-update) | async-done | bytes 147472 | tf_op jit(solution)/shard_map/reduce_scatter | solution.py:323
  1647.0 151.7 %reduce-scatter.22.cloned.1.call-done = f32[1,48,2048]{2,1,0:T(8,128)} async-done(((f32[1,768,2048]{2,1,0:T(8,128)}), f32[1,48,2048]{2,1,0:T(8,128)}) %reduce-scatter.22.cloned.1.call-update) | async-done | bytes 393232 | tf_op jit(solution)/shard_map/reduce_scatter | solution.py:323
  1798.7 151.0 %reduce-scatter.24.cloned.1.call-done = f32[1,48,2048]{2,1,0:T(8,128)} async-done(((f32[1,768,2048]{2,1,0:T(8,128)}), f32[1,48,2048]{2,1,0:T(8,128)}) %reduce-scatter.24.cloned.1.call-update) | async-done | bytes 393232 | tf_op jit(solution)/shard_map/reduce_scatter | solution.py:323
  1949.7 150.5 %reduce-scatter.26.cloned.1.call-done = f32[1,128,768]{2,1,0:T(8,128)} async-done(((f32[1,2048,768]{2,1,0:T(8,128)}), f32[1,128,768]{2,1,0:T(8,128)}) %reduce-scatter.26.cloned.1.call-update) | async-done | bytes 393232 | tf_op jit(solution)/shard_map/reduce_scatter | solution.py:323
  (635 shorter events, 351.1 us)
Async XLA Ops:
  7.2 9.2 copy-start.169
  7.2 10.4 copy-start.167
  7.2 10.7 copy-start.168
  7.2 60.4 %all-gather.8.cloned.1.call-start = ((), (), s32[]{:S(2)}) async-start(), calls=%async_computation.9 | async-start | bytes 1253376 | tf_op jit(solution)/shard_map/all_gather | solution.py:261
  7.9 117.5 %all-gather.12.cloned.1.call-start = ((), (), s32[]{:S(2)}) async-start(), calls=%async_computation.11 | async-start | bytes 1253376 | tf_op jit(solution)/shard_map/all_gather | solution.py:260
  8.7 174.6 %all-gather.10.cloned.1.call-start = ((), (), s32[]{:S(2)}) async-start(), calls=%async_computation.10 | async-start | bytes 1253376 | tf_op jit(solution)/shard_map/all_gather | solution.py:259
  9.4 231.6 %all-gather.14.cloned.1.call-start = ((), (), s32[]{:S(2)}) async-start(), calls=%async_computation.12 | async-start | bytes 1253376 | tf_op jit(solution)/shard_map/all_gather | solution.py:262
  10.0 301.0 %all-gather.16.cloned.1.call-start = ((), (), s32[]{:S(2)}) async-start(), calls=%async_computation.13 | async-start | bytes 3342336 | tf_op jit(solution)/shard_map/all_gather | solution.py:263
  10.6 369.7 %all-gather.20.cloned.1.call-start = ((), (), s32[]{:S(2)}) async-start(), calls=%async_computation.15 | async-start | bytes 3342336 | tf_op jit(solution)/shard_map/all_gather | solution.py:265
  11.2 438.6 %all-gather.18.cloned.1.call-start = ((), (), s32[]{:S(2)}) async-start(), calls=%async_computation.14 | async-start | bytes 3342336 | tf_op jit(solution)/shard_map/all_gather | solution.py:264
  11.9 978.9 %reduce-scatter.28.cloned.1.call-start = ((), (), s32[]{:S(2)}) async-start(), calls=%async_computation.23 | async-start | bytes 417792
  15.4 456.1 %copy-start.17 = (bf16[512,768]{1,0:T(8,128)(2,1)}, bf16[512,768]{1,0:T(8,128)(2,1)S(1)}, u32[]{:S(2)}) copy-start(bf16[512,768]{1,0:T(8,128)(2,1)S(1)} %get-tuple-element.36) | copy-start | bytes 2359300
  54.6 448.2 %copy-start.16 = (f32[256,768]{1,0:T(8,128)}, f32[256,768]{1,0:T(8,128)S(1)}, u32[]{:S(2)}) copy-start(f32[256,768]{1,0:T(8,128)S(1)} %copy.226) | copy-start | bytes 2359300
  203.4 6.3 copy-start.102
  311.0 138.7 %copy-start.137 = (f32[2,256]{1,0:T(2,128)S(1)}, f32[2,256]{1,0:T(2,128)}, u32[]{:S(2)}) copy-start(f32[2,256]{1,0:T(2,128)} %get-tuple-element.196) | copy-start | bytes 6148
  459.0 12.5 collective-permute-start
  510.8 6.3 copy-start.103
  521.6 5.1 copy-start.171
  536.4 24.5 %collective-permute-start.1 = (bf16[2,256,768]{2,1,0:T(8,128)(2,1)}, bf16[2,256,768]{2,1,0:T(8,128)(2,1)}, u32[]{:S(2)}, u32[]{:S(2)}) collective-permute-start(bf16[2,256,768]{2,1,0:T(8,128)(2,1)} %multiply_convert_fusion.24), channel_id=1, source_target_pairs={{0,16},{1,17},{2,18},{3,19},{4,20},{5,21},{6,22},{7,23},{8,24},{9,... | collective-permute-start | bytes 2359304 | tf_op jit(solution)/shard_map/ppermute | solution.py:21
  562.6 123.9 %copy-start = (bf16[2,256,768]{2,1,0:T(8,128)(2,1)}, bf16[2,256,768]{2,1,0:T(8,128)(2,1)S(1)}, u32[]{:S(2)}) copy-start(bf16[2,256,768]{2,1,0:T(8,128)(2,1)S(1)} %get-tuple-element.28) | copy-start | bytes 2359300
  563.5 24.4 %copy-start.139 = (f32[2,256]{1,0:T(2,128)}, f32[2,256]{1,0:T(2,128)S(1)}, u32[]{:S(2)}) copy-start(f32[2,256]{1,0:T(2,128)S(1)} %add_rsqrt_fusion.7) | copy-start | bytes 6148
  564.0 103.2 %copy-start.112 = (f32[2,256]{1,0:T(2,128)}, f32[2,256]{1,0:T(2,128)S(1)}, u32[]{:S(2)}) copy-start(f32[2,256]{1,0:T(2,128)S(1)} %get-tuple-element.168) | copy-start | bytes 6148
  601.0 12.3 copy-start.114
  652.3 8.5 copy-start.70
  691.4 6.8 copy-start.66
  693.1 5.1 copy-start.68
  710.3 4.8 copy-start.172
  722.9 11.0 slice-start.4
  727.0 20.4 copy-start.76
  727.0 6.9 slice-start.5
  749.2 5.1 copy-start.28
  749.2 5.1 copy-start.143
  749.7 6.4 copy-start.62
  749.7 8.3 collective-permute-start.2
  756.2 4.9 copy-start.147
  758.0 6.3 copy-start.175
  758.1 11.4 copy-start.51
  775.2 11.1 slice-start.2
  779.5 20.0 copy-start.77
  779.5 6.8 slice-start.3
  803.1 5.4 collective-permute-start.3
  806.6 4.9 copy-start.148
  808.4 6.3 copy-start.180
  808.6 11.4 copy-start.53
  825.7 5.1 copy-start.99
  825.7 5.2 copy-start.107
  825.7 11.9 slice-start
  830.9 6.8 slice-start.1
  871.9 244.9 %reduce-scatter.30.cloned.1.call-start = ((), (), s32[]{:S(2)}) async-start(), calls=%async_computation.24 | async-start | bytes 417792
  873.6 375.2 %reduce-scatter.14.cloned.1.call-start = ((), (), s32[]{:S(2)}) async-start(), calls=%async_computation.16 | async-start | bytes 2506752 | tf_op jit(solution)/shard_map/reduce_scatter | solution.py:323
  878.8 503.0 %reduce-scatter.16.cloned.1.call-start = ((), (), s32[]{:S(2)}) async-start(), calls=%async_computation.17 | async-start | bytes 2506752 | tf_op jit(solution)/shard_map/reduce_scatter | solution.py:323
  884.6 629.3 %reduce-scatter.18.cloned.1.call-start = ((), (), s32[]{:S(2)}) async-start(), calls=%async_computation.18 | async-start | bytes 2506752 | tf_op jit(solution)/shard_map/reduce_scatter | solution.py:323
  890.7 756.3 %reduce-scatter.20.cloned.1.call-start = ((), (), s32[]{:S(2)}) async-start(), calls=%async_computation.19 | async-start | bytes 2506752 | tf_op jit(solution)/shard_map/reduce_scatter | solution.py:323
  898.1 900.6 %reduce-scatter.22.cloned.1.call-start = ((), (), s32[]{:S(2)}) async-start(), calls=%async_computation.20 | async-start | bytes 6684672 | tf_op jit(solution)/shard_map/reduce_scatter | solution.py:323
  909.2 1040.5 %reduce-scatter.24.cloned.1.call-start = ((), (), s32[]{:S(2)}) async-start(), calls=%async_computation.21 | async-start | bytes 6684672 | tf_op jit(solution)/shard_map/reduce_scatter | solution.py:323
  920.5 1179.7 %reduce-scatter.26.cloned.1.call-start = ((), (), s32[]{:S(2)}) async-start(), calls=%async_computation.22 | async-start | bytes 6684672 | tf_op jit(solution)/shard_map/reduce_scatter | solution.py:323
  921.1 6.2 copy-start.52
  921.1 6.2 copy-start.127
  921.1 6.2 copy-start.174
  921.1 6.7 copy-start.176
  940.4 4.7 copy-start.79
  946.3 6.3 copy-start.105
  957.2 4.8 copy-start.170
  962.0 9.6 copy-start.57
  (144 other events, 342.6 us)
Sparse Core Ops, SparseCore 0:
  10.8 56.7 all-gather.7
  70.4 54.9 all-gather.11
  128.3 54.9 all-gather.9
  186.0 54.9 all-gather.13
  243.6 67.3 all-gather.15
  313.7 66.6 all-gather.19
  383.1 66.6 all-gather.17
  872.0 118.7 reduce-scatter.27
  996.1 120.6 reduce-scatter.29
  1122.2 126.6 reduce-scatter.13
  1255.1 126.5 reduce-scatter.15
  1387.1 126.7 reduce-scatter.17
  1520.1 126.8 reduce-scatter.19
  1652.7 145.9 reduce-scatter.21
  1804.3 145.2 reduce-scatter.23
  1955.3 144.8 reduce-scatter.25
where the time goes:
time: 2120 us; the launch traced here: 2110 us
  waiting for transfers between devices  1460 us (69%)
  matrix products  313 us (15%)
  local copies, waits for them, and re-layouts  147 us (7%)
  other arithmetic  125 us (6%)
  blocking collectives  35.8 us (2%)
    reduce_scatter x7, waiting for transfers between devices, on_device(): lax.psum_scatter(tuple((total[None] for total in totals)), 'dp', scatter_...  982 us
    unnamed x18, waiting for transfers between devices  143 us
    dot_general x36, matrix products, project(): jnp.einsum('bsd,de->bse', left, weight, preferred_element_type=jnp.float32)  113 us
    all_gather x1, waiting for transfers between devices, on_device(): lax.all_gather(sharded[5], 'dp', axis=1, tiled=True)  69.4 us
    all_gather x1, waiting for transfers between devices, on_device(): lax.all_gather(sharded[4], 'dp', axis=1, tiled=True)  66.5 us
    all_gather x1, waiting for transfers between devices, on_device(): lax.all_gather(sharded[6], 'dp', axis=1, tiled=True)  63 us
    dot_general x21, matrix products, weight_grad(): jnp.einsum('bsd,bse->de', left, grad_right, preferred_element_type=jnp.fl...  62.4 us
    all_gather x1, waiting for transfers between devices, on_device(): lax.all_gather(sharded[1], 'dp', axis=1, tiled=True)  52.6 us
  transfers between devices with their start and end apart: 20, of which 16 were waited for; matrix products, arithmetic and copies ran while one was open for 10% of the time, Pallas kernels for 0%

commit v1 on v0

v1 whole, which is shorter than its diff:
```python
import functools

import jax
import jax.numpy as jnp
import numpy as np
from jax import lax
from jax.experimental import pallas as pl
from jax.experimental.pallas import tpu as pltpu
from jax.sharding import PartitionSpec as P

D = 768
HEADS = 12
HEAD_DIM = 64
FF = 2048
WIDE = 16
SLOT = 256
HALF = D // 2
FHALF = FF // 2
PAIRS = HEADS // 2
LANES = 128
EPS = 1e-05
SCALE = 0.125
F32 = jnp.float32
BF16 = jnp.bfloat16
VMEM_BYTES = 56 * 1024 * 1024

X, Y, ZL, ZH = 1, 2, 4, 8
GATHER_ORDERS = (
    (ZH, Y, X, ZL),
    (ZH, ZL, X, Y),
    (ZH, Y, ZL, X),
    (ZL, X, ZH, Y),
    (ZH, Y, X, ZL),
    (ZH, ZL, Y, X),
)
SCATTER_ORDERS = ((X, Y, ZL, ZH), (Y, X, ZL, ZH))


def order_masks(order):
    masks = [0]
    for bit in order:
        masks = masks + [m ^ bit for m in masks]
    return masks


def flip(value, bit, count):
    return lax.ppermute(value, "dp", [(i, i ^ bit) for i in range(count)])


def swap(value):
    return lax.ppermute(value, "section", [(0, 1), (1, 0)])


def rope_consts():
    position = np.arange(SLOT)
    index = np.maximum(position - 1, 0)
    started = (position > 0).astype(np.float32)
    row_pos = (index // WIDE).astype(np.float32) * started
    col_pos = (index % WIDE).astype(np.float32) * started
    quarter = HEAD_DIM // 4
    freq = np.power(np.float32(10000.0), -np.arange(quarter, dtype=np.float32) / quarter)
    row_angle = row_pos[:, None] * freq[None, :]
    col_angle = col_pos[:, None] * freq[None, :]
    angle = np.concatenate([row_angle, row_angle, col_angle, col_angle], axis=1)
    angle = np.concatenate([angle, angle], axis=1).astype(np.float32)
    even = (np.arange(LANES) // quarter) % 2 == 0
    sine = np.sin(angle)
    return (
        np.cos(angle).astype(np.float32),
        np.where(even, -sine, 0.0).astype(np.float32),
        np.where(even, 0.0, sine).astype(np.float32),
    )


def dot(left, right):
    return jnp.dot(left, right, preferred_element_type=F32)


def dot_nt(left, right):
    return lax.dot_general(left, right, (((1,), (1,)), ((), ())), preferred_element_type=F32)


def dot_tn(left, right):
    return lax.dot_general(left, right, (((0,), (0,)), ((), ())), preferred_element_type=F32)


def turn(value, sin_a, sin_b):
    return pltpu.roll(value, LANES - 16, 1) * sin_a + pltpu.roll(value, 16, 1) * sin_b


def params(steps=1):
    return pltpu.CompilerParams(
        dimension_semantics=("arbitrary",) * steps, vmem_limit_bytes=VMEM_BYTES
    )


def cost(flops, nbytes):
    return pl.CostEstimate(flops=int(flops), bytes_accessed=int(nbytes), transcendentals=0)


def shape(*dims, dtype=BF16):
    return jax.ShapeDtypeStruct(dims, dtype)


def launch(kernel, prefetch, grid, inputs, in_specs, out_shape, out_specs, work, scratch=(), after=()):
    first = len(prefetch) + len(inputs)
    extra = len(after)

    def body(*refs):
        kernel(*refs[:first], *refs[first + extra :])

    return pl.pallas_call(
        body,
        grid_spec=pltpu.PrefetchScalarGridSpec(
            num_scalar_prefetch=len(prefetch),
            grid=grid,
            in_specs=list(in_specs) + [pl.BlockSpec(memory_space=pl.ANY)] * extra,
            out_specs=out_specs,
            scratch_shapes=list(scratch),
        ),
        out_shape=out_shape,
        compiler_params=params(len(grid)),
        cost_estimate=work,
    )(*prefetch, *inputs, *after)


def head_split(pair):
    lane = lax.broadcasted_iota(jnp.int32, pair.shape, 1)
    zero = jnp.zeros_like(pair)
    return jnp.where(lane < HEAD_DIM, pair, zero), jnp.where(lane < HEAD_DIM, zero, pair)


def attention_kernel(
    info, lim, x_ref, wq, wk, wv, cos, sin_a, sin_b, act_ref, qkv_ref, probs_ref, scale_ref
):
    image = pl.program_id(0)
    x = x_ref[...].astype(F32)
    r = lax.rsqrt(jnp.mean(x * x, axis=1, keepdims=True) + EPS)
    normed = (x * r).astype(BF16)
    act_ref[:, :D] = normed
    scale_ref[...] = jnp.broadcast_to(r, (SLOT, LANES))
    for part, weight in enumerate((wq, wk)):
        full = dot(normed, weight[...])
        for p in range(PAIRS):
            piece = full[:, p * LANES : (p + 1) * LANES]
            piece = piece * cos[...] + turn(piece, sin_a[...], sin_b[...])
            start = part * D + p * LANES
            qkv_ref[:, start : start + LANES] = piece.astype(BF16)
    qkv_ref[:, 2 * D :] = dot(normed, wv[...]).astype(BF16)
    row = lax.broadcasted_iota(jnp.int32, (SLOT, SLOT), 0)
    col = lax.broadcasted_iota(jnp.int32, (SLOT, SLOT), 1)
    mask = (col <= row) & (col < lim[info[1] * 2 + image])
    for p in range(PAIRS):
        lanes = slice(p * LANES, (p + 1) * LANES)
        query = qkv_ref[:, lanes]
        keys = head_split(qkv_ref[:, D + p * LANES : D + (p + 1) * LANES])
        values = head_split(qkv_ref[:, 2 * D + p * LANES : 2 * D + (p + 1) * LANES])
        probs = []
        for h in range(2):
            scores = jnp.where(mask, dot_nt(query, keys[h]), -1e30)
            top = jnp.max(scores, axis=1, keepdims=True)
            raised = jnp.exp(scores - top)
            total = jnp.sum(raised, axis=1, keepdims=True)
            probs.append((raised * (1.0 / total)).astype(BF16))
            probs_ref[0, 2 * p + h] = probs[h]
        mixed = dot(jnp.concatenate(probs, axis=1), jnp.concatenate(values, axis=0))
        act_ref[:, D + p * LANES : D + (p + 1) * LANES] = mixed.astype(BF16)


def attention(info, lim, x, x_rows, wq, wk, wv, tables, after=()):
    whole = lambda i, info, lim: (0, 0)
    table = pl.BlockSpec((SLOT, LANES), whole)
    weight = pl.BlockSpec((D, D), whole)
    return launch(
        attention_kernel,
        (info, lim,),
        (2,),
        (x, wq, wk, wv, *tables,),
        [
                pl.BlockSpec((SLOT, D), lambda i, info, lim: (info[x_rows] * 2 + i, 0)),
                weight,
                weight,
                weight,
                table,
                table,
                table,
            ],
        [
            shape(2 * SLOT, 2 * D),
            shape(2 * SLOT, 3 * D),
            shape(2, HEADS, SLOT, SLOT),
            shape(2 * SLOT, LANES, dtype=F32),
        ],
        [
                pl.BlockSpec((SLOT, 2 * D), lambda i, info, lim: (i, 0)),
                pl.BlockSpec((SLOT, 3 * D), lambda i, info, lim: (i, 0)),
                pl.BlockSpec((1, HEADS, SLOT, SLOT), lambda i, info, lim: (i, 0, 0, 0)),
                pl.BlockSpec((SLOT, LANES), lambda i, info, lim: (i, 0)),
            ],
        cost(3.6e9 + 24 * 4 * 256 * 256 * 128, 12e6),
        (),
        after,
    )


FBLOCK = 512


def feed_kernel(
    info, x_ref, mixed_ref, wo, wg, wu, middle_ref, normed_ref, scale_ref, hid_ref, s1_ref, s2_ref
):
    step = pl.program_id(0)

    @pl.when(step == 0)
    def _():
        middle = x_ref[...].astype(F32) + dot(mixed_ref[...], wo[...])
        r = lax.rsqrt(jnp.mean(middle * middle, axis=1, keepdims=True) + EPS)
        middle_ref[...] = middle
        normed_ref[...] = (middle * r).astype(BF16)
        scale_ref[...] = jnp.broadcast_to(r, scale_ref.shape)

    gate = dot(normed_ref[...], wg[...])
    up = dot(normed_ref[...], wu[...])
    sig = 1.0 / (1.0 + jnp.exp(-gate))
    silu = gate * sig
    hid_ref[...] = (silu * up).astype(BF16)
    s1_ref[...] = (up * (sig * (1.0 + gate * (1.0 - sig)))).astype(BF16)
    s2_ref[...] = silu.astype(BF16)


def feed(info, x, x_rows, act, wo, wg, wu, after=()):
    rows = 2 * SLOT
    whole = lambda j, info: (0, 0)
    col = pl.BlockSpec((D, FBLOCK), lambda j, info: (0, j))
    wide = pl.BlockSpec((rows, FBLOCK), lambda j, info: (0, j))
    return launch(
        feed_kernel,
        (info,),
        (FF // FBLOCK,),
        (x, act, wo, wg, wu,),
        [
                pl.BlockSpec((rows, D), lambda j, info: (info[x_rows], 0)),
                pl.BlockSpec((rows, D), lambda j, info: (0, 1)),
                pl.BlockSpec((D, D), whole),
                col,
                col,
            ],
        [
            shape(rows, D, dtype=F32),
            shape(rows, D),
            shape(rows, LANES, dtype=F32),
            shape(rows, FF),
            shape(rows, FF),
            shape(rows, FF),
        ],
        [
                pl.BlockSpec((rows, D), whole),
                pl.BlockSpec((rows, D), whole),
                pl.BlockSpec((rows, LANES), whole),
                wide,
                wide,
                wide,
            ],
        cost(2 * rows * D * (D + 2 * FF), 18e6),
        (),
        after,
    )


def leave_kernel(info, lim, middle_ref, hid_ref, wd, out_ref):
    image = pl.program_id(0)
    result = middle_ref[...] + dot(hid_ref[...], wd[...])
    row = lax.broadcasted_iota(jnp.int32, result.shape, 0)
    out_ref[...] = jnp.where(row < lim[info[1] * 2 + image], result, 0.0).astype(BF16)


def leave(info, lim, middle, hidden, wd, after=()):
    rows = 2 * SLOT
    return launch(
        leave_kernel,
        (info, lim,),
        (2,),
        (middle, hidden, wd,),
        [
                pl.BlockSpec((SLOT, D), lambda i, info, lim: (i, 0)),
                pl.BlockSpec((SLOT, FF), lambda i, info, lim: (i, 0)),
                pl.BlockSpec((FF, D), lambda i, info, lim: (0, 0)),
            ],
        shape(rows, D),
        pl.BlockSpec((SLOT, D), lambda i, info, lim: (i, 0)),
        cost(2 * rows * D * FF, 8e6),
        (),
        after,
    )


def feed_back_kernel(
    info,
    grad_ref,
    wd,
    wg,
    wu,
    s1_ref,
    s2_ref,
    normed_ref,
    scale_ref,
    wo,
    keep_ref,
    send_ref,
    gmid_ref,
    gz_ref,
    gmix_ref,
    total,
):
    step = pl.program_id(0)
    per_half = FHALF // FBLOCK
    grad_hidden = dot_nt(grad_ref[...], wd[...])
    ggate = (grad_hidden * s1_ref[...].astype(F32)).astype(BF16)
    gup = (grad_hidden * s2_ref[...].astype(F32)).astype(BF16)
    at = pl.multiple_of((step % per_half) * FBLOCK, FBLOCK)
    own = (step // per_half) == info[1]

    @pl.when(own)
    def _():
        keep_ref[:, pl.ds(at, FBLOCK)] = ggate
        keep_ref[:, pl.ds(at + FHALF, FBLOCK)] = gup

    @pl.when(jnp.logical_not(own))
    def _():
        send_ref[:, pl.ds(at, FBLOCK)] = ggate
        send_ref[:, pl.ds(at + FHALF, FBLOCK)] = gup

    part = dot_nt(ggate, wg[...]) + dot_nt(gup, wu[...])

    @pl.when(step == 0)
    def _():
        total[...] = part

    @pl.when(step > 0)
    def _():
        total[...] += part

    @pl.when(step == pl.num_programs(0) - 1)
    def _():
        gn = total[...]
        normed = normed_ref[...].astype(F32)
        mean = jnp.mean(gn * normed, axis=1, keepdims=True)
        gmid = grad_ref[...].astype(F32) + scale_ref[:, :1] * (gn - normed * mean)
        gz = gmid.astype(BF16)
        gmid_ref[...] = gmid
        gz_ref[...] = gz
        gmix_ref[...] = dot_nt(gz, wo[...]).astype(BF16)


def feed_back(info, grad, grad_rows, wd, wg, wu, s1, s2, normed, scale, wo, after=()):
    rows = 2 * SLOT
    whole = lambda j, info: (0, 0)
    col = pl.BlockSpec((D, FBLOCK), lambda j, info: (0, j))
    wide = pl.BlockSpec((rows, FBLOCK), lambda j, info: (0, j))
    full = pl.BlockSpec((rows, D), whole)
    return launch(
        feed_back_kernel,
        (info,),
        (FF // FBLOCK,),
        (grad, wd, wg, wu, s1, s2, normed, scale, wo,),
        [
                pl.BlockSpec((rows, D), lambda j, info: (info[grad_rows], 0)),
                pl.BlockSpec((FBLOCK, D), lambda j, info: (j, 0)),
                col,
                col,
                wide,
                wide,
                full,
                pl.BlockSpec((rows, LANES), whole),
                pl.BlockSpec((D, D), whole),
            ],
        [
            shape(rows, FF),
            shape(rows, FF),
            shape(rows, D, dtype=F32),
            shape(rows, D),
            shape(rows, D),
        ],
        [
                pl.BlockSpec((rows, FF), whole),
                pl.BlockSpec((rows, FF), whole),
                full,
                full,
                full,
            ],
        cost(2 * rows * D * (3 * FF + D), 24e6),
        [pltpu.VMEM((rows, D), F32)],
        after,
    )


def attention_back_kernel(
    info,
    gmix_ref,
    qkv_ref,
    probs_ref,
    wq,
    wk,
    wv,
    normed_ref,
    scale_ref,
    gmid_ref,
    gz_ref,
    cos,
    sin_a,
    sin_b,
    gin_ref,
    keep_ref,
    send_ref,
    grads,
):
    for p in range(PAIRS):
        lanes = slice(p * LANES, (p + 1) * LANES)
        gmix = gmix_ref[:, lanes]
        query = head_split(qkv_ref[:, lanes])
        keys = head_split(qkv_ref[:, D + p * LANES : D + (p + 1) * LANES])
        values = head_split(qkv_ref[:, 2 * D + p * LANES : 2 * D + (p + 1) * LANES])
        gmix_parts = head_split(gmix)
        gs_parts = []
        for h in range(2):
            probs = probs_ref[0, 2 * p + h].astype(F32)
            weighted = probs * dot_nt(gmix, values[h])
            inner = jnp.sum(weighted, axis=1, keepdims=True)
            gs_parts.append((weighted - probs * inner).astype(BF16))
        gq = dot(jnp.concatenate(gs_parts, axis=1), jnp.concatenate(keys, axis=0))
        gk = dot_tn(gs_parts[0], query[0]) + dot_tn(gs_parts[1], query[1])
        gv = dot_tn(probs_ref[0, 2 * p], gmix_parts[0]) + dot_tn(
            probs_ref[0, 2 * p + 1], gmix_parts[1]
        )
        gq = gq * cos[...] - turn(gq, sin_a[...], sin_b[...])
        gk = gk * cos[...] - turn(gk, sin_a[...], sin_b[...])
        grads[0, :, lanes] = gq.astype(BF16)
        grads[1, :, lanes] = gk.astype(BF16)
        grads[2, :, lanes] = gv.astype(BF16)
    gn = dot_nt(grads[0], wq[...]) + dot_nt(grads[1], wk[...]) + dot_nt(grads[2], wv[...])
    normed = normed_ref[...].astype(F32)
    mean = jnp.mean(gn * normed, axis=1, keepdims=True)
    gin = gmid_ref[...] + scale_ref[:, :1] * (gn - normed * mean)
    gin_ref[...] = gin.astype(BF16)
    for h in range(2):

        @pl.when(info[1] == h)
        def _():
            for out, half in ((keep_ref, h), (send_ref, 1 - h)):
                cols = slice(half * HALF, (half + 1) * HALF)
                out[:, :HALF] = gz_ref[:, cols]
                for part in range(3):
                    out[:, (part + 1) * HALF : (part + 2) * HALF] = grads[part, :, cols]


def attention_back(info, gmix, qkv, probs, wq, wk, wv, act, scale, gmid, gz, tables, after=()):
    rows = 2 * SLOT
    whole = lambda i, info: (0, 0)
    table = pl.BlockSpec((SLOT, LANES), whole)
    weight = pl.BlockSpec((D, D), whole)
    full = pl.BlockSpec((SLOT, D), lambda i, info: (i, 0))
    pack = pl.BlockSpec((SLOT, 4 * HALF), lambda i, info: (i, 0))
    return launch(
        attention_back_kernel,
        (info,),
        (2,),
        (gmix, qkv, probs, wq, wk, wv, act, scale, gmid, gz, *tables,),
        [
                full,
                pl.BlockSpec((SLOT, 3 * D), lambda i, info: (i, 0)),
                pl.BlockSpec((1, HEADS, SLOT, SLOT), lambda i, info: (i, 0, 0, 0)),
                weight,
                weight,
                weight,
                full,
                pl.BlockSpec((SLOT, LANES), lambda i, info: (i, 0)),
                full,
                full,
                table,
                table,
                table,
            ],
        [shape(rows, D), shape(rows, 4 * HALF), shape(rows, 4 * HALF)],
        [full, pack, pack],
        cost(2 * rows * D * 3 * D + 24 * 8 * 256 * 256 * 128, 16e6),
        [pltpu.VMEM((3, SLOT, D), BF16)],
        after,
    )


def spread(info, scratch, rows, row_from, row_count, lane_blocks, masks, keep, send, row_to):
    for place, mask in enumerate(masks):
        shard = info[0] ^ mask
        at = pl.multiple_of(shard * rows + row_from, 16)
        out = keep if place < 8 else send
        for block in range(lane_blocks):
            out[place % 8, pl.ds(row_to + block * row_count, row_count), :] = scratch[
                pl.ds(at, row_count), block * LANES : (block + 1) * LANES
            ]


def feed_weight_kernel(
    masks_p,
    masks_q,
    info,
    own_ref,
    oth_ref,
    g_own,
    g_oth,
    hid_own,
    hid_oth,
    gf_own,
    gf_oth,
    keep_p,
    send_p,
    keep_q,
    send_q,
    turned,
    tile,
    down,
):
    step = pl.program_id(0)
    rows = 2 * SLOT

    @pl.when(step == 0)
    def _():
        turned[:, :rows] = own_ref[...].T
        turned[:, rows:] = oth_ref[...].T

    @pl.when(step < 8)
    def _():
        tile[...] = (
            dot(turned[:, :rows], g_own[...]) + dot(turned[:, rows:], g_oth[...])
        ).astype(BF16)

    row_to = pl.multiple_of((step % 4) * 96, 16)

    @pl.when(step < 4)
    def _():
        spread(info, tile, 48, 0, 48, 2, masks_p, keep_p, send_p, row_to)

    @pl.when((step >= 4) & (step < 8))
    def _():
        spread(info, tile, 48, 0, 48, 2, masks_q, keep_q, send_q, row_to)

    @pl.when(step >= 8)
    def _():
        at = pl.multiple_of((step - 8) * FBLOCK, FBLOCK)
        down[pl.ds(at, FBLOCK), :] = (
            dot_tn(hid_own[...], gf_own[...]) + dot_tn(hid_oth[...], gf_oth[...])
        ).astype(BF16)

    @pl.when(step == 11)
    def _():
        spread(info, down, 128, 0, 64, 3, masks_p, keep_p, send_p, 384)
        spread(info, down, 128, 64, 64, 3, masks_q, keep_q, send_q, 384)


def feed_weight(info, masks, own, oth, g_own, g_oth, hid_own, hid_oth, gf_own, gf_oth, rows_of, after=()):
    rows = 2 * SLOT
    whole = lambda j, info: (0, 0)
    full = pl.BlockSpec((rows, D), whole)
    grad = pl.BlockSpec((rows, 256), lambda j, info: (0, jnp.minimum(j, 7)))
    hid = pl.BlockSpec((rows, FBLOCK), lambda j, info: (0, jnp.maximum(j - 8, 0)))
    out = pl.BlockSpec((8, 576, LANES), lambda j, info: (0, 0, 0))
    return launch(
        functools.partial(feed_weight_kernel, *masks),
        (info,),
        (12,),
        (own, oth, g_own, g_oth, hid_own, hid_oth, gf_own, gf_oth,),
        [
                full,
                full,
                grad,
                grad,
                hid,
                hid,
                pl.BlockSpec((rows, HALF), lambda j, info: (info[rows_of[0]], info[1])),
                pl.BlockSpec((rows, HALF), lambda j, info: (info[rows_of[1]], info[1])),
            ],
        [shape(8, 576, LANES)] * 4,
        [out] * 4,
        cost(2 * rows * D * 3 * FF, 20e6),
        [
                pltpu.VMEM((D, 2 * rows), BF16),
                pltpu.VMEM((D, 256), BF16),
                pltpu.VMEM((FF, HALF), BF16),
            ],
        after,
    )


def attention_weight_kernel(
    masks_p, masks_q, info, own_ref, oth_ref, g_own, g_oth, keep_p, send_p, keep_q, send_q, turned, tile
):
    step = pl.program_id(0)
    rows = 2 * SLOT

    @pl.when(step == 0)
    def _():
        turned[:, :rows] = own_ref[:, D:].T
        turned[:, rows:] = oth_ref[:, D:].T

    @pl.when(step == 1)
    def _():
        turned[:, :rows] = own_ref[:, :D].T
        turned[:, rows:] = oth_ref[:, :D].T

    tile[...] = (
        dot(turned[:, :rows], g_own[...]) + dot(turned[:, rows:], g_oth[...])
    ).astype(BF16)
    for at, (masks, keep, send, row_to) in enumerate(
        (
            (masks_q, keep_q, send_q, 144),
            (masks_p, keep_p, send_p, 0),
            (masks_p, keep_p, send_p, 144),
            (masks_q, keep_q, send_q, 0),
        )
    ):

        @pl.when(step == at)
        def _():
            spread(info, tile, 48, 0, 48, 3, masks, keep, send, row_to)


def attention_weight(info, masks, own, oth, g_own, g_oth, after=()):
    rows = 2 * SLOT
    whole = lambda j, info: (0, 0)
    full = pl.BlockSpec((rows, 2 * D), whole)
    grad = pl.BlockSpec((rows, HALF), lambda j, info: (0, j))
    out = pl.BlockSpec((8, 288, LANES), lambda j, info: (0, 0, 0))
    return launch(
        functools.partial(attention_weight_kernel, *masks),
        (info,),
        (4,),
        (own, oth, g_own, g_oth,),
        [full, full, grad, grad],
        [shape(8, 288, LANES)] * 4,
        [out] * 4,
        cost(2 * rows * D * 4 * D, 14e6),
        [pltpu.VMEM((D, 2 * rows), BF16), pltpu.VMEM((D, HALF), BF16)],
        after,
    )


def gather(own, order, count):
    have = own[None]
    for bit in order[:-1]:
        have = jnp.concatenate([have, flip(have, bit, count)], axis=0)
    return have, flip(have, order[-1], count)


def place_kernel(plan, n_src, info, *refs):
    srcs, outs, sem = refs[: 4 * n_src], refs[4 * n_src : -1], refs[-1]
    per_layer = len(outs) // 2

    def copies(first, side):
        found = []
        for n, (masks, pieces) in enumerate(plan):
            for place, mask in enumerate(masks):
                src = srcs[4 * n + 2 * side + place // 8]
                shard = info[0] ^ mask
                for row_from, rows, matrix, stride, offset in pieces:
                    at = pl.multiple_of(shard * stride + offset, 16)
                    found.append(
                        pltpu.make_async_copy(
                            src.at[place % 8, row_from : row_from + rows],
                            outs[first * per_layer + matrix].at[pl.ds(at, rows)],
                            sem,
                        )
                    )
        return found

    for section in range(2):

        @pl.when(info[1] == section)
        def _():
            for side in range(2):
                for copy in copies(section ^ side, side):
                    copy.start()

    for side in range(2):
        for copy in copies(side, side):
            copy.wait()


def place(info, plan, sources, dims, after=()):
    flat = [piece for source in sources for piece in source]
    anywhere = pl.BlockSpec(memory_space=pl.ANY)
    outs = launch(
        functools.partial(place_kernel, plan, len(sources)),
        (info,),
        (1,),
        (*flat,),
        [anywhere] * len(flat),
        [shape(*d) for d in dims] * 2,
        [pl.BlockSpec(d, lambda i, info: (0, 0)) for d in dims] * 2,
        cost(0, 4 * 2 * sum(a * b for a, b in dims)),
        [pltpu.SemaphoreType.DMA],
        after,
    )
    return outs[: len(dims)], outs[len(dims) :]


def gather_all(info, shards, count):
    w_q, w_k, w_v, w_o, w_g, w_u, w_d = shards
    half = w_d.shape[0] // 2
    row = w_q.shape[0]
    owns = (
        jnp.concatenate([w_q, w_k], axis=0),
        jnp.concatenate([w_v, w_o], axis=0),
        w_g,
        w_u,
        w_d[:half],
        w_d[half:],
    )
    found = []
    for own, order in zip(owns, GATHER_ORDERS):
        have, last = gather(own, order, count)
        found.append((have, last, swap(have), swap(last)))
    masks = [order_masks(order) for order in GATHER_ORDERS]
    pair = lambda a, b: ((0, row, a, row, 0), (row, row, b, row, 0))
    plan = ((masks[0], pair(0, 1)), (masks[1], pair(2, 3)))
    first = place(info, plan, found[0:2], ((D, D),) * 4)
    plan = ((masks[2], ((0, row, 0, row, 0),)), (masks[3], ((0, row, 1, row, 0),)))
    second = place(info, plan, found[2:4], ((D, FF),) * 2)
    plan = (
        (masks[4], ((0, half, 0, 2 * half, 0),)),
        (masks[5], ((0, half, 0, 2 * half, half),)),
    )
    third = place(info, plan, found[4:6], ((FF, D),))
    return tuple(tuple(first[n]) + tuple(second[n]) + tuple(third[n]) for n in range(2))


def gather_plain(section, shards):
    mine = [lax.all_gather(s, "dp", axis=0, tiled=True) for s in shards]
    theirs = [swap(m) for m in mine]
    low = tuple(jnp.where(section == 0, m, t) for m, t in zip(mine, theirs))
    high = tuple(jnp.where(section == 0, t, m) for m, t in zip(mine, theirs))
    return low, high


def scatter(keep, send, order, count):
    parts = [keep]
    for stage, bit in enumerate(order):
        parts.append(flip(send, bit, count))
        size = 8 >> stage
        if size == 1:
            break
        lower = size // 2
        send = sum(p[lower:size].astype(F32) for p in parts).astype(BF16)
    return sum(p[0].astype(F32) for p in parts)


def unpack_kernel(plan, gained, info, *refs):
    n_src = 1 + max(p[0] for p in plan)
    n_gain = len(gained)
    srcs, refs = refs[: 2 * n_src], refs[2 * n_src :]
    gain, weights, outs = refs[0], refs[1 : 1 + n_gain], refs[1 + n_gain :]
    for section in range(2):

        @pl.when(info[1] == section)
        def _():
            total = jnp.zeros((gain.shape[0], 1), F32)
            for n, (src, row_from, rows, row_to, scale, has_gain, out) in enumerate(plan):
                for side in range(2):
                    piece = srcs[2 * src + (section ^ side)]
                    width = outs[out].shape[1] // 2
                    for block in range(width // LANES):
                        at = row_from + block * rows
                        value = piece[at : at + rows, :]
                        col = side * width + block * LANES
                        if has_gain:
                            weight = weights[gained.index(n)][:, col : col + LANES].astype(F32)
                            total += scale * jnp.sum(weight * value, axis=1, keepdims=True)
                            value = value * (gain[...] * scale)
                        outs[out][row_to : row_to + rows, col : col + LANES] = value
            outs[-1][...] = jnp.broadcast_to(total, outs[-1].shape)


def unpack_all(info, plan, sources, gain, weights, dims, after=()):
    gained = tuple(n for n, p in enumerate(plan) if p[5])
    flat = [piece for source in sources for piece in source]
    return launch(
        functools.partial(unpack_kernel, plan, gained),
        (info,),
        (1,),
        (*flat, gain, *weights,),
        [pl.BlockSpec(v.shape, lambda i, info: (0, 0)) for v in (*flat, gain, *weights)],
        [shape(*d, dtype=F32) for d in dims],
        [pl.BlockSpec(d, lambda i, info: (0, 0)) for d in dims],
        cost(0, 8 * sum(a * b for a, b in dims)),
        (),
        after,
    )


def halves(section, first, second):
    mine = jnp.where(section == 0, first, second)
    return mine, swap(jnp.where(section == 0, second, first))


def on_device(
    tokens,
    heights,
    out_grad,
    w_query,
    w_key,
    w_value,
    w_out,
    w_gate,
    w_up,
    w_down,
    gain_attn,
    gain_ffn,
):
    section = lax.axis_index("section")
    me = lax.axis_index("dp")
    count = lax.axis_size("dp")
    halving = count == 16
    info = jnp.stack([me, section, 1 - section, jnp.zeros_like(me)]).astype(jnp.int32)
    own_rows, oth_rows, no_rows = 1, 2, 3
    lim = WIDE * heights + 1
    gain_one = gain_attn[0].astype(F32)[:, None]
    gain_two = gain_ffn[0].astype(F32)[:, None]
    fold = lambda w, g: (w[0].astype(F32) * g).astype(BF16)
    shards = (
        fold(w_query, gain_one * SCALE),
        fold(w_key, gain_one),
        fold(w_value, gain_one),
        w_out[0],
        fold(w_gate, gain_two),
        fold(w_up, gain_two),
        w_down[0],
    )
    if halving:
        layers = gather_all(info, shards, count)
    else:
        layers = gather_plain(section, shards)
    tables = tuple(jnp.asarray(t) for t in rope_consts())
    rows = 2 * SLOT
    slots = jnp.arange(SLOT)
    valid = (slots[None, :] < lim[:, None]).reshape(-1, 1)
    grad = jnp.where(valid, out_grad, jnp.zeros_like(out_grad))

    kept = []
    x, x_rows = tokens, own_rows
    for layer, (w_q, w_k, w_v, w_o, w_g, w_u, w_d) in enumerate(layers):
        act, qkv, probs, scale_one = attention(info, lim, x, x_rows, w_q, w_k, w_v, tables)
        middle, normed, scale_two, hidden, s1, s2 = feed(info, x, x_rows, act, w_o, w_g, w_u)
        others = (swap(act), swap(normed), swap(hidden))
        kept.append((act, qkv, probs, scale_one, normed, scale_two, hidden, s1, s2, others))
        if layer == 0:
            first = leave(info, lim, middle, hidden, w_d)
            x, x_rows = first, no_rows

    masks = tuple(order_masks(order[::-1]) for order in SCATTER_ORDERS)
    grad_own, grad_oth, grad_rows, oth_at = grad, grad, own_rows, oth_rows
    sums = [None, None]
    gins = [None, None]
    parts = [None, None]
    pending = None
    for layer in (1, 0):
        w_q, w_k, w_v, w_o, w_g, w_u, w_d = layers[layer]
        act, qkv, probs, scale_one, normed, scale_two, hidden, s1, s2, others = kept[layer]
        act_oth, normed_oth, hidden_oth = others
        keep, send, gmid, gz, gmix = feed_back(
            info, grad_own, grad_rows, w_d, w_g, w_u, s1, s2, normed, scale_two, w_o
        )
        recv = swap(send)
        earlier = (send,)
        if layer == 1:
            second = leave(info, lim, middle, hidden, w_d, after=earlier)
            earlier = (second,)
        elif halving:
            pending = attention_weight(info, masks, *parts[1], after=earlier)
            earlier = (pending[1],)
        if halving:
            formed = feed_weight(
                info,
                masks,
                normed,
                normed_oth,
                keep,
                recv,
                hidden,
                hidden_oth,
                grad_own,
                grad_oth,
                (grad_rows, oth_at),
                after=earlier,
            )
            earlier = (formed[1],)
        gin, keep_t, send_t = attention_back(
            info, gmix, qkv, probs, w_q, w_k, w_v, act, scale_one, gmid, gz, tables, after=earlier
        )
        recv_t = swap(send_t)
        gin_oth = swap(gin)
        gins[layer] = (gin, gin_oth)
        parts[layer] = (act, act_oth, keep_t, recv_t)
        if halving:
            kp, sp, kq, sq = formed
            sums[layer] = (
                scatter(kp, sp, SCATTER_ORDERS[0], count),
                scatter(kq, sq, SCATTER_ORDERS[1], count),
            )
        else:
            cut = lambda v, at: lax.dynamic_slice_in_dim(v, at * rows, rows, 0)
            pick = lambda v, at: cut(v, info[at]) if v.shape[0] > rows else v
            gf = jnp.concatenate([pick(grad_own, grad_rows), pick(grad_oth, oth_at)], axis=0)
            gf = lax.dynamic_slice_in_dim(gf, section * HALF, HALF, 1)
            both = lambda a, b: jnp.concatenate([a, b], axis=0)
            form = lambda a, g: lax.psum_scatter(
                lax.dot_general(a, g, (((0,), (0,)), ((), ())), preferred_element_type=F32),
                "dp",
                scatter_dimension=0,
                tiled=True,
            )
            acts, gts = both(act, act_oth), both(keep_t, recv_t)
            gus = both(keep, recv)
            nor = both(normed, normed_oth)
            sums[layer] = (
                form(acts[:, :D], gts[:, HALF : 2 * HALF]),
                form(acts[:, :D], gts[:, 2 * HALF : 3 * HALF]),
                form(acts[:, :D], gts[:, 3 * HALF :]),
                form(acts[:, D:], gts[:, :HALF]),
                form(nor, gus[:, :FHALF]),
                form(nor, gus[:, FHALF:]),
                form(both(hidden, hidden_oth), gf),
            )
        grad_own, grad_oth, grad_rows, oth_at = gin, gin_oth, no_rows, no_rows

    if halving:
        last = attention_weight(info, masks, *parts[0])
        for layer, (kp, sp, kq, sq) in ((1, pending), (0, last)):
            sums[layer] += (
                scatter(kp, sp, SCATTER_ORDERS[0], count),
                scatter(kq, sq, SCATTER_ORDERS[1], count),
            )
    shares = [halves(section, first, second) for first, second in zip(*sums)]
    if halving:
        row, tall = shards[0].shape[0], shards[6].shape[0] // 2
        split, side = row * FHALF // LANES, row * HALF // LANES
        plan = (
            (0, 0, row, 0, 1.0, True, 0),
            (1, 0, row, 0, 1.0, True, 1),
            (0, split, tall, 0, 1.0, False, 2),
            (1, split, tall, tall, 1.0, False, 2),
        )
        grad_g, grad_u, grad_d, gain_grad_two = unpack_all(
            info,
            plan,
            shares[:2],
            gain_two,
            (w_gate[0], w_up[0]),
            ((row, FF), (row, FF), (2 * tall, D), (row, LANES)),
        )
        plan = (
            (0, 0, row, 0, SCALE, True, 0),
            (0, side, row, 0, 1.0, True, 1),
            (1, 0, row, 0, 1.0, True, 2),
            (1, side, row, 0, 1.0, False, 3),
        )
        grad_q, grad_k, grad_v, grad_o, gain_grad_one = unpack_all(
            info,
            plan,
            shares[2:],
            gain_one,
            (w_query[0], w_key[0], w_value[0]),
            ((row, D),) * 4 + ((row, LANES),),
        )
        gain_grad_one, gain_grad_two = gain_grad_one[:, 0], gain_grad_two[:, 0]
    else:

        def cols(pair):
            mine, theirs = pair
            low = jnp.concatenate([mine, theirs], axis=1)
            return jnp.where(section == 0, low, jnp.concatenate([theirs, mine], axis=1))

        grad_q, grad_k, grad_v, grad_o, grad_g, grad_u, grad_d = (cols(s) for s in shares)
        along = lambda w, g: jnp.sum(w[0].astype(F32) * g, axis=1)
        gain_grad_one = SCALE * along(w_query, grad_q)
        gain_grad_one += along(w_key, grad_k) + along(w_value, grad_v)
        gain_grad_two = along(w_gate, grad_g) + along(w_up, grad_u)
        grad_q, grad_k, grad_v = grad_q * (gain_one * SCALE), grad_k * gain_one, grad_v * gain_one
        grad_g, grad_u = grad_g * gain_two, grad_u * gain_two

    def share(first, second, first_oth, second_oth):
        mine = jnp.where(section == 0, first, second)
        theirs = jnp.where(section == 0, first_oth, second_oth)
        return jnp.where(
            section == 0,
            jnp.concatenate([mine, theirs], axis=0),
            jnp.concatenate([theirs, mine], axis=0),
        )[None]

    theirs = swap(jnp.where(section == 0, second, first))
    activations = share(first, second, theirs, theirs)
    input_grads = share(gins[0][0], gins[1][0], gins[0][1], gins[1][1])
    return (
        activations,
        input_grads,
        grad_q[None],
        grad_k[None],
        grad_v[None],
        grad_o[None],
        grad_g[None],
        grad_u[None],
        grad_d[None],
        gain_grad_one[None],
        gain_grad_two[None],
    )


def solution(mesh):
    rows = P("dp", None)
    weight = P("section", "dp", None)
    gain = P("section", "dp")
    return jax.shard_map(
        on_device,
        mesh=mesh,
        in_specs=(rows, P("dp"), rows) + (weight,) * 7 + (gain,) * 2,
        out_specs=(weight,) * 9 + (gain,) * 2,
        check_vma=False,
    )
```

time: 2120 us -> 563 us (0.27)
  waiting for transfers between devices: 1460 us -> 183 us
  matrix products: 313 us -> 0 us
  Pallas kernels: 0 us -> 212 us
  local copies, waits for them, and re-layouts: 147 us -> 12.8 us
  starting transfers between devices: 9.93 us -> 103 us
  other arithmetic: 125 us -> 40.7 us
  blocking collectives: 35.8 us -> 0 us
    reduce_scatter x7 -> x0, waiting for transfers between devices: 982 us -> none  [on_device(): lax.psum_scatter(tuple((total[None] for total in totals)), 'dp', scatter_...]
    all_gather x7 -> x0, waiting for transfers between devices: 334 us -> none  [the longest x1 69.4 us: on_device(): lax.all_gather(sharded[5], 'dp', axis=1, tiled=True)]
    dot_general x96 -> x0, matrix products: 276 us -> none  [the longest x36 113 us: project(): jnp.einsum('bsd,de->bse', left, weight, preferred_element_type=jnp.float32)]
    pallas_call x0 -> x19, Pallas kernels: none -> 212 us  [launch(): pl.pallas_call(body, grid_spec=pltpu.PrefetchScalarGridSpec(num_scalar_pr...]
    ppermute x4 -> x85, waiting for transfers between devices: 0.01 us -> 183 us  [the longest x56 179 us: flip(): return lax.ppermute(value, 'dp', [(i, i ^ bit) for i in range(count)])]
    unnamed x18 -> x0, waiting for transfers between devices: 143 us -> none
    ppermute x4 -> x85, starting transfers between devices: 8.91 us -> 103 us  [the longest x56 54.5 us: flip(): return lax.ppermute(value, 'dp', [(i, i ^ bit) for i in range(count)])]
    convert_element_type x21 -> x2, local copies, waits for them, and re-layouts: 38.8 us -> 1.38 us  [the longest x1 0.69 us: on_device(): gain_one = gain_attn[0].astype(F32)[:, None]]
  transfers between devices with their start and end apart: 20 -> 85, of which waited for: 16 -> 30; matrix products, arithmetic and copies ran while one was open for 10% -> 8% of each run, Pallas kernels for 0% -> 22%
where the time goes in v1:
time: 563 us; the launch traced here: 554 us
  Pallas kernels  212 us (38%)
  waiting for transfers between devices  183 us (33%)
  starting transfers between devices  103 us (18%)
  other arithmetic  40.7 us (7%)
  local copies, waits for them, and re-layouts  12.8 us (2%)
    pallas_call x19, Pallas kernels, launch(): pl.pallas_call(body, grid_spec=pltpu.PrefetchScalarGridSpec(num_scalar_pr...  212 us
    ppermute x56, waiting for transfers between devices, flip(): return lax.ppermute(value, 'dp', [(i, i ^ bit) for i in range(count)])  179 us
    ppermute x56, starting transfers between devices, flip(): return lax.ppermute(value, 'dp', [(i, i ^ bit) for i in range(count)])  54.5 us
    ppermute x29, starting transfers between devices, swap(): return lax.ppermute(value, 'section', [(0, 1), (1, 0)])  48 us
    convert_element_type x24, other arithmetic, scatter(): send = sum((p[lower:size].astype(F32) for p in parts)).astype(BF16)  20.4 us
  transfers between devices with their start and end apart: 85, of which 30 were waited for; matrix products, arithmetic and copies ran while one was open for 8% of the time, Pallas kernels for 22%

profile of v1, /device:TPU:1, one launch (start us, length us, event | category | flops | bytes accessed | tf_op | source)
XLA Modules:
  0.0 553.7 jit_solution(1137403347567651765)
XLA Ops:
  3.1 3.2 collective-permute-start
  8.3 2.4 collective-permute-start.24
  12.9 14.9 %collective-permute-done.24 = bf16[1,64,768]{2,1,0:T(8,128)(2,1)S(1)} collective-permute-done((bf16[1,64,768]{2,1,0:T(8,128)(2,1)S(1)}, bf16[1,64,768]{2,1,0:T(8,128)(2,1)S(1)}, u32[]{:S(2)}, u32[]{:S(2)}) %collective-permute-start.24) | collective-permute-done | bytes 98336 | tf_op jit(solution)/shard_map/ppermute | solution.py:47
  27.8 8.4 %collective-permute-done.30 = bf16[1,64,768]{2,1,0:T(8,128)(2,1)S(1)} collective-permute-done((bf16[1,64,768]{2,1,0:T(8,128)(2,1)S(1)}, bf16[1,64,768]{2,1,0:T(8,128)(2,1)S(1)}, u32[]{:S(2)}, u32[]{:S(2)}) %collective-permute-start.30) | collective-permute-done | bytes 98336 | tf_op jit(solution)/shard_map/ppermute | solution.py:47
  43.5 4.4 collective-permute-done.1
  48.5 7.8 %collective-permute-done.13 = bf16[2,48,2048]{2,1,0:T(8,128)(2,1)S(1)} collective-permute-done((bf16[2,48,2048]{2,1,0:T(8,128)(2,1)S(1)}, bf16[2,48,2048]{2,1,0:T(8,128)(2,1)S(1)}, u32[]{:S(2)}, u32[]{:S(2)}) %collective-permute-start.13) | collective-permute-done | bytes 393248 | tf_op jit(solution)/shard_map/ppermute | solution.py:47
  57.6 1.9 collective-permute-start.14
  60.0 3.2 collective-permute-start.20
  64.7 1.8 collective-permute-start.27
  66.7 4.8 collective-permute-done.2
  71.4 4.7 collective-permute-start.28
  76.2 7.9 %collective-permute-done.8 = bf16[4,96,768]{2,1,0:T(8,128)(2,1)S(1)} collective-permute-done((bf16[4,96,768]{2,1,0:T(8,128)(2,1)S(1)}, bf16[4,96,768]{2,1,0:T(8,128)(2,1)S(1)}, u32[]{:S(2)}, u32[]{:S(2)}) %collective-permute-start.8) | collective-permute-done | bytes 589856 | tf_op jit(solution)/shard_map/ppermute | solution.py:47
  84.8 5.3 collective-permute-done.14
  90.7 7.7 %collective-permute-start.34 = (bf16[8,64,768]{2,1,0:T(8,128)(2,1)S(1)}, bf16[8,64,768]{2,1,0:T(8,128)(2,1)S(1)}, u32[]{:S(2)}, u32[]{:S(2)}) collective-permute-start(bf16[8,64,768]{2,1,0:T(8,128)(2,1)S(1)} %pad_maximum_fusion.7.refs_5_), channel_id=1, source_target_pairs={{0,16},{16,0},{1,17},{17,1},{2,18},{18,2},{3,19},{19,3},{4,20},{20... | collective-permute-start | bytes 2359304 | tf_op jit(solution)/shard_map/ppermute | solution.py:51
  98.4 9.4 %collective-permute-done.27.refs_2_ = bf16[8,64,768]{2,1,0:T(8,128)(2,1)S(1)} collective-permute-done((bf16[8,64,768]{2,1,0:T(8,128)(2,1)S(1)}, bf16[8,64,768]{2,1,0:T(8,128)(2,1)S(1)}, u32[]{:S(2)}, u32[]{:S(2)}) %collective-permute-start.27) | collective-permute-done | bytes 786464 | tf_op jit(solution)/shard_map/ppermute | solution.py:47
  107.8 7.5 %collective-permute-start.4 = (bf16[8,96,768]{2,1,0:T(8,128)(2,1)S(1)}, bf16[8,96,768]{2,1,0:T(8,128)(2,1)S(1)}, u32[]{:S(2)}, u32[]{:S(2)}) collective-permute-start(bf16[8,96,768]{2,1,0:T(8,128)(2,1)S(1)} %pad_maximum_fusion.2.refs_1_), channel_id=1, source_target_pairs={{0,16},{16,0},{1,17},{17,1},{2,18},{18,2},{3,19},{19,3},{4,20},{20... | collective-permute-start | bytes 3538952 | tf_op jit(solution)/shard_map/ppermute | solution.py:51
  118.5 14.7 %collective-permute-done.3.refs_2_ = bf16[8,96,768]{2,1,0:T(8,128)(2,1)S(1)} collective-permute-done((bf16[8,96,768]{2,1,0:T(8,128)(2,1)S(1)}, bf16[8,96,768]{2,1,0:T(8,128)(2,1)S(1)}, u32[]{:S(2)}, u32[]{:S(2)}) %collective-permute-start.3) | collective-permute-done | bytes 1179680 | tf_op jit(solution)/shard_map/ppermute | solution.py:47
  134.1 4.4 collective-permute-start.5
  138.5 4.8 collective-permute-done.9.refs_6_
  144.4 1.8 collective-permute-done.29.refs_4_
  147.7 5.9 %collective-permute-done.15.refs_2_ = bf16[8,48,2048]{2,1,0:T(8,128)(2,1)} collective-permute-done((bf16[8,48,2048]{2,1,0:T(8,128)(2,1)S(1)}, bf16[8,48,2048]{2,1,0:T(8,128)(2,1)}, u32[]{:S(2)}, u32[]{:S(2)}) %collective-permute-start.15) | collective-permute-done | bytes 1572896 | tf_op jit(solution)/shard_map/ppermute | solution.py:47
  154.7 22.3 %collective-permute-done.21.refs_6_ = bf16[8,48,2048]{2,1,0:T(8,128)(2,1)} collective-permute-done((bf16[8,48,2048]{2,1,0:T(8,128)(2,1)S(1)}, bf16[8,48,2048]{2,1,0:T(8,128)(2,1)}, u32[]{:S(2)}, u32[]{:S(2)}) %collective-permute-start.21) | collective-permute-done | bytes 1572896 | tf_op jit(solution)/shard_map/ppermute | solution.py:47
  179.6 2.8 broadcast_select_fusion.refs_1_.refs_7_.refs_8_
  182.4 6.2 %shard_map.234 = (bf16[2048,768]{1,0:T(8,128)(2,1)}, bf16[2048,768]{1,0:T(8,128)(2,1)}) custom-call(s32[4]{0:T(128)} %pad_add_fusion.refs_0_, bf16[8,64,768]{2,1,0:T(8,128)(2,1)} %copy-done.4, bf16[8,64,768]{2,1,0:T(8,128)(2,1)} %copy-done.23, bf16[8,64,768]{2,1,0:T(8,128)(2,1)} %copy-done.24, bf16[8,64,768]{2,1,0:T(8,128)(2,1)} %copy-done.27, ...), custom_call_target="tpu_custom_call" | custom-call | bytes 12582912 | tf_op jit(solution)/shard_map/pallas_call | solution.py:112
  188.6 8.0 %shard_map.230 = (bf16[768,768]{1,0:T(8,128)(2,1)}, bf16[768,768]{1,0:T(8,128)(2,1)}, bf16[768,768]{1,0:T(8,128)(2,1)}, bf16[768,768]{1,0:T(8,128)(2,1)}, bf16[7...) custom-call(s32[4]{0:T(128)} %pad_add_fusion.refs_0_, ...), custom_call_target="tpu_custom_call" | custom-call | bytes 18874368 | tf_op jit(solution)/shard_map/pallas_call | solution.py:112
  196.6 12.5 %shard_map.231 = (bf16[512,1536]{1,0:T(8,128)(2,1)}, bf16[512,2304]{1,0:T(8,128)(2,1)}, bf16[2,12,256,256]{3,2,1,0:T(8,128)(2,1)}, f32[512,128]{1,0:T(8,128)}) custom-call(s32[4]{0:T(128)} %pad_add_fusion.refs_0_, s32[4]{0:T(128)} %copy-done.54, bf16[1024,768]{1,0:T(8,128)(2,1)} %refs_1_.1, bf16[768,768]{1,0:T(8,128)(2,1)} %get-tuple-element.86.refs_3_.refs_4_, ...), custom_call_target="tpu_custom_call" | custom-call | flops 4405306368 | bytes 12000000 | tf_op jit(solution)/shard_map/pallas_call | solution.py:112
  209.1 10.0 %shard_map.232 = (bf16[768,2048]{1,0:T(8,128)(2,1)}, bf16[768,2048]{1,0:T(8,128)(2,1)}, bf16[768,2048]{1,0:T(8,128)(2,1)}, bf16[768,2048]{1,0:T(8,128)(2,1)}) custom-call(s32[4]{0:T(128)} %pad_add_fusion.refs_0_, bf16[8,48,2048]{2,1,0:T(8,128)(2,1)} %copy-done, bf16[8,48,2048]{2,1,0:T(8,128)(2,1)} %collective-permute-done.15.refs_2_, ...), custom_call_target="tpu_custom_call" | custom-call | bytes 25165824 | tf_op jit(solution)/shard_map/pallas_call | solution.py:112
  219.1 10.8 %shard_map.233 = (f32[512,768]{1,0:T(8,128)}, bf16[512,768]{1,0:T(8,128)(2,1)}, f32[512,128]{1,0:T(8,128)}, bf16[512,2048]{1,0:T(8,128)(2,1)}, bf16[512,2048]{1,0:T(8,128)(2,1)}, /*index=5*/bf16[512,2048]{1,0:T(8,128)(2,1)}) custom-call(s32[4]{0:T(128)} %pad_add_fusion.refs_0_, bf16[1024,768]{1,0:T(8,128)(2,1)} %refs_1_.1, ...), custom_call_target="tpu_custom_call" | custom-call | flops 3825205248 | bytes 18000000 | tf_op jit(solution)/shard_map/pallas_call | solution.py:112
  230.0 5.9 %shard_map.235.refs_2_.refs_1_ = bf16[512,768]{1,0:T(8,128)(2,1)} custom-call(s32[4]{0:T(128)} %pad_add_fusion.refs_0_, s32[4]{0:T(128)} %copy-done.54, f32[512,768]{1,0:T(8,128)} %get-tuple-element.93.refs_2_, bf16[512,2048]{1,0:T(8,128)(2,1)} %get-tuple-element.94.refs_3_.refs_5_, bf16[2048,768]{1,0:T(8,128)(2,1)} %get-tuple-element.95.refs_4_.refs_2_), custom_call_target="tpu_custom_call" | custom-call | flops 1610612736 | bytes 8000000 | tf_op jit(solution)/shard_map/pallas_call | solution.py:112
  235.9 12.5 %shard_map.236 = (bf16[512,1536]{1,0:T(8,128)(2,1)}, bf16[512,2304]{1,0:T(8,128)(2,1)}, bf16[2,12,256,256]{3,2,1,0:T(8,128)(2,1)}, f32[512,128]{1,0:T(8,128)}) custom-call(s32[4]{0:T(128)} %pad_add_fusion.refs_0_, s32[4]{0:T(128)} %copy-done.54, bf16[512,768]{1,0:T(8,128)(2,1)} %shard_map.235.refs_2_.refs_1_, ...), custom_call_target="tpu_custom_call" | custom-call | flops 4405306368 | bytes 12000000 | tf_op jit(solution)/shard_map/pallas_call | solution.py:112
  248.4 10.8 %shard_map.237 = (f32[512,768]{1,0:T(8,128)}, bf16[512,768]{1,0:T(8,128)(2,1)}, f32[512,128]{1,0:T(8,128)}, bf16[512,2048]{1,0:T(8,128)(2,1)}, bf16[512,2048]{1,0:T(8,128)(2,1)}, /*index=5*/bf16[512,2048]{1,0:T(8,128)(2,1)}) custom-call(s32[4]{0:T(128)} %pad_add_fusion.refs_0_, bf16[512,768]{1,0:T(8,128)(2,1)} %shard_map.235.refs_2_.refs_1_, ...), custom_call_target="tpu_custom_call" | custom-call | flops 3825205248 | bytes 18000000 | tf_op jit(solution)/shard_map/pallas_call | solution.py:112
  259.2 17.9 %shard_map.238 = (bf16[512,2048]{1,0:T(8,128)(2,1)}, bf16[512,2048]{1,0:T(8,128)(2,1)}, f32[512,768]{1,0:T(8,128)}, bf16[512,768]{1,0:T(8,128)(2,1)}, bf16[512,768]{1,0:T(8,128)(2,1)}) custom-call(s32[4]{0:T(128)} %pad_add_fusion.refs_0_, bf16[1024,768]{1,0:T(8,128)(2,1)} %broadcast_select_fusion.refs_1_.refs_7_.refs_8_, ...), custom_call_target="tpu_custom_call" | custom-call | flops 5435817984 | bytes 24000000 | tf_op jit(solution)/shard_map/pallas_call | solution.py:112
  277.7 5.9 %shard_map.239.refs_9_ = bf16[512,768]{1,0:T(8,128)(2,1)} custom-call(s32[4]{0:T(128)} %pad_add_fusion.refs_0_, s32[4]{0:T(128)} %copy-done.54, f32[512,768]{1,0:T(8,128)} %get-tuple-element.103.refs_2_, bf16[512,2048]{1,0:T(8,128)(2,1)} %get-tuple-element.104.refs_3_.refs_5_, bf16[2048,768]{1,0:T(8,128)(2,1)} %get-tuple-element.105.refs_2_.refs_4_, ...), custom_call_target="tpu_custom_call" | custom-call | flops 1610612736 | bytes 8000000 | tf_op jit(solution)/shard_map/pallas_call | solution.py:112
  283.6 1.8 collective-permute-done.37.refs_2_
  287.6 17.0 %shard_map.240 = (bf16[8,576,128]{2,1,0:T(8,128)(2,1)}, bf16[8,576,128]{2,1,0:T(8,128)(2,1)}, bf16[8,576,128]{2,1,0:T(8,128)(2,1)}, bf16[8,576,128]{2,1,0:T(8,128)(2,1)}) custom-call(s32[4]{0:T(128)} %pad_add_fusion.refs_0_, bf16[512,768]{1,0:T(8,128)(2,1)} %get-tuple-element.108.refs_7_.refs_1_, bf16[512,768]{1,0:T(8,128)(2,1)} %copy-done.61, ...), custom_call_target="tpu_custom_call" | custom-call | flops 4831838208 | bytes 20000000 | tf_op jit(solution)/shard_map/pallas_call | solution.py:112
  308.7 16.6 %shard_map.241 = (bf16[512,768]{1,0:T(8,128)(2,1)}, bf16[512,1536]{1,0:T(8,128)(2,1)}, bf16[512,1536]{1,0:T(8,128)(2,1)}) custom-call(s32[4]{0:T(128)} %pad_add_fusion.refs_0_, bf16[512,768]{1,0:T(8,128)(2,1)} %get-tuple-element.111.refs_1_, bf16[512,2304]{1,0:T(8,128)(2,1)} %get-tuple-element.112.refs_2_, ...), custom_call_target="tpu_custom_call" | custom-call | flops 3422552064 | bytes 16000000 | tf_op jit(solution)/shard_map/pallas_call | solution.py:112
  325.3 6.9 %collective-permute-done.71 = bf16[8,576,128]{2,1,0:T(8,128)(2,1)} collective-permute-done((bf16[8,576,128]{2,1,0:T(8,128)(2,1)}, bf16[8,576,128]{2,1,0:T(8,128)(2,1)}, u32[]{:S(2)}, u32[]{:S(2)}) %collective-permute-start.71) | collective-permute-done | bytes 1179680 | tf_op jit(solution)/shard_map/ppermute | solution.py:47
  336.0 17.8 %shard_map.242 = (bf16[512,2048]{1,0:T(8,128)(2,1)}, bf16[512,2048]{1,0:T(8,128)(2,1)}, f32[512,768]{1,0:T(8,128)}, bf16[512,768]{1,0:T(8,128)(2,1)}, bf16[512,768]{1,0:T(8,128)(2,1)}) custom-call(s32[4]{0:T(128)} %pad_add_fusion.refs_0_, bf16[512,768]{1,0:T(8,128)(2,1)} %get-tuple-element.119.refs_1_.refs_7_, ...), custom_call_target="tpu_custom_call" | custom-call | flops 5435817984 | bytes 24000000 | tf_op jit(solution)/shard_map/pallas_call | solution.py:112
  359.0 1.8 maximum_select_fusion
  361.6 8.6 %collective-permute-done.81 = bf16[4,576,128]{2,1,0:T(8,128)(2,1)} collective-permute-done((bf16[4,576,128]{2,1,0:T(8,128)(2,1)}, bf16[4,576,128]{2,1,0:T(8,128)(2,1)}, u32[]{:S(2)}, u32[]{:S(2)}) %collective-permute-start.81) | collective-permute-done | bytes 589856 | tf_op jit(solution)/shard_map/ppermute | solution.py:47
  373.2 10.1 %shard_map.243 = (bf16[8,288,128]{2,1,0:T(8,128)(2,1)}, bf16[8,288,128]{2,1,0:T(8,128)(2,1)}, bf16[8,288,128]{2,1,0:T(8,128)(2,1)}, bf16[8,288,128]{2,1,0:T(8,128)(2,1)}) custom-call(s32[4]{0:T(128)} %pad_add_fusion.refs_0_, bf16[512,1536]{1,0:T(8,128)(2,1)} %get-tuple-element.99.refs_2_.refs_7_.refs_1_, bf16[512,1536]{1,0:T(8,128)(2,1)} %collective-permute-done.44.refs_2_, ...), custom_call_target="tpu_custom_call" | custom-call | flops 2415919104 | bytes 14000000 | tf_op jit(solution)/shard_map/pallas_call | solution.py:112
  388.8 16.8 %shard_map.244 = (bf16[8,576,128]{2,1,0:T(8,128)(2,1)}, bf16[8,576,128]{2,1,0:T(8,128)(2,1)}, bf16[8,576,128]{2,1,0:T(8,128)(2,1)}, bf16[8,576,128]{2,1,0:T(8,128)(2,1)}) custom-call(s32[4]{0:T(128)} %pad_add_fusion.refs_0_, bf16[512,768]{1,0:T(8,128)(2,1)} %get-tuple-element.122.refs_7_.refs_1_, bf16[512,768]{1,0:T(8,128)(2,1)} %copy-done.59, ...), custom_call_target="tpu_custom_call" | custom-call | flops 4831838208 | bytes 20000000 | tf_op jit(solution)/shard_map/pallas_call | solution.py:112
  408.3 16.7 %shard_map.245 = (bf16[512,768]{1,0:T(8,128)(2,1)}, bf16[512,1536]{1,0:T(8,128)(2,1)}, bf16[512,1536]{1,0:T(8,128)(2,1)}) custom-call(s32[4]{0:T(128)} %pad_add_fusion.refs_0_, bf16[512,768]{1,0:T(8,128)(2,1)} %get-tuple-element.124.refs_1_, bf16[512,2304]{1,0:T(8,128)(2,1)} %get-tuple-element.125.refs_2_, ...), custom_call_target="tpu_custom_call" | custom-call | flops 3422552064 | bytes 16000000 | tf_op jit(solution)/shard_map/pallas_call | solution.py:112
  428.2 11.2 %collective-permute-done.63 = bf16[4,288,128]{2,1,0:T(8,128)(2,1)S(1)} collective-permute-done((bf16[4,288,128]{2,1,0:T(8,128)(2,1)S(1)}, bf16[4,288,128]{2,1,0:T(8,128)(2,1)S(1)}, u32[]{:S(2)}, u32[]{:S(2)}) %collective-permute-start.63) | collective-permute-done | bytes 294944 | tf_op jit(solution)/shard_map/ppermute | solution.py:47
  441.3 2.3 collective-permute-done.55
  443.7 2.1 collective-permute-start.46
  449.2 4.5 collective-permute-done.76
  456.8 2.6 collective-permute-start.74
  460.6 10.0 %shard_map.246 = (bf16[8,288,128]{2,1,0:T(8,128)(2,1)}, bf16[8,288,128]{2,1,0:T(8,128)(2,1)}, bf16[8,288,128]{2,1,0:T(8,128)(2,1)}, bf16[8,288,128]{2,1,0:T(8,128)(2,1)}) custom-call(s32[4]{0:T(128)} %pad_add_fusion.refs_0_, bf16[512,1536]{1,0:T(8,128)(2,1)} %get-tuple-element.89.refs_2_.refs_7_.refs_1_, bf16[512,1536]{1,0:T(8,128)(2,1)} %collective-permute-done.47.refs_2_, ...), custom_call_target="tpu_custom_call" | custom-call | flops 2415919104 | bytes 14000000 | tf_op jit(solution)/shard_map/pallas_call | solution.py:112
  475.7 3.4 collective-permute-done.69
  481.3 4.1 collective-permute-done.78
  491.6 12.9 %collective-permute-done.70 = bf16[1,576,128]{2,1,0:T(8,128)(2,1)S(1)} collective-permute-done((bf16[1,576,128]{2,1,0:T(8,128)(2,1)S(1)}, bf16[1,576,128]{2,1,0:T(8,128)(2,1)S(1)}, u32[]{:S(2)}, u32[]{:S(2)}) %collective-permute-start.70) | collective-permute-done | bytes 147488 | tf_op jit(solution)/shard_map/ppermute | solution.py:47
  505.8 2.1 select_bitcast_fusion.5
  507.9 1.8 collective-permute-start.59
  509.7 2.6 collective-permute-start.75
  512.3 2.0 select_bitcast_fusion.3
  515.0 3.9 collective-permute-done.51
  519.0 5.7 %collective-permute-done.60 = bf16[2,288,128]{2,1,0:T(8,128)(2,1)S(1)} collective-permute-done((bf16[2,288,128]{2,1,0:T(8,128)(2,1)S(1)}, bf16[2,288,128]{2,1,0:T(8,128)(2,1)S(1)}, u32[]{:S(2)}, u32[]{:S(2)}) %collective-permute-start.60) | collective-permute-done | bytes 147488 | tf_op jit(solution)/shard_map/ppermute | solution.py:47
  524.8 2.4 collective-permute-start.61
  527.2 1.9 collective-permute-done.52
  530.8 8.0 %collective-permute-start.57 = (f32[288,128]{1,0:T(8,128)S(1)}, f32[288,128]{1,0:T(8,128)S(1)}, u32[]{:S(2)}, u32[]{:S(2)}) collective-permute-start(f32[288,128]{1,0:T(8,128)S(1)} %get-tuple-element.167), channel_id=1, source_target_pairs={{0,16},{16,0},{1,17},{17,1},{2,18},{18,2},{3,19},{19,3},{4,20},{20... | collective-permute-start | bytes 442376 | tf_op jit(solution)/shard_map/ppermute | solution.py:51
  540.5 1.8 maximum_select_fusion.1
  543.1 3.6 shard_map.248
  548.8 3.1 shard_map.247
  (321 shorter events, 93.0 us)
Async XLA Ops:
  3.1 34.1 %collective-permute-start = (bf16[1,96,768]{2,1,0:T(8,128)(2,1)S(1)}, bf16[1,96,768]{2,1,0:T(8,128)(2,1)S(1)}, u32[]{:S(2)}, u32[]{:S(2)}) collective-permute-start(bf16[1,96,768]{2,1,0:T(8,128)(2,1)S(1)} %maximum_bitcast_fusion), channel_id=1, source_target_pairs={{0,8},{1,9},{2,10},{3,11},{4,12},{5,13},{6,14},{7,15},{8,0},{9,1},... | collective-permute-start | bytes 442376 | tf_op jit(solution)/shard_map/ppermute | solution.py:47
  7.2 31.6 %collective-permute-start.6 = (bf16[1,96,768]{2,1,0:T(8,128)(2,1)S(1)}, bf16[1,96,768]{2,1,0:T(8,128)(2,1)S(1)}, u32[]{:S(2)}, u32[]{:S(2)}) collective-permute-start(bf16[1,96,768]{2,1,0:T(8,128)(2,1)S(1)} %maximum_bitcast_fusion.1), channel_id=1, source_target_pairs={{0,8},{1,9},{2,10},{3,11},{4,12},{5,13},{6,14},{7,15},{8,0},{9,1},... | collective-permute-start | bytes 442376 | tf_op jit(solution)/shard_map/ppermute | solution.py:47
  8.3 19.5 %collective-permute-start.24 = (bf16[1,64,768]{2,1,0:T(8,128)(2,1)S(1)}, bf16[1,64,768]{2,1,0:T(8,128)(2,1)S(1)}, u32[]{:S(2)}, u32[]{:S(2)}) collective-permute-start(bf16[1,64,768]{2,1,0:T(8,128)(2,1)S(1)} %get-tuple-element.172), channel_id=1, source_target_pairs={{0,8},{1,9},{2,10},{3,11},{4,12},{5,13},{6,14},{7,15},{8,0},{9,1},... | collective-permute-start | bytes 294920 | tf_op jit(solution)/shard_map/ppermute | solution.py:47
  11.5 27.6 %collective-permute-start.12 = (bf16[1,48,2048]{2,1,0:T(8,128)(2,1)S(1)}, bf16[1,48,2048]{2,1,0:T(8,128)(2,1)S(1)}, u32[]{:S(2)}, u32[]{:S(2)}) collective-permute-start(bf16[1,48,2048]{2,1,0:T(8,128)(2,1)S(1)} %get-tuple-element.178), channel_id=1, source_target_pairs={{0,8},{1,9},{2,10},{3,11},{4,12},{5,13},{6,14},{7,15},{8,0},{9,1},... | collective-permute-start | bytes 589832 | tf_op jit(solution)/shard_map/ppermute | solution.py:47
  11.6 28.0 %collective-permute-start.18 = (bf16[1,48,2048]{2,1,0:T(8,128)(2,1)S(1)}, bf16[1,48,2048]{2,1,0:T(8,128)(2,1)S(1)}, u32[]{:S(2)}, u32[]{:S(2)}) collective-permute-start(bf16[1,48,2048]{2,1,0:T(8,128)(2,1)S(1)} %get-tuple-element.177), channel_id=1, source_target_pairs={{0,4},{1,5},{2,6},{3,7},{4,0},{5,1},{6,2},{7,3},{8,12},{9,13},{10,... | collective-permute-start | bytes 589832 | tf_op jit(solution)/shard_map/ppermute | solution.py:47
  39.1 18.5 %collective-permute-start.7 = (bf16[2,96,768]{2,1,0:T(8,128)(2,1)S(1)}, bf16[2,96,768]{2,1,0:T(8,128)(2,1)S(1)}, u32[]{:S(2)}, u32[]{:S(2)}) collective-permute-start(bf16[2,96,768]{2,1,0:T(8,128)(2,1)S(1)} %pad_maximum_fusion.15), channel_id=1, source_target_pairs={{0,4},{1,5},{2,6},{3,7},{4,0},{5,1},{6,2},{7,3},{8,12},{9,13},{10,... | collective-permute-start | bytes 884744 | tf_op jit(solution)/shard_map/ppermute | solution.py:47
  39.5 16.8 %collective-permute-start.13 = (bf16[2,48,2048]{2,1,0:T(8,128)(2,1)S(1)}, bf16[2,48,2048]{2,1,0:T(8,128)(2,1)S(1)}, u32[]{:S(2)}, u32[]{:S(2)}) collective-permute-start(bf16[2,48,2048]{2,1,0:T(8,128)(2,1)S(1)} %pad_maximum_fusion.10), channel_id=1, source_target_pairs={{0,2},{1,3},{2,0},{3,1},{4,6},{5,7},{6,4},{7,5},{8,10},{9,11},{10,... | collective-permute-start | bytes 1179656 | tf_op jit(solution)/shard_map/ppermute | solution.py:47
  41.4 18.2 %collective-permute-start.19 = (bf16[2,48,2048]{2,1,0:T(8,128)(2,1)S(1)}, bf16[2,48,2048]{2,1,0:T(8,128)(2,1)S(1)}, u32[]{:S(2)}, u32[]{:S(2)}) collective-permute-start(bf16[2,48,2048]{2,1,0:T(8,128)(2,1)S(1)} %pad_maximum_fusion.11), channel_id=1, source_target_pairs={{0,1},{1,0},{2,3},{3,2},{4,5},{5,4},{6,7},{7,6},{8,9},{9,8},{10,11... | collective-permute-start | bytes 1179656 | tf_op jit(solution)/shard_map/ppermute | solution.py:47
  42.2 17.8 %collective-permute-start.26 = (bf16[4,64,768]{2,1,0:T(8,128)(2,1)S(1)}, bf16[4,64,768]{2,1,0:T(8,128)(2,1)S(1)}, u32[]{:S(2)}, u32[]{:S(2)}) collective-permute-start(bf16[4,64,768]{2,1,0:T(8,128)(2,1)S(1)} %pad_maximum_fusion.12), channel_id=1, source_target_pairs={{0,1},{1,0},{2,3},{3,2},{4,5},{5,4},{6,7},{7,6},{8,9},{9,8},{10,11... | collective-permute-start | bytes 1179656 | tf_op jit(solution)/shard_map/ppermute | solution.py:47
  47.9 16.9 %collective-permute-start.32 = (bf16[4,64,768]{2,1,0:T(8,128)(2,1)S(1)}, bf16[4,64,768]{2,1,0:T(8,128)(2,1)S(1)}, u32[]{:S(2)}, u32[]{:S(2)}) collective-permute-start(bf16[4,64,768]{2,1,0:T(8,128)(2,1)S(1)} %pad_maximum_fusion.13), channel_id=1, source_target_pairs={{0,2},{1,3},{2,0},{3,1},{4,6},{5,7},{6,4},{7,5},{8,10},{9,11},{10,... | collective-permute-start | bytes 1179656 | tf_op jit(solution)/shard_map/ppermute | solution.py:47
  56.3 15.1 %collective-permute-start.2 = (bf16[4,96,768]{2,1,0:T(8,128)(2,1)S(1)}, bf16[4,96,768]{2,1,0:T(8,128)(2,1)S(1)}, u32[]{:S(2)}, u32[]{:S(2)}) collective-permute-start(bf16[4,96,768]{2,1,0:T(8,128)(2,1)S(1)} %pad_maximum_fusion.8), channel_id=1, source_target_pairs={{0,1},{1,0},{2,3},{3,2},{4,5},{5,4},{6,7},{7,6},{8,9},{9,8},{10,11... | collective-permute-start | bytes 1769480 | tf_op jit(solution)/shard_map/ppermute | solution.py:47
  57.6 32.5 %collective-permute-start.14 = (bf16[4,48,2048]{2,1,0:T(8,128)(2,1)S(1)}, bf16[4,48,2048]{2,1,0:T(8,128)(2,1)S(1)}, u32[]{:S(2)}, u32[]{:S(2)}) collective-permute-start(bf16[4,48,2048]{2,1,0:T(8,128)(2,1)S(1)} %pad_maximum_fusion.4), channel_id=1, source_target_pairs={{0,4},{1,5},{2,6},{3,7},{4,0},{5,1},{6,2},{7,3},{8,12},{9,13},{10,... | collective-permute-start | bytes 2359304 | tf_op jit(solution)/shard_map/ppermute | solution.py:47
  59.6 24.5 %collective-permute-start.8 = (bf16[4,96,768]{2,1,0:T(8,128)(2,1)S(1)}, bf16[4,96,768]{2,1,0:T(8,128)(2,1)S(1)}, u32[]{:S(2)}, u32[]{:S(2)}) collective-permute-start(bf16[4,96,768]{2,1,0:T(8,128)(2,1)S(1)} %pad_maximum_fusion.9), channel_id=1, source_target_pairs={{0,1},{1,0},{2,3},{3,2},{4,5},{5,4},{6,7},{7,6},{8,9},{9,8},{10,11... | collective-permute-start | bytes 1769480 | tf_op jit(solution)/shard_map/ppermute | solution.py:47
  60.0 30.7 %collective-permute-start.20 = (bf16[4,48,2048]{2,1,0:T(8,128)(2,1)S(1)}, bf16[4,48,2048]{2,1,0:T(8,128)(2,1)S(1)}, u32[]{:S(2)}, u32[]{:S(2)}) collective-permute-start(bf16[4,48,2048]{2,1,0:T(8,128)(2,1)S(1)} %pad_maximum_fusion.5), channel_id=1, source_target_pairs={{0,8},{1,9},{2,10},{3,11},{4,12},{5,13},{6,14},{7,15},{8,0},{9,1},... | collective-permute-start | bytes 2359304 | tf_op jit(solution)/shard_map/ppermute | solution.py:47
  64.7 43.0 %collective-permute-start.27 = (bf16[8,64,768]{2,1,0:T(8,128)(2,1)S(1)}, bf16[8,64,768]{2,1,0:T(8,128)(2,1)S(1)}, u32[]{:S(2)}, u32[]{:S(2)}) collective-permute-start(bf16[8,64,768]{2,1,0:T(8,128)(2,1)S(1)} %pad_maximum_fusion.6.refs_1_), channel_id=1, source_target_pairs={{0,4},{1,5},{2,6},{3,7},{4,0},{5,1},{6,2},{7,3},{8,12},{9,13},{10,... | collective-permute-start | bytes 2359304 | tf_op jit(solution)/shard_map/ppermute | solution.py:47
  71.4 44.0 %collective-permute-start.28 = (bf16[8,64,768]{2,1,0:T(8,128)(2,1)S(1)}, bf16[8,64,768]{2,1,0:T(8,128)(2,1)S(1)}, u32[]{:S(2)}, u32[]{:S(2)}) collective-permute-start(bf16[8,64,768]{2,1,0:T(8,128)(2,1)S(1)} %pad_maximum_fusion.6.refs_1_), channel_id=1, source_target_pairs={{0,16},{16,0},{1,17},{17,1},{2,18},{18,2},{3,19},{19,3},{4,20},{20... | collective-permute-start | bytes 2359304 | tf_op jit(solution)/shard_map/ppermute | solution.py:51
  84.1 32.9 %collective-permute-start.33 = (bf16[8,64,768]{2,1,0:T(8,128)(2,1)S(1)}, bf16[8,64,768]{2,1,0:T(8,128)(2,1)S(1)}, u32[]{:S(2)}, u32[]{:S(2)}) collective-permute-start(bf16[8,64,768]{2,1,0:T(8,128)(2,1)S(1)} %pad_maximum_fusion.7.refs_5_), channel_id=1, source_target_pairs={{0,1},{1,0},{2,3},{3,2},{4,5},{5,4},{6,7},{7,6},{8,9},{9,8},{10,11... | collective-permute-start | bytes 2359304 | tf_op jit(solution)/shard_map/ppermute | solution.py:47
  90.1 43.0 %collective-permute-start.3 = (bf16[8,96,768]{2,1,0:T(8,128)(2,1)S(1)}, bf16[8,96,768]{2,1,0:T(8,128)(2,1)S(1)}, u32[]{:S(2)}, u32[]{:S(2)}) collective-permute-start(bf16[8,96,768]{2,1,0:T(8,128)(2,1)S(1)} %pad_maximum_fusion.2.refs_1_), channel_id=1, source_target_pairs={{0,4},{1,5},{2,6},{3,7},{4,0},{5,1},{6,2},{7,3},{8,12},{9,13},{10,... | collective-permute-start | bytes 3538952 | tf_op jit(solution)/shard_map/ppermute | solution.py:47
  90.7 27.0 %collective-permute-start.34 = (bf16[8,64,768]{2,1,0:T(8,128)(2,1)S(1)}, bf16[8,64,768]{2,1,0:T(8,128)(2,1)S(1)}, u32[]{:S(2)}, u32[]{:S(2)}) collective-permute-start(bf16[8,64,768]{2,1,0:T(8,128)(2,1)S(1)} %pad_maximum_fusion.7.refs_5_), channel_id=1, source_target_pairs={{0,16},{16,0},{1,17},{17,1},{2,18},{18,2},{3,19},{19,3},{4,20},{20... | collective-permute-start | bytes 2359304 | tf_op jit(solution)/shard_map/ppermute | solution.py:51
  107.8 26.3 %collective-permute-start.4 = (bf16[8,96,768]{2,1,0:T(8,128)(2,1)S(1)}, bf16[8,96,768]{2,1,0:T(8,128)(2,1)S(1)}, u32[]{:S(2)}, u32[]{:S(2)}) collective-permute-start(bf16[8,96,768]{2,1,0:T(8,128)(2,1)S(1)} %pad_maximum_fusion.2.refs_1_), channel_id=1, source_target_pairs={{0,16},{16,0},{1,17},{17,1},{2,18},{18,2},{3,19},{19,3},{4,20},{20... | collective-permute-start | bytes 3538952 | tf_op jit(solution)/shard_map/ppermute | solution.py:51
  115.4 27.9 %collective-permute-start.9 = (bf16[8,96,768]{2,1,0:T(8,128)(2,1)S(1)}, bf16[8,96,768]{2,1,0:T(8,128)(2,1)}, u32[]{:S(2)}, u32[]{:S(2)}) collective-permute-start(bf16[8,96,768]{2,1,0:T(8,128)(2,1)S(1)} %pad_maximum_fusion.3.refs_5_), channel_id=1, source_target_pairs={{0,2},{1,3},{2,0},{3,1},{4,6},{5,7},{6,4},{7,5},{8,10},{9,11},{10,... | collective-permute-start | bytes 3538952 | tf_op jit(solution)/shard_map/ppermute | solution.py:47
  117.0 27.3 %collective-permute-start.10 = (bf16[8,96,768]{2,1,0:T(8,128)(2,1)S(1)}, bf16[8,96,768]{2,1,0:T(8,128)(2,1)S(1)}, u32[]{:S(2)}, u32[]{:S(2)}) collective-permute-start(bf16[8,96,768]{2,1,0:T(8,128)(2,1)S(1)} %pad_maximum_fusion.3.refs_5_), channel_id=1, source_target_pairs={{0,16},{16,0},{1,17},{17,1},{2,18},{18,2},{3,19},{19,3},{4,20},{20... | collective-permute-start | bytes 3538952 | tf_op jit(solution)/shard_map/ppermute | solution.py:51
  117.7 35.9 %collective-permute-start.15 = (bf16[8,48,2048]{2,1,0:T(8,128)(2,1)S(1)}, bf16[8,48,2048]{2,1,0:T(8,128)(2,1)}, u32[]{:S(2)}, u32[]{:S(2)}) collective-permute-start(bf16[8,48,2048]{2,1,0:T(8,128)(2,1)S(1)} %pad_maximum_fusion.refs_1_), channel_id=1, source_target_pairs={{0,1},{1,0},{2,3},{3,2},{4,5},{5,4},{6,7},{7,6},{8,9},{9,8},{10,11... | collective-permute-start | bytes 4718600 | tf_op jit(solution)/shard_map/ppermute | solution.py:47
  133.2 43.9 %collective-permute-start.21 = (bf16[8,48,2048]{2,1,0:T(8,128)(2,1)S(1)}, bf16[8,48,2048]{2,1,0:T(8,128)(2,1)}, u32[]{:S(2)}, u32[]{:S(2)}) collective-permute-start(bf16[8,48,2048]{2,1,0:T(8,128)(2,1)S(1)} %pad_maximum_fusion.1.refs_5_), channel_id=1, source_target_pairs={{0,2},{1,3},{2,0},{3,1},{4,6},{5,7},{6,4},{7,5},{8,10},{9,11},{10,... | collective-permute-start | bytes 4718600 | tf_op jit(solution)/shard_map/ppermute | solution.py:47
  134.1 43.6 %collective-permute-start.5 = (bf16[8,96,768]{2,1,0:T(8,128)(2,1)S(1)}, bf16[8,96,768]{2,1,0:T(8,128)(2,1)S(1)}, u32[]{:S(2)}, u32[]{:S(2)}) collective-permute-start(bf16[8,96,768]{2,1,0:T(8,128)(2,1)S(1)} %collective-permute-done.3.refs_2_), channel_id=1, source_target_pairs={{0,16},{16,0},{1,17},{17,1},{2,18},{18,2},{3,19},{19,3},{4,20},{20... | collective-permute-start | bytes 3538952 | tf_op jit(solution)/shard_map/ppermute | solution.py:51
  146.2 42.3 %collective-permute-start.11 = (bf16[8,96,768]{2,1,0:T(8,128)(2,1)}, bf16[8,96,768]{2,1,0:T(8,128)(2,1)}, u32[]{:S(2)}, u32[]{:S(2)}) collective-permute-start(bf16[8,96,768]{2,1,0:T(8,128)(2,1)} %collective-permute-done.9.refs_6_), channel_id=1, source_target_pairs={{0,16},{16,0},{1,17},{17,1},{2,18},{18,2},{3,19},{19,3},{4,20},{20... | collective-permute-start | bytes 3538952 | tf_op jit(solution)/shard_map/ppermute | solution.py:51
  147.4 61.7 %collective-permute-start.16 = (bf16[8,48,2048]{2,1,0:T(8,128)(2,1)S(1)}, bf16[8,48,2048]{2,1,0:T(8,128)(2,1)}, u32[]{:S(2)}, u32[]{:S(2)}) collective-permute-start(bf16[8,48,2048]{2,1,0:T(8,128)(2,1)S(1)} %pad_maximum_fusion.refs_1_), channel_id=1, source_target_pairs={{0,16},{16,0},{1,17},{17,1},{2,18},{18,2},{3,19},{19,3},{4,20},{20... | collective-permute-start | bytes 4718600 | tf_op jit(solution)/shard_map/ppermute | solution.py:51
  153.7 55.4 %collective-permute-start.22 = (bf16[8,48,2048]{2,1,0:T(8,128)(2,1)S(1)}, bf16[8,48,2048]{2,1,0:T(8,128)(2,1)}, u32[]{:S(2)}, u32[]{:S(2)}) collective-permute-start(bf16[8,48,2048]{2,1,0:T(8,128)(2,1)S(1)} %pad_maximum_fusion.1.refs_5_), channel_id=1, source_target_pairs={{0,16},{16,0},{1,17},{17,1},{2,18},{18,2},{3,19},{19,3},{4,20},{20... | collective-permute-start | bytes 4718600 | tf_op jit(solution)/shard_map/ppermute | solution.py:51
  177.0 32.1 %collective-permute-start.17 = (bf16[8,48,2048]{2,1,0:T(8,128)(2,1)}, bf16[8,48,2048]{2,1,0:T(8,128)(2,1)}, u32[]{:S(2)}, u32[]{:S(2)}) collective-permute-start(bf16[8,48,2048]{2,1,0:T(8,128)(2,1)} %collective-permute-done.15.refs_2_), channel_id=1, source_target_pairs={{0,16},{16,0},{1,17},{17,1},{2,18},{18,2},{3,19},{19,3},{4,20},{20... | collective-permute-start | bytes 4718600 | tf_op jit(solution)/shard_map/ppermute | solution.py:51
  177.7 31.4 %collective-permute-start.23 = (bf16[8,48,2048]{2,1,0:T(8,128)(2,1)}, bf16[8,48,2048]{2,1,0:T(8,128)(2,1)}, u32[]{:S(2)}, u32[]{:S(2)}) collective-permute-start(bf16[8,48,2048]{2,1,0:T(8,128)(2,1)} %collective-permute-done.21.refs_6_), channel_id=1, source_target_pairs={{0,16},{16,0},{1,17},{17,1},{2,18},{18,2},{3,19},{19,3},{4,20},{20... | collective-permute-start | bytes 4718600 | tf_op jit(solution)/shard_map/ppermute | solution.py:51
  304.5 27.7 %collective-permute-start.71 = (bf16[8,576,128]{2,1,0:T(8,128)(2,1)}, bf16[8,576,128]{2,1,0:T(8,128)(2,1)}, u32[]{:S(2)}, u32[]{:S(2)}) collective-permute-start(bf16[8,576,128]{2,1,0:T(8,128)(2,1)} %get-tuple-element.118.refs_14_), channel_id=1, source_target_pairs={{0,1},{1,0},{2,3},{3,2},{4,5},{5,4},{6,7},{7,6},{8,9},{9,8},{10,11... | collective-permute-start | bytes 3538952 | tf_op jit(solution)/shard_map/ppermute | solution.py:47
  305.3 29.1 %collective-permute-start.36 = (bf16[512,768]{1,0:T(8,128)(2,1)S(1)}, bf16[512,768]{1,0:T(8,128)(2,1)S(1)}, u32[]{:S(2)}, u32[]{:S(2)}) collective-permute-start(bf16[512,768]{1,0:T(8,128)(2,1)S(1)} %get-tuple-element.170), channel_id=1, source_target_pairs={{0,16},{16,0},{1,17},{17,1},{2,18},{18,2},{3,19},{19,3},{4,20},{20... | collective-permute-start | bytes 2359304 | tf_op jit(solution)/shard_map/ppermute | solution.py:51
  306.5 47.4 %collective-permute-start.80 = (bf16[8,576,128]{2,1,0:T(8,128)(2,1)S(1)}, bf16[8,576,128]{2,1,0:T(8,128)(2,1)S(1)}, u32[]{:S(2)}, u32[]{:S(2)}) collective-permute-start(bf16[8,576,128]{2,1,0:T(8,128)(2,1)S(1)} %copy-done.58), channel_id=1, source_target_pairs={{0,2},{1,3},{2,0},{3,1},{4,6},{5,7},{6,4},{7,5},{8,10},{9,11},{10,... | collective-permute-start | bytes 3538952 | tf_op jit(solution)/shard_map/ppermute | solution.py:47
  307.9 79.7 %collective-permute-start.42 = (bf16[512,2048]{1,0:T(8,128)(2,1)}, bf16[512,2048]{1,0:T(8,128)(2,1)}, u32[]{:S(2)}, u32[]{:S(2)}) collective-permute-start(bf16[512,2048]{1,0:T(8,128)(2,1)} %get-tuple-element.94.refs_3_.refs_5_), channel_id=1, source_target_pairs={{0,16},{16,0},{1,17},{17,1},{2,18},{18,2},{3,19},{19,3},{4,20},{20... | collective-permute-start | bytes 6291464 | tf_op jit(solution)/shard_map/ppermute | solution.py:51
  308.7 49.9 %collective-permute-start.44 = (bf16[512,1536]{1,0:T(8,128)(2,1)}, bf16[512,1536]{1,0:T(8,128)(2,1)}, u32[]{:S(2)}, u32[]{:S(2)}) collective-permute-start(bf16[512,1536]{1,0:T(8,128)(2,1)} %get-tuple-element.99.refs_2_.refs_7_.refs_1_), channel_id=1, source_target_pairs={{0,16},{16,0},{1,17},{17,1},{2,18},{18,2},{3,19},{19,3},{4,20},{20... | collective-permute-start | bytes 4718600 | tf_op jit(solution)/shard_map/ppermute | solution.py:51
  332.2 28.6 %collective-permute-start.45 = (bf16[512,1536]{1,0:T(8,128)(2,1)}, bf16[512,1536]{1,0:T(8,128)(2,1)}, u32[]{:S(2)}, u32[]{:S(2)}) collective-permute-start(bf16[512,1536]{1,0:T(8,128)(2,1)} %get-tuple-element.133), channel_id=1, source_target_pairs={{0,16},{16,0},{1,17},{17,1},{2,18},{18,2},{3,19},{19,3},{4,20},{20... | collective-permute-start | bytes 4718600 | tf_op jit(solution)/shard_map/ppermute | solution.py:51
  334.5 20.7 %collective-permute-start.72 = (bf16[4,576,128]{2,1,0:T(8,128)(2,1)S(1)}, bf16[4,576,128]{2,1,0:T(8,128)(2,1)}, u32[]{:S(2)}, u32[]{:S(2)}) collective-permute-start(bf16[4,576,128]{2,1,0:T(8,128)(2,1)S(1)} %add_convert_fusion.2), channel_id=1, source_target_pairs={{0,2},{1,3},{2,0},{3,1},{4,6},{5,7},{6,4},{7,5},{8,10},{9,11},{10,... | collective-permute-start | bytes 1769480 | tf_op jit(solution)/shard_map/ppermute | solution.py:47
  353.8 34.1 %collective-permute-start.41 = (bf16[512,2048]{1,0:T(8,128)(2,1)}, bf16[512,2048]{1,0:T(8,128)(2,1)}, u32[]{:S(2)}, u32[]{:S(2)}) collective-permute-start(bf16[512,2048]{1,0:T(8,128)(2,1)} %get-tuple-element.131.refs_5_), channel_id=1, source_target_pairs={{0,16},{16,0},{1,17},{17,1},{2,18},{18,2},{3,19},{19,3},{4,20},{20... | collective-permute-start | bytes 6291464 | tf_op jit(solution)/shard_map/ppermute | solution.py:51
  355.2 15.0 %collective-permute-start.81 = (bf16[4,576,128]{2,1,0:T(8,128)(2,1)}, bf16[4,576,128]{2,1,0:T(8,128)(2,1)}, u32[]{:S(2)}, u32[]{:S(2)}) collective-permute-start(bf16[4,576,128]{2,1,0:T(8,128)(2,1)} %add_convert_fusion), channel_id=1, source_target_pairs={{0,1},{1,0},{2,3},{3,2},{4,5},{5,4},{6,7},{7,6},{8,9},{9,8},{10,11... | collective-permute-start | bytes 1769480 | tf_op jit(solution)/shard_map/ppermute | solution.py:47
  358.6 13.7 %collective-permute-start.73 = (bf16[2,576,128]{2,1,0:T(8,128)(2,1)S(1)}, bf16[2,576,128]{2,1,0:T(8,128)(2,1)S(1)}, u32[]{:S(2)}, u32[]{:S(2)}) collective-permute-start(bf16[2,576,128]{2,1,0:T(8,128)(2,1)S(1)} %add_convert_fusion.6), channel_id=1, source_target_pairs={{0,4},{1,5},{2,6},{3,7},{4,0},{5,1},{6,2},{7,3},{8,12},{9,13},{10,... | collective-permute-start | bytes 884744 | tf_op jit(solution)/shard_map/ppermute | solution.py:47
  360.9 26.2 %collective-permute-start.40 = (bf16[512,768]{1,0:T(8,128)(2,1)}, bf16[512,768]{1,0:T(8,128)(2,1)S(1)}, u32[]{:S(2)}, u32[]{:S(2)}) collective-permute-start(bf16[512,768]{1,0:T(8,128)(2,1)} %get-tuple-element.122.refs_7_.refs_1_), channel_id=1, source_target_pairs={{0,16},{16,0},{1,17},{17,1},{2,18},{18,2},{3,19},{19,3},{4,20},{20... | collective-permute-start | bytes 2359304 | tf_op jit(solution)/shard_map/ppermute | solution.py:51
  370.2 17.7 %collective-permute-start.43 = (bf16[512,768]{1,0:T(8,128)(2,1)S(1)}, bf16[512,768]{1,0:T(8,128)(2,1)S(1)}, u32[]{:S(2)}, u32[]{:S(2)}) collective-permute-start(bf16[512,768]{1,0:T(8,128)(2,1)S(1)} %copy-done.21), channel_id=1, source_target_pairs={{0,16},{16,0},{1,17},{17,1},{2,18},{18,2},{3,19},{19,3},{4,20},{20... | collective-permute-start | bytes 2359304 | tf_op jit(solution)/shard_map/ppermute | solution.py:51
  385.1 21.8 %collective-permute-start.53 = (bf16[8,288,128]{2,1,0:T(8,128)(2,1)}, bf16[8,288,128]{2,1,0:T(8,128)(2,1)S(1)}, u32[]{:S(2)}, u32[]{:S(2)}) collective-permute-start(bf16[8,288,128]{2,1,0:T(8,128)(2,1)} %get-tuple-element.134.refs_9_), channel_id=1, source_target_pairs={{0,1},{1,0},{2,3},{3,2},{4,5},{5,4},{6,7},{7,6},{8,9},{9,8},{10,11... | collective-permute-start | bytes 1769480 | tf_op jit(solution)/shard_map/ppermute | solution.py:47
  387.1 69.7 %collective-permute-start.47 = (bf16[512,1536]{1,0:T(8,128)(2,1)S(1)}, bf16[512,1536]{1,0:T(8,128)(2,1)}, u32[]{:S(2)}, u32[]{:S(2)}) collective-permute-start(bf16[512,1536]{1,0:T(8,128)(2,1)S(1)} %copy-done.9), channel_id=1, source_target_pairs={{0,16},{16,0},{1,17},{17,1},{2,18},{18,2},{3,19},{19,3},{4,20},{20... | collective-permute-start | bytes 4718600 | tf_op jit(solution)/shard_map/ppermute | solution.py:51
  387.7 38.3 %collective-permute-start.62 = (bf16[8,288,128]{2,1,0:T(8,128)(2,1)}, bf16[8,288,128]{2,1,0:T(8,128)(2,1)S(1)}, u32[]{:S(2)}, u32[]{:S(2)}) collective-permute-start(bf16[8,288,128]{2,1,0:T(8,128)(2,1)} %get-tuple-element.145), channel_id=1, source_target_pairs={{0,2},{1,3},{2,0},{3,1},{4,6},{5,7},{6,4},{7,5},{8,10},{9,11},{10,... | collective-permute-start | bytes 1769480 | tf_op jit(solution)/shard_map/ppermute | solution.py:47
  405.6 41.7 %collective-permute-start.67 = (bf16[8,576,128]{2,1,0:T(8,128)(2,1)}, bf16[8,576,128]{2,1,0:T(8,128)(2,1)S(1)}, u32[]{:S(2)}, u32[]{:S(2)}) collective-permute-start(bf16[8,576,128]{2,1,0:T(8,128)(2,1)} %get-tuple-element.135.refs_14_), channel_id=1, source_target_pairs={{0,1},{1,0},{2,3},{3,2},{4,5},{5,4},{6,7},{7,6},{8,9},{9,8},{10,11... | collective-permute-start | bytes 3538952 | tf_op jit(solution)/shard_map/ppermute | solution.py:47
  407.0 19.4 %collective-permute-start.54 = (bf16[4,288,128]{2,1,0:T(8,128)(2,1)S(1)}, bf16[4,288,128]{2,1,0:T(8,128)(2,1)}, u32[]{:S(2)}, u32[]{:S(2)}) collective-permute-start(bf16[4,288,128]{2,1,0:T(8,128)(2,1)S(1)} %add_convert_fusion.10), channel_id=1, source_target_pairs={{0,2},{1,3},{2,0},{3,1},{4,6},{5,7},{6,4},{7,5},{8,10},{9,11},{10,... | collective-permute-start | bytes 884744 | tf_op jit(solution)/shard_map/ppermute | solution.py:47
  425.0 34.5 %collective-permute-start.48 = (bf16[512,1536]{1,0:T(8,128)(2,1)}, bf16[512,1536]{1,0:T(8,128)(2,1)S(1)}, u32[]{:S(2)}, u32[]{:S(2)}) collective-permute-start(bf16[512,1536]{1,0:T(8,128)(2,1)} %get-tuple-element.138), channel_id=1, source_target_pairs={{0,16},{16,0},{1,17},{17,1},{2,18},{18,2},{3,19},{19,3},{4,20},{20... | collective-permute-start | bytes 4718600 | tf_op jit(solution)/shard_map/ppermute | solution.py:51
  426.0 27.7 %collective-permute-start.76 = (bf16[8,576,128]{2,1,0:T(8,128)(2,1)}, bf16[8,576,128]{2,1,0:T(8,128)(2,1)S(1)}, u32[]{:S(2)}, u32[]{:S(2)}) collective-permute-start(bf16[8,576,128]{2,1,0:T(8,128)(2,1)} %get-tuple-element.153), channel_id=1, source_target_pairs={{0,2},{1,3},{2,0},{3,1},{4,6},{5,7},{6,4},{7,5},{8,10},{9,11},{10,... | collective-permute-start | bytes 3538952 | tf_op jit(solution)/shard_map/ppermute | solution.py:47
  426.3 13.1 %collective-permute-start.63 = (bf16[4,288,128]{2,1,0:T(8,128)(2,1)S(1)}, bf16[4,288,128]{2,1,0:T(8,128)(2,1)S(1)}, u32[]{:S(2)}, u32[]{:S(2)}) collective-permute-start(bf16[4,288,128]{2,1,0:T(8,128)(2,1)S(1)} %add_convert_fusion.8), channel_id=1, source_target_pairs={{0,1},{1,0},{2,3},{3,2},{4,5},{5,4},{6,7},{7,6},{8,9},{9,8},{10,11... | collective-permute-start | bytes 884744 | tf_op jit(solution)/shard_map/ppermute | solution.py:47
  443.7 31.0 %collective-permute-start.46 = (bf16[512,768]{1,0:T(8,128)(2,1)}, bf16[512,768]{1,0:T(8,128)(2,1)}, u32[]{:S(2)}, u32[]{:S(2)}) collective-permute-start(bf16[512,768]{1,0:T(8,128)(2,1)} %get-tuple-element.136), channel_id=1, source_target_pairs={{0,16},{16,0},{1,17},{17,1},{2,18},{18,2},{3,19},{19,3},{4,20},{20... | collective-permute-start | bytes 2359304 | tf_op jit(solution)/shard_map/ppermute | solution.py:51
  453.7 16.9 %collective-permute-start.68 = (bf16[4,576,128]{2,1,0:T(8,128)(2,1)}, bf16[4,576,128]{2,1,0:T(8,128)(2,1)}, u32[]{:S(2)}, u32[]{:S(2)}) collective-permute-start(bf16[4,576,128]{2,1,0:T(8,128)(2,1)} %add_convert_fusion.3), channel_id=1, source_target_pairs={{0,2},{1,3},{2,0},{3,1},{4,6},{5,7},{6,4},{7,5},{8,10},{9,11},{10,... | collective-permute-start | bytes 1769480 | tf_op jit(solution)/shard_map/ppermute | solution.py:47
  455.0 17.8 %collective-permute-start.77 = (bf16[4,576,128]{2,1,0:T(8,128)(2,1)}, bf16[4,576,128]{2,1,0:T(8,128)(2,1)}, u32[]{:S(2)}, u32[]{:S(2)}) collective-permute-start(bf16[4,576,128]{2,1,0:T(8,128)(2,1)} %add_convert_fusion.1), channel_id=1, source_target_pairs={{0,1},{1,0},{2,3},{3,2},{4,5},{5,4},{6,7},{7,6},{8,9},{9,8},{10,11... | collective-permute-start | bytes 1769480 | tf_op jit(solution)/shard_map/ppermute | solution.py:47
  456.8 34.0 %collective-permute-start.74 = (bf16[1,576,128]{2,1,0:T(8,128)(2,1)}, bf16[1,576,128]{2,1,0:T(8,128)(2,1)}, u32[]{:S(2)}, u32[]{:S(2)}) collective-permute-start(bf16[1,576,128]{2,1,0:T(8,128)(2,1)} %add_convert_fusion.14), channel_id=1, source_target_pairs={{0,8},{1,9},{2,10},{3,11},{4,12},{5,13},{6,14},{7,15},{8,0},{9,1},... | collective-permute-start | bytes 442376 | tf_op jit(solution)/shard_map/ppermute | solution.py:47
  460.6 47.3 %collective-permute-start.83 = (bf16[1,576,128]{2,1,0:T(8,128)(2,1)}, bf16[1,576,128]{2,1,0:T(8,128)(2,1)}, u32[]{:S(2)}, u32[]{:S(2)}) collective-permute-start(bf16[1,576,128]{2,1,0:T(8,128)(2,1)} %add_convert_fusion.12), channel_id=1, source_target_pairs={{0,8},{1,9},{2,10},{3,11},{4,12},{5,13},{6,14},{7,15},{8,0},{9,1},... | collective-permute-start | bytes 442376 | tf_op jit(solution)/shard_map/ppermute | solution.py:47
  470.7 17.5 %collective-permute-start.49 = (bf16[8,288,128]{2,1,0:T(8,128)(2,1)}, bf16[8,288,128]{2,1,0:T(8,128)(2,1)S(1)}, u32[]{:S(2)}, u32[]{:S(2)}) collective-permute-start(bf16[8,288,128]{2,1,0:T(8,128)(2,1)} %get-tuple-element.140), channel_id=1, source_target_pairs={{0,1},{1,0},{2,3},{3,2},{4,5},{5,4},{6,7},{7,6},{8,9},{9,8},{10,11... | collective-permute-start | bytes 1769480 | tf_op jit(solution)/shard_map/ppermute | solution.py:47
  485.4 39.4 %collective-permute-start.56 = (bf16[1,288,128]{2,1,0:T(8,128)(2,1)S(1)}, bf16[1,288,128]{2,1,0:T(8,128)(2,1)S(1)}, u32[]{:S(2)}, u32[]{:S(2)}) collective-permute-start(bf16[1,288,128]{2,1,0:T(8,128)(2,1)S(1)} %copy-done.53), channel_id=1, source_target_pairs={{0,8},{1,9},{2,10},{3,11},{4,12},{5,13},{6,14},{7,15},{8,0},{9,1},... | collective-permute-start | bytes 221192 | tf_op jit(solution)/shard_map/ppermute | solution.py:47
  488.2 50.6 %collective-permute-start.65 = (bf16[1,288,128]{2,1,0:T(8,128)(2,1)S(1)}, bf16[1,288,128]{2,1,0:T(8,128)(2,1)S(1)}, u32[]{:S(2)}, u32[]{:S(2)}) collective-permute-start(bf16[1,288,128]{2,1,0:T(8,128)(2,1)S(1)} %copy-done.52), channel_id=1, source_target_pairs={{0,8},{1,9},{2,10},{3,11},{4,12},{5,13},{6,14},{7,15},{8,0},{9,1},... | collective-permute-start | bytes 221192 | tf_op jit(solution)/shard_map/ppermute | solution.py:47
  489.0 15.5 %collective-permute-start.70 = (bf16[1,576,128]{2,1,0:T(8,128)(2,1)S(1)}, bf16[1,576,128]{2,1,0:T(8,128)(2,1)S(1)}, u32[]{:S(2)}, u32[]{:S(2)}) collective-permute-start(bf16[1,576,128]{2,1,0:T(8,128)(2,1)S(1)} %add_convert_fusion.15), channel_id=1, source_target_pairs={{0,8},{1,9},{2,10},{3,11},{4,12},{5,13},{6,14},{7,15},{8,0},{9,1},... | collective-permute-start | bytes 442376 | tf_op jit(solution)/shard_map/ppermute | solution.py:47
  490.9 18.8 %collective-permute-start.79 = (bf16[1,576,128]{2,1,0:T(8,128)(2,1)S(1)}, bf16[1,576,128]{2,1,0:T(8,128)(2,1)S(1)}, u32[]{:S(2)}, u32[]{:S(2)}) collective-permute-start(bf16[1,576,128]{2,1,0:T(8,128)(2,1)S(1)} %add_convert_fusion.13), channel_id=1, source_target_pairs={{0,8},{1,9},{2,10},{3,11},{4,12},{5,13},{6,14},{7,15},{8,0},{9,1},... | collective-permute-start | bytes 442376 | tf_op jit(solution)/shard_map/ppermute | solution.py:47
  509.7 32.6 %collective-permute-start.75 = (f32[576,128]{1,0:T(8,128)S(1)}, f32[576,128]{1,0:T(8,128)S(1)}, u32[]{:S(2)}, u32[]{:S(2)}) collective-permute-start(f32[576,128]{1,0:T(8,128)S(1)} %get-tuple-element.163), channel_id=1, source_target_pairs={{0,16},{16,0},{1,17},{17,1},{2,18},{18,2},{3,19},{19,3},{4,20},{20... | collective-permute-start | bytes 884744 | tf_op jit(solution)/shard_map/ppermute | solution.py:51
  514.4 28.0 %collective-permute-start.84 = (f32[576,128]{1,0:T(8,128)S(1)}, f32[576,128]{1,0:T(8,128)S(1)}, u32[]{:S(2)}, u32[]{:S(2)}) collective-permute-start(f32[576,128]{1,0:T(8,128)S(1)} %get-tuple-element.161), channel_id=1, source_target_pairs={{0,16},{16,0},{1,17},{17,1},{2,18},{18,2},{3,19},{19,3},{4,20},{20... | collective-permute-start | bytes 884744 | tf_op jit(solution)/shard_map/ppermute | solution.py:51
  524.8 14.0 %collective-permute-start.61 = (bf16[1,288,128]{2,1,0:T(8,128)(2,1)S(1)}, bf16[1,288,128]{2,1,0:T(8,128)(2,1)S(1)}, u32[]{:S(2)}, u32[]{:S(2)}) collective-permute-start(bf16[1,288,128]{2,1,0:T(8,128)(2,1)S(1)} %add_convert_fusion.21), channel_id=1, source_target_pairs={{0,8},{1,9},{2,10},{3,11},{4,12},{5,13},{6,14},{7,15},{8,0},{9,1},... | collective-permute-start | bytes 221192 | tf_op jit(solution)/shard_map/ppermute | solution.py:47
  530.8 17.3 %collective-permute-start.57 = (f32[288,128]{1,0:T(8,128)S(1)}, f32[288,128]{1,0:T(8,128)S(1)}, u32[]{:S(2)}, u32[]{:S(2)}) collective-permute-start(f32[288,128]{1,0:T(8,128)S(1)} %get-tuple-element.167), channel_id=1, source_target_pairs={{0,16},{16,0},{1,17},{17,1},{2,18},{18,2},{3,19},{19,3},{4,20},{20... | collective-permute-start | bytes 442376 | tf_op jit(solution)/shard_map/ppermute | solution.py:51
  (85 other events, 1254.6 us)

commit v2 on v1

v2 whole, which is shorter than its diff:
```python
import functools

import jax
import jax.numpy as jnp
import numpy as np
from jax import lax
from jax.experimental import pallas as pl
from jax.experimental.pallas import tpu as pltpu
from jax.sharding import PartitionSpec as P

D = 768
HEADS = 12
HEAD_DIM = 64
FF = 2048
WIDE = 16
SLOT = 256
HALF = D // 2
FHALF = FF // 2
PAIRS = HEADS // 2
LANES = 128
EPS = 1e-05
SCALE = 0.125
F32 = jnp.float32
BF16 = jnp.bfloat16
VMEM_BYTES = 24 * 1024 * 1024

X, Y, ZL, ZH = 1, 2, 4, 8
GATHER = (
    ((ZH, ZL, Y, X), None),
    ((ZH, ZL, X, Y), None),
    ((X, ZH, ZL, Y), None),
    ((ZH, ZL, X, Y), None),
    ((ZL, ZH, X, Y), None),
    ((Y, X, ZH, ZL), None),
)
SCATTER = {
    "D1": (Y, ZH, ZL, X),
    "G1": (X, Y, ZL, ZH),
    "T1": (Y, ZL, X, ZH),
    "D0": (X, Y, ZL, ZH),
    "G0": (Y, X, ZL, ZH),
    "T0": (Y, ZL, X, ZH),
}
ORDER = (
    "g50", "g20", "g00", "g10", "g21", "g01", "g11", "g30", "g51", "g02", "g12", "g31", "g40",
    "g03", "g22", "g13", "g41", "v0", "g42", "w0", "g52", "g32", "w1", "g43", "v1", "g33", "g23",
    "A0", "v2", "w3", "F0", "xa0", "g53", "w2", "w4", "w5", "v3", "dw2", "dw3", "L0", "v4", "A1",
    "v5", "F1", "B1", "xf1", "xs1", "K1", "D1", "xf0", "rD10", "xt1", "G1", "rD11", "xa1", "rG10",
    "B0", "dxa0", "xs0", "T1", "rG11", "rT10", "K0", "G0", "rD12", "rG12", "rT11", "rG00", "xt0",
    "L1", "T0", "rT00", "oi", "rG01", "rT12", "oa", "rG13", "rD13", "rT01", "D0", "rD00", "zG1",
    "rT13", "doa", "rG02", "rT02", "ob", "rD01", "rG03", "rT03", "zT1", "rD02", "zD1", "zG0", "hG",
    "rD03", "zT0", "hT", "zD0", "dhG", "hD", "u2", "u1",
)


def order_masks(order):
    masks = [0]
    for bit in order:
        masks = masks + [m ^ bit for m in masks]
    return masks


def mirrored(order):
    return tuple({X: Y, Y: X}.get(bit, bit) for bit in order)


def flip(value, bit, count, other=None):
    if other is None or other == bit:
        return lax.ppermute(value, "dp", [(i, i ^ bit) for i in range(count)])
    pairs = [(i, i ^ bit) for i in range(count)]
    pairs += [(count + i, count + (i ^ other)) for i in range(count)]
    return lax.ppermute(value, ("section", "dp"), pairs)


def swap(value):
    return lax.ppermute(value, "section", [(0, 1), (1, 0)])


def rope_consts():
    position = np.arange(SLOT)
    index = np.maximum(position - 1, 0)
    started = (position > 0).astype(np.float32)
    row_pos = (index // WIDE).astype(np.float32) * started
    col_pos = (index % WIDE).astype(np.float32) * started
    quarter = HEAD_DIM // 4
    freq = np.power(np.float32(10000.0), -np.arange(quarter, dtype=np.float32) / quarter)
    row_angle = row_pos[:, None] * freq[None, :]
    col_angle = col_pos[:, None] * freq[None, :]
    angle = np.concatenate([row_angle, row_angle, col_angle, col_angle], axis=1)
    angle = np.concatenate([angle, angle], axis=1).astype(np.float32)
    even = (np.arange(LANES) // quarter) % 2 == 0
    sine = np.sin(angle)
    return (
        np.cos(angle).astype(np.float32),
        np.where(even, -sine, 0.0).astype(np.float32),
        np.where(even, 0.0, sine).astype(np.float32),
    )


def dot(left, right):
    return jnp.dot(left, right, preferred_element_type=F32)


def dot_nt(left, right):
    return lax.dot_general(left, right, (((1,), (1,)), ((), ())), preferred_element_type=F32)


def dot_tn(left, right):
    return lax.dot_general(left, right, (((0,), (0,)), ((), ())), preferred_element_type=F32)


def turn(value, sin_a, sin_b):
    return pltpu.roll(value, LANES - 16, 1) * sin_a + pltpu.roll(value, 16, 1) * sin_b


def params(steps=1):
    return pltpu.CompilerParams(
        dimension_semantics=("arbitrary",) * steps, vmem_limit_bytes=VMEM_BYTES
    )


def cost(flops, nbytes):
    return pl.CostEstimate(flops=1, bytes_accessed=1, transcendentals=0)


def shape(*dims, dtype=BF16):
    return jax.ShapeDtypeStruct(dims, dtype)


def kept(*dims, dtype=BF16):
    return pltpu.HBM(dims, dtype)


def far(*arrays):
    return tuple(pltpu.with_memory_space_constraint(a, pltpu.HBM) for a in arrays)


def launch(kernel, prefetch, grid, inputs, in_specs, out_shape, out_specs, work, scratch=()):
    return pl.pallas_call(
        kernel,
        grid_spec=pltpu.PrefetchScalarGridSpec(
            num_scalar_prefetch=len(prefetch),
            grid=grid,
            in_specs=list(in_specs),
            out_specs=out_specs,
            scratch_shapes=list(scratch),
        ),
        out_shape=out_shape,
        compiler_params=params(len(grid)),
        cost_estimate=work,
    )(*prefetch, *inputs)


def head_split(pair):
    lane = lax.broadcasted_iota(jnp.int32, pair.shape, 1)
    zero = jnp.zeros_like(pair)
    return jnp.where(lane < HEAD_DIM, pair, zero), jnp.where(lane < HEAD_DIM, zero, pair)


class Gathered:
    def __init__(self, sources, dims, masks=None, pieces=None):
        self.sources, self.dims, self.masks, self.pieces = tuple(sources), dims, masks, pieces

    def load(self, info, srcs, mats):
        if self.masks is None:
            for src, mat in zip(srcs, mats):
                mat[...] = src[...]
            return
        for section in range(2):

            @pl.when(info[1] == section)
            def _():
                for side in range(2):
                    part = section ^ side
                    for at, mask in enumerate(self.masks[part]):
                        src, shard = srcs[2 * side + at // 8], info[0] ^ mask
                        for row_from, rows, matrix, rest in self.pieces[part]:
                            mats[matrix][(shard, *rest)] = src[at % 8, row_from : row_from + rows]

    def scratch(self):
        kinds = [pltpu.VMEM(d, BF16) for d in self.dims]
        return kinds + [pltpu.SemaphoreType.DMA((len(self.dims),))]


def matrix(ref, rows=None, cols=slice(None)):
    if rows is not None:
        n, count = rows
        size = ref.shape[0] // count
        value = ref[pl.ds(pl.multiple_of(n * size, size), size)]
    else:
        value = ref[(slice(None),) * (len(ref.shape) - 1) + (cols,)]
    return value.reshape(-1, value.shape[-1])


ANYWHERE = pl.BlockSpec(memory_space=pl.ANY)


def loaded(gathered, kernel, n_in, n_out, info, *refs):
    n_src, n_mat = len(gathered.sources), len(gathered.dims)
    ins, srcs, refs = refs[:n_in], refs[n_in : n_in + n_src], refs[n_in + n_src :]
    outs, wholes, refs = refs[:n_out], refs[n_out : n_out + n_mat], refs[n_out + n_mat :]
    mats, out_sems, refs = refs[:n_mat], refs[n_mat], refs[n_mat + 1 :]
    step = pl.program_id(0)
    back = [
        pltpu.make_async_copy(mat, whole, out_sems.at[n])
        for n, (mat, whole) in enumerate(zip(mats, wholes))
    ]

    @pl.when(step == 0)
    def _():
        gathered.load(info, srcs, mats)
        for copy in back:
            copy.start()

    kernel(info, *ins, *mats, *outs, *refs)

    @pl.when(step == pl.num_programs(0) - 1)
    def _():
        for copy in back:
            copy.wait()


def launch_loaded(
    gathered, kernel, prefetch, grid, inputs, in_specs, out_shape, out_specs, work, scratch=()
):
    n_in = len(prefetch) - 1 + len(inputs)
    return launch(
        functools.partial(loaded, gathered, kernel, n_in, len(out_shape)),
        prefetch,
        grid,
        (*inputs, *gathered.sources),
        [*in_specs, *[pl.BlockSpec(memory_space=pltpu.VMEM)] * len(gathered.sources)],
        [*out_shape, *[kept(*d) for d in gathered.dims]],
        [*out_specs, *[ANYWHERE] * len(gathered.dims)],
        work,
        [*gathered.scratch(), *scratch],
    )


def attention_kernel(
    info, lim, x_ref, cos, sin_a, sin_b, wq, wk, wv, wo, act_ref, qkv_ref, probs_ref, scale_ref
):
    image = pl.program_id(0)
    x = x_ref[...].astype(F32)
    r = lax.rsqrt(jnp.mean(x * x, axis=1, keepdims=True) + EPS)
    normed = (x * r).astype(BF16)
    act_ref[:, :D] = normed
    scale_ref[...] = jnp.broadcast_to(r, (SLOT, LANES))
    for part, weight in enumerate((wq, wk)):
        full = dot(normed, matrix(weight))
        for p in range(PAIRS):
            piece = full[:, p * LANES : (p + 1) * LANES]
            piece = piece * cos[...] + turn(piece, sin_a[...], sin_b[...])
            start = part * D + p * LANES
            qkv_ref[:, start : start + LANES] = piece.astype(BF16)
    qkv_ref[:, 2 * D :] = dot(normed, matrix(wv)).astype(BF16)
    row = lax.broadcasted_iota(jnp.int32, (SLOT, SLOT), 0)
    col = lax.broadcasted_iota(jnp.int32, (SLOT, SLOT), 1)
    mask = (col <= row) & (col < lim[info[1] * 2 + image])
    for p in range(PAIRS):
        lanes = slice(p * LANES, (p + 1) * LANES)
        query = qkv_ref[:, lanes]
        keys = head_split(qkv_ref[:, D + p * LANES : D + (p + 1) * LANES])
        values = head_split(qkv_ref[:, 2 * D + p * LANES : 2 * D + (p + 1) * LANES])
        probs = []
        for h in range(2):
            scores = jnp.where(mask, dot_nt(query, keys[h]), -1e30)
            top = jnp.max(scores, axis=1, keepdims=True)
            raised = jnp.exp(scores - top)
            total = jnp.sum(raised, axis=1, keepdims=True)
            probs.append((raised * (1.0 / total)).astype(BF16))
            probs_ref[0, 2 * p + h] = probs[h]
        mixed = dot(jnp.concatenate(probs, axis=1), jnp.concatenate(values, axis=0))
        act_ref[:, D + p * LANES : D + (p + 1) * LANES] = mixed.astype(BF16)


def attention(info, lim, x, x_rows, gathered, tables):
    table = pl.BlockSpec((SLOT, LANES), lambda i, info, lim: (0, 0))
    return launch_loaded(
        gathered,
        attention_kernel,
        (info, lim),
        (2,),
        (x, *tables),
        [
            pl.BlockSpec((SLOT, D), lambda i, info, lim: (info[x_rows] * 2 + i, 0)),
            table,
            table,
            table,
        ],
        [
            shape(2 * SLOT, 2 * D),
            kept(2 * SLOT, 3 * D),
            kept(2, HEADS, SLOT, SLOT),
            kept(2 * SLOT, LANES, dtype=F32),
        ],
        [
            pl.BlockSpec((SLOT, 2 * D), lambda i, info, lim: (i, 0)),
            pl.BlockSpec((SLOT, 3 * D), lambda i, info, lim: (i, 0)),
            pl.BlockSpec((1, HEADS, SLOT, SLOT), lambda i, info, lim: (i, 0, 0, 0)),
            pl.BlockSpec((SLOT, LANES), lambda i, info, lim: (i, 0)),
        ],
        cost(3.6e9 + 24 * 4 * 256 * 256 * 128, 12e6),
    )


FBLOCK = 512


PACK = 1024


def feed_kernel(info, x_ref, mixed_ref, wo, wg, wu, middle_ref, scale_ref, pack_ref, s1_ref, s2_ref, normed):
    step = pl.program_id(0)
    lead = PACK // FBLOCK

    @pl.when(step == 0)
    def _():
        middle = x_ref[...].astype(F32) + dot(mixed_ref[...], wo[...])
        r = lax.rsqrt(jnp.mean(middle * middle, axis=1, keepdims=True) + EPS)
        middle_ref[...] = middle
        scale_ref[...] = jnp.broadcast_to(r, scale_ref.shape)
        normed[:, :D] = (middle * r).astype(BF16)
        normed[:, D:] = jnp.zeros((normed.shape[0], PACK - D), BF16)

    for part in range(lead):

        @pl.when(step == part)
        def _():
            pack_ref[...] = normed[:, part * FBLOCK : (part + 1) * FBLOCK]

    @pl.when(step >= lead)
    def _():
        cols = pl.ds(pl.multiple_of((step - lead) * FBLOCK, FBLOCK), FBLOCK)
        gate = dot(normed[:, :D], matrix(wg, cols=cols))
        up = dot(normed[:, :D], matrix(wu, cols=cols))
        sig = 0.5 * jnp.tanh(0.5 * gate) + 0.5
        silu = gate * sig
        pack_ref[...] = (silu * up).astype(BF16)
        s1_ref[...] = (up * (sig * (1.0 + gate * (1.0 - sig)))).astype(BF16)
        s2_ref[...] = silu.astype(BF16)


def feed(info, x, x_rows, act, wo, gathered):
    rows = 2 * SLOT
    lead = PACK // FBLOCK
    whole = lambda j, info: (0, 0)
    wide = pl.BlockSpec((rows, FBLOCK), lambda j, info: (0, jnp.maximum(j - lead, 0)))
    return launch_loaded(
        gathered,
        feed_kernel,
        (info,),
        (lead + FF // FBLOCK,),
        (x, act, wo),
        [
            pl.BlockSpec((rows, D), lambda j, info: (info[x_rows], 0)),
            pl.BlockSpec((rows, D), lambda j, info: (0, 1)),
            pl.BlockSpec((D, D), whole),
        ],
        [
            shape(rows, D, dtype=F32),
            kept(rows, LANES, dtype=F32),
            shape(rows, PACK + FF),
            kept(rows, FF),
            kept(rows, FF),
        ],
        [
            pl.BlockSpec((rows, D), whole),
            pl.BlockSpec((rows, LANES), whole),
            pl.BlockSpec((rows, FBLOCK), lambda j, info: (0, j)),
            wide,
            wide,
        ],
        cost(2 * rows * D * (D + 2 * FF), 18e6),
        [pltpu.VMEM((rows, PACK), BF16)],
    )


def leave_kernel(info, lim, middle_ref, low, high, wd, out_ref):
    image = pl.program_id(0)
    result = middle_ref[...] + dot(low[...], matrix(wd, (0, 2))) + dot(high[...], matrix(wd, (1, 2)))
    row = lax.broadcasted_iota(jnp.int32, result.shape, 0)
    out_ref[...] = jnp.where(row < lim[info[1] * 2 + image], result, 0.0).astype(BF16)


def leave(info, lim, middle, pack, wd):
    rows = 2 * SLOT
    args = (
        (info, lim),
        (2,),
        (middle, pack, pack),
        [
            pl.BlockSpec((SLOT, D), lambda i, info, lim: (i, 0)),
            pl.BlockSpec((SLOT, PACK), lambda i, info, lim: (i, 1)),
            pl.BlockSpec((SLOT, PACK), lambda i, info, lim: (i, 2)),
        ],
        [shape(rows, D)],
        [pl.BlockSpec((SLOT, D), lambda i, info, lim: (i, 0))],
        cost(2 * rows * D * FF, 8e6),
    )
    if isinstance(wd, Gathered):
        return launch_loaded(wd, leave_kernel, *args)
    prefetch, grid, inputs, in_specs, *rest = args
    in_specs = [*in_specs, pl.BlockSpec((FF, D), lambda i, info, lim: (0, 0))]
    return launch(leave_kernel, prefetch, grid, (*inputs, wd), in_specs, *rest)


def feed_back_kernel(
    info,
    grad_ref,
    wg,
    wu,
    s1_ref,
    s2_ref,
    normed_ref,
    scale_ref,
    wo,
    wd,
    keep_ref,
    send_ref,
    gmid_ref,
    gz_ref,
    gmix_ref,
    total,
):
    step = pl.program_id(0)
    per_half = FHALF // FBLOCK
    down = wd[...] if wd.shape[0] == FBLOCK else matrix(wd, (step, FF // FBLOCK))
    grad_hidden = dot_nt(grad_ref[...], down)
    ggate = (grad_hidden * s1_ref[...].astype(F32)).astype(BF16)
    gup = (grad_hidden * s2_ref[...].astype(F32)).astype(BF16)
    at = pl.multiple_of((step % per_half) * FBLOCK, FBLOCK)
    own = (step // per_half) == info[1]

    @pl.when(own)
    def _():
        keep_ref[:, pl.ds(at, FBLOCK)] = ggate
        keep_ref[:, pl.ds(at + FHALF, FBLOCK)] = gup

    @pl.when(jnp.logical_not(own))
    def _():
        send_ref[:, pl.ds(at, FBLOCK)] = ggate
        send_ref[:, pl.ds(at + FHALF, FBLOCK)] = gup

    part = dot_nt(ggate, wg[...]) + dot_nt(gup, wu[...])

    @pl.when(step == 0)
    def _():
        total[...] = part

    @pl.when(step > 0)
    def _():
        total[...] += part

    @pl.when(step == pl.num_programs(0) - 1)
    def _():
        gn = total[...]
        normed = normed_ref[...].astype(F32)
        mean = jnp.mean(gn * normed, axis=1, keepdims=True)
        gmid = grad_ref[...].astype(F32) + scale_ref[:, :1] * (gn - normed * mean)
        gz = gmid.astype(BF16)
        gmid_ref[...] = gmid
        gz_ref[...] = gz
        gmix_ref[...] = dot_nt(gz, wo[...]).astype(BF16)


def feed_back(info, grad, grad_rows, wd, wg, wu, s1, s2, pack, scale, wo):
    rows = 2 * SLOT
    whole = lambda j, info: (0, 0)
    col = pl.BlockSpec((D, FBLOCK), lambda j, info: (0, j))
    wide = pl.BlockSpec((rows, FBLOCK), lambda j, info: (0, j))
    full = pl.BlockSpec((rows, D), whole)
    args = (
        (info,),
        (FF // FBLOCK,),
        (grad, *far(wg, wu, s1, s2), pack, *far(scale, wo)),
        [
            pl.BlockSpec((rows, D), lambda j, info: (info[grad_rows], 0)),
            col,
            col,
            wide,
            wide,
            full,
            pl.BlockSpec((rows, LANES), whole),
            pl.BlockSpec((D, D), whole),
        ],
        [
            shape(rows, FF),
            shape(rows, FF),
            shape(rows, D, dtype=F32),
            shape(rows, D),
            shape(rows, D),
        ],
        [
            pl.BlockSpec((rows, FF), whole),
            pl.BlockSpec((rows, FF), whole),
            full,
            full,
            full,
        ],
        cost(2 * rows * D * (3 * FF + D), 24e6),
        [pltpu.VMEM((rows, D), F32)],
    )
    if isinstance(wd, Gathered):
        return launch_loaded(wd, feed_back_kernel, *args)
    prefetch, grid, inputs, in_specs, *rest = args
    in_specs = [*in_specs, pl.BlockSpec((FBLOCK, D), lambda j, info: (j, 0))]
    return launch(feed_back_kernel, prefetch, grid, (*inputs, *far(wd)), in_specs, *rest)


def attention_back_kernel(
    info,
    gmix_ref,
    qkv_ref,
    probs_ref,
    wq,
    wk,
    wv,
    normed_ref,
    scale_ref,
    gmid_ref,
    gz_ref,
    cos,
    sin_a,
    sin_b,
    gin_ref,
    keep_ref,
    send_ref,
    grads,
):
    for p in range(PAIRS):
        lanes = slice(p * LANES, (p + 1) * LANES)
        gmix = gmix_ref[:, lanes]
        query = head_split(qkv_ref[:, lanes])
        keys = head_split(qkv_ref[:, D + p * LANES : D + (p + 1) * LANES])
        values = head_split(qkv_ref[:, 2 * D + p * LANES : 2 * D + (p + 1) * LANES])
        gmix_parts = head_split(gmix)
        gs_parts = []
        for h in range(2):
            probs = probs_ref[0, 2 * p + h].astype(F32)
            weighted = probs * dot_nt(gmix, values[h])
            inner = jnp.sum(weighted, axis=1, keepdims=True)
            gs_parts.append((weighted - probs * inner).astype(BF16))
        gq = dot(jnp.concatenate(gs_parts, axis=1), jnp.concatenate(keys, axis=0))
        gk = dot_tn(gs_parts[0], query[0]) + dot_tn(gs_parts[1], query[1])
        gv = dot_tn(probs_ref[0, 2 * p], gmix_parts[0]) + dot_tn(
            probs_ref[0, 2 * p + 1], gmix_parts[1]
        )
        gq = gq * cos[...] - turn(gq, sin_a[...], sin_b[...])
        gk = gk * cos[...] - turn(gk, sin_a[...], sin_b[...])
        grads[0, :, lanes] = gq.astype(BF16)
        grads[1, :, lanes] = gk.astype(BF16)
        grads[2, :, lanes] = gv.astype(BF16)
    gn = dot_nt(grads[0], wq[...]) + dot_nt(grads[1], wk[...]) + dot_nt(grads[2], wv[...])
    normed = normed_ref[...].astype(F32)
    mean = jnp.mean(gn * normed, axis=1, keepdims=True)
    gin = gmid_ref[...] + scale_ref[:, :1] * (gn - normed * mean)
    gin_ref[...] = gin.astype(BF16)
    send_ref[:, 4 * HALF :] = gin.astype(BF16)
    for h in range(2):

        @pl.when(info[1] == h)
        def _():
            for out, half in ((keep_ref, h), (send_ref, 1 - h)):
                cols = slice(half * HALF, (half + 1) * HALF)
                out[:, :HALF] = gz_ref[:, cols]
                for part in range(3):
                    out[:, (part + 1) * HALF : (part + 2) * HALF] = grads[part, :, cols]


def attention_back(info, gmix, qkv, probs, wq, wk, wv, act, scale, gmid, gz, tables):
    rows = 2 * SLOT
    whole = lambda i, info: (0, 0)
    table = pl.BlockSpec((SLOT, LANES), whole)
    weight = pl.BlockSpec((D, D), whole)
    full = pl.BlockSpec((SLOT, D), lambda i, info: (i, 0))
    pack = pl.BlockSpec((SLOT, 4 * HALF), lambda i, info: (i, 0))
    longer = pl.BlockSpec((SLOT, 6 * HALF), lambda i, info: (i, 0))
    return launch(
        attention_back_kernel,
        (info,),
        (2,),
        (gmix, *far(qkv, probs, wq, wk, wv), act, *far(scale), gmid, gz, *tables),
        [
                full,
                pl.BlockSpec((SLOT, 3 * D), lambda i, info: (i, 0)),
                pl.BlockSpec((1, HEADS, SLOT, SLOT), lambda i, info: (i, 0, 0, 0)),
                weight,
                weight,
                weight,
                full,
                pl.BlockSpec((SLOT, LANES), lambda i, info: (i, 0)),
                full,
                full,
                table,
                table,
                table,
            ],
        [shape(rows, D), shape(rows, 4 * HALF), shape(rows, 6 * HALF)],
        [full, pack, longer],
        cost(2 * rows * D * 3 * D + 24 * 8 * 256 * 256 * 128, 16e6),
        [pltpu.VMEM((3, SLOT, D), BF16)],
    )


def spread(info, masks, scratch, rows, lane_blocks, keep, send, row_to):
    for place, (low, high) in enumerate(zip(*masks)):
        shard = info[0] ^ (low + (high - low) * info[1])
        at = pl.multiple_of(shard * rows, 16)
        out = keep if place < 8 else send
        for block in range(lane_blocks):
            out[place % 8, pl.ds(row_to + block * rows, rows), :] = scratch[
                pl.ds(at, rows), block * LANES : (block + 1) * LANES
            ]


def gate_weight_kernel(masks, info, own_ref, oth_ref, g_own, g_oth, keep, send, turned, tile):
    step = pl.program_id(0)
    rows = 2 * SLOT

    @pl.when(step == 0)
    def _():
        turned[:, :rows] = own_ref[...].T
        turned[:, rows:] = oth_ref[...].T

    tile[...] = (
        dot(turned[:, :rows], g_own[...]) + dot(turned[:, rows:], g_oth[...])
    ).astype(BF16)
    spread(info, masks, tile, 48, 4, keep, send, pl.multiple_of(step * 192, 16))


def gate_weight(info, masks, own, oth, g_own, g_oth):
    rows = 2 * SLOT
    full = pl.BlockSpec((rows, D), lambda j, info: (0, 0))
    grad = pl.BlockSpec((rows, 512), lambda j, info: (0, j))
    out = pl.BlockSpec((8, 768, LANES), lambda j, info: (0, 0, 0))
    return launch(
        functools.partial(gate_weight_kernel, masks),
        (info,),
        (4,),
        (own, oth, g_own, g_oth),
        [full, full, grad, grad],
        [shape(8, 768, LANES)] * 2,
        [out] * 2,
        cost(2 * rows * D * 2 * FF, 14e6),
        [pltpu.VMEM((D, 2 * rows), BF16), pltpu.VMEM((D, 512), BF16)],
    )


def down_weight_kernel(masks, info, hid_own, hid_oth, gf_own, gf_oth, keep, send, down):
    step = pl.program_id(0)
    at = pl.multiple_of(step * FBLOCK, FBLOCK)
    down[pl.ds(at, FBLOCK), :] = (
        dot_tn(hid_own[...], gf_own[...]) + dot_tn(hid_oth[...], gf_oth[...])
    ).astype(BF16)

    @pl.when(step == FF // FBLOCK - 1)
    def _():
        spread(info, masks, down, 128, 3, keep, send, 0)


def down_weight(info, masks, pack_own, pack_oth, gf_own, gf_oth, rows_of, col):
    rows = 2 * SLOT
    hid = pl.BlockSpec((rows, FBLOCK), lambda j, info: (0, j + PACK // FBLOCK))
    out = pl.BlockSpec((8, 384, LANES), lambda j, info: (0, 0, 0))
    return launch(
        functools.partial(down_weight_kernel, masks),
        (info,),
        (FF // FBLOCK,),
        (pack_own, pack_oth, gf_own, gf_oth),
        [
            hid,
            hid,
            pl.BlockSpec((rows, HALF), lambda j, info: (info[rows_of[0]], info[1])),
            pl.BlockSpec((rows, HALF), lambda j, info: (info[rows_of[1]], col + info[1])),
        ],
        [shape(8, 384, LANES)] * 2,
        [out] * 2,
        cost(2 * rows * D * FF, 9e6),
        [pltpu.VMEM((FF, HALF), BF16)],
    )


def attention_weight_kernel(masks, info, own_ref, oth_ref, g_own, g_oth, keep, send, turned, tile):
    step = pl.program_id(0)
    rows = 2 * SLOT

    @pl.when(step == 0)
    def _():
        turned[:, :rows] = own_ref[:, D:].T
        turned[:, rows:] = oth_ref[:, D:].T

    @pl.when(step == 1)
    def _():
        turned[:, :rows] = own_ref[:, :D].T
        turned[:, rows:] = oth_ref[:, :D].T

    tile[...] = (
        dot(turned[:, :rows], g_own[...]) + dot(turned[:, rows:], g_oth[...])
    ).astype(BF16)
    spread(info, masks, tile, 48, 3, keep, send, pl.multiple_of(step * 144, 16))


def attention_weight(info, masks, own, oth, g_own, g_oth):
    rows = 2 * SLOT
    full = pl.BlockSpec((rows, 2 * D), lambda j, info: (0, 0))
    grad = pl.BlockSpec((rows, HALF), lambda j, info: (0, j))
    out = pl.BlockSpec((8, 576, LANES), lambda j, info: (0, 0, 0))
    return launch(
        functools.partial(attention_weight_kernel, masks),
        (info,),
        (4,),
        (own, oth, g_own, g_oth),
        [full, full, grad, grad],
        [shape(8, 576, LANES)] * 2,
        [out] * 2,
        cost(2 * rows * D * 4 * D, 14e6),
        [pltpu.VMEM((D, 2 * rows), BF16), pltpu.VMEM((D, HALF), BF16)],
    )


def gather_plain(section, shards):
    mine = [lax.all_gather(s, "dp", axis=0, tiled=True) for s in shards]
    theirs = [swap(m) for m in mine]
    low = tuple(jnp.where(section == 0, m, t) for m, t in zip(mine, theirs))
    high = tuple(jnp.where(section == 0, t, m) for m, t in zip(mine, theirs))
    return low, high


def unpack_kernel(plan, gained, info, *refs):
    n_src = 1 + max(p[0] for p in plan)
    n_gain = len(gained)
    srcs, refs = refs[: 2 * n_src], refs[2 * n_src :]
    gain, weights, outs = refs[0], refs[1 : 1 + n_gain], refs[1 + n_gain :]
    for section in range(2):

        @pl.when(info[1] == section)
        def _():
            total = jnp.zeros((gain.shape[0], 1), F32)
            for n, (src, row_from, rows, row_to, scale, has_gain, out) in enumerate(plan):
                for side in range(2):
                    piece = srcs[2 * src + (section ^ side)]
                    width = outs[out].shape[1] // 2
                    for block in range(width // LANES):
                        at = row_from + block * rows
                        value = piece[at : at + rows, :]
                        col = side * width + block * LANES
                        if has_gain:
                            weight = weights[gained.index(n)][:, col : col + LANES].astype(F32)
                            total += scale * jnp.sum(weight * value, axis=1, keepdims=True)
                            value = value * (gain[...] * scale)
                        outs[out][row_to : row_to + rows, col : col + LANES] = value
            outs[-1][...] = jnp.broadcast_to(total, outs[-1].shape)


def unpack_all(info, plan, sources, gain, weights, dims):
    gained = tuple(n for n, p in enumerate(plan) if p[5])
    flat = [piece for source in sources for piece in source]
    return launch(
        functools.partial(unpack_kernel, plan, gained),
        (info,),
        (1,),
        (*flat, gain, *weights,),
        [pl.BlockSpec(v.shape, lambda i, info: (0, 0)) for v in (*flat, gain, *weights)],
        [shape(*d, dtype=F32) for d in dims],
        [pl.BlockSpec(d, lambda i, info: (0, 0)) for d in dims],
        cost(0, 8 * sum(a * b for a, b in dims)),
        (),
    )


def on_device(
    tokens,
    heights,
    out_grad,
    w_query,
    w_key,
    w_value,
    w_out,
    w_gate,
    w_up,
    w_down,
    gain_attn,
    gain_ffn,
):
    section = lax.axis_index("section")
    me = lax.axis_index("dp")
    count = lax.axis_size("dp")
    halving = count == 16
    rows = 2 * SLOT
    info = jnp.stack([me, section, 1 - section, jnp.zeros_like(me)]).astype(jnp.int32)
    own_rows, oth_rows, no_rows = 1, 2, 3
    token = [info]
    lim = WIDE * heights + 1
    gain_one = gain_attn[0].astype(F32)[:, None]
    gain_two = gain_ffn[0].astype(F32)[:, None]
    fold = lambda w, g: (w[0].astype(F32) * g).astype(BF16)
    shards = (
        fold(w_query, gain_one * SCALE),
        fold(w_key, gain_one),
        fold(w_value, gain_one),
        w_out[0],
        fold(w_gate, gain_two),
        fold(w_up, gain_two),
        w_down[0],
    )
    half, row = shards[6].shape[0] // 2, shards[0].shape[0]
    tables = tuple(jnp.asarray(t) for t in rope_consts())
    slots = jnp.arange(SLOT)
    valid = (slots[None, :] < lim[:, None]).reshape(-1, 1)
    grad = jnp.where(valid, out_grad, jnp.zeros_like(out_grad))

    def tie(*arrays):
        out = lax.optimization_barrier((*arrays, token[0]))
        token[0] = out[-1]
        return out[:-1] if len(arrays) > 1 else out[0]

    env = {}
    have, parts = {}, {}
    pair = lambda a, b: ((0, row, a, ()), (row, row, b, ()))
    pieces = (
        (pair(0, 1), pair(2, 3)),
        (((0, row, 0, ()),), ((0, row, 1, ()),)),
        (((0, half, 0, (0,)),), ((0, half, 0, (1,)),)),
    )
    if halving:
        dims = (((count, row, D),) * 4, ((count, row, FF),) * 2, ((count, 2, half, D),))
    else:
        dims = (((D, D),) * 4, ((D, FF),) * 2, ((FF, D),))
    flat = lambda found: tuple(w.reshape(-1, w.shape[-1]) for w in found)
    wholes, weights = {}, {}
    if halving:
        groups = (
            (jnp.concatenate(shards[0:2], axis=0), jnp.concatenate(shards[2:4], axis=0)),
            (shards[4], shards[5]),
            (shards[6][:half], shards[6][half:]),
        )
        for n, (first, second) in enumerate(groups):
            mine = jnp.where(section == 0, first, second)
            theirs = swap(jnp.where(section == 0, second, first))
            have[n] = jnp.where(section == 0, mine, theirs)[None]
            have[n + 3] = jnp.where(section == 0, theirs, mine)[None]
    else:
        for layer, found in enumerate(gather_plain(section, shards)):
            for group, some in enumerate((found[:4], found[4:6], found[6:])):
                wholes[3 * layer + group] = Gathered(some, dims[group])

    def double(stream, stage):
        order, after = GATHER[stream]
        if stage:
            env["g", stream, stage - 1] = got = tie(env["g", stream, stage - 1])
            have[stream] = jnp.concatenate([have[stream], got], axis=0)
        elif after is not None:
            env[("g",) + after] = tie(env[("g",) + after])
        have[stream] = tie(have[stream])
        env["g", stream, stage] = flip(
            have[stream], order[stage], count, mirrored(order)[stage]
        )

    def gathered(stream):
        if not halving:
            return wholes[stream]
        order = GATHER[stream][0]
        masks = (order_masks(order), order_masks(mirrored(order)))
        theirs, last = tie(env["w", stream], env["v", stream])
        sources = (have[stream], env["g", stream, 3], theirs, last)
        return Gathered(sources, dims[stream % 3], masks, pieces[stream % 3])

    def halve(name, stage):
        order = SCATTER[name]
        if stage:
            parts[name].append(tie(env["r", name, stage - 1]))
            size = 8 >> (stage - 1)
            send = sum(p[size // 2 : size].astype(F32) for p in parts[name]).astype(BF16)
        else:
            parts[name], send = [env[name][0]], env[name][1]
        env["r", name, stage] = flip(tie(send), order[stage], count, mirrored(order)[stage])

    def total(name):
        parts[name].append(tie(env["r", name, 3]))
        env["z", name] = tie(sum(p[0].astype(F32) for p in parts[name]))

    def attend(layer):
        x, x_rows = (tokens, own_rows) if layer == 0 else (env["L", 0], no_rows)
        out = tie(*attention(token[0], lim, x, x_rows, gathered(3 * layer), tables))
        env["A", layer], weights[3 * layer] = out[:4], flat(out[4:])

    def feed_on(layer):
        x, x_rows = (tokens, own_rows) if layer == 0 else (env["L", 0], no_rows)
        w_o, source = weights[3 * layer][3], gathered(3 * layer + 1)
        out = tie(*feed(token[0], x, x_rows, env["A", layer][0], w_o, source))
        env["F", layer], weights[3 * layer + 1] = out[:5], flat(out[5:])

    def leave_off(layer):
        middle, _, pack, _, _ = env["F", layer]
        w_d = gathered(2) if layer == 0 else weights[5][0]
        out = leave(token[0], lim, middle, pack, w_d)
        out = tie(*out) if len(out) > 1 else (tie(*out),)
        env["L", layer] = out[0]
        if layer == 0:
            weights[2] = flat(out[1:])

    def cotangent(layer):
        if layer == 1:
            return grad, grad, own_rows, oth_rows
        return env["K", 1][0], env["xt1"], no_rows, no_rows

    def feed_in(layer):
        own, _, at, _ = cotangent(layer)
        _, scale, pack, s1, s2 = env["F", layer]
        w_g, w_u = weights[3 * layer + 1]
        w_d = gathered(5) if layer == 1 else weights[2][0]
        w_o = weights[3 * layer][3]
        out = tie(*feed_back(token[0], own, at, w_d, w_g, w_u, s1, s2, pack, scale, w_o))
        env["B", layer] = out[:5]
        if layer == 1:
            weights[5] = flat(out[5:])

    def attend_in(layer):
        act, qkv, probs, scale = env["A", layer]
        _, _, gmid, gz, gmix = env["B", layer]
        w = weights[3 * layer][:3]
        env["K", layer] = tie(
            *attention_back(token[0], gmix, qkv, probs, *w, act, scale, gmid, gz, tables)
        )

    def masks_of(name):
        order = SCATTER[name][::-1]
        return order_masks(order), order_masks(mirrored(order))

    def form(name):
        layer = int(name[1])
        if name[0] == "D":
            key, col = "xf%d" % layer, 0
            env[key] = tie(env[key])
            if layer == 0:
                env["xt1"], col = tie(env["xt1"]), 4
            own, oth, at, oth_at = cotangent(layer)
            args = (env["F", layer][2], env[key], own, oth, (at, oth_at), col)
            made = down_weight(token[0], masks_of(name), *args)
        elif name[0] == "G":
            other, recv = tie(env["xf%d" % layer], env["xs%d" % layer])
            args = (env["F", layer][2], other, env["B", layer][0], recv)
            made = gate_weight(token[0], masks_of(name), *args)
        else:
            other, recv = tie(env["xa%d" % layer], env["xt%d" % layer])
            args = (env["A", layer][0], other, env["K", layer][1], recv)
            made = attention_weight(token[0], masks_of(name), *args)
        env[name] = tie(*made)

    sent = {
        "a": lambda layer: env["A", layer][0],
        "f": lambda layer: env["F", layer][2],
        "s": lambda layer: env["B", layer][1],
        "t": lambda layer: env["K", layer][2],
    }

    def both(mine, theirs):
        low = jnp.concatenate([mine, theirs], axis=0)
        return jnp.where(section == 0, low, jnp.concatenate([theirs, mine], axis=0))[None]

    pick = lambda first, second: jnp.where(section == 0, first, second)

    def unpacked(names, plan, gain, local, out_dims):
        sources = [(env["m", n], tie(env["h", n])) for n in names]
        return unpack_all(token[0], plan, sources, gain, local, out_dims)

    def run(name):
        kind, rest = name[0], name[1:]
        if kind == "g":
            double(int(rest[0]), int(rest[1]))
        elif kind == "w":
            env["w", int(rest)] = swap(tie(have[int(rest)]))
        elif kind == "v":
            key = ("g", int(rest), 3)
            env[key] = tie(env[key])
            env["v", int(rest)] = swap(env[key])
        elif kind == "r":
            halve(rest[:2], int(rest[2]))
        elif kind == "z":
            total(rest)
        elif kind == "d":
            kind, rest = rest[0], rest[1:]
            keys = {
                "g": lambda: ("g", int(rest[0]), int(rest[1])),
                "r": lambda: ("r", rest[:2], int(rest[2])),
                "x": lambda: "x" + rest,
                "o": lambda: "o" + rest,
                "h": lambda: ("h", rest),
            }
            key = keys.get(kind, lambda: (kind, int(rest)))()
            env[key] = tie(env[key])
        elif kind == "x":
            env[name] = swap(tie(sent[rest[0]](int(rest[1]))))
        elif kind == "h":
            first, second = env["z", rest + "0"], env["z", rest + "1"]
            env["m", rest], other = tie(pick(first, second), pick(second, first))
            env["h", rest] = swap(other)
        elif name == "u1":
            plan = (
                (0, 0, row, 0, 1.0, True, 0),
                (0, row * FHALF // LANES, row, 0, 1.0, True, 1),
                (1, 0, 2 * half, 0, 1.0, False, 2),
            )
            out_dims = ((row, FF), (row, FF), (2 * half, D), (row, LANES))
            env["u1"] = unpacked("GD", plan, gain_two, (w_gate[0], w_up[0]), out_dims)
        elif name == "u2":
            side = row * HALF // LANES
            plan = (
                (0, side, row, 0, SCALE, True, 0),
                (0, 2 * side, row, 0, 1.0, True, 1),
                (0, 3 * side, row, 0, 1.0, True, 2),
                (0, 0, row, 0, 1.0, False, 3),
            )
            local = (w_query[0], w_key[0], w_value[0])
            out_dims = ((row, D),) * 4 + ((row, LANES),)
            env["u2"] = unpacked("T", plan, gain_one, local, out_dims)
        elif name == "oa":
            env["oa"] = swap(tie(pick(env["L", 1], env["L", 0])))
        elif name == "ob":
            env["ob"] = both(pick(env["L", 0], env["L", 1]), tie(env["oa"]))
        elif name == "oi":
            other = [v[:, 4 * HALF :] for v in tie(env["xt0"], env["xt1"])]
            env["oi"] = both(pick(env["K", 0][0], env["K", 1][0]), pick(*other))
        else:
            layer = int(rest)
            {"A": attend, "F": feed_on, "L": leave_off, "B": feed_in, "K": attend_in}[kind](layer)

    for name in ORDER:
        if name[0] in "DGT":
            if halving:
                form(name)
        elif halving or name[0] in "xoAFLBK":
            run(name)

    if halving:
        grad_g, grad_u, grad_d, gain_grad_two = env["u1"]
        grad_q, grad_k, grad_v, grad_o, gain_grad_one = env["u2"]
        gain_grad_one, gain_grad_two = gain_grad_one[:, 0], gain_grad_two[:, 0]
    else:
        cut = lambda v, at: lax.dynamic_slice_in_dim(v, info[at] * rows, rows, 0)
        join = lambda a, b: jnp.concatenate([a, b], axis=0)

        def reduced(a, g):
            full = lax.dot_general(a, g, (((0,), (0,)), ((), ())), preferred_element_type=F32)
            return lax.psum_scatter(full, "dp", scatter_dimension=0, tiled=True)

        found = []
        for layer in range(2):
            own, oth, at, oth_at = cotangent(layer)
            oth = oth if layer == 1 else oth[:, 4 * HALF :]
            gf = lax.dynamic_slice_in_dim(
                join(cut(own, at), cut(oth, oth_at)), section * HALF, HALF, 1
            )
            acts = join(env["A", layer][0], env["xa%d" % layer])
            gts = join(env["K", layer][1], env["xt%d" % layer][:, : 4 * HALF])
            gus = join(env["B", layer][0], env["xs%d" % layer])
            pack = join(env["F", layer][2], env["xf%d" % layer])
            nor, hid = pack[:, :D], pack[:, PACK:]
            found.append(
                (
                    reduced(acts[:, :D], gts[:, HALF : 2 * HALF]),
                    reduced(acts[:, :D], gts[:, 2 * HALF : 3 * HALF]),
                    reduced(acts[:, :D], gts[:, 3 * HALF :]),
                    reduced(acts[:, D:], gts[:, :HALF]),
                    reduced(nor, gus[:, :FHALF]),
                    reduced(nor, gus[:, FHALF:]),
                    reduced(hid, gf),
                )
            )

        def cols(first, second):
            mine, theirs = pick(first, second), swap(pick(second, first))
            low = jnp.concatenate([mine, theirs], axis=1)
            return pick(low, jnp.concatenate([theirs, mine], axis=1))

        grads = [cols(first, second) for first, second in zip(*found)]
        grad_q, grad_k, grad_v, grad_o, grad_g, grad_u, grad_d = grads
        along = lambda w, g: jnp.sum(w[0].astype(F32) * g, axis=1)
        gain_grad_one = SCALE * along(w_query, grad_q)
        gain_grad_one += along(w_key, grad_k) + along(w_value, grad_v)
        gain_grad_two = along(w_gate, grad_g) + along(w_up, grad_u)
        grad_q, grad_k, grad_v = grad_q * (gain_one * SCALE), grad_k * gain_one, grad_v * gain_one
        grad_g, grad_u = grad_g * gain_two, grad_u * gain_two

    return (
        env["ob"],
        env["oi"],
        grad_q[None],
        grad_k[None],
        grad_v[None],
        grad_o[None],
        grad_g[None],
        grad_u[None],
        grad_d[None],
        gain_grad_one[None],
        gain_grad_two[None],
    )


def solution(mesh):
    rows = P("dp", None)
    weight = P("section", "dp", None)
    gain = P("section", "dp")
    return jax.shard_map(
        on_device,
        mesh=mesh,
        in_specs=(rows, P("dp"), rows) + (weight,) * 7 + (gain,) * 2,
        out_specs=(weight,) * 9 + (gain,) * 2,
        check_vma=False,
    )
```

time: 563 us -> 402 us (0.71)
  Pallas kernels: 212 us -> 146 us
  waiting for transfers between devices: 183 us -> 129 us
  starting transfers between devices: 103 us -> 76 us
  other arithmetic: 40.7 us -> 31.1 us
    ppermute x56 -> x24, waiting for transfers between devices: 179 us -> 76.8 us  [flip(): return lax.ppermute(value, 'dp', [(i, i ^ bit) for i in range(count)])]
    pallas_call x19 -> x18, Pallas kernels: 212 us -> 146 us  [launch(): pl.pallas_call(kernel, grid_spec=pltpu.PrefetchScalarGridSpec(num_scalar_...]
    ppermute x0 -> x24, waiting for transfers between devices: none -> 50.3 us  [flip(): return lax.ppermute(value, ('section', 'dp'), pairs)]
    ppermute x56 -> x24, starting transfers between devices: 54.5 us -> 24.2 us  [flip(): return lax.ppermute(value, 'dp', [(i, i ^ bit) for i in range(count)])]
    ppermute x0 -> x24, starting transfers between devices: none -> 23.6 us  [flip(): return lax.ppermute(value, ('section', 'dp'), pairs)]
    ppermute x29 -> x27, starting transfers between devices: 48 us -> 28.2 us  [swap(): return lax.ppermute(value, 'section', [(0, 1), (1, 0)])]
    convert_element_type x24 -> x18, other arithmetic: 20.4 us -> 9.23 us  [halve(): sum((p[size // 2:size].astype(F32) for p in parts[name])).astype(BF16)]
    select_n x6 -> x7, other arithmetic: 11.2 us -> 5.38 us  [the longest x3 3.12 us: on_device(): theirs = swap(jnp.where(section == 0, second, first))]
  transfers between devices with their start and end apart: 85 -> 75, of which waited for: 30 -> 28; matrix products, arithmetic and copies ran while one was open for 8% -> 7% of each run, Pallas kernels for 22% -> 32%
where the time goes in v2:
time: 402 us; the launch traced here: 398 us
  Pallas kernels  146 us (36%)
  waiting for transfers between devices  129 us (32%)
  starting transfers between devices  76 us (19%)
  other arithmetic  31.1 us (8%)
  local copies, waits for them, and re-layouts  13.4 us (3%)
    pallas_call x18, Pallas kernels, launch(): pl.pallas_call(kernel, grid_spec=pltpu.PrefetchScalarGridSpec(num_scalar_...  146 us
    ppermute x24, waiting for transfers between devices, flip(): return lax.ppermute(value, 'dp', [(i, i ^ bit) for i in range(count)])  76.8 us
    ppermute x24, waiting for transfers between devices, flip(): return lax.ppermute(value, ('section', 'dp'), pairs)  50.3 us
    ppermute x27, starting transfers between devices, swap(): return lax.ppermute(value, 'section', [(0, 1), (1, 0)])  28.2 us
    ppermute x24, starting transfers between devices, flip(): return lax.ppermute(value, 'dp', [(i, i ^ bit) for i in range(count)])  24.2 us
    ppermute x24, starting transfers between devices, flip(): return lax.ppermute(value, ('section', 'dp'), pairs)  23.6 us
    unnamed x114, local copies, waits for them, and re-layouts  12 us
    convert_element_type x18, other arithmetic, halve(): sum((p[size // 2:size].astype(F32) for p in parts[name])).astype(BF16)  9.23 us
  transfers between devices with their start and end apart: 75, of which 28 were waited for; matrix products, arithmetic and copies ran while one was open for 7% of the time, Pallas kernels for 32%

profile of v2, /device:TPU:1, one launch (start us, length us, event | category | flops | bytes accessed | tf_op | source)
XLA Modules:
  0.0 397.6 jit_solution(15938961740561359593)
XLA Ops:
  9.7 2.8 collective-permute-start.1
  12.5 2.4 collective-permute-start.5
  15.1 2.1 collective-permute-start.8
  17.3 8.7 %collective-permute-done.5 = bf16[1,96,768]{2,1,0:T(8,128)(2,1)S(1)} collective-permute-done((bf16[1,96,768]{2,1,0:T(8,128)(2,1)S(1)}, bf16[1,96,768]{2,1,0:T(8,128)(2,1)S(1)}, u32[]{:S(2)}, u32[]{:S(2)}) %collective-permute-start.5) | collective-permute-done | bytes 147488 | tf_op jit(solution)/shard_map/ppermute | solution.py:69
  27.1 3.1 collective-permute-done.8
  32.4 2.7 collective-permute-done.7
  35.1 2.0 collective-permute-done.6
  38.0 7.5 %collective-permute-done.11 = bf16[2,48,2048]{2,1,0:T(8,128)(2,1)S(1)} collective-permute-done((bf16[2,48,2048]{2,1,0:T(8,128)(2,1)S(1)}, bf16[2,48,2048]{2,1,0:T(8,128)(2,1)S(1)}, u32[]{:S(2)}, u32[]{:S(2)}) %collective-permute-start.11) | collective-permute-done | bytes 393248 | tf_op jit(solution)/shard_map/ppermute | solution.py:69
  45.7 1.5 collective-permute-start.10
  48.1 10.6 %collective-permute-done.10 = bf16[1,96,768]{2,1,0:T(8,128)(2,1)S(1)} collective-permute-done((bf16[1,96,768]{2,1,0:T(8,128)(2,1)S(1)}, bf16[1,96,768]{2,1,0:T(8,128)(2,1)S(1)}, u32[]{:S(2)}, u32[]{:S(2)}) %collective-permute-start.10) | collective-permute-done | bytes 147488 | tf_op jit(solution)/shard_map/ppermute | solution.py:69
  58.8 1.6 collective-permute-start.18
  60.8 2.1 collective-permute-done.4
  63.1 3.1 collective-permute-done.15
  66.2 2.1 collective-permute-start.20
  68.4 2.0 collective-permute-start.17
  70.3 6.3 %collective-permute-done.18.refs_6_ = bf16[8,96,768]{2,1,0:T(8,128)(2,1)S(1)} collective-permute-done((bf16[8,96,768]{2,1,0:T(8,128)(2,1)S(1)}, bf16[8,96,768]{2,1,0:T(8,128)(2,1)S(1)}, u32[]{:S(2)}, u32[]{:S(2)}) %collective-permute-start.18) | collective-permute-done | bytes 1179680 | tf_op jit(solution)/shard_map/ppermute | solution.py:72
  76.6 11.0 %collective-permute-done.17 = bf16[2,48,2048]{2,1,0:T(8,128)(2,1)S(1)} collective-permute-done((bf16[2,48,2048]{2,1,0:T(8,128)(2,1)S(1)}, bf16[2,48,2048]{2,1,0:T(8,128)(2,1)S(1)}, u32[]{:S(2)}, u32[]{:S(2)}) %collective-permute-start.17) | collective-permute-done | bytes 393248 | tf_op jit(solution)/shard_map/ppermute | solution.py:69
  90.4 11.4 %collective-permute-done.14 = bf16[2,64,768]{2,1,0:T(8,128)(2,1)S(1)} collective-permute-done((bf16[2,64,768]{2,1,0:T(8,128)(2,1)S(1)}, bf16[2,64,768]{2,1,0:T(8,128)(2,1)S(1)}, u32[]{:S(2)}, u32[]{:S(2)}) %collective-permute-start.14) | collective-permute-done | bytes 196640 | tf_op jit(solution)/shard_map/ppermute | solution.py:72
  101.9 1.5 collective-permute-start.19
  103.7 3.2 collective-permute-start.23
  108.8 2.2 collective-permute-done.19
  111.0 4.4 %collective-permute-start.26 = (bf16[8,48,2048]{2,1,0:T(8,128)(2,1)S(1)}, bf16[8,48,2048]{2,1,0:T(8,128)(2,1)S(1)}, u32[]{:S(2)}, u32[]{:S(2)}) collective-permute-start(bf16[8,48,2048]{2,1,0:T(8,128)(2,1)S(1)} %collective-permute-done.20.refs_4_), channel_id=1, source_target_pairs={{0,16},{16,0},{1,17},{17,1},{2,18},{18,2},{3,19},{19,3},{4,20},{20... | collective-permute-start | bytes 4718600 | tf_op jit(solution)/shard_map/ppermute | solution.py:76
  118.3 8.5 %collective-permute-done.27.refs_5_ = bf16[8,64,768]{2,1,0:T(8,128)(2,1)S(1)} collective-permute-done((bf16[8,64,768]{2,1,0:T(8,128)(2,1)S(1)}, bf16[8,64,768]{2,1,0:T(8,128)(2,1)S(1)}, u32[]{:S(2)}, u32[]{:S(2)}) %collective-permute-start.27) | collective-permute-done | bytes 786464 | tf_op jit(solution)/shard_map/ppermute | solution.py:72
  126.8 11.4 %shard_map.230 = (bf16[512,1536]{1,0:T(8,128)(2,1)S(1)}, bf16[512,2304]{1,0:T(8,128)(2,1)}, bf16[2,12,256,256]{3,2,1,0:T(8,128)(2,1)}, f32[512,128]{1,0:T(8,128)...) custom-call(s32[4]{0:T(128)S(1)} %pad_add_fusion.info, ...), custom_call_target="tpu_custom_call" | custom-call | flops 1 | bytes 1 | tf_op jit(solution)/shard_map/pallas_call | solution.py:139
  138.3 2.6 collective-permute-start.31
  142.1 8.3 %shard_map.231 = (f32[512,768]{1,0:T(8,128)S(1)}, f32[512,128]{1,0:T(8,128)}, bf16[512,3072]{1,0:T(8,128)(2,1)S(1)}, bf16[512,2048]{1,0:T(8,128)(2,1)}, bf16[512...) custom-call(s32[4]{0:T(128)S(1)} %pad_add_fusion.info, ...), custom_call_target="tpu_custom_call" | custom-call | flops 1 | bytes 1 | tf_op jit(solution)/shard_map/pallas_call | solution.py:139
  154.9 3.0 shard_map.232
  160.3 11.1 %shard_map.233 = (bf16[512,1536]{1,0:T(8,128)(2,1)S(1)}, bf16[512,2304]{1,0:T(8,128)(2,1)}, bf16[2,12,256,256]{3,2,1,0:T(8,128)(2,1)}, f32[512,128]{1,0:T(8,128)...) custom-call(s32[4]{0:T(128)S(1)} %pad_add_fusion.info, ...), custom_call_target="tpu_custom_call" | custom-call | flops 1 | bytes 1 | tf_op jit(solution)/shard_map/pallas_call | solution.py:139
  172.5 5.2 %collective-permute-done.36.refs_9_ = bf16[8,64,768]{2,1,0:T(8,128)(2,1)} collective-permute-done((bf16[8,64,768]{2,1,0:T(8,128)(2,1)}, bf16[8,64,768]{2,1,0:T(8,128)(2,1)}, u32[]{:S(2)}, u32[]{:S(2)}) %collective-permute-start.36) | collective-permute-done | bytes 786464 | tf_op jit(solution)/shard_map/ppermute | solution.py:69
  178.7 1.8 broadcast_select_fusion.refs_0_.gf_own.gf_oth
  182.1 11.1 %shard_map.234 = (f32[512,768]{1,0:T(8,128)S(1)}, f32[512,128]{1,0:T(8,128)}, bf16[512,3072]{1,0:T(8,128)(2,1)S(1)}, bf16[512,2048]{1,0:T(8,128)(2,1)}, bf16[512...) custom-call(s32[4]{0:T(128)S(1)} %pad_add_fusion.info, ...), custom_call_target="tpu_custom_call" | custom-call | flops 1 | bytes 1 | tf_op jit(solution)/shard_map/pallas_call | solution.py:139
  194.4 15.8 %shard_map.235 = (bf16[512,2048]{1,0:T(8,128)(2,1)S(1)}, bf16[512,2048]{1,0:T(8,128)(2,1)S(1)}, f32[512,768]{1,0:T(8,128)S(1)}, bf16[512,768]{1,0:T(8,128)(2,1)S...) custom-call(s32[4]{0:T(128)S(1)} %pad_add_fusion.info, ...), custom_call_target="tpu_custom_call" | custom-call | flops 1 | bytes 1 | tf_op jit(solution)/shard_map/pallas_call | solution.py:139
  210.8 14.1 %shard_map.236 = (bf16[512,768]{1,0:T(8,128)(2,1)S(1)}, bf16[512,1536]{1,0:T(8,128)(2,1)S(1)}, bf16[512,2304]{1,0:T(8,128)(2,1)S(1)}) custom-call(s32[4]{0:T(128)S(1)} %pad_add_fusion.info, bf16[512,768]{1,0:T(8,128)(2,1)S(1)} %get-tuple-element.651.gmix_ref, bf16[512,2304]{1,0:T(8,128)(2,1)} %get-tuple-element.652.qkv_ref, ...), custom_call_target="tpu_custom_call" | custom-call | flops 1 | bytes 1 | tf_op jit(solution)/shard_map/pallas_call | solution.py:139
  224.9 4.3 %shard_map.237 = (bf16[8,384,128]{2,1,0:T(8,128)(2,1)S(1)}, bf16[8,384,128]{2,1,0:T(8,128)(2,1)S(1)}) custom-call(s32[4]{0:T(128)S(1)} %pad_add_fusion.info, bf16[512,3072]{1,0:T(8,128)(2,1)S(1)} %get-tuple-element.647.refs_5_.hid_own.own_ref.low.high, bf16[512,3072]{1,0:T(8,128)(2,1)S(1)} %collective-permute-done.39.hid_oth.oth_ref, ...), custom_call_target="tpu_custom_call" | custom-call | flops 1 | bytes 1 | tf_op jit(solution)/shard_map/pallas_call | solution.py:139
  230.9 6.1 %shard_map.238 = (bf16[8,768,128]{2,1,0:T(8,128)(2,1)S(1)}, bf16[8,768,128]{2,1,0:T(8,128)(2,1)S(1)}) custom-call(s32[4]{0:T(128)S(1)} %pad_add_fusion.info, bf16[512,3072]{1,0:T(8,128)(2,1)S(1)} %get-tuple-element.647.refs_5_.hid_own.own_ref.low.high, bf16[512,3072]{1,0:T(8,128)(2,1)S(1)} %collective-permute-done.39.hid_oth.oth_ref, ...), custom_call_target="tpu_custom_call" | custom-call | flops 1 | bytes 1 | tf_op jit(solution)/shard_map/pallas_call | solution.py:139
  237.0 3.4 collective-permute-done.40
  242.2 13.9 %shard_map.239 = (bf16[512,2048]{1,0:T(8,128)(2,1)S(1)}, bf16[512,2048]{1,0:T(8,128)(2,1)S(1)}, f32[512,768]{1,0:T(8,128)S(1)}, bf16[512,768]{1,0:T(8,128)(2,1)S(1)}, bf16[512,768]{1,0:T(8,128)(2,1)S(1)}) custom-call(s32[4]{0:T(128)S(1)} %pad_add_fusion.info, bf16[512,768]{1,0:T(8,128)(2,1)S(1)} %get-tuple-element.692.grad_ref.gf_own, ...), custom_call_target="tpu_custom_call" | custom-call | flops 1 | bytes 1 | tf_op jit(solution)/shard_map/pallas_call | solution.py:139
  257.3 6.7 %shard_map.240 = (bf16[8,576,128]{2,1,0:T(8,128)(2,1)S(1)}, bf16[8,576,128]{2,1,0:T(8,128)(2,1)S(1)}) custom-call(s32[4]{0:T(128)S(1)} %pad_add_fusion.info, bf16[512,1536]{1,0:T(8,128)(2,1)S(1)} %copy-done.3, bf16[512,1536]{1,0:T(8,128)(2,1)S(1)} %collective-permute-done.42.oth_ref, bf16[512,1536]{1,0:T(8,128)(2,1)S(1)} %get-tuple-element.711.g_own, ...), custom_call_target="tpu_custom_call" | custom-call | flops 1 | bytes 1 | tf_op jit(solution)/shard_map/pallas_call | solution.py:139
  266.9 14.9 %shard_map.241 = (bf16[512,768]{1,0:T(8,128)(2,1)S(1)}, bf16[512,1536]{1,0:T(8,128)(2,1)S(1)}, bf16[512,2304]{1,0:T(8,128)(2,1)}) custom-call(s32[4]{0:T(128)S(1)} %pad_add_fusion.info, bf16[512,768]{1,0:T(8,128)(2,1)S(1)} %get-tuple-element.723.gmix_ref, bf16[512,2304]{1,0:T(8,128)(2,1)} %get-tuple-element.724.qkv_ref, ...), custom_call_target="tpu_custom_call" | custom-call | flops 1 | bytes 1 | tf_op jit(solution)/shard_map/pallas_call | solution.py:139
  283.0 7.2 %shard_map.242 = (bf16[8,768,128]{2,1,0:T(8,128)(2,1)S(1)}, bf16[8,768,128]{2,1,0:T(8,128)(2,1)}) custom-call(s32[4]{0:T(128)S(1)} %pad_add_fusion.info, bf16[512,3072]{1,0:T(8,128)(2,1)S(1)} %get-tuple-element.736.refs_2_.refs_3_.normed_ref.own_ref.hid_own, bf16[512,3072]{1,0:T(8,128)(2,1)S(1)} %collective-permute-done.46.oth_ref.hid_oth, ...), custom_call_target="tpu_custom_call" | custom-call | flops 1 | bytes 1 | tf_op jit(solution)/shard_map/pallas_call | solution.py:139
  297.5 1.9 copy-done.1
  299.4 1.9 copy-done.19
  301.3 2.8 shard_map.243
  306.0 7.1 %shard_map.244 = (bf16[8,576,128]{2,1,0:T(8,128)(2,1)S(1)}, bf16[8,576,128]{2,1,0:T(8,128)(2,1)S(1)}) custom-call(s32[4]{0:T(128)S(1)} %pad_add_fusion.info, bf16[512,1536]{1,0:T(8,128)(2,1)S(1)} %copy-done.6, bf16[512,1536]{1,0:T(8,128)(2,1)S(1)} %copy-done.30, bf16[512,1536]{1,0:T(8,128)(2,1)S(1)} %copy-done.32, ...), custom_call_target="tpu_custom_call" | custom-call | flops 1 | bytes 1 | tf_op jit(solution)/shard_map/pallas_call | solution.py:139
  314.2 1.6 add_convert_fusion
  315.9 1.5 collective-permute-done.56
  318.6 3.1 collective-permute-done.59
  324.0 1.5 collective-permute-start.54
  330.1 4.5 %shard_map.245 = (bf16[8,384,128]{2,1,0:T(8,128)(2,1)S(1)}, bf16[8,384,128]{2,1,0:T(8,128)(2,1)S(1)}) custom-call(s32[4]{0:T(128)S(1)} %pad_add_fusion.info, bf16[512,3072]{1,0:T(8,128)(2,1)S(1)} %get-tuple-element.736.refs_2_.refs_3_.normed_ref.own_ref.hid_own, bf16[512,3072]{1,0:T(8,128)(2,1)S(1)} %copy-done.10, bf16[512,768]{1,0:T(8,128)(2,1)S(1)} %copy-done.12, ...), custom_call_target="tpu_custom_call" | custom-call | flops 1 | bytes 1 | tf_op jit(solution)/shard_map/pallas_call | solution.py:139
  337.7 3.8 collective-permute-done.61
  343.4 1.8 collective-permute-start.67
  346.2 4.0 %collective-permute-done.64 = bf16[8,384,128]{2,1,0:T(8,128)(2,1)S(1)} collective-permute-done((bf16[8,384,128]{2,1,0:T(8,128)(2,1)S(1)}, bf16[8,384,128]{2,1,0:T(8,128)(2,1)S(1)}, u32[]{:S(2)}, u32[]{:S(2)}) %collective-permute-start.64) | collective-permute-done | bytes 786464 | tf_op jit(solution)/shard_map/ppermute | solution.py:72
  350.3 6.8 %collective-permute-done.63 = bf16[2,768,128]{2,1,0:T(8,128)(2,1)S(1)} collective-permute-done((bf16[2,768,128]{2,1,0:T(8,128)(2,1)S(1)}, bf16[2,768,128]{2,1,0:T(8,128)(2,1)S(1)}, u32[]{:S(2)}, u32[]{:S(2)}) %collective-permute-start.63) | collective-permute-done | bytes 393248 | tf_op jit(solution)/shard_map/ppermute | solution.py:69
  359.6 2.3 collective-permute-start.65
  361.9 6.4 %collective-permute-done.66 = bf16[4,384,128]{2,1,0:T(8,128)(2,1)S(1)} collective-permute-done((bf16[4,384,128]{2,1,0:T(8,128)(2,1)S(1)}, bf16[4,384,128]{2,1,0:T(8,128)(2,1)S(1)}, u32[]{:S(2)}, u32[]{:S(2)}) %collective-permute-start.66) | collective-permute-done | bytes 393248 | tf_op jit(solution)/shard_map/ppermute | solution.py:72
  369.4 5.7 %collective-permute-done.69 = bf16[1,768,128]{2,1,0:T(8,128)(2,1)S(1)} collective-permute-done((bf16[1,768,128]{2,1,0:T(8,128)(2,1)S(1)}, bf16[1,768,128]{2,1,0:T(8,128)(2,1)S(1)}, u32[]{:S(2)}, u32[]{:S(2)}) %collective-permute-start.69) | collective-permute-done | bytes 196640 | tf_op jit(solution)/shard_map/ppermute | solution.py:69
  376.3 1.5 collective-permute-start.73
  377.8 3.4 collective-permute-done.68
  381.5 2.4 collective-permute-start.71
  383.9 3.0 collective-permute-done.72
  387.0 3.3 collective-permute-start.74
  390.3 2.1 maximum_select_fusion
  392.4 1.7 shard_map.246
  394.7 2.1 shard_map.247
  (287 shorter events, 76.3 us)
Async XLA Ops:
  12.5 13.5 %collective-permute-start.5 = (bf16[1,96,768]{2,1,0:T(8,128)(2,1)S(1)}, bf16[1,96,768]{2,1,0:T(8,128)(2,1)S(1)}, u32[]{:S(2)}, u32[]{:S(2)}) collective-permute-start(bf16[1,96,768]{2,1,0:T(8,128)(2,1)S(1)} %get-tuple-element.467), channel_id=1, source_target_pairs={{0,8},{1,9},{2,10},{3,11},{4,12},{5,13},{6,14},{7,15},{8,0},{9,1},... | collective-permute-start | bytes 442376 | tf_op jit(solution)/shard_map/ppermute | solution.py:69
  15.1 15.1 %collective-permute-start.8 = (bf16[1,48,2048]{2,1,0:T(8,128)(2,1)S(1)}, bf16[1,48,2048]{2,1,0:T(8,128)(2,1)S(1)}, u32[]{:S(2)}, u32[]{:S(2)}) collective-permute-start(bf16[1,48,2048]{2,1,0:T(8,128)(2,1)S(1)} %get-tuple-element.473), channel_id=1, source_target_pairs={{0,8},{1,9},{2,10},{3,11},{4,12},{5,13},{6,14},{7,15},{8,0},{9,1},... | collective-permute-start | bytes 589832 | tf_op jit(solution)/shard_map/ppermute | solution.py:69
  26.1 11.1 %collective-permute-start.6 = (bf16[2,96,768]{2,1,0:T(8,128)(2,1)S(1)}, bf16[2,96,768]{2,1,0:T(8,128)(2,1)S(1)}, u32[]{:S(2)}, u32[]{:S(2)}) collective-permute-start(bf16[2,96,768]{2,1,0:T(8,128)(2,1)S(1)} %pad_maximum_fusion.14), channel_id=1, source_target_pairs={{0,4},{1,5},{2,6},{3,7},{4,0},{5,1},{6,2},{7,3},{8,12},{9,13},{10,... | collective-permute-start | bytes 884744 | tf_op jit(solution)/shard_map/ppermute | solution.py:69
  30.3 15.3 %collective-permute-start.11 = (bf16[2,48,2048]{2,1,0:T(8,128)(2,1)S(1)}, bf16[2,48,2048]{2,1,0:T(8,128)(2,1)S(1)}, u32[]{:S(2)}, u32[]{:S(2)}) collective-permute-start(bf16[2,48,2048]{2,1,0:T(8,128)(2,1)S(1)} %pad_maximum_fusion.10), channel_id=1, source_target_pairs={{0,4},{1,5},{2,6},{3,7},{4,0},{5,1},{6,2},{7,3},{8,12},{9,13},{10,... | collective-permute-start | bytes 1179656 | tf_op jit(solution)/shard_map/ppermute | solution.py:69
  37.2 21.6 %collective-permute-start.9 = (bf16[4,96,768]{2,1,0:T(8,128)(2,1)S(1)}, bf16[4,96,768]{2,1,0:T(8,128)(2,1)S(1)}, u32[]{:S(2)}, u32[]{:S(2)}) collective-permute-start(bf16[4,96,768]{2,1,0:T(8,128)(2,1)S(1)} %pad_maximum_fusion.8), channel_id=1, source_target_pairs={{0,2},{1,3},{2,0},{3,1},{4,6},{5,7},{6,4},{7,5},{8,10},{9,11},{10,... | collective-permute-start | bytes 1769480 | tf_op jit(solution)/shard_map/ppermute | solution.py:72
  45.6 17.3 %collective-permute-start.16 = (bf16[4,48,2048]{2,1,0:T(8,128)(2,1)S(1)}, bf16[4,48,2048]{2,1,0:T(8,128)(2,1)S(1)}, u32[]{:S(2)}, u32[]{:S(2)}) collective-permute-start(bf16[4,48,2048]{2,1,0:T(8,128)(2,1)S(1)} %pad_maximum_fusion.4), channel_id=1, source_target_pairs={{0,1},{1,0},{2,3},{3,2},{4,5},{5,4},{6,7},{7,6},{8,9},{9,8},{10,11... | collective-permute-start | bytes 2359304 | tf_op jit(solution)/shard_map/ppermute | solution.py:72
  45.7 13.0 %collective-permute-start.10 = (bf16[1,96,768]{2,1,0:T(8,128)(2,1)S(1)}, bf16[1,96,768]{2,1,0:T(8,128)(2,1)S(1)}, u32[]{:S(2)}, u32[]{:S(2)}) collective-permute-start(bf16[1,96,768]{2,1,0:T(8,128)(2,1)S(1)} %get-tuple-element.485), channel_id=1, source_target_pairs={{0,8},{1,9},{2,10},{3,11},{4,12},{5,13},{6,14},{7,15},{8,0},{9,1},... | collective-permute-start | bytes 442376 | tf_op jit(solution)/shard_map/ppermute | solution.py:69
  47.2 15.7 %collective-permute-start.4 = (bf16[2,64,768]{2,1,0:T(8,128)(2,1)S(1)}, bf16[2,64,768]{2,1,0:T(8,128)(2,1)S(1)}, u32[]{:S(2)}, u32[]{:S(2)}) collective-permute-start(bf16[2,64,768]{2,1,0:T(8,128)(2,1)S(1)} %pad_maximum_fusion.16), channel_id=1, source_target_pairs={{0,8},{1,9},{2,10},{3,11},{4,12},{5,13},{6,14},{7,15},{8,0},{9,1},... | collective-permute-start | bytes 589832 | tf_op jit(solution)/shard_map/ppermute | solution.py:69
  58.8 17.8 %collective-permute-start.18 = (bf16[8,96,768]{2,1,0:T(8,128)(2,1)S(1)}, bf16[8,96,768]{2,1,0:T(8,128)(2,1)S(1)}, u32[]{:S(2)}, u32[]{:S(2)}) collective-permute-start(bf16[8,96,768]{2,1,0:T(8,128)(2,1)S(1)} %pad_maximum_fusion.2.refs_5_), channel_id=1, source_target_pairs={{0,1},{1,0},{2,3},{3,2},{4,5},{5,4},{6,7},{7,6},{8,9},{9,8},{10,11... | collective-permute-start | bytes 3538952 | tf_op jit(solution)/shard_map/ppermute | solution.py:72
  66.2 40.8 %collective-permute-start.20 = (bf16[8,48,2048]{2,1,0:T(8,128)(2,1)S(1)}, bf16[8,48,2048]{2,1,0:T(8,128)(2,1)S(1)}, u32[]{:S(2)}, u32[]{:S(2)}) collective-permute-start(bf16[8,48,2048]{2,1,0:T(8,128)(2,1)S(1)} %pad_maximum_fusion.refs_3_), channel_id=1, source_target_pairs={{0,2},{1,3},{2,0},{3,1},{4,6},{5,7},{6,4},{7,5},{8,10},{9,11},{10,... | collective-permute-start | bytes 4718600 | tf_op jit(solution)/shard_map/ppermute | solution.py:72
  68.4 19.3 %collective-permute-start.17 = (bf16[2,48,2048]{2,1,0:T(8,128)(2,1)S(1)}, bf16[2,48,2048]{2,1,0:T(8,128)(2,1)S(1)}, u32[]{:S(2)}, u32[]{:S(2)}) collective-permute-start(bf16[2,48,2048]{2,1,0:T(8,128)(2,1)S(1)} %pad_maximum_fusion.12), channel_id=1, source_target_pairs={{0,8},{1,9},{2,10},{3,11},{4,12},{5,13},{6,14},{7,15},{8,0},{9,1},... | collective-permute-start | bytes 1179656 | tf_op jit(solution)/shard_map/ppermute | solution.py:69
  87.8 19.2 %collective-permute-start.21 = (bf16[4,48,2048]{2,1,0:T(8,128)(2,1)S(1)}, bf16[4,48,2048]{2,1,0:T(8,128)(2,1)S(1)}, u32[]{:S(2)}, u32[]{:S(2)}) collective-permute-start(bf16[4,48,2048]{2,1,0:T(8,128)(2,1)S(1)} %pad_maximum_fusion.5), channel_id=1, source_target_pairs={{0,1},{1,0},{2,3},{3,2},{4,5},{5,4},{6,7},{7,6},{8,9},{9,8},{10,11... | collective-permute-start | bytes 2359304 | tf_op jit(solution)/shard_map/ppermute | solution.py:72
  88.2 13.5 %collective-permute-start.14 = (bf16[2,64,768]{2,1,0:T(8,128)(2,1)S(1)}, bf16[2,64,768]{2,1,0:T(8,128)(2,1)S(1)}, u32[]{:S(2)}, u32[]{:S(2)}) collective-permute-start(bf16[2,64,768]{2,1,0:T(8,128)(2,1)S(1)} %pad_maximum_fusion.17), channel_id=1, source_target_pairs={{0,1},{1,0},{2,3},{3,2},{4,5},{5,4},{6,7},{7,6},{8,9},{9,8},{10,11... | collective-permute-start | bytes 589832 | tf_op jit(solution)/shard_map/ppermute | solution.py:72
  89.3 12.5 %collective-permute-start.13 = (bf16[2,96,768]{2,1,0:T(8,128)(2,1)S(1)}, bf16[2,96,768]{2,1,0:T(8,128)(2,1)S(1)}, u32[]{:S(2)}, u32[]{:S(2)}) collective-permute-start(bf16[2,96,768]{2,1,0:T(8,128)(2,1)S(1)} %pad_maximum_fusion.15), channel_id=1, source_target_pairs={{0,4},{1,5},{2,6},{3,7},{4,0},{5,1},{6,2},{7,3},{8,12},{9,13},{10,... | collective-permute-start | bytes 884744 | tf_op jit(solution)/shard_map/ppermute | solution.py:69
  101.9 9.1 %collective-permute-start.19 = (bf16[4,96,768]{2,1,0:T(8,128)(2,1)S(1)}, bf16[4,96,768]{2,1,0:T(8,128)(2,1)S(1)}, u32[]{:S(2)}, u32[]{:S(2)}) collective-permute-start(bf16[4,96,768]{2,1,0:T(8,128)(2,1)S(1)} %pad_maximum_fusion.9), channel_id=1, source_target_pairs={{0,1},{1,0},{2,3},{3,2},{4,5},{5,4},{6,7},{7,6},{8,9},{9,8},{10,11... | collective-permute-start | bytes 1769480 | tf_op jit(solution)/shard_map/ppermute | solution.py:72
  103.4 12.1 %collective-permute-start.12 = (bf16[4,64,768]{2,1,0:T(8,128)(2,1)S(1)}, bf16[4,64,768]{2,1,0:T(8,128)(2,1)S(1)}, u32[]{:S(2)}, u32[]{:S(2)}) collective-permute-start(bf16[4,64,768]{2,1,0:T(8,128)(2,1)S(1)} %pad_maximum_fusion.11), channel_id=1, source_target_pairs={{0,4},{1,5},{2,6},{3,7},{4,0},{5,1},{6,2},{7,3},{8,12},{9,13},{10,... | collective-permute-start | bytes 1179656 | tf_op jit(solution)/shard_map/ppermute | solution.py:69
  103.7 13.1 %collective-permute-start.23 = (bf16[8,96,768]{2,1,0:T(8,128)(2,1)S(1)}, bf16[8,96,768]{2,1,0:T(8,128)(2,1)S(1)}, u32[]{:S(2)}, u32[]{:S(2)}) collective-permute-start(bf16[8,96,768]{2,1,0:T(8,128)(2,1)S(1)} %pad_maximum_fusion.2.refs_5_), channel_id=1, source_target_pairs={{0,16},{16,0},{1,17},{17,1},{2,18},{18,2},{3,19},{19,3},{4,20},{20... | collective-permute-start | bytes 3538952 | tf_op jit(solution)/shard_map/ppermute | solution.py:76
  107.0 10.1 %collective-permute-start.24 = (bf16[8,96,768]{2,1,0:T(8,128)(2,1)S(1)}, bf16[8,96,768]{2,1,0:T(8,128)(2,1)S(1)}, u32[]{:S(2)}, u32[]{:S(2)}) collective-permute-start(bf16[8,96,768]{2,1,0:T(8,128)(2,1)S(1)} %collective-permute-done.18.refs_6_), channel_id=1, source_target_pairs={{0,16},{16,0},{1,17},{17,1},{2,18},{18,2},{3,19},{19,3},{4,20},{20... | collective-permute-start | bytes 3538952 | tf_op jit(solution)/shard_map/ppermute | solution.py:76
  107.0 31.2 %collective-permute-start.25 = (bf16[8,48,2048]{2,1,0:T(8,128)(2,1)S(1)}, bf16[8,48,2048]{2,1,0:T(8,128)(2,1)S(1)}, u32[]{:S(2)}, u32[]{:S(2)}) collective-permute-start(bf16[8,48,2048]{2,1,0:T(8,128)(2,1)S(1)} %pad_maximum_fusion.refs_3_), channel_id=1, source_target_pairs={{0,16},{16,0},{1,17},{17,1},{2,18},{18,2},{3,19},{19,3},{4,20},{20... | collective-permute-start | bytes 4718600 | tf_op jit(solution)/shard_map/ppermute | solution.py:76
  111.0 29.9 %collective-permute-start.26 = (bf16[8,48,2048]{2,1,0:T(8,128)(2,1)S(1)}, bf16[8,48,2048]{2,1,0:T(8,128)(2,1)S(1)}, u32[]{:S(2)}, u32[]{:S(2)}) collective-permute-start(bf16[8,48,2048]{2,1,0:T(8,128)(2,1)S(1)} %collective-permute-done.20.refs_4_), channel_id=1, source_target_pairs={{0,16},{16,0},{1,17},{17,1},{2,18},{18,2},{3,19},{19,3},{4,20},{20... | collective-permute-start | bytes 4718600 | tf_op jit(solution)/shard_map/ppermute | solution.py:76
  115.6 11.2 %collective-permute-start.27 = (bf16[8,64,768]{2,1,0:T(8,128)(2,1)S(1)}, bf16[8,64,768]{2,1,0:T(8,128)(2,1)S(1)}, u32[]{:S(2)}, u32[]{:S(2)}) collective-permute-start(bf16[8,64,768]{2,1,0:T(8,128)(2,1)S(1)} %pad_maximum_fusion.6.refs_4_), channel_id=1, source_target_pairs={{0,2},{1,3},{2,0},{3,1},{4,6},{5,7},{6,4},{7,5},{8,10},{9,11},{10,... | collective-permute-start | bytes 2359304 | tf_op jit(solution)/shard_map/ppermute | solution.py:72
  116.8 35.1 %collective-permute-start.29 = (bf16[8,96,768]{2,1,0:T(8,128)(2,1)S(1)}, bf16[8,96,768]{2,1,0:T(8,128)(2,1)S(1)}, u32[]{:S(2)}, u32[]{:S(2)}) collective-permute-start(bf16[8,96,768]{2,1,0:T(8,128)(2,1)S(1)} %pad_maximum_fusion.3.refs_5_), channel_id=1, source_target_pairs={{0,2},{1,3},{2,0},{3,1},{4,6},{5,7},{6,4},{7,5},{8,10},{9,11},{10,... | collective-permute-start | bytes 3538952 | tf_op jit(solution)/shard_map/ppermute | solution.py:72
  117.1 40.8 %collective-permute-start.32 = (bf16[8,48,2048]{2,1,0:T(8,128)(2,1)}, bf16[8,48,2048]{2,1,0:T(8,128)(2,1)}, u32[]{:S(2)}, u32[]{:S(2)}) collective-permute-start(bf16[8,48,2048]{2,1,0:T(8,128)(2,1)} %pad_maximum_fusion.1.refs_3_), channel_id=1, source_target_pairs={{0,2},{1,3},{2,0},{3,1},{4,6},{5,7},{6,4},{7,5},{8,10},{9,11},{10,... | collective-permute-start | bytes 4718600 | tf_op jit(solution)/shard_map/ppermute | solution.py:72
  126.8 23.7 %collective-permute-start.22 = (bf16[4,64,768]{2,1,0:T(8,128)(2,1)S(1)}, bf16[4,64,768]{2,1,0:T(8,128)(2,1)S(1)}, u32[]{:S(2)}, u32[]{:S(2)}) collective-permute-start(bf16[4,64,768]{2,1,0:T(8,128)(2,1)S(1)} %pad_maximum_fusion.13), channel_id=1, source_target_pairs={{0,8},{1,9},{2,10},{3,11},{4,12},{5,13},{6,14},{7,15},{8,0},{9,1},... | collective-permute-start | bytes 1179656 | tf_op jit(solution)/shard_map/ppermute | solution.py:69
  138.3 15.9 %collective-permute-start.31 = (bf16[8,96,768]{2,1,0:T(8,128)(2,1)S(1)}, bf16[8,96,768]{2,1,0:T(8,128)(2,1)S(1)}, u32[]{:S(2)}, u32[]{:S(2)}) collective-permute-start(bf16[8,96,768]{2,1,0:T(8,128)(2,1)S(1)} %pad_maximum_fusion.3.refs_5_), channel_id=1, source_target_pairs={{0,16},{16,0},{1,17},{17,1},{2,18},{18,2},{3,19},{19,3},{4,20},{20... | collective-permute-start | bytes 3538952 | tf_op jit(solution)/shard_map/ppermute | solution.py:76
  151.9 8.3 %collective-permute-start.33 = (bf16[8,96,768]{2,1,0:T(8,128)(2,1)S(1)}, bf16[8,96,768]{2,1,0:T(8,128)(2,1)S(1)}, u32[]{:S(2)}, u32[]{:S(2)}) collective-permute-start(bf16[8,96,768]{2,1,0:T(8,128)(2,1)S(1)} %collective-permute-done.29.refs_6_), channel_id=1, source_target_pairs={{0,16},{16,0},{1,17},{17,1},{2,18},{18,2},{3,19},{19,3},{4,20},{20... | collective-permute-start | bytes 3538952 | tf_op jit(solution)/shard_map/ppermute | solution.py:76
  153.8 26.7 %collective-permute-start.34 = (bf16[8,48,2048]{2,1,0:T(8,128)(2,1)}, bf16[8,48,2048]{2,1,0:T(8,128)(2,1)}, u32[]{:S(2)}, u32[]{:S(2)}) collective-permute-start(bf16[8,48,2048]{2,1,0:T(8,128)(2,1)} %pad_maximum_fusion.1.refs_3_), channel_id=1, source_target_pairs={{0,16},{16,0},{1,17},{17,1},{2,18},{18,2},{3,19},{19,3},{4,20},{20... | collective-permute-start | bytes 4718600 | tf_op jit(solution)/shard_map/ppermute | solution.py:76
  157.9 22.6 %collective-permute-start.35 = (bf16[8,48,2048]{2,1,0:T(8,128)(2,1)}, bf16[8,48,2048]{2,1,0:T(8,128)(2,1)}, u32[]{:S(2)}, u32[]{:S(2)}) collective-permute-start(bf16[8,48,2048]{2,1,0:T(8,128)(2,1)} %collective-permute-done.32.refs_4_), channel_id=1, source_target_pairs={{0,16},{16,0},{1,17},{17,1},{2,18},{18,2},{3,19},{19,3},{4,20},{20... | collective-permute-start | bytes 4718600 | tf_op jit(solution)/shard_map/ppermute | solution.py:76
  158.4 19.3 %collective-permute-start.36 = (bf16[8,64,768]{2,1,0:T(8,128)(2,1)}, bf16[8,64,768]{2,1,0:T(8,128)(2,1)}, u32[]{:S(2)}, u32[]{:S(2)}) collective-permute-start(bf16[8,64,768]{2,1,0:T(8,128)(2,1)} %pad_maximum_fusion.7.refs_8_), channel_id=1, source_target_pairs={{0,4},{1,5},{2,6},{3,7},{4,0},{5,1},{6,2},{7,3},{8,12},{9,13},{10,... | collective-permute-start | bytes 2359304 | tf_op jit(solution)/shard_map/ppermute | solution.py:69
  159.8 34.5 %collective-permute-start.37 = (bf16[8,64,768]{2,1,0:T(8,128)(2,1)}, bf16[8,64,768]{2,1,0:T(8,128)(2,1)}, u32[]{:S(2)}, u32[]{:S(2)}) collective-permute-start(bf16[8,64,768]{2,1,0:T(8,128)(2,1)} %pad_maximum_fusion.7.refs_8_), channel_id=1, source_target_pairs={{0,16},{16,0},{1,17},{17,1},{2,18},{18,2},{3,19},{19,3},{4,20},{20... | collective-permute-start | bytes 2359304 | tf_op jit(solution)/shard_map/ppermute | solution.py:76
  177.7 16.7 %collective-permute-start.38 = (bf16[8,64,768]{2,1,0:T(8,128)(2,1)}, bf16[8,64,768]{2,1,0:T(8,128)(2,1)}, u32[]{:S(2)}, u32[]{:S(2)}) collective-permute-start(bf16[8,64,768]{2,1,0:T(8,128)(2,1)} %collective-permute-done.36.refs_9_), channel_id=1, source_target_pairs={{0,16},{16,0},{1,17},{17,1},{2,18},{18,2},{3,19},{19,3},{4,20},{20... | collective-permute-start | bytes 2359304 | tf_op jit(solution)/shard_map/ppermute | solution.py:76
  210.2 14.7 %collective-permute-start.39 = (bf16[512,3072]{1,0:T(8,128)(2,1)S(1)}, bf16[512,3072]{1,0:T(8,128)(2,1)S(1)}, u32[]{:S(2)}, u32[]{:S(2)}) collective-permute-start(bf16[512,3072]{1,0:T(8,128)(2,1)S(1)} %get-tuple-element.647.refs_5_.hid_own.own_ref.low.high), channel_id=1, source_target_pairs={{0,16},{16,0},{1,17},{17,1},{2,18},{18,2},{3,19},{19,3},{4,20},{20... | collective-permute-start | bytes 9437192 | tf_op jit(solution)/shard_map/ppermute | solution.py:76
  210.3 20.6 %collective-permute-start.41 = (bf16[512,2048]{1,0:T(8,128)(2,1)S(1)}, bf16[512,2048]{1,0:T(8,128)(2,1)S(1)}, u32[]{:S(2)}, u32[]{:S(2)}) collective-permute-start(bf16[512,2048]{1,0:T(8,128)(2,1)S(1)} %get-tuple-element.673), channel_id=1, source_target_pairs={{0,16},{16,0},{1,17},{17,1},{2,18},{18,2},{3,19},{19,3},{4,20},{20... | collective-permute-start | bytes 6291464 | tf_op jit(solution)/shard_map/ppermute | solution.py:76
  210.8 45.3 %collective-permute-start.44 = (bf16[512,1536]{1,0:T(8,128)(2,1)S(1)}, bf16[512,1536]{1,0:T(8,128)(2,1)S(1)}, u32[]{:S(2)}, u32[]{:S(2)}) collective-permute-start(bf16[512,1536]{1,0:T(8,128)(2,1)S(1)} %copy-done.5), channel_id=1, source_target_pairs={{0,16},{16,0},{1,17},{17,1},{2,18},{18,2},{3,19},{19,3},{4,20},{20... | collective-permute-start | bytes 4718600 | tf_op jit(solution)/shard_map/ppermute | solution.py:76
  229.2 11.2 %collective-permute-start.40 = (bf16[8,384,128]{2,1,0:T(8,128)(2,1)S(1)}, bf16[8,384,128]{2,1,0:T(8,128)(2,1)S(1)}, u32[]{:S(2)}, u32[]{:S(2)}) collective-permute-start(bf16[8,384,128]{2,1,0:T(8,128)(2,1)S(1)} %get-tuple-element.672), channel_id=1, source_target_pairs={{0,2},{1,3},{2,0},{3,1},{4,6},{5,7},{6,4},{7,5},{8,10},{9,11},{10,... | collective-permute-start | bytes 2359304 | tf_op jit(solution)/shard_map/ppermute | solution.py:72
  230.4 26.9 %collective-permute-start.43 = (bf16[512,2304]{1,0:T(8,128)(2,1)S(1)}, bf16[512,2304]{1,0:T(8,128)(2,1)S(1)}, u32[]{:S(2)}, u32[]{:S(2)}) collective-permute-start(bf16[512,2304]{1,0:T(8,128)(2,1)S(1)} %get-tuple-element.688), channel_id=1, source_target_pairs={{0,16},{16,0},{1,17},{17,1},{2,18},{18,2},{3,19},{19,3},{4,20},{20... | collective-permute-start | bytes 7077896 | tf_op jit(solution)/shard_map/ppermute | solution.py:76
  230.4 52.6 %collective-permute-start.46 = (bf16[512,3072]{1,0:T(8,128)(2,1)S(1)}, bf16[512,3072]{1,0:T(8,128)(2,1)S(1)}, u32[]{:S(2)}, u32[]{:S(2)}) collective-permute-start(bf16[512,3072]{1,0:T(8,128)(2,1)S(1)} %get-tuple-element.736.refs_2_.refs_3_.normed_ref.own_ref.hid_own), channel_id=1, source_target_pairs={{0,16},{16,0},{1,17},{17,1},{2,18},{18,2},{3,19},{19,3},{4,20},{20... | collective-permute-start | bytes 9437192 | tf_op jit(solution)/shard_map/ppermute | solution.py:76
  240.6 16.8 %collective-permute-start.42 = (bf16[512,1536]{1,0:T(8,128)(2,1)S(1)}, bf16[512,1536]{1,0:T(8,128)(2,1)S(1)}, u32[]{:S(2)}, u32[]{:S(2)}) collective-permute-start(bf16[512,1536]{1,0:T(8,128)(2,1)S(1)} %copy-done.3), channel_id=1, source_target_pairs={{0,16},{16,0},{1,17},{17,1},{2,18},{18,2},{3,19},{19,3},{4,20},{20... | collective-permute-start | bytes 4718600 | tf_op jit(solution)/shard_map/ppermute | solution.py:76
  241.9 22.2 %collective-permute-start.45 = (bf16[8,768,128]{2,1,0:T(8,128)(2,1)S(1)}, bf16[8,768,128]{2,1,0:T(8,128)(2,1)S(1)}, u32[]{:S(2)}, u32[]{:S(2)}) collective-permute-start(bf16[8,768,128]{2,1,0:T(8,128)(2,1)S(1)} %get-tuple-element.717), channel_id=1, source_target_pairs={{0,1},{1,0},{2,3},{3,2},{4,5},{5,4},{6,7},{7,6},{8,9},{9,8},{10,11... | collective-permute-start | bytes 4718600 | tf_op jit(solution)/shard_map/ppermute | solution.py:72
  256.1 26.9 %collective-permute-start.47 = (bf16[512,2048]{1,0:T(8,128)(2,1)S(1)}, bf16[512,2048]{1,0:T(8,128)(2,1)S(1)}, u32[]{:S(2)}, u32[]{:S(2)}) collective-permute-start(bf16[512,2048]{1,0:T(8,128)(2,1)S(1)} %get-tuple-element.737), channel_id=1, source_target_pairs={{0,16},{16,0},{1,17},{17,1},{2,18},{18,2},{3,19},{19,3},{4,20},{20... | collective-permute-start | bytes 6291464 | tf_op jit(solution)/shard_map/ppermute | solution.py:76
  264.3 27.0 %collective-permute-start.48 = (bf16[8,576,128]{2,1,0:T(8,128)(2,1)S(1)}, bf16[8,576,128]{2,1,0:T(8,128)(2,1)S(1)}, u32[]{:S(2)}, u32[]{:S(2)}) collective-permute-start(bf16[8,576,128]{2,1,0:T(8,128)(2,1)S(1)} %get-tuple-element.747), channel_id=1, source_target_pairs={{0,2},{1,3},{2,0},{3,1},{4,6},{5,7},{6,4},{7,5},{8,10},{9,11},{10,... | collective-permute-start | bytes 3538952 | tf_op jit(solution)/shard_map/ppermute | solution.py:72
  264.8 25.6 %collective-permute-start.49 = (bf16[4,768,128]{2,1,0:T(8,128)(2,1)S(1)}, bf16[4,768,128]{2,1,0:T(8,128)(2,1)S(1)}, u32[]{:S(2)}, u32[]{:S(2)}) collective-permute-start(bf16[4,768,128]{2,1,0:T(8,128)(2,1)S(1)} %add_convert_fusion.1), channel_id=1, source_target_pairs={{0,2},{1,3},{2,0},{3,1},{4,6},{5,7},{6,4},{7,5},{8,10},{9,11},{10,... | collective-permute-start | bytes 2359304 | tf_op jit(solution)/shard_map/ppermute | solution.py:72
  265.9 24.3 %collective-permute-start.50 = (bf16[4,384,128]{2,1,0:T(8,128)(2,1)S(1)}, bf16[4,384,128]{2,1,0:T(8,128)(2,1)S(1)}, u32[]{:S(2)}, u32[]{:S(2)}) collective-permute-start(bf16[4,384,128]{2,1,0:T(8,128)(2,1)S(1)} %add_convert_fusion.7), channel_id=1, source_target_pairs={{0,8},{1,9},{2,10},{3,11},{4,12},{5,13},{6,14},{7,15},{8,0},{9,1},... | collective-permute-start | bytes 1179656 | tf_op jit(solution)/shard_map/ppermute | solution.py:69
  292.4 11.8 %collective-permute-start.53 = (bf16[512,2304]{1,0:T(8,128)(2,1)}, bf16[512,2304]{1,0:T(8,128)(2,1)}, u32[]{:S(2)}, u32[]{:S(2)}) collective-permute-start(bf16[512,2304]{1,0:T(8,128)(2,1)} %get-tuple-element.768), channel_id=1, source_target_pairs={{0,16},{16,0},{1,17},{17,1},{2,18},{18,2},{3,19},{19,3},{4,20},{20... | collective-permute-start | bytes 7077896 | tf_op jit(solution)/shard_map/ppermute | solution.py:76
  293.5 19.9 %collective-permute-start.52 = (bf16[8,768,128]{2,1,0:T(8,128)(2,1)}, bf16[8,768,128]{2,1,0:T(8,128)(2,1)}, u32[]{:S(2)}, u32[]{:S(2)}) collective-permute-start(bf16[8,768,128]{2,1,0:T(8,128)(2,1)} %get-tuple-element.767), channel_id=1, source_target_pairs={{0,2},{1,3},{2,0},{3,1},{4,6},{5,7},{6,4},{7,5},{8,10},{9,11},{10,... | collective-permute-start | bytes 4718600 | tf_op jit(solution)/shard_map/ppermute | solution.py:72
  294.1 21.7 %collective-permute-start.51 = (bf16[4,576,128]{2,1,0:T(8,128)(2,1)}, bf16[4,576,128]{2,1,0:T(8,128)(2,1)S(1)}, u32[]{:S(2)}, u32[]{:S(2)}) collective-permute-start(bf16[4,576,128]{2,1,0:T(8,128)(2,1)} %add_convert_fusion.3), channel_id=1, source_target_pairs={{0,4},{1,5},{2,6},{3,7},{4,0},{5,1},{6,2},{7,3},{8,12},{9,13},{10,... | collective-permute-start | bytes 1769480 | tf_op jit(solution)/shard_map/ppermute | solution.py:69
  296.0 21.5 %collective-permute-start.56 = (bf16[2,768,128]{2,1,0:T(8,128)(2,1)S(1)}, bf16[2,768,128]{2,1,0:T(8,128)(2,1)S(1)}, u32[]{:S(2)}, u32[]{:S(2)}) collective-permute-start(bf16[2,768,128]{2,1,0:T(8,128)(2,1)S(1)} %copy-done.50), channel_id=1, source_target_pairs={{0,4},{1,5},{2,6},{3,7},{4,0},{5,1},{6,2},{7,3},{8,12},{9,13},{10,... | collective-permute-start | bytes 1179656 | tf_op jit(solution)/shard_map/ppermute | solution.py:69
  296.9 24.8 %collective-permute-start.59 = (bf16[2,384,128]{2,1,0:T(8,128)(2,1)S(1)}, bf16[2,384,128]{2,1,0:T(8,128)(2,1)S(1)}, u32[]{:S(2)}, u32[]{:S(2)}) collective-permute-start(bf16[2,384,128]{2,1,0:T(8,128)(2,1)S(1)} %add_convert_fusion.13), channel_id=1, source_target_pairs={{0,4},{1,5},{2,6},{3,7},{4,0},{5,1},{6,2},{7,3},{8,12},{9,13},{10,... | collective-permute-start | bytes 589832 | tf_op jit(solution)/shard_map/ppermute | solution.py:69
  313.4 16.6 %collective-permute-start.58 = (bf16[8,576,128]{2,1,0:T(8,128)(2,1)S(1)}, bf16[8,576,128]{2,1,0:T(8,128)(2,1)S(1)}, u32[]{:S(2)}, u32[]{:S(2)}) collective-permute-start(bf16[8,576,128]{2,1,0:T(8,128)(2,1)S(1)} %get-tuple-element.795), channel_id=1, source_target_pairs={{0,2},{1,3},{2,0},{3,1},{4,6},{5,7},{6,4},{7,5},{8,10},{9,11},{10,... | collective-permute-start | bytes 3538952 | tf_op jit(solution)/shard_map/ppermute | solution.py:72
  321.7 12.9 %collective-permute-start.57 = (bf16[1,768,128]{2,1,0:T(8,128)(2,1)S(1)}, bf16[1,768,128]{2,1,0:T(8,128)(2,1)S(1)}, u32[]{:S(2)}, u32[]{:S(2)}) collective-permute-start(bf16[1,768,128]{2,1,0:T(8,128)(2,1)S(1)} %add_convert_fusion.12), channel_id=1, source_target_pairs={{0,8},{1,9},{2,10},{3,11},{4,12},{5,13},{6,14},{7,15},{8,0},{9,1},... | collective-permute-start | bytes 589832 | tf_op jit(solution)/shard_map/ppermute | solution.py:69
  322.8 14.2 %collective-permute-start.55 = (bf16[2,576,128]{2,1,0:T(8,128)(2,1)S(1)}, bf16[2,576,128]{2,1,0:T(8,128)(2,1)S(1)}, u32[]{:S(2)}, u32[]{:S(2)}) collective-permute-start(bf16[2,576,128]{2,1,0:T(8,128)(2,1)S(1)} %add_convert_fusion.9), channel_id=1, source_target_pairs={{0,1},{1,0},{2,3},{3,2},{4,5},{5,4},{6,7},{7,6},{8,9},{9,8},{10,11... | collective-permute-start | bytes 884744 | tf_op jit(solution)/shard_map/ppermute | solution.py:72
  324.0 13.6 %collective-permute-start.54 = (bf16[512,768]{1,0:T(8,128)(2,1)S(1)}, bf16[512,768]{1,0:T(8,128)(2,1)S(1)}, u32[]{:S(2)}, u32[]{:S(2)}) collective-permute-start(bf16[512,768]{1,0:T(8,128)(2,1)S(1)} %get-tuple-element.787), channel_id=1, source_target_pairs={{0,16},{16,0},{1,17},{17,1},{2,18},{18,2},{3,19},{19,3},{4,20},{20... | collective-permute-start | bytes 2359304 | tf_op jit(solution)/shard_map/ppermute | solution.py:76
  325.5 15.9 %collective-permute-start.61 = (bf16[4,768,128]{2,1,0:T(8,128)(2,1)S(1)}, bf16[4,768,128]{2,1,0:T(8,128)(2,1)S(1)}, u32[]{:S(2)}, u32[]{:S(2)}) collective-permute-start(bf16[4,768,128]{2,1,0:T(8,128)(2,1)S(1)} %add_convert_fusion), channel_id=1, source_target_pairs={{0,1},{1,0},{2,3},{3,2},{4,5},{5,4},{6,7},{7,6},{8,9},{9,8},{10,11... | collective-permute-start | bytes 2359304 | tf_op jit(solution)/shard_map/ppermute | solution.py:72
  334.6 10.7 %collective-permute-start.60 = (bf16[4,576,128]{2,1,0:T(8,128)(2,1)S(1)}, bf16[4,576,128]{2,1,0:T(8,128)(2,1)S(1)}, u32[]{:S(2)}, u32[]{:S(2)}) collective-permute-start(bf16[4,576,128]{2,1,0:T(8,128)(2,1)S(1)} %add_convert_fusion.2), channel_id=1, source_target_pairs={{0,4},{1,5},{2,6},{3,7},{4,0},{5,1},{6,2},{7,3},{8,12},{9,13},{10,... | collective-permute-start | bytes 1769480 | tf_op jit(solution)/shard_map/ppermute | solution.py:69
  334.9 15.3 %collective-permute-start.64 = (bf16[8,384,128]{2,1,0:T(8,128)(2,1)S(1)}, bf16[8,384,128]{2,1,0:T(8,128)(2,1)S(1)}, u32[]{:S(2)}, u32[]{:S(2)}) collective-permute-start(bf16[8,384,128]{2,1,0:T(8,128)(2,1)S(1)} %get-tuple-element.836), channel_id=1, source_target_pairs={{0,1},{1,0},{2,3},{3,2},{4,5},{5,4},{6,7},{7,6},{8,9},{9,8},{10,11... | collective-permute-start | bytes 2359304 | tf_op jit(solution)/shard_map/ppermute | solution.py:72
  337.0 31.4 %collective-permute-start.70 = (bf16[1,384,128]{2,1,0:T(8,128)(2,1)S(1)}, bf16[1,384,128]{2,1,0:T(8,128)(2,1)S(1)}, u32[]{:S(2)}, u32[]{:S(2)}) collective-permute-start(bf16[1,384,128]{2,1,0:T(8,128)(2,1)S(1)} %add_convert_fusion.17), channel_id=1, source_target_pairs={{0,1},{1,0},{2,3},{3,2},{4,5},{5,4},{6,7},{7,6},{8,9},{9,8},{10,11... | collective-permute-start | bytes 294920 | tf_op jit(solution)/shard_map/ppermute | solution.py:72
  342.7 14.4 %collective-permute-start.63 = (bf16[2,768,128]{2,1,0:T(8,128)(2,1)S(1)}, bf16[2,768,128]{2,1,0:T(8,128)(2,1)S(1)}, u32[]{:S(2)}, u32[]{:S(2)}) collective-permute-start(bf16[2,768,128]{2,1,0:T(8,128)(2,1)S(1)} %add_convert_fusion.5), channel_id=1, source_target_pairs={{0,4},{1,5},{2,6},{3,7},{4,0},{5,1},{6,2},{7,3},{8,12},{9,13},{10,... | collective-permute-start | bytes 1179656 | tf_op jit(solution)/shard_map/ppermute | solution.py:69
  343.4 16.0 %collective-permute-start.67 = (bf16[1,576,128]{2,1,0:T(8,128)(2,1)S(1)}, bf16[1,576,128]{2,1,0:T(8,128)(2,1)S(1)}, u32[]{:S(2)}, u32[]{:S(2)}) collective-permute-start(bf16[1,576,128]{2,1,0:T(8,128)(2,1)S(1)} %add_convert_fusion.15), channel_id=1, source_target_pairs={{0,8},{1,9},{2,10},{3,11},{4,12},{5,13},{6,14},{7,15},{8,0},{9,1},... | collective-permute-start | bytes 442376 | tf_op jit(solution)/shard_map/ppermute | solution.py:69
  345.4 14.0 %collective-permute-start.62 = (bf16[2,576,128]{2,1,0:T(8,128)(2,1)S(1)}, bf16[2,576,128]{2,1,0:T(8,128)(2,1)S(1)}, u32[]{:S(2)}, u32[]{:S(2)}) collective-permute-start(bf16[2,576,128]{2,1,0:T(8,128)(2,1)S(1)} %add_convert_fusion.8), channel_id=1, source_target_pairs={{0,1},{1,0},{2,3},{3,2},{4,5},{5,4},{6,7},{7,6},{8,9},{9,8},{10,11... | collective-permute-start | bytes 884744 | tf_op jit(solution)/shard_map/ppermute | solution.py:72
  358.1 10.1 %collective-permute-start.66 = (bf16[4,384,128]{2,1,0:T(8,128)(2,1)S(1)}, bf16[4,384,128]{2,1,0:T(8,128)(2,1)S(1)}, u32[]{:S(2)}, u32[]{:S(2)}) collective-permute-start(bf16[4,384,128]{2,1,0:T(8,128)(2,1)S(1)} %add_convert_fusion.4), channel_id=1, source_target_pairs={{0,2},{1,3},{2,0},{3,1},{4,6},{5,7},{6,4},{7,5},{8,10},{9,11},{10,... | collective-permute-start | bytes 1179656 | tf_op jit(solution)/shard_map/ppermute | solution.py:72
  359.3 15.8 %collective-permute-start.69 = (bf16[1,768,128]{2,1,0:T(8,128)(2,1)S(1)}, bf16[1,768,128]{2,1,0:T(8,128)(2,1)S(1)}, u32[]{:S(2)}, u32[]{:S(2)}) collective-permute-start(bf16[1,768,128]{2,1,0:T(8,128)(2,1)S(1)} %add_convert_fusion.11), channel_id=1, source_target_pairs={{0,8},{1,9},{2,10},{3,11},{4,12},{5,13},{6,14},{7,15},{8,0},{9,1},... | collective-permute-start | bytes 589832 | tf_op jit(solution)/shard_map/ppermute | solution.py:69
  359.6 21.7 %collective-permute-start.65 = (bf16[1,576,128]{2,1,0:T(8,128)(2,1)S(1)}, bf16[1,576,128]{2,1,0:T(8,128)(2,1)S(1)}, u32[]{:S(2)}, u32[]{:S(2)}) collective-permute-start(bf16[1,576,128]{2,1,0:T(8,128)(2,1)S(1)} %add_convert_fusion.14), channel_id=1, source_target_pairs={{0,8},{1,9},{2,10},{3,11},{4,12},{5,13},{6,14},{7,15},{8,0},{9,1},... | collective-permute-start | bytes 442376 | tf_op jit(solution)/shard_map/ppermute | solution.py:69
  376.3 10.6 %collective-permute-start.73 = (f32[768,128]{1,0:T(8,128)S(1)}, f32[768,128]{1,0:T(8,128)S(1)}, u32[]{:S(2)}, u32[]{:S(2)}) collective-permute-start(f32[768,128]{1,0:T(8,128)S(1)} %get-tuple-element.883), channel_id=1, source_target_pairs={{0,16},{16,0},{1,17},{17,1},{2,18},{18,2},{3,19},{19,3},{4,20},{20... | collective-permute-start | bytes 1179656 | tf_op jit(solution)/shard_map/ppermute | solution.py:76
  381.5 10.8 %collective-permute-start.71 = (f32[576,128]{1,0:T(8,128)S(1)}, f32[576,128]{1,0:T(8,128)S(1)}, u32[]{:S(2)}, u32[]{:S(2)}) collective-permute-start(f32[576,128]{1,0:T(8,128)S(1)} %get-tuple-element.876), channel_id=1, source_target_pairs={{0,16},{16,0},{1,17},{17,1},{2,18},{18,2},{3,19},{19,3},{4,20},{20... | collective-permute-start | bytes 884744 | tf_op jit(solution)/shard_map/ppermute | solution.py:76
  (68 other events, 656.3 us)

commit v3 on v2

--- a/solution.py
+++ b/solution.py
@@ -27,31 +27,28 @@
 X, Y, ZL, ZH = 1, 2, 4, 8
 GATHER = (
     ((ZH, ZL, Y, X), None),
+    ((ZH, X, ZL, Y), None),
+    ((Y, ZH, ZL, X), None),
+    ((ZH, ZL, Y, X), None),
     ((ZH, ZL, X, Y), None),
-    ((X, ZH, ZL, Y), None),
-    ((ZH, ZL, X, Y), None),
-    ((ZL, ZH, X, Y), None),
-    ((Y, X, ZH, ZL), None),
+    ((ZH, X, Y, ZL), None),
 )
 SCATTER = {
-    "D1": (Y, ZH, ZL, X),
-    "G1": (X, Y, ZL, ZH),
-    "T1": (Y, ZL, X, ZH),
-    "D0": (X, Y, ZL, ZH),
+    "D1": (X, ZL, Y, ZH),
+    "G1": (Y, ZL, X, ZH),
+    "T1": (ZL, X, Y, ZH),
     "G0": (Y, X, ZL, ZH),
-    "T0": (Y, ZL, X, ZH),
+    "T0": (X, Y, ZL, ZH),
 }
 ORDER = (
-    "g50", "g20", "g00", "g10", "g21", "g01", "g11", "g30", "g51", "g02", "g12", "g31", "g40",
-    "g03", "g22", "g13", "g41", "v0", "g42", "w0", "g52", "g32", "w1", "g43", "v1", "g33", "g23",
-    "A0", "v2", "w3", "F0", "xa0", "g53", "w2", "w4", "w5", "v3", "dw2", "dw3", "L0", "v4", "A1",
-    "v5", "F1", "B1", "xf1", "xs1", "K1", "D1", "xf0", "rD10", "xt1", "G1", "rD11", "xa1", "rG10",
-    "B0", "dxa0", "xs0", "T1", "rG11", "rT10", "K0", "G0", "rD12", "rG12", "rT11", "rG00", "xt0",
-    "L1", "T0", "rT00", "oi", "rG01", "rT12", "oa", "rG13", "rD13", "rT01", "D0", "rD00", "zG1",
-    "rT13", "doa", "rG02", "rT02", "ob", "rD01", "rG03", "rT03", "zT1", "rD02", "zD1", "zG0", "hG",
-    "rD03", "zT0", "hT", "zD0", "dhG", "hD", "u2", "u1",
+    "g40", "g10", "g20", "g00", "g50", "g01", "g30", "g21", "g11", "g02", "g31", "g51", "g12",
+    "g32", "g52", "g03", "g33", "g13", "g53", "g22", "w1", "g41", "w0", "v0", "g23", "v3", "w3",
+    "g42", "A0", "w2", "dg42", "v1", "g43", "xa0", "F0", "v2", "w4", "w5", "L0", "A1", "v5", "xf0",
+    "xa1", "v4", "F1", "B1", "xf1", "dxa0", "K1", "xs1", "B0", "xt1", "G1", "rG10", "xs0", "D1",
+    "G0", "rG00", "rG11", "L1", "T1", "rD10", "K0", "rG12", "rT10", "xt0", "rG01", "T0", "rD11",
+    "rT00", "oa", "rT11", "rG02", "rD12", "doa", "rT01", "ob", "rG13", "rT12", "rG03", "oi", "rD13",
+    "zG1", "rT02", "zG0", "rT13", "rT03", "zD1", "hG", "zT1", "zT0", "hT", "u1", "u2",
 )
-
 
 def order_masks(order):
     masks = [0]
@@ -332,6 +329,7 @@
     @pl.when(step >= lead)
     def _():
         cols = pl.ds(pl.multiple_of((step - lead) * FBLOCK, FBLOCK), FBLOCK)
+        cols = slice(None) if wg.shape[-1] == FBLOCK else cols
         gate = dot(normed[:, :D], matrix(wg, cols=cols))
         up = dot(normed[:, :D], matrix(wu, cols=cols))
         sig = 0.5 * jnp.tanh(0.5 * gate) + 0.5
@@ -341,14 +339,13 @@
         s2_ref[...] = silu.astype(BF16)
 
 
-def feed(info, x, x_rows, act, wo, gathered):
+def feed(info, x, x_rows, act, wo, w):
     rows = 2 * SLOT
     lead = PACK // FBLOCK
     whole = lambda j, info: (0, 0)
-    wide = pl.BlockSpec((rows, FBLOCK), lambda j, info: (0, jnp.maximum(j - lead, 0)))
-    return launch_loaded(
-        gathered,
-        feed_kernel,
+    late = lambda j: jnp.maximum(j - lead, 0)
+    wide = pl.BlockSpec((rows, FBLOCK), lambda j, info: (0, late(j)))
+    args = (
         (info,),
         (lead + FF // FBLOCK,),
         (x, act, wo),
@@ -374,6 +371,13 @@
         cost(2 * rows * D * (D + 2 * FF), 18e6),
         [pltpu.VMEM((rows, PACK), BF16)],
     )
+    if isinstance(w, Gathered):
+        return launch_loaded(w, feed_kernel, *args)
+    prefetch, grid, inputs, in_specs, *rest = args
+    gate = pl.BlockSpec((D, FBLOCK), lambda j, info: (0, late(j)))
+    up = pl.BlockSpec((D, FBLOCK), lambda j, info: (1, late(j)))
+    in_specs = [*in_specs, gate, up]
+    return launch(feed_kernel, prefetch, grid, (*inputs, *far(w, w)), in_specs, *rest)
 
 
 def leave_kernel(info, lim, middle_ref, low, high, wd, out_ref):
@@ -405,6 +409,9 @@
     return launch(leave_kernel, prefetch, grid, (*inputs, wd), in_specs, *rest)
 
 
+GRADS = FF + FBLOCK
+
+
 def feed_back_kernel(
     info,
     grad_ref,
@@ -419,7 +426,6 @@
     keep_ref,
     send_ref,
     gmid_ref,
-    gz_ref,
     gmix_ref,
     total,
 ):
@@ -460,11 +466,18 @@
         gmid = grad_ref[...].astype(F32) + scale_ref[:, :1] * (gn - normed * mean)
         gz = gmid.astype(BF16)
         gmid_ref[...] = gmid
-        gz_ref[...] = gz
         gmix_ref[...] = dot_nt(gz, wo[...]).astype(BF16)
-
-
-def feed_back(info, grad, grad_rows, wd, wg, wu, s1, s2, pack, scale, wo):
+        pad = jnp.zeros((gz.shape[0], GRADS - FF - HALF), BF16)
+        for h in range(2):
+
+            @pl.when(info[1] == h)
+            def _():
+                for out, half in ((keep_ref, h), (send_ref, 1 - h)):
+                    out[:, FF : FF + HALF] = gz[:, half * HALF : (half + 1) * HALF]
+                    out[:, FF + HALF :] = pad
+
+
+def feed_back(info, grad, grad_rows, wd, wg, wu, up_row, s1, s2, pack, scale, wo):
     rows = 2 * SLOT
     whole = lambda j, info: (0, 0)
     col = pl.BlockSpec((D, FBLOCK), lambda j, info: (0, j))
@@ -477,7 +490,7 @@
         [
             pl.BlockSpec((rows, D), lambda j, info: (info[grad_rows], 0)),
             col,
-            col,
+            pl.BlockSpec((D, FBLOCK), lambda j, info: (up_row, j)),
             wide,
             wide,
             full,
@@ -485,16 +498,14 @@
             pl.BlockSpec((D, D), whole),
         ],
         [
-            shape(rows, FF),
-            shape(rows, FF),
+            shape(rows, GRADS),
+            shape(rows, GRADS),
             shape(rows, D, dtype=F32),
-            shape(rows, D),
             shape(rows, D),
         ],
         [
-            pl.BlockSpec((rows, FF), whole),
-            pl.BlockSpec((rows, FF), whole),
-            full,
+            pl.BlockSpec((rows, GRADS), whole),
+            pl.BlockSpec((rows, GRADS), whole),
             full,
             full,
         ],
@@ -519,7 +530,6 @@
     normed_ref,
     scale_ref,
     gmid_ref,
-    gz_ref,
     cos,
     sin_a,
     sin_b,
@@ -556,31 +566,30 @@
     mean = jnp.mean(gn * normed, axis=1, keepdims=True)
     gin = gmid_ref[...] + scale_ref[:, :1] * (gn - normed * mean)
     gin_ref[...] = gin.astype(BF16)
-    send_ref[:, 4 * HALF :] = gin.astype(BF16)
+    send_ref[:, 3 * HALF :] = gin.astype(BF16)
     for h in range(2):
 
         @pl.when(info[1] == h)
         def _():
             for out, half in ((keep_ref, h), (send_ref, 1 - h)):
                 cols = slice(half * HALF, (half + 1) * HALF)
-                out[:, :HALF] = gz_ref[:, cols]
                 for part in range(3):
-                    out[:, (part + 1) * HALF : (part + 2) * HALF] = grads[part, :, cols]
-
-
-def attention_back(info, gmix, qkv, probs, wq, wk, wv, act, scale, gmid, gz, tables):
+                    out[:, part * HALF : (part + 1) * HALF] = grads[part, :, cols]
+
+
+def attention_back(info, gmix, qkv, probs, wq, wk, wv, act, scale, gmid, tables):
     rows = 2 * SLOT
     whole = lambda i, info: (0, 0)
     table = pl.BlockSpec((SLOT, LANES), whole)
     weight = pl.BlockSpec((D, D), whole)
     full = pl.BlockSpec((SLOT, D), lambda i, info: (i, 0))
-    pack = pl.BlockSpec((SLOT, 4 * HALF), lambda i, info: (i, 0))
-    longer = pl.BlockSpec((SLOT, 6 * HALF), lambda i, info: (i, 0))
+    pack = pl.BlockSpec((SLOT, 3 * HALF), lambda i, info: (i, 0))
+    longer = pl.BlockSpec((SLOT, 5 * HALF), lambda i, info: (i, 0))
     return launch(
         attention_back_kernel,
         (info,),
         (2,),
-        (gmix, *far(qkv, probs, wq, wk, wv), act, *far(scale), gmid, gz, *tables),
+        (gmix, *far(qkv, probs, wq, wk, wv), act, *far(scale), gmid, *tables),
         [
                 full,
                 pl.BlockSpec((SLOT, 3 * D), lambda i, info: (i, 0)),
@@ -591,30 +600,133 @@
                 full,
                 pl.BlockSpec((SLOT, LANES), lambda i, info: (i, 0)),
                 full,
-                full,
                 table,
                 table,
                 table,
             ],
-        [shape(rows, D), shape(rows, 4 * HALF), shape(rows, 6 * HALF)],
+        [shape(rows, D), shape(rows, 3 * HALF), shape(rows, 5 * HALF)],
         [full, pack, longer],
         cost(2 * rows * D * 3 * D + 24 * 8 * 256 * 256 * 128, 16e6),
         [pltpu.VMEM((3, SLOT, D), BF16)],
     )
 
 
-def spread(info, masks, scratch, rows, lane_blocks, keep, send, row_to):
-    for place, (low, high) in enumerate(zip(*masks)):
-        shard = info[0] ^ (low + (high - low) * info[1])
+def spread(info, where, scratch, rows, lane_blocks, outs, row_to):
+    for place in range(16):
+        if len(outs) == 2:
+            low, high = where[0][place], where[1][place]
+            shard = info[0] ^ (low + (high - low) * info[1])
+        else:
+            shard = ((info[0] ^ where[place % 4]) & 12) + place // 4
         at = pl.multiple_of(shard * rows, 16)
-        out = keep if place < 8 else send
+        out = outs[place // 8] if len(outs) == 2 else outs[0]
+        slot = place % 8 if len(outs) == 2 else place
         for block in range(lane_blocks):
-            out[place % 8, pl.ds(row_to + block * rows, rows), :] = scratch[
+            out[slot, pl.ds(row_to + block * rows, rows), :] = scratch[
                 pl.ds(at, rows), block * LANES : (block + 1) * LANES
             ]
 
 
-def gate_weight_kernel(masks, info, own_ref, oth_ref, g_own, g_oth, keep, send, turned, tile):
+def spread_shapes(planar, rows):
+    count, dims = (1, (16, rows, LANES)) if planar else (2, (8, rows, LANES))
+    return [shape(*dims)] * count, [pl.BlockSpec(dims, lambda j, info: (0, 0, 0))] * count
+
+
+def feed_weight_kernel(where, gates, downs, info, *refs):
+    rows = 2 * SLOT
+    steps = FF // FBLOCK
+    first = (steps + 1) * gates
+    outs = list(refs[: len(refs) - 2 * gates - downs])
+    refs = list(refs[len(outs) :])
+    if gates:
+        (own_ref, oth_ref, act_own, act_oth, g_own, g_oth), outs = outs[:6], outs[6:]
+        turned, tile = refs[:2]
+    if downs:
+        (hid_own, hid_oth, gf_own, gf_oth), outs = outs[:4], outs[4:]
+        down = refs[-1]
+    step = pl.program_id(0)
+    if gates:
+
+        @pl.when(step == 0)
+        def _():
+            turned[:, :rows] = own_ref[...].T
+            turned[:, rows:] = oth_ref[...].T
+
+        @pl.when(step == steps)
+        def _():
+            turned[:, :rows] = act_own[...].T
+            turned[:, rows:] = act_oth[...].T
+
+        @pl.when(step <= steps)
+        def _():
+            tile[...] = (
+                dot(turned[:, :rows], g_own[...]) + dot(turned[:, rows:], g_oth[...])
+            ).astype(BF16)
+
+        @pl.when(step < steps)
+        def _():
+            spread(info, where, tile, 48, 4, outs, pl.multiple_of(step * 192, 16))
+
+        @pl.when(step == steps)
+        def _():
+            spread(info, where, tile, 48, 3, outs, 768)
+
+    if downs:
+
+        @pl.when(step >= first)
+        def _():
+            at = pl.multiple_of((step - first) * FBLOCK, FBLOCK)
+            down[pl.ds(at, FBLOCK), :] = (
+                dot_tn(hid_own[...], gf_own[...]) + dot_tn(hid_oth[...], gf_oth[...])
+            ).astype(BF16)
+
+        @pl.when(step == first + steps - 1)
+        def _():
+            spread(info, where, down, 128, 3, outs, 912 * gates)
+
+
+def feed_weight(info, where, planar, gates, downs):
+    rows = 2 * SLOT
+    steps = FF // FBLOCK
+    first = (steps + 1) * bool(gates)
+    whole = lambda j, info: (0, 0)
+    inputs, specs, scratch = [], [], []
+    if gates:
+        full = pl.BlockSpec((rows, D), whole)
+        mixed = pl.BlockSpec((rows, D), lambda j, info: (0, 1))
+        grad = pl.BlockSpec((rows, FBLOCK), lambda j, info: (0, jnp.minimum(j, steps)))
+        inputs += gates
+        specs += [full, full, mixed, mixed, grad, grad]
+        scratch += [pltpu.VMEM((D, 2 * rows), BF16), pltpu.VMEM((D, FBLOCK), BF16)]
+    if downs:
+        *arrays, own_at, oth_at, col = downs
+        hid = pl.BlockSpec(
+            (rows, FBLOCK), lambda j, info: (0, jnp.maximum(j - first, 0) + PACK // FBLOCK)
+        )
+        inputs += arrays
+        specs += [
+            hid,
+            hid,
+            pl.BlockSpec((rows, HALF), lambda j, info: (info[own_at], info[1])),
+            pl.BlockSpec((rows, HALF), lambda j, info: (info[oth_at], col + info[1])),
+        ]
+        scratch += [pltpu.VMEM((FF, HALF), BF16)]
+    out_shape, out_specs = spread_shapes(planar, 912 * bool(gates) + 384 * bool(downs))
+    return launch(
+        functools.partial(feed_weight_kernel, where, bool(gates), bool(downs)),
+        (info,),
+        (first + steps * bool(downs),),
+        inputs,
+        specs,
+        out_shape,
+        out_specs,
+        cost(2 * rows * D * 3 * FF, 20e6),
+        scratch,
+    )
+
+
+def attention_weight_kernel(where, info, own_ref, oth_ref, g_own, g_oth, *refs):
+    outs, (turned, tile) = refs[:-2], refs[-2:]
     step = pl.program_id(0)
     rows = 2 * SLOT
 
@@ -626,95 +738,23 @@
     tile[...] = (
         dot(turned[:, :rows], g_own[...]) + dot(turned[:, rows:], g_oth[...])
     ).astype(BF16)
-    spread(info, masks, tile, 48, 4, keep, send, pl.multiple_of(step * 192, 16))
-
-
-def gate_weight(info, masks, own, oth, g_own, g_oth):
+    spread(info, where, tile, 48, 3, outs, pl.multiple_of(step * 144, 16))
+
+
+def attention_weight(info, where, planar, own, oth, g_own, g_oth):
     rows = 2 * SLOT
     full = pl.BlockSpec((rows, D), lambda j, info: (0, 0))
-    grad = pl.BlockSpec((rows, 512), lambda j, info: (0, j))
-    out = pl.BlockSpec((8, 768, LANES), lambda j, info: (0, 0, 0))
+    grad = pl.BlockSpec((rows, HALF), lambda j, info: (0, j))
+    out_shape, out_specs = spread_shapes(planar, 432)
     return launch(
-        functools.partial(gate_weight_kernel, masks),
+        functools.partial(attention_weight_kernel, where),
         (info,),
-        (4,),
+        (3,),
         (own, oth, g_own, g_oth),
         [full, full, grad, grad],
-        [shape(8, 768, LANES)] * 2,
-        [out] * 2,
-        cost(2 * rows * D * 2 * FF, 14e6),
-        [pltpu.VMEM((D, 2 * rows), BF16), pltpu.VMEM((D, 512), BF16)],
-    )
-
-
-def down_weight_kernel(masks, info, hid_own, hid_oth, gf_own, gf_oth, keep, send, down):
-    step = pl.program_id(0)
-    at = pl.multiple_of(step * FBLOCK, FBLOCK)
-    down[pl.ds(at, FBLOCK), :] = (
-        dot_tn(hid_own[...], gf_own[...]) + dot_tn(hid_oth[...], gf_oth[...])
-    ).astype(BF16)
-
-    @pl.when(step == FF // FBLOCK - 1)
-    def _():
-        spread(info, masks, down, 128, 3, keep, send, 0)
-
-
-def down_weight(info, masks, pack_own, pack_oth, gf_own, gf_oth, rows_of, col):
-    rows = 2 * SLOT
-    hid = pl.BlockSpec((rows, FBLOCK), lambda j, info: (0, j + PACK // FBLOCK))
-    out = pl.BlockSpec((8, 384, LANES), lambda j, info: (0, 0, 0))
-    return launch(
-        functools.partial(down_weight_kernel, masks),
-        (info,),
-        (FF // FBLOCK,),
-        (pack_own, pack_oth, gf_own, gf_oth),
-        [
-            hid,
-            hid,
-            pl.BlockSpec((rows, HALF), lambda j, info: (info[rows_of[0]], info[1])),
-            pl.BlockSpec((rows, HALF), lambda j, info: (info[rows_of[1]], col + info[1])),
-        ],
-        [shape(8, 384, LANES)] * 2,
-        [out] * 2,
-        cost(2 * rows * D * FF, 9e6),
-        [pltpu.VMEM((FF, HALF), BF16)],
-    )
-
-
-def attention_weight_kernel(masks, info, own_ref, oth_ref, g_own, g_oth, keep, send, turned, tile):
-    step = pl.program_id(0)
-    rows = 2 * SLOT
-
-    @pl.when(step == 0)
-    def _():
-        turned[:, :rows] = own_ref[:, D:].T
-        turned[:, rows:] = oth_ref[:, D:].T
-
-    @pl.when(step == 1)
-    def _():
-        turned[:, :rows] = own_ref[:, :D].T
-        turned[:, rows:] = oth_ref[:, :D].T
-
-    tile[...] = (
-        dot(turned[:, :rows], g_own[...]) + dot(turned[:, rows:], g_oth[...])
-    ).astype(BF16)
-    spread(info, masks, tile, 48, 3, keep, send, pl.multiple_of(step * 144, 16))
-
-
-def attention_weight(info, masks, own, oth, g_own, g_oth):
-    rows = 2 * SLOT
-    full = pl.BlockSpec((rows, 2 * D), lambda j, info: (0, 0))
-    grad = pl.BlockSpec((rows, HALF), lambda j, info: (0, j))
-    out = pl.BlockSpec((8, 576, LANES), lambda j, info: (0, 0, 0))
-    return launch(
-        functools.partial(attention_weight_kernel, masks),
-        (info,),
-        (4,),
-        (own, oth, g_own, g_oth),
-        [full, full, grad, grad],
-        [shape(8, 576, LANES)] * 2,
-        [out] * 2,
-        cost(2 * rows * D * 4 * D, 14e6),
+        out_shape,
+        out_specs,
+        cost(2 * rows * D * 3 * D, 14e6),
         [pltpu.VMEM((D, 2 * rows), BF16), pltpu.VMEM((D, HALF), BF16)],
     )
 
@@ -860,24 +900,38 @@
     def gathered(stream):
         if not halving:
             return wholes[stream]
+        if ("q", stream) in env:
+            return tie(env["q", stream])
         order = GATHER[stream][0]
         masks = (order_masks(order), order_masks(mirrored(order)))
         theirs, last = tie(env["w", stream], env["v", stream])
         sources = (have[stream], env["g", stream, 3], theirs, last)
         return Gathered(sources, dims[stream % 3], masks, pieces[stream % 3])
 
+    plane = [[4 * z + i for i in range(4)] for z in range(4)]
+
+    def reduce(name):
+        env["c", name] = lax.psum_scatter(
+            tie(env[name][0]), "dp", scatter_dimension=0, axis_index_groups=plane, tiled=True
+        )
+
     def halve(name, stage):
         order = SCATTER[name]
         if stage:
             parts[name].append(tie(env["r", name, stage - 1]))
-            size = 8 >> (stage - 1)
+        elif len(order) == 2:
+            parts[name] = [tie(env["c", name])]
+        else:
+            parts[name] = [env[name][0]]
+        if stage == 0 and len(order) == 4:
+            send = env[name][1]
+        else:
+            size = 1 << (len(order) - stage)
             send = sum(p[size // 2 : size].astype(F32) for p in parts[name]).astype(BF16)
-        else:
-            parts[name], send = [env[name][0]], env[name][1]
         env["r", name, stage] = flip(tie(send), order[stage], count, mirrored(order)[stage])
 
     def total(name):
-        parts[name].append(tie(env["r", name, 3]))
+        parts[name].append(tie(env["r", name, len(SCATTER[name]) - 1]))
         env["z", name] = tie(sum(p[0].astype(F32) for p in parts[name]))
 
     def attend(layer):
@@ -889,7 +943,8 @@
         x, x_rows = (tokens, own_rows) if layer == 0 else (env["L", 0], no_rows)
         w_o, source = weights[3 * layer][3], gathered(3 * layer + 1)
         out = tie(*feed(token[0], x, x_rows, env["A", layer][0], w_o, source))
-        env["F", layer], weights[3 * layer + 1] = out[:5], flat(out[5:])
+        env["F", layer] = out[:5]
+        weights[3 * layer + 1] = flat(out[5:]) if len(out) > 5 else (source, source)
 
     def leave_off(layer):
         middle, _, pack, _, _ = env["F", layer]
@@ -903,7 +958,7 @@
     def cotangent(layer):
         if layer == 1:
             return grad, grad, own_rows, oth_rows
-        return env["K", 1][0], env["xt1"], no_rows, no_rows
+        return env["K", 1][0], env.get("xt1"), no_rows, no_rows
 
     def feed_in(layer):
         own, _, at, _ = cotangent(layer)
@@ -911,42 +966,47 @@
         w_g, w_u = weights[3 * layer + 1]
         w_d = gathered(5) if layer == 1 else weights[2][0]
         w_o = weights[3 * layer][3]
-        out = tie(*feed_back(token[0], own, at, w_d, w_g, w_u, s1, s2, pack, scale, w_o))
-        env["B", layer] = out[:5]
+        up_row = w_g.shape[0] // D - 1
+        out = tie(*feed_back(token[0], own, at, w_d, w_g, w_u, up_row, s1, s2, pack, scale, w_o))
+        env["B", layer] = out[:4]
         if layer == 1:
-            weights[5] = flat(out[5:])
+            weights[5] = flat(out[4:])
 
     def attend_in(layer):
         act, qkv, probs, scale = env["A", layer]
-        _, _, gmid, gz, gmix = env["B", layer]
+        _, _, gmid, gmix = env["B", layer]
         w = weights[3 * layer][:3]
         env["K", layer] = tie(
-            *attention_back(token[0], gmix, qkv, probs, *w, act, scale, gmid, gz, tables)
+            *attention_back(token[0], gmix, qkv, probs, *w, act, scale, gmid, tables)
         )
-
-    def masks_of(name):
-        order = SCATTER[name][::-1]
-        return order_masks(order), order_masks(mirrored(order))
 
     def form(name):
         layer = int(name[1])
-        if name[0] == "D":
-            key, col = "xf%d" % layer, 0
-            env[key] = tie(env[key])
-            if layer == 0:
-                env["xt1"], col = tie(env["xt1"]), 4
-            own, oth, at, oth_at = cotangent(layer)
-            args = (env["F", layer][2], env[key], own, oth, (at, oth_at), col)
-            made = down_weight(token[0], masks_of(name), *args)
-        elif name[0] == "G":
-            other, recv = tie(env["xf%d" % layer], env["xs%d" % layer])
-            args = (env["F", layer][2], other, env["B", layer][0], recv)
-            made = gate_weight(token[0], masks_of(name), *args)
+        order = SCATTER[name][::-1]
+        planar = len(order) == 2
+        where = order_masks(order) if planar else (order_masks(order), order_masks(mirrored(order)))
+        if name[0] in "DG":
+            key = "xf%d" % layer
+            pack, env[key] = env["F", layer][2], tie(env[key])
+            gates, downs = (), ()
+            if name[0] == "G":
+                more = "xa%d" % layer
+                env[more], recv = tie(env[more], env["xs%d" % layer])
+                act, keep = env["A", layer][0], env["B", layer][0]
+                gates = (pack, env[key], act, env[more], keep, recv)
+            if name[0] == "D" or "D%d" % layer not in SCATTER:
+                if layer == 0:
+                    env["xt1"] = tie(env["xt1"])
+                own, oth, at, oth_at = cotangent(layer)
+                downs = (pack, env[key], own, oth, at, oth_at, 0 if layer == 1 else 3)
+            made = feed_weight(token[0], where, planar, gates, downs)
         else:
-            other, recv = tie(env["xa%d" % layer], env["xt%d" % layer])
+            more = "xa%d" % layer
+            env[more], recv = tie(env[more], env["xt%d" % layer])
+            other = env[more]
             args = (env["A", layer][0], other, env["K", layer][1], recv)
-            made = attention_weight(token[0], masks_of(name), *args)
-        env[name] = tie(*made)
+            made = attention_weight(token[0], where, planar, *args)
+        env[name] = tie(*made) if len(made) > 1 else (tie(*made),)
 
     sent = {
         "a": lambda layer: env["A", layer][0],
@@ -975,6 +1035,12 @@
             key = ("g", int(rest), 3)
             env[key] = tie(env[key])
             env["v", int(rest)] = swap(env[key])
+        elif kind == "q":
+            stream = int(rest)
+            part = tie(have[stream])[0]
+            env["q", stream] = lax.all_gather(part, ("section", "dp"), tiled=True)
+        elif kind == "c":
+            reduce(rest)
         elif kind == "r":
             halve(rest[:2], int(rest[2]))
         elif kind == "z":
@@ -987,40 +1053,48 @@
                 "x": lambda: "x" + rest,
                 "o": lambda: "o" + rest,
                 "h": lambda: ("h", rest),
+                "c": lambda: ("c", rest),
             }
             key = keys.get(kind, lambda: (kind, int(rest)))()
             env[key] = tie(env[key])
         elif kind == "x":
             env[name] = swap(tie(sent[rest[0]](int(rest[1]))))
         elif kind == "h":
-            first, second = env["z", rest + "0"], env["z", rest + "1"]
+            first, second = (
+                jnp.concatenate([env["z", k + at] for k in rest + "D" if ("z", k + at) in env])
+                if rest == "G"
+                else env["z", rest + at]
+                for at in "01"
+            )
             env["m", rest], other = tie(pick(first, second), pick(second, first))
             env["h", rest] = swap(other)
         elif name == "u1":
+            side = row * FHALF // LANES
+            last = 2 * side + row * HALF // LANES
             plan = (
                 (0, 0, row, 0, 1.0, True, 0),
-                (0, row * FHALF // LANES, row, 0, 1.0, True, 1),
-                (1, 0, 2 * half, 0, 1.0, False, 2),
+                (0, side, row, 0, 1.0, True, 1),
+                (0, 2 * side, row, 0, 1.0, False, 2),
+                (0, last, 2 * half, 0, 1.0, False, 3),
             )
-            out_dims = ((row, FF), (row, FF), (2 * half, D), (row, LANES))
-            env["u1"] = unpacked("GD", plan, gain_two, (w_gate[0], w_up[0]), out_dims)
+            out_dims = ((row, FF), (row, FF), (row, D), (2 * half, D), (row, LANES))
+            env["u1"] = unpacked("G", plan, gain_two, (w_gate[0], w_up[0]), out_dims)
         elif name == "u2":
             side = row * HALF // LANES
             plan = (
-                (0, side, row, 0, SCALE, True, 0),
-                (0, 2 * side, row, 0, 1.0, True, 1),
-                (0, 3 * side, row, 0, 1.0, True, 2),
-                (0, 0, row, 0, 1.0, False, 3),
+                (0, 0, row, 0, SCALE, True, 0),
+                (0, side, row, 0, 1.0, True, 1),
+                (0, 2 * side, row, 0, 1.0, True, 2),
             )
             local = (w_query[0], w_key[0], w_value[0])
-            out_dims = ((row, D),) * 4 + ((row, LANES),)
+            out_dims = ((row, D),) * 3 + ((row, LANES),)
             env["u2"] = unpacked("T", plan, gain_one, local, out_dims)
         elif name == "oa":
             env["oa"] = swap(tie(pick(env["L", 1], env["L", 0])))
         elif name == "ob":
             env["ob"] = both(pick(env["L", 0], env["L", 1]), tie(env["oa"]))
         elif name == "oi":
-            other = [v[:, 4 * HALF :] for v in tie(env["xt0"], env["xt1"])]
+            other = [v[:, 3 * HALF :] for v in tie(env["xt0"], env["xt1"])]
             env["oi"] = both(pick(env["K", 0][0], env["K", 1][0]), pick(*other))
         else:
             layer = int(rest)
@@ -1034,8 +1108,8 @@
             run(name)
 
     if halving:
-        grad_g, grad_u, grad_d, gain_grad_two = env["u1"]
-        grad_q, grad_k, grad_v, grad_o, gain_grad_one = env["u2"]
+        grad_g, grad_u, grad_o, grad_d, gain_grad_two = env["u1"]
+        grad_q, grad_k, grad_v, gain_grad_one = env["u2"]
         gain_grad_one, gain_grad_two = gain_grad_one[:, 0], gain_grad_two[:, 0]
     else:
         cut = lambda v, at: lax.dynamic_slice_in_dim(v, info[at] * rows, rows, 0)
@@ -1048,23 +1122,23 @@
         found = []
         for layer in range(2):
             own, oth, at, oth_at = cotangent(layer)
-            oth = oth if layer == 1 else oth[:, 4 * HALF :]
+            oth = oth if layer == 1 else oth[:, 3 * HALF :]
             gf = lax.dynamic_slice_in_dim(
                 join(cut(own, at), cut(oth, oth_at)), section * HALF, HALF, 1
             )
             acts = join(env["A", layer][0], env["xa%d" % layer])
-            gts = join(env["K", layer][1], env["xt%d" % layer][:, : 4 * HALF])
+            gts = join(env["K", layer][1], env["xt%d" % layer][:, : 3 * HALF])
             gus = join(env["B", layer][0], env["xs%d" % layer])
             pack = join(env["F", layer][2], env["xf%d" % layer])
             nor, hid = pack[:, :D], pack[:, PACK:]
             found.append(
                 (
+                    reduced(acts[:, :D], gts[:, :HALF]),
                     reduced(acts[:, :D], gts[:, HALF : 2 * HALF]),
-                    reduced(acts[:, :D], gts[:, 2 * HALF : 3 * HALF]),
-                    reduced(acts[:, :D], gts[:, 3 * HALF :]),
-                    reduced(acts[:, D:], gts[:, :HALF]),
+                    reduced(acts[:, :D], gts[:, 2 * HALF :]),
+                    reduced(acts[:, D:], gus[:, FF : FF + HALF]),
                     reduced(nor, gus[:, :FHALF]),
-                    reduced(nor, gus[:, FHALF:]),
+                    reduced(nor, gus[:, FHALF:FF]),
                     reduced(hid, gf),
                 )
             )

time: 402 us -> 397 us (0.988)
  waiting for transfers between devices: 129 us -> 117 us
  Pallas kernels: 146 us -> 155 us
  other arithmetic: 31.1 us -> 37.5 us
  local copies, waits for them, and re-layouts: 13.4 us -> 8.67 us
    ppermute x24 -> x22, waiting for transfers between devices: 50.3 us -> 31.4 us  [flip(): return lax.ppermute(value, ('section', 'dp'), pairs)]
    pallas_call x18 -> x17, Pallas kernels: 146 us -> 155 us  [launch(): pl.pallas_call(kernel, grid_spec=pltpu.PrefetchScalarGridSpec(num_scalar_...]
    convert_element_type x18 -> x15, other arithmetic: 9.23 us -> 16 us  [halve(): sum((p[size // 2:size].astype(F32) for p in parts[name])).astype(BF16)]
    unnamed x114 -> x109, local copies, waits for them, and re-layouts: 12 us -> 6 us
    ppermute x24 -> x22, starting transfers between devices: 24.2 us -> 29.9 us  [flip(): return lax.ppermute(value, 'dp', [(i, i ^ bit) for i in range(count)])]
    ppermute x24 -> x22, waiting for transfers between devices: 76.8 us -> 82 us  [flip(): return lax.ppermute(value, 'dp', [(i, i ^ bit) for i in range(count)])]
    ppermute x24 -> x22, starting transfers between devices: 23.6 us -> 19.4 us  [flip(): return lax.ppermute(value, ('section', 'dp'), pairs)]
    ppermute x27 -> x26, starting transfers between devices: 28.2 us -> 24.1 us  [swap(): return lax.ppermute(value, 'section', [(0, 1), (1, 0)])]
  transfers between devices with their start and end apart: 75 -> 70, of which waited for: 28 -> 26; matrix products, arithmetic and copies ran while one was open for 7% -> 9% of each run, Pallas kernels for 32% -> 39%
where the time goes in v3:
time: 397 us; the launch traced here: 393 us
  Pallas kernels  155 us (39%)
  waiting for transfers between devices  117 us (29%)
  starting transfers between devices  73.4 us (18%)
  other arithmetic  37.5 us (9%)
  local copies, waits for them, and re-layouts  8.67 us (2%)
    pallas_call x17, Pallas kernels, launch(): pl.pallas_call(kernel, grid_spec=pltpu.PrefetchScalarGridSpec(num_scalar_...  155 us
    ppermute x22, waiting for transfers between devices, flip(): return lax.ppermute(value, 'dp', [(i, i ^ bit) for i in range(count)])  82 us
    ppermute x22, waiting for transfers between devices, flip(): return lax.ppermute(value, ('section', 'dp'), pairs)  31.4 us
    ppermute x22, starting transfers between devices, flip(): return lax.ppermute(value, 'dp', [(i, i ^ bit) for i in range(count)])  29.9 us
    ppermute x26, starting transfers between devices, swap(): return lax.ppermute(value, 'section', [(0, 1), (1, 0)])  24.1 us
    ppermute x22, starting transfers between devices, flip(): return lax.ppermute(value, ('section', 'dp'), pairs)  19.4 us
    convert_element_type x15, other arithmetic, halve(): sum((p[size // 2:size].astype(F32) for p in parts[name])).astype(BF16)  16 us
  transfers between devices with their start and end apart: 70, of which 26 were waited for; matrix products, arithmetic and copies ran while one was open for 9% of the time, Pallas kernels for 39%

profile of v3, /device:TPU:1, one launch (start us, length us, event | category | flops | bytes accessed | tf_op | source)
XLA Modules:
  0.0 392.9 jit_solution(14375857871783806044)
XLA Ops:
  11.2 3.5 collective-permute-start.4
  16.0 10.0 %collective-permute-done.4 = bf16[1,96,768]{2,1,0:T(8,128)(2,1)S(1)} collective-permute-done((bf16[1,96,768]{2,1,0:T(8,128)(2,1)S(1)}, bf16[1,96,768]{2,1,0:T(8,128)(2,1)S(1)}, u32[]{:S(2)}, u32[]{:S(2)}) %collective-permute-start.4) | collective-permute-done | bytes 147488 | tf_op jit(solution)/shard_map/ppermute | solution.py:66
  27.0 3.2 collective-permute-done.9
  31.4 2.2 collective-permute-start.6
  33.7 5.8 %collective-permute-done.8 = bf16[2,96,768]{2,1,0:T(8,128)(2,1)S(1)} collective-permute-done((bf16[2,96,768]{2,1,0:T(8,128)(2,1)S(1)}, bf16[2,96,768]{2,1,0:T(8,128)(2,1)S(1)}, u32[]{:S(2)}, u32[]{:S(2)}) %collective-permute-start.8) | collective-permute-done | bytes 294944 | tf_op jit(solution)/shard_map/ppermute | solution.py:66
  39.5 4.1 %collective-permute-done.6 = bf16[1,64,768]{2,1,0:T(8,128)(2,1)S(1)} collective-permute-done((bf16[1,64,768]{2,1,0:T(8,128)(2,1)S(1)}, bf16[1,64,768]{2,1,0:T(8,128)(2,1)S(1)}, u32[]{:S(2)}, u32[]{:S(2)}) %collective-permute-start.6) | collective-permute-done | bytes 98336 | tf_op jit(solution)/shard_map/ppermute | solution.py:66
  43.6 1.8 collective-permute-start.11
  47.4 3.9 collective-permute-done.11
  51.3 1.6 collective-permute-start.15
  53.0 4.9 %collective-permute-done.10 = bf16[2,64,768]{2,1,0:T(8,128)(2,1)S(1)} collective-permute-done((bf16[2,64,768]{2,1,0:T(8,128)(2,1)S(1)}, bf16[2,64,768]{2,1,0:T(8,128)(2,1)S(1)}, u32[]{:S(2)}, u32[]{:S(2)}) %collective-permute-start.10) | collective-permute-done | bytes 196640 | tf_op jit(solution)/shard_map/ppermute | solution.py:69
  60.0 1.7 collective-permute-done.15
  61.9 5.0 %collective-permute-start.19 = (bf16[1,48,2048]{2,1,0:T(8,128)(2,1)S(1)}, bf16[1,48,2048]{2,1,0:T(8,128)(2,1)S(1)}, u32[]{:S(2)}, u32[]{:S(2)}) collective-permute-start(bf16[1,48,2048]{2,1,0:T(8,128)(2,1)S(1)} %get-tuple-element.488), channel_id=1, source_target_pairs={{0,8},{1,9},{2,10},{3,11},{4,12},{5,13},{6,14},{7,15},{8,0},{9,1},... | collective-permute-start | bytes 589832 | tf_op jit(solution)/shard_map/ppermute | solution.py:66
  68.1 4.7 %collective-permute-start.5 = (bf16[2,64,768]{2,1,0:T(8,128)(2,1)S(1)}, bf16[2,64,768]{2,1,0:T(8,128)(2,1)S(1)}, u32[]{:S(2)}, u32[]{:S(2)}) collective-permute-start(bf16[2,64,768]{2,1,0:T(8,128)(2,1)S(1)} %pad_maximum_fusion.16), channel_id=1, source_target_pairs={{0,8},{1,9},{2,10},{3,11},{4,12},{5,13},{6,14},{7,15},{8,0},{9,1},... | collective-permute-start | bytes 589832 | tf_op jit(solution)/shard_map/ppermute | solution.py:66
  74.0 10.5 %collective-permute-done.5 = bf16[2,64,768]{2,1,0:T(8,128)(2,1)S(1)} collective-permute-done((bf16[2,64,768]{2,1,0:T(8,128)(2,1)S(1)}, bf16[2,64,768]{2,1,0:T(8,128)(2,1)S(1)}, u32[]{:S(2)}, u32[]{:S(2)}) %collective-permute-start.5) | collective-permute-done | bytes 196640 | tf_op jit(solution)/shard_map/ppermute | solution.py:66
  84.5 1.9 collective-permute-start.27
  86.6 1.5 collective-permute-start.20
  88.1 2.1 collective-permute-start.22
  90.2 5.4 %collective-permute-done.17 = bf16[4,64,768]{2,1,0:T(8,128)(2,1)S(1)} collective-permute-done((bf16[4,64,768]{2,1,0:T(8,128)(2,1)S(1)}, bf16[4,64,768]{2,1,0:T(8,128)(2,1)S(1)}, u32[]{:S(2)}, u32[]{:S(2)}) %collective-permute-start.17) | collective-permute-done | bytes 393248 | tf_op jit(solution)/shard_map/ppermute | solution.py:66
  95.6 4.4 %collective-permute-start.23 = (bf16[8,96,768]{2,1,0:T(8,128)(2,1)S(1)}, bf16[8,96,768]{2,1,0:T(8,128)(2,1)S(1)}, u32[]{:S(2)}, u32[]{:S(2)}) collective-permute-start(bf16[8,96,768]{2,1,0:T(8,128)(2,1)S(1)} %collective-permute-done.18.refs_6_), channel_id=1, source_target_pairs={{0,16},{16,0},{1,17},{17,1},{2,18},{18,2},{3,19},{19,3},{4,20},{20... | collective-permute-start | bytes 3538952 | tf_op jit(solution)/shard_map/ppermute | solution.py:73
  100.1 3.9 collective-permute-done.20
  104.2 2.8 collective-permute-start.26
  107.0 11.5 %shard_map.230 = (bf16[512,1536]{1,0:T(8,128)(2,1)}, bf16[512,2304]{1,0:T(8,128)(2,1)}, bf16[2,12,256,256]{3,2,1,0:T(8,128)(2,1)}, f32[512,128]{1,0:T(8,128)}, b...) custom-call(s32[4]{0:T(128)S(1)} %pad_add_fusion.info, ...), custom_call_target="tpu_custom_call" | custom-call | flops 1 | bytes 1 | tf_op jit(solution)/shard_map/pallas_call | solution.py:136
  118.5 1.4 collective-permute-done.28
  120.4 1.5 collective-permute-start.24
  124.0 9.3 %shard_map.231 = (f32[512,768]{1,0:T(8,128)S(1)}, f32[512,128]{1,0:T(8,128)}, bf16[512,3072]{1,0:T(8,128)(2,1)S(1)}, bf16[512,2048]{1,0:T(8,128)(2,1)}, bf16[512...) custom-call(s32[4]{0:T(128)S(1)} %pad_add_fusion.info, ...), custom_call_target="tpu_custom_call" | custom-call | flops 1 | bytes 1 | tf_op jit(solution)/shard_map/pallas_call | solution.py:136
  133.3 2.2 collective-permute-done.25.refs_5_
  135.5 2.7 collective-permute-start.30
  140.5 3.0 shard_map.232
  143.5 11.4 %shard_map.233 = (bf16[512,1536]{1,0:T(8,128)(2,1)S(1)}, bf16[512,2304]{1,0:T(8,128)(2,1)}, bf16[2,12,256,256]{3,2,1,0:T(8,128)(2,1)}, f32[512,128]{1,0:T(8,128)...) custom-call(s32[4]{0:T(128)S(1)} %pad_add_fusion.info, ...), custom_call_target="tpu_custom_call" | custom-call | flops 1 | bytes 1 | tf_op jit(solution)/shard_map/pallas_call | solution.py:136
  156.1 1.6 collective-permute-done.33.refs_9_
  159.1 1.8 broadcast_select_fusion.refs_0_.refs_2_.refs_3_
  163.2 11.2 %shard_map.234 = (f32[512,768]{1,0:T(8,128)S(1)}, f32[512,128]{1,0:T(8,128)}, bf16[512,3072]{1,0:T(8,128)(2,1)S(1)}, bf16[512,2048]{1,0:T(8,128)(2,1)}, bf16[512...) custom-call(s32[4]{0:T(128)S(1)} %pad_add_fusion.info, ...), custom_call_target="tpu_custom_call" | custom-call | flops 1 | bytes 1 | tf_op jit(solution)/shard_map/pallas_call | solution.py:136
  174.4 14.9 %shard_map.235 = (bf16[512,2560]{1,0:T(8,128)(2,1)S(1)}, bf16[512,2560]{1,0:T(8,128)(2,1)S(1)}, f32[512,768]{1,0:T(8,128)S(1)}, bf16[512,768]{1,0:T(8,128)(2,1)S(1)}, bf16[16,2,64,768]{3,2,1,0:T(8,128)(2,1)}) custom-call(s32[4]{0:T(128)S(1)} %pad_add_fusion.info, bf16[1024,768]{1,0:T(8,128)(2,1)S(1)} %broadcast_select_fusion.refs_0_.refs_2_.refs_3_, ...), custom_call_target="tpu_custom_call" | custom-call | flops 1 | bytes 1 | tf_op jit(solution)/shard_map/pallas_call | solution.py:136
  189.7 13.9 %shard_map.236 = (bf16[512,768]{1,0:T(8,128)(2,1)S(1)}, bf16[512,1152]{1,0:T(8,128)(2,1)S(1)}, bf16[512,1920]{1,0:T(8,128)(2,1)S(1)}) custom-call(s32[4]{0:T(128)S(1)} %pad_add_fusion.info, bf16[512,768]{1,0:T(8,128)(2,1)S(1)} %get-tuple-element.617.gmix_ref, bf16[512,2304]{1,0:T(8,128)(2,1)} %get-tuple-element.618.qkv_ref, ...), custom_call_target="tpu_custom_call" | custom-call | flops 1 | bytes 1 | tf_op jit(solution)/shard_map/pallas_call | solution.py:136
  204.4 15.4 %shard_map.237 = (bf16[512,2560]{1,0:T(8,128)(2,1)S(1)}, bf16[512,2560]{1,0:T(8,128)(2,1)}, f32[512,768]{1,0:T(8,128)S(1)}, bf16[512,768]{1,0:T(8,128)(2,1)S(1)}) custom-call(s32[4]{0:T(128)S(1)} %pad_add_fusion.info, bf16[512,768]{1,0:T(8,128)(2,1)S(1)} %get-tuple-element.633.grad_ref.refs_8_, bf16[768,2048]{1,0:T(8,128)(2,1)} %bitcast.105, ...), custom_call_target="tpu_custom_call" | custom-call | flops 1 | bytes 1 | tf_op jit(solution)/shard_map/pallas_call | solution.py:136
  219.8 9.2 %shard_map.238 = (bf16[8,912,128]{2,1,0:T(8,128)(2,1)S(1)}, bf16[8,912,128]{2,1,0:T(8,128)(2,1)}) custom-call(s32[4]{0:T(128)S(1)} %pad_add_fusion.info, bf16[512,3072]{1,0:T(8,128)(2,1)S(1)} %get-tuple-element.630.refs_5_.refs_0_.low.high, bf16[512,3072]{1,0:T(8,128)(2,1)S(1)} %collective-permute-done.42.refs_1_, bf16[512,1536]{1,0:T(8,128)(2,1)S(1)} %copy-done.1, ...), custom_call_target="tpu_custom_call" | custom-call | flops 1 | bytes 1 | tf_op jit(solution)/shard_map/pallas_call | solution.py:136
  229.5 2.2 collective-permute-start.43
  231.7 5.2 %shard_map.239 = (bf16[8,384,128]{2,1,0:T(8,128)(2,1)S(1)}, bf16[8,384,128]{2,1,0:T(8,128)(2,1)}) custom-call(s32[4]{0:T(128)S(1)} %pad_add_fusion.info, bf16[512,3072]{1,0:T(8,128)(2,1)S(1)} %get-tuple-element.630.refs_5_.refs_0_.low.high, bf16[512,3072]{1,0:T(8,128)(2,1)S(1)} %collective-permute-done.42.refs_1_, ...), custom_call_target="tpu_custom_call" | custom-call | flops 1 | bytes 1 | tf_op jit(solution)/shard_map/pallas_call | solution.py:136
  237.8 15.5 %shard_map.240 = (bf16[8,1296,128]{2,1,0:T(8,128)(2,1)S(1)}, bf16[8,1296,128]{2,1,0:T(8,128)(2,1)}) custom-call(s32[4]{0:T(128)S(1)} %pad_add_fusion.info, bf16[512,3072]{1,0:T(8,128)(2,1)S(1)} %get-tuple-element.663.refs_2_.refs_3_.normed_ref.refs_0_.refs_6_, bf16[512,3072]{1,0:T(8,128)(2,1)S(1)} %collective-permute-done.46.refs_1_.refs_7_, ...), custom_call_target="tpu_custom_call" | custom-call | flops 1 | bytes 1 | tf_op jit(solution)/shard_map/pallas_call | solution.py:136
  254.4 1.8 add_convert_fusion.1
  256.3 2.8 shard_map.241
  259.2 5.7 %shard_map.242 = (bf16[8,432,128]{2,1,0:T(8,128)(2,1)S(1)}, bf16[8,432,128]{2,1,0:T(8,128)(2,1)}) custom-call(s32[4]{0:T(128)S(1)} %pad_add_fusion.info, bf16[512,1536]{1,0:T(8,128)(2,1)S(1)} %copy-done.1, bf16[512,1536]{1,0:T(8,128)(2,1)S(1)} %collective-permute-done.34.refs_3_.oth_ref, bf16[512,1152]{1,0:T(8,128)(2,1)S(1)} %copy-done.28, ...), custom_call_target="tpu_custom_call" | custom-call | flops 1 | bytes 1 | tf_op jit(solution)/shard_map/pallas_call | solution.py:136
  264.9 15.2 %shard_map.243 = (bf16[512,768]{1,0:T(8,128)(2,1)S(1)}, bf16[512,1152]{1,0:T(8,128)(2,1)S(1)}, bf16[512,1920]{1,0:T(8,128)(2,1)}) custom-call(s32[4]{0:T(128)S(1)} %pad_add_fusion.info, bf16[512,768]{1,0:T(8,128)(2,1)S(1)} %copy-done.38, bf16[512,2304]{1,0:T(8,128)(2,1)} %get-tuple-element.700.qkv_ref, ...), custom_call_target="tpu_custom_call" | custom-call | flops 1 | bytes 1 | tf_op jit(solution)/shard_map/pallas_call | solution.py:136
  280.2 2.3 add_convert_fusion.3
  282.9 1.6 collective-permute-done.49
  284.4 1.6 add_convert_fusion
  292.6 6.6 %shard_map.244 = (bf16[8,432,128]{2,1,0:T(8,128)(2,1)S(1)}, bf16[8,432,128]{2,1,0:T(8,128)(2,1)S(1)}) custom-call(s32[4]{0:T(128)S(1)} %pad_add_fusion.info, bf16[512,1536]{1,0:T(8,128)(2,1)} %get-tuple-element.613.refs_1_.refs_2_.normed_ref.own_ref, bf16[512,1536]{1,0:T(8,128)(2,1)} %collective-permute-done.40.refs_3_.oth_ref, ...), custom_call_target="tpu_custom_call" | custom-call | flops 1 | bytes 1 | tf_op jit(solution)/shard_map/pallas_call | solution.py:136
  299.2 12.8 %collective-permute-done.50 = bf16[8,384,128]{2,1,0:T(8,128)(2,1)} collective-permute-done((bf16[8,384,128]{2,1,0:T(8,128)(2,1)}, bf16[8,384,128]{2,1,0:T(8,128)(2,1)}, u32[]{:S(2)}, u32[]{:S(2)}) %collective-permute-start.50) | collective-permute-done | bytes 786464 | tf_op jit(solution)/shard_map/ppermute | solution.py:69
  315.4 3.0 collective-permute-start.51
  319.2 1.4 add_convert_fusion.2
  322.8 3.6 collective-permute-done.55
  328.0 3.1 collective-permute-done.57
  332.2 1.4 collective-permute-start.61
  333.6 1.5 collective-permute-start.60
  336.5 9.6 %collective-permute-done.56 = bf16[2,1296,128]{2,1,0:T(8,128)(2,1)S(1)} collective-permute-done((bf16[2,1296,128]{2,1,0:T(8,128)(2,1)S(1)}, bf16[2,1296,128]{2,1,0:T(8,128)(2,1)S(1)}, u32[]{:S(2)}, u32[]{:S(2)}) %collective-permute-start.56) | collective-permute-done | bytes 663584 | tf_op jit(solution)/shard_map/ppermute | solution.py:66
  350.4 2.2 collective-permute-start.62
  353.9 15.1 %collective-permute-done.64 = bf16[1,1296,128]{2,1,0:T(8,128)(2,1)S(1)} collective-permute-done((bf16[1,1296,128]{2,1,0:T(8,128)(2,1)S(1)}, bf16[1,1296,128]{2,1,0:T(8,128)(2,1)S(1)}, u32[]{:S(2)}, u32[]{:S(2)}) %collective-permute-start.64) | collective-permute-done | bytes 331808 | tf_op jit(solution)/shard_map/ppermute | solution.py:66
  372.5 2.4 collective-permute-start.65
  374.9 1.9 collective-permute-start.69
  376.8 5.1 %collective-permute-done.66 = bf16[1,432,128]{2,1,0:T(8,128)(2,1)S(1)} collective-permute-done((bf16[1,432,128]{2,1,0:T(8,128)(2,1)S(1)}, bf16[1,432,128]{2,1,0:T(8,128)(2,1)S(1)}, u32[]{:S(2)}, u32[]{:S(2)}) %collective-permute-start.66) | collective-permute-done | bytes 110624 | tf_op jit(solution)/shard_map/ppermute | solution.py:66
  382.9 1.4 collective-permute-done.65
  385.3 2.1 maximum_select_fusion
  387.5 2.1 shard_map.246
  390.3 1.7 shard_map.245
  (267 shorter events, 64.0 us)
Async XLA Ops:
  3.1 7.9 %collective-permute-start.1 = (bf16[48,2048]{1,0:T(8,128)(2,1)S(1)}, bf16[48,2048]{1,0:T(8,128)(2,1)S(1)}, u32[]{:S(2)}, u32[]{:S(2)}) collective-permute-start(bf16[48,2048]{1,0:T(8,128)(2,1)S(1)} %broadcast_select_fusion.4), channel_id=1, source_target_pairs={{0,16},{16,0},{1,17},{17,1},{2,18},{18,2},{3,19},{19,3},{4,20},{20... | collective-permute-start | bytes 589832 | tf_op jit(solution)/shard_map/ppermute | solution.py:73
  11.2 14.8 %collective-permute-start.4 = (bf16[1,96,768]{2,1,0:T(8,128)(2,1)S(1)}, bf16[1,96,768]{2,1,0:T(8,128)(2,1)S(1)}, u32[]{:S(2)}, u32[]{:S(2)}) collective-permute-start(bf16[1,96,768]{2,1,0:T(8,128)(2,1)S(1)} %get-tuple-element.429), channel_id=1, source_target_pairs={{0,8},{1,9},{2,10},{3,11},{4,12},{5,13},{6,14},{7,15},{8,0},{9,1},... | collective-permute-start | bytes 442376 | tf_op jit(solution)/shard_map/ppermute | solution.py:66
  14.7 11.3 %collective-permute-start.2 = (bf16[1,64,768]{2,1,0:T(8,128)(2,1)S(1)}, bf16[1,64,768]{2,1,0:T(8,128)(2,1)S(1)}, u32[]{:S(2)}, u32[]{:S(2)}) collective-permute-start(bf16[1,64,768]{2,1,0:T(8,128)(2,1)S(1)} %get-tuple-element.427), channel_id=1, source_target_pairs={{0,2},{1,3},{2,0},{3,1},{4,6},{5,7},{6,4},{7,5},{8,10},{9,11},{10,... | collective-permute-start | bytes 294920 | tf_op jit(solution)/shard_map/ppermute | solution.py:69
  15.9 14.3 %collective-permute-start.9 = (bf16[1,48,2048]{2,1,0:T(8,128)(2,1)S(1)}, bf16[1,48,2048]{2,1,0:T(8,128)(2,1)S(1)}, u32[]{:S(2)}, u32[]{:S(2)}) collective-permute-start(bf16[1,48,2048]{2,1,0:T(8,128)(2,1)S(1)} %get-tuple-element.442), channel_id=1, source_target_pairs={{0,8},{1,9},{2,10},{3,11},{4,12},{5,13},{6,14},{7,15},{8,0},{9,1},... | collective-permute-start | bytes 589832 | tf_op jit(solution)/shard_map/ppermute | solution.py:66
  26.0 13.4 %collective-permute-start.8 = (bf16[2,96,768]{2,1,0:T(8,128)(2,1)S(1)}, bf16[2,96,768]{2,1,0:T(8,128)(2,1)S(1)}, u32[]{:S(2)}, u32[]{:S(2)}) collective-permute-start(bf16[2,96,768]{2,1,0:T(8,128)(2,1)S(1)} %pad_maximum_fusion.14), channel_id=1, source_target_pairs={{0,4},{1,5},{2,6},{3,7},{4,0},{5,1},{6,2},{7,3},{8,12},{9,13},{10,... | collective-permute-start | bytes 884744 | tf_op jit(solution)/shard_map/ppermute | solution.py:66
  30.3 16.4 %collective-permute-start.12 = (bf16[2,48,2048]{2,1,0:T(8,128)(2,1)S(1)}, bf16[2,48,2048]{2,1,0:T(8,128)(2,1)S(1)}, u32[]{:S(2)}, u32[]{:S(2)}) collective-permute-start(bf16[2,48,2048]{2,1,0:T(8,128)(2,1)S(1)} %pad_maximum_fusion.10), channel_id=1, source_target_pairs={{0,1},{1,0},{2,3},{3,2},{4,5},{5,4},{6,7},{7,6},{8,9},{9,8},{10,11... | collective-permute-start | bytes 1179656 | tf_op jit(solution)/shard_map/ppermute | solution.py:69
  31.3 8.2 %collective-permute-start.7 = (bf16[1,96,768]{2,1,0:T(8,128)(2,1)S(1)}, bf16[1,96,768]{2,1,0:T(8,128)(2,1)S(1)}, u32[]{:S(2)}, u32[]{:S(2)}) collective-permute-start(bf16[1,96,768]{2,1,0:T(8,128)(2,1)S(1)} %get-tuple-element.440), channel_id=1, source_target_pairs={{0,8},{1,9},{2,10},{3,11},{4,12},{5,13},{6,14},{7,15},{8,0},{9,1},... | collective-permute-start | bytes 442376 | tf_op jit(solution)/shard_map/ppermute | solution.py:66
  31.4 12.1 %collective-permute-start.6 = (bf16[1,64,768]{2,1,0:T(8,128)(2,1)S(1)}, bf16[1,64,768]{2,1,0:T(8,128)(2,1)S(1)}, u32[]{:S(2)}, u32[]{:S(2)}) collective-permute-start(bf16[1,64,768]{2,1,0:T(8,128)(2,1)S(1)} %get-tuple-element.439), channel_id=1, source_target_pairs={{0,8},{1,9},{2,10},{3,11},{4,12},{5,13},{6,14},{7,15},{8,0},{9,1},... | collective-permute-start | bytes 294920 | tf_op jit(solution)/shard_map/ppermute | solution.py:66
  43.6 7.7 %collective-permute-start.11 = (bf16[2,96,768]{2,1,0:T(8,128)(2,1)S(1)}, bf16[2,96,768]{2,1,0:T(8,128)(2,1)S(1)}, u32[]{:S(2)}, u32[]{:S(2)}) collective-permute-start(bf16[2,96,768]{2,1,0:T(8,128)(2,1)S(1)} %pad_maximum_fusion.15), channel_id=1, source_target_pairs={{0,4},{1,5},{2,6},{3,7},{4,0},{5,1},{6,2},{7,3},{8,12},{9,13},{10,... | collective-permute-start | bytes 884744 | tf_op jit(solution)/shard_map/ppermute | solution.py:66
  45.4 12.5 %collective-permute-start.16 = (bf16[4,96,768]{2,1,0:T(8,128)(2,1)S(1)}, bf16[4,96,768]{2,1,0:T(8,128)(2,1)S(1)}, u32[]{:S(2)}, u32[]{:S(2)}) collective-permute-start(bf16[4,96,768]{2,1,0:T(8,128)(2,1)S(1)} %pad_maximum_fusion.8), channel_id=1, source_target_pairs={{0,2},{1,3},{2,0},{3,1},{4,6},{5,7},{6,4},{7,5},{8,10},{9,11},{10,... | collective-permute-start | bytes 1769480 | tf_op jit(solution)/shard_map/ppermute | solution.py:69
  46.8 21.4 %collective-permute-start.14 = (bf16[4,48,2048]{2,1,0:T(8,128)(2,1)S(1)}, bf16[4,48,2048]{2,1,0:T(8,128)(2,1)S(1)}, u32[]{:S(2)}, u32[]{:S(2)}) collective-permute-start(bf16[4,48,2048]{2,1,0:T(8,128)(2,1)S(1)} %pad_maximum_fusion.4), channel_id=1, source_target_pairs={{0,4},{1,5},{2,6},{3,7},{4,0},{5,1},{6,2},{7,3},{8,12},{9,13},{10,... | collective-permute-start | bytes 2359304 | tf_op jit(solution)/shard_map/ppermute | solution.py:66
  51.3 10.4 %collective-permute-start.15 = (bf16[4,96,768]{2,1,0:T(8,128)(2,1)S(1)}, bf16[4,96,768]{2,1,0:T(8,128)(2,1)S(1)}, u32[]{:S(2)}, u32[]{:S(2)}) collective-permute-start(bf16[4,96,768]{2,1,0:T(8,128)(2,1)S(1)} %pad_maximum_fusion.9), channel_id=1, source_target_pairs={{0,2},{1,3},{2,0},{3,1},{4,6},{5,7},{6,4},{7,5},{8,10},{9,11},{10,... | collective-permute-start | bytes 1769480 | tf_op jit(solution)/shard_map/ppermute | solution.py:69
  58.0 30.1 %collective-permute-start.18 = (bf16[8,96,768]{2,1,0:T(8,128)(2,1)S(1)}, bf16[8,96,768]{2,1,0:T(8,128)(2,1)S(1)}, u32[]{:S(2)}, u32[]{:S(2)}) collective-permute-start(bf16[8,96,768]{2,1,0:T(8,128)(2,1)S(1)} %pad_maximum_fusion.2.refs_5_), channel_id=1, source_target_pairs={{0,1},{1,0},{2,3},{3,2},{4,5},{5,4},{6,7},{7,6},{8,9},{9,8},{10,11... | collective-permute-start | bytes 3538952 | tf_op jit(solution)/shard_map/ppermute | solution.py:69
  58.8 14.2 %collective-permute-start.13 = (bf16[4,64,768]{2,1,0:T(8,128)(2,1)S(1)}, bf16[4,64,768]{2,1,0:T(8,128)(2,1)S(1)}, u32[]{:S(2)}, u32[]{:S(2)}) collective-permute-start(bf16[4,64,768]{2,1,0:T(8,128)(2,1)S(1)} %pad_maximum_fusion.11), channel_id=1, source_target_pairs={{0,2},{1,3},{2,0},{3,1},{4,6},{5,7},{6,4},{7,5},{8,10},{9,11},{10,... | collective-permute-start | bytes 1179656 | tf_op jit(solution)/shard_map/ppermute | solution.py:69
  61.8 38.3 %collective-permute-start.21 = (bf16[8,96,768]{2,1,0:T(8,128)(2,1)S(1)}, bf16[8,96,768]{2,1,0:T(8,128)(2,1)S(1)}, u32[]{:S(2)}, u32[]{:S(2)}) collective-permute-start(bf16[8,96,768]{2,1,0:T(8,128)(2,1)S(1)} %pad_maximum_fusion.3.refs_5_), channel_id=1, source_target_pairs={{0,1},{1,0},{2,3},{3,2},{4,5},{5,4},{6,7},{7,6},{8,9},{9,8},{10,11... | collective-permute-start | bytes 3538952 | tf_op jit(solution)/shard_map/ppermute | solution.py:69
  61.9 24.6 %collective-permute-start.19 = (bf16[1,48,2048]{2,1,0:T(8,128)(2,1)S(1)}, bf16[1,48,2048]{2,1,0:T(8,128)(2,1)S(1)}, u32[]{:S(2)}, u32[]{:S(2)}) collective-permute-start(bf16[1,48,2048]{2,1,0:T(8,128)(2,1)S(1)} %get-tuple-element.488), channel_id=1, source_target_pairs={{0,8},{1,9},{2,10},{3,11},{4,12},{5,13},{6,14},{7,15},{8,0},{9,1},... | collective-permute-start | bytes 589832 | tf_op jit(solution)/shard_map/ppermute | solution.py:66
  68.1 16.4 %collective-permute-start.5 = (bf16[2,64,768]{2,1,0:T(8,128)(2,1)S(1)}, bf16[2,64,768]{2,1,0:T(8,128)(2,1)S(1)}, u32[]{:S(2)}, u32[]{:S(2)}) collective-permute-start(bf16[2,64,768]{2,1,0:T(8,128)(2,1)S(1)} %pad_maximum_fusion.16), channel_id=1, source_target_pairs={{0,8},{1,9},{2,10},{3,11},{4,12},{5,13},{6,14},{7,15},{8,0},{9,1},... | collective-permute-start | bytes 589832 | tf_op jit(solution)/shard_map/ppermute | solution.py:66
  84.5 35.4 %collective-permute-start.27 = (bf16[8,48,2048]{2,1,0:T(8,128)(2,1)S(1)}, bf16[8,48,2048]{2,1,0:T(8,128)(2,1)S(1)}, u32[]{:S(2)}, u32[]{:S(2)}) collective-permute-start(bf16[8,48,2048]{2,1,0:T(8,128)(2,1)S(1)} %pad_maximum_fusion.refs_3_), channel_id=1, source_target_pairs={{0,2},{1,3},{2,0},{3,1},{4,6},{5,7},{6,4},{7,5},{8,10},{9,11},{10,... | collective-permute-start | bytes 4718600 | tf_op jit(solution)/shard_map/ppermute | solution.py:69
  86.5 9.1 %collective-permute-start.17 = (bf16[4,64,768]{2,1,0:T(8,128)(2,1)S(1)}, bf16[4,64,768]{2,1,0:T(8,128)(2,1)S(1)}, u32[]{:S(2)}, u32[]{:S(2)}) collective-permute-start(bf16[4,64,768]{2,1,0:T(8,128)(2,1)S(1)} %pad_maximum_fusion.12), channel_id=1, source_target_pairs={{0,4},{1,5},{2,6},{3,7},{4,0},{5,1},{6,2},{7,3},{8,12},{9,13},{10,... | collective-permute-start | bytes 1179656 | tf_op jit(solution)/shard_map/ppermute | solution.py:66
  86.6 17.4 %collective-permute-start.20 = (bf16[2,48,2048]{2,1,0:T(8,128)(2,1)S(1)}, bf16[2,48,2048]{2,1,0:T(8,128)(2,1)S(1)}, u32[]{:S(2)}, u32[]{:S(2)}) collective-permute-start(bf16[2,48,2048]{2,1,0:T(8,128)(2,1)S(1)} %pad_maximum_fusion.13), channel_id=1, source_target_pairs={{0,4},{1,5},{2,6},{3,7},{4,0},{5,1},{6,2},{7,3},{8,12},{9,13},{10,... | collective-permute-start | bytes 1179656 | tf_op jit(solution)/shard_map/ppermute | solution.py:66
  88.1 18.8 %collective-permute-start.22 = (bf16[8,96,768]{2,1,0:T(8,128)(2,1)S(1)}, bf16[8,96,768]{2,1,0:T(8,128)(2,1)S(1)}, u32[]{:S(2)}, u32[]{:S(2)}) collective-permute-start(bf16[8,96,768]{2,1,0:T(8,128)(2,1)S(1)} %pad_maximum_fusion.2.refs_5_), channel_id=1, source_target_pairs={{0,16},{16,0},{1,17},{17,1},{2,18},{18,2},{3,19},{19,3},{4,20},{20... | collective-permute-start | bytes 3538952 | tf_op jit(solution)/shard_map/ppermute | solution.py:73
  95.6 11.4 %collective-permute-start.23 = (bf16[8,96,768]{2,1,0:T(8,128)(2,1)S(1)}, bf16[8,96,768]{2,1,0:T(8,128)(2,1)S(1)}, u32[]{:S(2)}, u32[]{:S(2)}) collective-permute-start(bf16[8,96,768]{2,1,0:T(8,128)(2,1)S(1)} %collective-permute-done.18.refs_6_), channel_id=1, source_target_pairs={{0,16},{16,0},{1,17},{17,1},{2,18},{18,2},{3,19},{19,3},{4,20},{20... | collective-permute-start | bytes 3538952 | tf_op jit(solution)/shard_map/ppermute | solution.py:73
  104.1 15.8 %collective-permute-start.28 = (bf16[4,48,2048]{2,1,0:T(8,128)(2,1)S(1)}, bf16[4,48,2048]{2,1,0:T(8,128)(2,1)S(1)}, u32[]{:S(2)}, u32[]{:S(2)}) collective-permute-start(bf16[4,48,2048]{2,1,0:T(8,128)(2,1)S(1)} %pad_maximum_fusion.7), channel_id=1, source_target_pairs={{0,1},{1,0},{2,3},{3,2},{4,5},{5,4},{6,7},{7,6},{8,9},{9,8},{10,11... | collective-permute-start | bytes 2359304 | tf_op jit(solution)/shard_map/ppermute | solution.py:69
  104.2 19.3 %collective-permute-start.26 = (bf16[8,48,2048]{2,1,0:T(8,128)(2,1)S(1)}, bf16[8,48,2048]{2,1,0:T(8,128)(2,1)S(1)}, u32[]{:S(2)}, u32[]{:S(2)}) collective-permute-start(bf16[8,48,2048]{2,1,0:T(8,128)(2,1)S(1)} %pad_maximum_fusion.refs_3_), channel_id=1, source_target_pairs={{0,16},{16,0},{1,17},{17,1},{2,18},{18,2},{3,19},{19,3},{4,20},{20... | collective-permute-start | bytes 4718600 | tf_op jit(solution)/shard_map/ppermute | solution.py:73
  119.9 15.6 %collective-permute-start.25 = (bf16[8,64,768]{2,1,0:T(8,128)(2,1)S(1)}, bf16[8,64,768]{2,1,0:T(8,128)(2,1)S(1)}, u32[]{:S(2)}, u32[]{:S(2)}) collective-permute-start(bf16[8,64,768]{2,1,0:T(8,128)(2,1)S(1)} %pad_maximum_fusion.6.refs_4_), channel_id=1, source_target_pairs={{0,1},{1,0},{2,3},{3,2},{4,5},{5,4},{6,7},{7,6},{8,9},{9,8},{10,11... | collective-permute-start | bytes 2359304 | tf_op jit(solution)/shard_map/ppermute | solution.py:69
  120.4 17.8 %collective-permute-start.24 = (bf16[8,64,768]{2,1,0:T(8,128)(2,1)S(1)}, bf16[8,64,768]{2,1,0:T(8,128)(2,1)S(1)}, u32[]{:S(2)}, u32[]{:S(2)}) collective-permute-start(bf16[8,64,768]{2,1,0:T(8,128)(2,1)S(1)} %pad_maximum_fusion.6.refs_4_), channel_id=1, source_target_pairs={{0,16},{16,0},{1,17},{17,1},{2,18},{18,2},{3,19},{19,3},{4,20},{20... | collective-permute-start | bytes 2359304 | tf_op jit(solution)/shard_map/ppermute | solution.py:73
  123.2 34.5 %collective-permute-start.38 = (bf16[8,48,2048]{2,1,0:T(8,128)(2,1)}, bf16[8,48,2048]{2,1,0:T(8,128)(2,1)}, u32[]{:S(2)}, u32[]{:S(2)}) collective-permute-start(bf16[8,48,2048]{2,1,0:T(8,128)(2,1)} %pad_maximum_fusion.1.refs_3_), channel_id=1, source_target_pairs={{0,2},{1,3},{2,0},{3,1},{4,6},{5,7},{6,4},{7,5},{8,10},{9,11},{10,... | collective-permute-start | bytes 4718600 | tf_op jit(solution)/shard_map/ppermute | solution.py:69
  123.5 20.0 %collective-permute-start.31 = (bf16[8,96,768]{2,1,0:T(8,128)(2,1)S(1)}, bf16[8,96,768]{2,1,0:T(8,128)(2,1)S(1)}, u32[]{:S(2)}, u32[]{:S(2)}) collective-permute-start(bf16[8,96,768]{2,1,0:T(8,128)(2,1)S(1)} %pad_maximum_fusion.3.refs_5_), channel_id=1, source_target_pairs={{0,16},{16,0},{1,17},{17,1},{2,18},{18,2},{3,19},{19,3},{4,20},{20... | collective-permute-start | bytes 3538952 | tf_op jit(solution)/shard_map/ppermute | solution.py:73
  123.7 19.8 %collective-permute-start.32 = (bf16[8,96,768]{2,1,0:T(8,128)(2,1)S(1)}, bf16[8,96,768]{2,1,0:T(8,128)(2,1)S(1)}, u32[]{:S(2)}, u32[]{:S(2)}) collective-permute-start(bf16[8,96,768]{2,1,0:T(8,128)(2,1)S(1)} %collective-permute-done.21.refs_6_), channel_id=1, source_target_pairs={{0,16},{16,0},{1,17},{17,1},{2,18},{18,2},{3,19},{19,3},{4,20},{20... | collective-permute-start | bytes 3538952 | tf_op jit(solution)/shard_map/ppermute | solution.py:73
  138.2 19.5 %collective-permute-start.33 = (bf16[8,64,768]{2,1,0:T(8,128)(2,1)}, bf16[8,64,768]{2,1,0:T(8,128)(2,1)}, u32[]{:S(2)}, u32[]{:S(2)}) collective-permute-start(bf16[8,64,768]{2,1,0:T(8,128)(2,1)} %pad_maximum_fusion.5.refs_8_), channel_id=1, source_target_pairs={{0,4},{1,5},{2,6},{3,7},{4,0},{5,1},{6,2},{7,3},{8,12},{9,13},{10,... | collective-permute-start | bytes 2359304 | tf_op jit(solution)/shard_map/ppermute | solution.py:66
  140.1 20.7 %collective-permute-start.37 = (bf16[8,48,2048]{2,1,0:T(8,128)(2,1)}, bf16[8,48,2048]{2,1,0:T(8,128)(2,1)}, u32[]{:S(2)}, u32[]{:S(2)}) collective-permute-start(bf16[8,48,2048]{2,1,0:T(8,128)(2,1)} %pad_maximum_fusion.1.refs_3_), channel_id=1, source_target_pairs={{0,16},{16,0},{1,17},{17,1},{2,18},{18,2},{3,19},{19,3},{4,20},{20... | collective-permute-start | bytes 4718600 | tf_op jit(solution)/shard_map/ppermute | solution.py:73
  158.5 31.2 %collective-permute-start.40 = (bf16[512,1536]{1,0:T(8,128)(2,1)}, bf16[512,1536]{1,0:T(8,128)(2,1)}, u32[]{:S(2)}, u32[]{:S(2)}) collective-permute-start(bf16[512,1536]{1,0:T(8,128)(2,1)} %get-tuple-element.613.refs_1_.refs_2_.normed_ref.own_ref), channel_id=1, source_target_pairs={{0,16},{16,0},{1,17},{17,1},{2,18},{18,2},{3,19},{19,3},{4,20},{20... | collective-permute-start | bytes 4718600 | tf_op jit(solution)/shard_map/ppermute | solution.py:73
  158.5 15.8 %collective-permute-start.35 = (bf16[8,64,768]{2,1,0:T(8,128)(2,1)}, bf16[8,64,768]{2,1,0:T(8,128)(2,1)}, u32[]{:S(2)}, u32[]{:S(2)}) collective-permute-start(bf16[8,64,768]{2,1,0:T(8,128)(2,1)} %pad_maximum_fusion.5.refs_8_), channel_id=1, source_target_pairs={{0,16},{16,0},{1,17},{17,1},{2,18},{18,2},{3,19},{19,3},{4,20},{20... | collective-permute-start | bytes 2359304 | tf_op jit(solution)/shard_map/ppermute | solution.py:73
  159.0 15.3 %collective-permute-start.36 = (bf16[8,64,768]{2,1,0:T(8,128)(2,1)}, bf16[8,64,768]{2,1,0:T(8,128)(2,1)}, u32[]{:S(2)}, u32[]{:S(2)}) collective-permute-start(bf16[8,64,768]{2,1,0:T(8,128)(2,1)} %collective-permute-done.33.refs_9_), channel_id=1, source_target_pairs={{0,16},{16,0},{1,17},{17,1},{2,18},{18,2},{3,19},{19,3},{4,20},{20... | collective-permute-start | bytes 2359304 | tf_op jit(solution)/shard_map/ppermute | solution.py:73
  189.2 30.6 %collective-permute-start.42 = (bf16[512,3072]{1,0:T(8,128)(2,1)S(1)}, bf16[512,3072]{1,0:T(8,128)(2,1)S(1)}, u32[]{:S(2)}, u32[]{:S(2)}) collective-permute-start(bf16[512,3072]{1,0:T(8,128)(2,1)S(1)} %get-tuple-element.630.refs_5_.refs_0_.low.high), channel_id=1, source_target_pairs={{0,16},{16,0},{1,17},{17,1},{2,18},{18,2},{3,19},{19,3},{4,20},{20... | collective-permute-start | bytes 9437192 | tf_op jit(solution)/shard_map/ppermute | solution.py:73
  203.7 16.2 %collective-permute-start.41 = (bf16[512,2560]{1,0:T(8,128)(2,1)S(1)}, bf16[512,2560]{1,0:T(8,128)(2,1)S(1)}, u32[]{:S(2)}, u32[]{:S(2)}) collective-permute-start(bf16[512,2560]{1,0:T(8,128)(2,1)S(1)} %get-tuple-element.629), channel_id=1, source_target_pairs={{0,16},{16,0},{1,17},{17,1},{2,18},{18,2},{3,19},{19,3},{4,20},{20... | collective-permute-start | bytes 7864328 | tf_op jit(solution)/shard_map/ppermute | solution.py:73
  203.9 16.0 %collective-permute-start.34 = (bf16[512,1536]{1,0:T(8,128)(2,1)S(1)}, bf16[512,1536]{1,0:T(8,128)(2,1)S(1)}, u32[]{:S(2)}, u32[]{:S(2)}) collective-permute-start(bf16[512,1536]{1,0:T(8,128)(2,1)S(1)} %copy-done.1), channel_id=1, source_target_pairs={{0,16},{16,0},{1,17},{17,1},{2,18},{18,2},{3,19},{19,3},{4,20},{20... | collective-permute-start | bytes 4718600 | tf_op jit(solution)/shard_map/ppermute | solution.py:73
  204.2 33.5 %collective-permute-start.46 = (bf16[512,3072]{1,0:T(8,128)(2,1)S(1)}, bf16[512,3072]{1,0:T(8,128)(2,1)S(1)}, u32[]{:S(2)}, u32[]{:S(2)}) collective-permute-start(bf16[512,3072]{1,0:T(8,128)(2,1)S(1)} %get-tuple-element.663.refs_2_.refs_3_.normed_ref.refs_0_.refs_6_), channel_id=1, source_target_pairs={{0,16},{16,0},{1,17},{17,1},{2,18},{18,2},{3,19},{19,3},{4,20},{20... | collective-permute-start | bytes 9437192 | tf_op jit(solution)/shard_map/ppermute | solution.py:73
  229.0 8.8 %collective-permute-start.45 = (bf16[512,2560]{1,0:T(8,128)(2,1)}, bf16[512,2560]{1,0:T(8,128)(2,1)S(1)}, u32[]{:S(2)}, u32[]{:S(2)}) collective-permute-start(bf16[512,2560]{1,0:T(8,128)(2,1)} %get-tuple-element.662), channel_id=1, source_target_pairs={{0,16},{16,0},{1,17},{17,1},{2,18},{18,2},{3,19},{19,3},{4,20},{20... | collective-permute-start | bytes 7864328 | tf_op jit(solution)/shard_map/ppermute | solution.py:73
  229.4 8.4 %collective-permute-start.44 = (bf16[512,1920]{1,0:T(8,128)(2,1)S(1)}, bf16[512,1920]{1,0:T(8,128)(2,1)S(1)}, u32[]{:S(2)}, u32[]{:S(2)}) collective-permute-start(bf16[512,1920]{1,0:T(8,128)(2,1)S(1)} %get-tuple-element.658), channel_id=1, source_target_pairs={{0,16},{16,0},{1,17},{17,1},{2,18},{18,2},{3,19},{19,3},{4,20},{20... | collective-permute-start | bytes 5898248 | tf_op jit(solution)/shard_map/ppermute | solution.py:73
  229.5 24.9 %collective-permute-start.43 = (bf16[8,912,128]{2,1,0:T(8,128)(2,1)}, bf16[8,912,128]{2,1,0:T(8,128)(2,1)}, u32[]{:S(2)}, u32[]{:S(2)}) collective-permute-start(bf16[8,912,128]{2,1,0:T(8,128)(2,1)} %get-tuple-element.657), channel_id=1, source_target_pairs={{0,2},{1,3},{2,0},{3,1},{4,6},{5,7},{6,4},{7,5},{8,10},{9,11},{10,... | collective-permute-start | bytes 5603336 | tf_op jit(solution)/shard_map/ppermute | solution.py:69
  253.3 31.1 %collective-permute-start.49 = (bf16[8,1296,128]{2,1,0:T(8,128)(2,1)}, bf16[8,1296,128]{2,1,0:T(8,128)(2,1)S(1)}, u32[]{:S(2)}, u32[]{:S(2)}) collective-permute-start(bf16[8,1296,128]{2,1,0:T(8,128)(2,1)} %get-tuple-element.720), channel_id=1, source_target_pairs={{0,2},{1,3},{2,0},{3,1},{4,6},{5,7},{6,4},{7,5},{8,10},{9,11},{10,... | collective-permute-start | bytes 7962632 | tf_op jit(solution)/shard_map/ppermute | solution.py:69
  256.2 24.0 %collective-permute-start.47 = (bf16[4,912,128]{2,1,0:T(8,128)(2,1)S(1)}, bf16[4,912,128]{2,1,0:T(8,128)(2,1)S(1)}, u32[]{:S(2)}, u32[]{:S(2)}) collective-permute-start(bf16[4,912,128]{2,1,0:T(8,128)(2,1)S(1)} %add_convert_fusion.1), channel_id=1, source_target_pairs={{0,4},{1,5},{2,6},{3,7},{4,0},{5,1},{6,2},{7,3},{8,12},{9,13},{10,... | collective-permute-start | bytes 2801672 | tf_op jit(solution)/shard_map/ppermute | solution.py:66
  282.5 10.1 %collective-permute-start.48 = (bf16[512,1920]{1,0:T(8,128)(2,1)}, bf16[512,1920]{1,0:T(8,128)(2,1)S(1)}, u32[]{:S(2)}, u32[]{:S(2)}) collective-permute-start(bf16[512,1920]{1,0:T(8,128)(2,1)} %get-tuple-element.718), channel_id=1, source_target_pairs={{0,16},{16,0},{1,17},{17,1},{2,18},{18,2},{3,19},{19,3},{4,20},{20... | collective-permute-start | bytes 5898248 | tf_op jit(solution)/shard_map/ppermute | solution.py:73
  286.3 32.1 %collective-permute-start.53 = (bf16[4,1296,128]{2,1,0:T(8,128)(2,1)}, bf16[4,1296,128]{2,1,0:T(8,128)(2,1)}, u32[]{:S(2)}, u32[]{:S(2)}) collective-permute-start(bf16[4,1296,128]{2,1,0:T(8,128)(2,1)} %add_convert_fusion), channel_id=1, source_target_pairs={{0,1},{1,0},{2,3},{3,2},{4,5},{5,4},{6,7},{7,6},{8,9},{9,8},{10,11... | collective-permute-start | bytes 3981320 | tf_op jit(solution)/shard_map/ppermute | solution.py:69
  286.5 25.5 %collective-permute-start.50 = (bf16[8,384,128]{2,1,0:T(8,128)(2,1)}, bf16[8,384,128]{2,1,0:T(8,128)(2,1)}, u32[]{:S(2)}, u32[]{:S(2)}) collective-permute-start(bf16[8,384,128]{2,1,0:T(8,128)(2,1)} %get-tuple-element.733), channel_id=1, source_target_pairs={{0,1},{1,0},{2,3},{3,2},{4,5},{5,4},{6,7},{7,6},{8,9},{9,8},{10,11... | collective-permute-start | bytes 2359304 | tf_op jit(solution)/shard_map/ppermute | solution.py:69
  287.8 25.3 %collective-permute-start.54 = (bf16[8,432,128]{2,1,0:T(8,128)(2,1)}, bf16[8,432,128]{2,1,0:T(8,128)(2,1)}, u32[]{:S(2)}, u32[]{:S(2)}) collective-permute-start(bf16[8,432,128]{2,1,0:T(8,128)(2,1)} %get-tuple-element.743), channel_id=1, source_target_pairs={{0,4},{1,5},{2,6},{3,7},{4,0},{5,1},{6,2},{7,3},{8,12},{9,13},{10,... | collective-permute-start | bytes 2654216 | tf_op jit(solution)/shard_map/ppermute | solution.py:66
  291.9 34.9 %collective-permute-start.58 = (bf16[2,912,128]{2,1,0:T(8,128)(2,1)S(1)}, bf16[2,912,128]{2,1,0:T(8,128)(2,1)S(1)}, u32[]{:S(2)}, u32[]{:S(2)}) collective-permute-start(bf16[2,912,128]{2,1,0:T(8,128)(2,1)S(1)} %copy-done.49), channel_id=1, source_target_pairs={{0,1},{1,0},{2,3},{3,2},{4,5},{5,4},{6,7},{7,6},{8,9},{9,8},{10,11... | collective-permute-start | bytes 1400840 | tf_op jit(solution)/shard_map/ppermute | solution.py:69
  313.2 13.2 %collective-permute-start.55 = (bf16[8,432,128]{2,1,0:T(8,128)(2,1)S(1)}, bf16[8,432,128]{2,1,0:T(8,128)(2,1)S(1)}, u32[]{:S(2)}, u32[]{:S(2)}) collective-permute-start(bf16[8,432,128]{2,1,0:T(8,128)(2,1)S(1)} %get-tuple-element.756), channel_id=1, source_target_pairs={{0,1},{1,0},{2,3},{3,2},{4,5},{5,4},{6,7},{7,6},{8,9},{9,8},{10,11... | collective-permute-start | bytes 2654216 | tf_op jit(solution)/shard_map/ppermute | solution.py:69
  314.6 7.2 %collective-permute-start.52 = (bf16[4,384,128]{2,1,0:T(8,128)(2,1)S(1)}, bf16[4,384,128]{2,1,0:T(8,128)(2,1)S(1)}, u32[]{:S(2)}, u32[]{:S(2)}) collective-permute-start(bf16[4,384,128]{2,1,0:T(8,128)(2,1)S(1)} %add_convert_fusion.6), channel_id=1, source_target_pairs={{0,4},{1,5},{2,6},{3,7},{4,0},{5,1},{6,2},{7,3},{8,12},{9,13},{10,... | collective-permute-start | bytes 1179656 | tf_op jit(solution)/shard_map/ppermute | solution.py:66
  315.4 7.4 %collective-permute-start.51 = (bf16[512,768]{1,0:T(8,128)(2,1)S(1)}, bf16[512,768]{1,0:T(8,128)(2,1)S(1)}, u32[]{:S(2)}, u32[]{:S(2)}) collective-permute-start(bf16[512,768]{1,0:T(8,128)(2,1)S(1)} %get-tuple-element.739), channel_id=1, source_target_pairs={{0,16},{16,0},{1,17},{17,1},{2,18},{18,2},{3,19},{19,3},{4,20},{20... | collective-permute-start | bytes 2359304 | tf_op jit(solution)/shard_map/ppermute | solution.py:73
  318.4 12.7 %collective-permute-start.57 = (bf16[4,432,128]{2,1,0:T(8,128)(2,1)S(1)}, bf16[4,432,128]{2,1,0:T(8,128)(2,1)S(1)}, u32[]{:S(2)}, u32[]{:S(2)}) collective-permute-start(bf16[4,432,128]{2,1,0:T(8,128)(2,1)S(1)} %add_convert_fusion.5), channel_id=1, source_target_pairs={{0,1},{1,0},{2,3},{3,2},{4,5},{5,4},{6,7},{7,6},{8,9},{9,8},{10,11... | collective-permute-start | bytes 1327112 | tf_op jit(solution)/shard_map/ppermute | solution.py:69
  326.4 19.7 %collective-permute-start.56 = (bf16[2,1296,128]{2,1,0:T(8,128)(2,1)S(1)}, bf16[2,1296,128]{2,1,0:T(8,128)(2,1)S(1)}, u32[]{:S(2)}, u32[]{:S(2)}) collective-permute-start(bf16[2,1296,128]{2,1,0:T(8,128)(2,1)S(1)} %add_convert_fusion.2), channel_id=1, source_target_pairs={{0,4},{1,5},{2,6},{3,7},{4,0},{5,1},{6,2},{7,3},{8,12},{9,13},{10,... | collective-permute-start | bytes 1990664 | tf_op jit(solution)/shard_map/ppermute | solution.py:66
  332.2 15.1 %collective-permute-start.61 = (bf16[2,384,128]{2,1,0:T(8,128)(2,1)S(1)}, bf16[2,384,128]{2,1,0:T(8,128)(2,1)S(1)}, u32[]{:S(2)}, u32[]{:S(2)}) collective-permute-start(bf16[2,384,128]{2,1,0:T(8,128)(2,1)S(1)} %add_convert_fusion.11), channel_id=1, source_target_pairs={{0,2},{1,3},{2,0},{3,1},{4,6},{5,7},{6,4},{7,5},{8,10},{9,11},{10,... | collective-permute-start | bytes 589832 | tf_op jit(solution)/shard_map/ppermute | solution.py:69
  333.6 14.7 %collective-permute-start.60 = (bf16[1,912,128]{2,1,0:T(8,128)(2,1)S(1)}, bf16[1,912,128]{2,1,0:T(8,128)(2,1)S(1)}, u32[]{:S(2)}, u32[]{:S(2)}) collective-permute-start(bf16[1,912,128]{2,1,0:T(8,128)(2,1)S(1)} %add_convert_fusion.8), channel_id=1, source_target_pairs={{0,8},{1,9},{2,10},{3,11},{4,12},{5,13},{6,14},{7,15},{8,0},{9,1},... | collective-permute-start | bytes 700424 | tf_op jit(solution)/shard_map/ppermute | solution.py:66
  335.1 14.4 %collective-permute-start.59 = (bf16[4,432,128]{2,1,0:T(8,128)(2,1)S(1)}, bf16[4,432,128]{2,1,0:T(8,128)(2,1)S(1)}, u32[]{:S(2)}, u32[]{:S(2)}) collective-permute-start(bf16[4,432,128]{2,1,0:T(8,128)(2,1)S(1)} %add_convert_fusion.4), channel_id=1, source_target_pairs={{0,2},{1,3},{2,0},{3,1},{4,6},{5,7},{6,4},{7,5},{8,10},{9,11},{10,... | collective-permute-start | bytes 1327112 | tf_op jit(solution)/shard_map/ppermute | solution.py:69
  335.9 34.4 %collective-permute-start.63 = (bf16[2,432,128]{2,1,0:T(8,128)(2,1)S(1)}, bf16[2,432,128]{2,1,0:T(8,128)(2,1)S(1)}, u32[]{:S(2)}, u32[]{:S(2)}) collective-permute-start(bf16[2,432,128]{2,1,0:T(8,128)(2,1)S(1)} %add_convert_fusion.10), channel_id=1, source_target_pairs={{0,2},{1,3},{2,0},{3,1},{4,6},{5,7},{6,4},{7,5},{8,10},{9,11},{10,... | collective-permute-start | bytes 663560 | tf_op jit(solution)/shard_map/ppermute | solution.py:69
  349.6 19.5 %collective-permute-start.64 = (bf16[1,1296,128]{2,1,0:T(8,128)(2,1)S(1)}, bf16[1,1296,128]{2,1,0:T(8,128)(2,1)S(1)}, u32[]{:S(2)}, u32[]{:S(2)}) collective-permute-start(bf16[1,1296,128]{2,1,0:T(8,128)(2,1)S(1)} %add_convert_fusion.7), channel_id=1, source_target_pairs={{0,8},{1,9},{2,10},{3,11},{4,12},{5,13},{6,14},{7,15},{8,0},{9,1},... | collective-permute-start | bytes 995336 | tf_op jit(solution)/shard_map/ppermute | solution.py:66
  350.4 20.9 %collective-permute-start.62 = (bf16[2,432,128]{2,1,0:T(8,128)(2,1)S(1)}, bf16[2,432,128]{2,1,0:T(8,128)(2,1)S(1)}, u32[]{:S(2)}, u32[]{:S(2)}) collective-permute-start(bf16[2,432,128]{2,1,0:T(8,128)(2,1)S(1)} %add_convert_fusion.9), channel_id=1, source_target_pairs={{0,4},{1,5},{2,6},{3,7},{4,0},{5,1},{6,2},{7,3},{8,12},{9,13},{10,... | collective-permute-start | bytes 663560 | tf_op jit(solution)/shard_map/ppermute | solution.py:66
  352.6 18.8 %collective-permute-start.67 = (bf16[1,384,128]{2,1,0:T(8,128)(2,1)S(1)}, bf16[1,384,128]{2,1,0:T(8,128)(2,1)S(1)}, u32[]{:S(2)}, u32[]{:S(2)}) collective-permute-start(bf16[1,384,128]{2,1,0:T(8,128)(2,1)S(1)} %add_convert_fusion.14), channel_id=1, source_target_pairs={{0,8},{1,9},{2,10},{3,11},{4,12},{5,13},{6,14},{7,15},{8,0},{9,1},... | collective-permute-start | bytes 294920 | tf_op jit(solution)/shard_map/ppermute | solution.py:66
  372.3 9.6 %collective-permute-start.66 = (bf16[1,432,128]{2,1,0:T(8,128)(2,1)S(1)}, bf16[1,432,128]{2,1,0:T(8,128)(2,1)S(1)}, u32[]{:S(2)}, u32[]{:S(2)}) collective-permute-start(bf16[1,432,128]{2,1,0:T(8,128)(2,1)S(1)} %add_convert_fusion.13), channel_id=1, source_target_pairs={{0,8},{1,9},{2,10},{3,11},{4,12},{5,13},{6,14},{7,15},{8,0},{9,1},... | collective-permute-start | bytes 331784 | tf_op jit(solution)/shard_map/ppermute | solution.py:66
  372.5 11.8 %collective-permute-start.65 = (bf16[1,432,128]{2,1,0:T(8,128)(2,1)S(1)}, bf16[1,432,128]{2,1,0:T(8,128)(2,1)S(1)}, u32[]{:S(2)}, u32[]{:S(2)}) collective-permute-start(bf16[1,432,128]{2,1,0:T(8,128)(2,1)S(1)} %add_convert_fusion.12), channel_id=1, source_target_pairs={{0,8},{1,9},{2,10},{3,11},{4,12},{5,13},{6,14},{7,15},{8,0},{9,1},... | collective-permute-start | bytes 331784 | tf_op jit(solution)/shard_map/ppermute | solution.py:66
  374.9 12.5 %collective-permute-start.69 = (f32[1296,128]{1,0:T(8,128)S(1)}, f32[1296,128]{1,0:T(8,128)S(1)}, u32[]{:S(2)}, u32[]{:S(2)}) collective-permute-start(f32[1296,128]{1,0:T(8,128)S(1)} %get-tuple-element.822), channel_id=1, source_target_pairs={{0,16},{16,0},{1,17},{17,1},{2,18},{18,2},{3,19},{19,3},{4,20},{20... | collective-permute-start | bytes 1990664 | tf_op jit(solution)/shard_map/ppermute | solution.py:73
  384.4 5.9 %collective-permute-start.68 = (f32[432,128]{1,0:T(8,128)S(1)}, f32[432,128]{1,0:T(8,128)S(1)}, u32[]{:S(2)}, u32[]{:S(2)}) collective-permute-start(f32[432,128]{1,0:T(8,128)S(1)} %get-tuple-element.821), channel_id=1, source_target_pairs={{0,16},{16,0},{1,17},{17,1},{2,18},{18,2},{3,19},{19,3},{4,20},{20... | collective-permute-start | bytes 663560 | tf_op jit(solution)/shard_map/ppermute | solution.py:73
  (60 other events, 592.4 us)

commit v4 on v3

--- a/solution.py
+++ b/solution.py
@@ -30,7 +30,7 @@
     ((ZH, X, ZL, Y), None),
     ((Y, ZH, ZL, X), None),
     ((ZH, ZL, Y, X), None),
-    ((ZH, ZL, X, Y), None),
+    ((ZH, ZL, Y, X), None),
     ((ZH, X, Y, ZL), None),
 )
 SCATTER = {
@@ -41,13 +41,13 @@
     "T0": (X, Y, ZL, ZH),
 }
 ORDER = (
-    "g40", "g10", "g20", "g00", "g50", "g01", "g30", "g21", "g11", "g02", "g31", "g51", "g12",
-    "g32", "g52", "g03", "g33", "g13", "g53", "g22", "w1", "g41", "w0", "v0", "g23", "v3", "w3",
-    "g42", "A0", "w2", "dg42", "v1", "g43", "xa0", "F0", "v2", "w4", "w5", "L0", "A1", "v5", "xf0",
-    "xa1", "v4", "F1", "B1", "xf1", "dxa0", "K1", "xs1", "B0", "xt1", "G1", "rG10", "xs0", "D1",
-    "G0", "rG00", "rG11", "L1", "T1", "rD10", "K0", "rG12", "rT10", "xt0", "rG01", "T0", "rD11",
-    "rT00", "oa", "rT11", "rG02", "rD12", "doa", "rT01", "ob", "rG13", "rT12", "rG03", "oi", "rD13",
-    "zG1", "rT02", "zG0", "rT13", "rT03", "zD1", "hG", "zT1", "zT0", "hT", "u1", "u2",
+    "g40", "g10", "g20", "g50", "g00", "g01", "g30", "g21", "g11", "dg30", "g31", "g02", "g51",
+    "g12", "g32", "g52", "g03", "g33", "g53", "g13", "g22", "w1", "g41", "w0", "v0", "g23", "v3",
+    "w3", "g42", "A0", "w2", "dg42", "v1", "g43", "xa0", "F0", "v2", "w4", "w5", "L0", "A1", "v5",
+    "xf0", "xa1", "v4", "F1", "B1", "xf1", "dxa0", "K1", "xs1", "B0", "xt1", "G1", "rG10", "xs0",
+    "D1", "G0", "rG00", "rG11", "L1", "T1", "rD10", "K0", "rG12", "rT10", "xt0", "rG01", "T0",
+    "rD11", "rT00", "oa", "rT11", "rG02", "rD12", "doa", "rT01", "ob", "rG13", "rT12", "rG03",
+    "rD13", "zG1", "rT02", "zG0", "rT13", "rT03", "zD1", "hG", "oi", "zT1", "zT0", "hT", "u1", "u2",
 )
 
 def order_masks(order):

time: 397 us -> 389 us (0.980)
  waiting for transfers between devices: 117 us -> 87.5 us
  starting transfers between devices: 73.4 us -> 93.8 us
    ppermute x22, waiting for transfers between devices: 82 us -> 54.3 us  [flip(): return lax.ppermute(value, 'dp', [(i, i ^ bit) for i in range(count)])]
    ppermute x26, starting transfers between devices: 24.1 us -> 41.5 us  [swap(): return lax.ppermute(value, 'section', [(0, 1), (1, 0)])]
  transfers between devices with their start and end apart: 70 -> 70, of which waited for: 26 -> 25; matrix products, arithmetic and copies ran while one was open for 9% -> 10% of each run, Pallas kernels for 39% -> 40%
where the time goes in v4:
time: 389 us; the launch traced here: 385 us
  Pallas kernels  155 us (40%)
  starting transfers between devices  93.8 us (24%)
  waiting for transfers between devices  87.5 us (22%)
  other arithmetic  38.3 us (10%)
  local copies, waits for them, and re-layouts  8.67 us (2%)
    pallas_call x17, Pallas kernels, launch(): pl.pallas_call(kernel, grid_spec=pltpu.PrefetchScalarGridSpec(num_scalar_...  155 us
    ppermute x22, waiting for transfers between devices, flip(): return lax.ppermute(value, 'dp', [(i, i ^ bit) for i in range(count)])  54.3 us
    ppermute x26, starting transfers between devices, swap(): return lax.ppermute(value, 'section', [(0, 1), (1, 0)])  41.5 us
    ppermute x22, starting transfers between devices, flip(): return lax.ppermute(value, 'dp', [(i, i ^ bit) for i in range(count)])  32.6 us
    ppermute x22, waiting for transfers between devices, flip(): return lax.ppermute(value, ('section', 'dp'), pairs)  28.1 us
    ppermute x22, starting transfers between devices, flip(): return lax.ppermute(value, ('section', 'dp'), pairs)  19.7 us
    convert_element_type x15, other arithmetic, halve(): sum((p[size // 2:size].astype(F32) for p in parts[name])).astype(BF16)  16.7 us
  transfers between devices with their start and end apart: 70, of which 25 were waited for; matrix products, arithmetic and copies ran while one was open for 10% of the time, Pallas kernels for 40%

profile of v4, /device:TPU:1, one launch (start us, length us, event | category | flops | bytes accessed | tf_op | source)
XLA Modules:
  0.0 384.6 jit_solution(12896884013642548477)
XLA Ops:
  11.2 3.5 collective-permute-start.4
  16.0 10.0 %collective-permute-done.4 = bf16[1,96,768]{2,1,0:T(8,128)(2,1)S(1)} collective-permute-done((bf16[1,96,768]{2,1,0:T(8,128)(2,1)S(1)}, bf16[1,96,768]{2,1,0:T(8,128)(2,1)S(1)}, u32[]{:S(2)}, u32[]{:S(2)}) %collective-permute-start.4) | collective-permute-done | bytes 147488 | tf_op jit(solution)/shard_map/ppermute | solution.py:66
  26.1 3.9 %collective-permute-start.9 = (bf16[2,96,768]{2,1,0:T(8,128)(2,1)S(1)}, bf16[2,96,768]{2,1,0:T(8,128)(2,1)S(1)}, u32[]{:S(2)}, u32[]{:S(2)}) collective-permute-start(bf16[2,96,768]{2,1,0:T(8,128)(2,1)S(1)} %pad_maximum_fusion.14), channel_id=1, source_target_pairs={{0,4},{1,5},{2,6},{3,7},{4,0},{5,1},{6,2},{7,3},{8,12},{9,13},{10,... | collective-permute-start | bytes 884744 | tf_op jit(solution)/shard_map/ppermute | solution.py:66
  31.5 5.1 %collective-permute-done.10 = bf16[1,96,768]{2,1,0:T(8,128)(2,1)S(1)} collective-permute-done((bf16[1,96,768]{2,1,0:T(8,128)(2,1)S(1)}, bf16[1,96,768]{2,1,0:T(8,128)(2,1)S(1)}, u32[]{:S(2)}, u32[]{:S(2)}) %collective-permute-start.10) | collective-permute-done | bytes 147488 | tf_op jit(solution)/shard_map/ppermute | solution.py:66
  36.6 2.2 collective-permute-start.13
  38.8 1.6 collective-permute-done.9
  40.5 2.4 collective-permute-start.16
  43.0 4.8 %collective-permute-done.13 = bf16[2,96,768]{2,1,0:T(8,128)(2,1)S(1)} collective-permute-done((bf16[2,96,768]{2,1,0:T(8,128)(2,1)S(1)}, bf16[2,96,768]{2,1,0:T(8,128)(2,1)S(1)}, u32[]{:S(2)}, u32[]{:S(2)}) %collective-permute-start.13) | collective-permute-done | bytes 294944 | tf_op jit(solution)/shard_map/ppermute | solution.py:66
  47.8 1.3 collective-permute-start.15
  50.4 5.7 %collective-permute-done.12 = bf16[2,64,768]{2,1,0:T(8,128)(2,1)S(1)} collective-permute-done((bf16[2,64,768]{2,1,0:T(8,128)(2,1)S(1)}, bf16[2,64,768]{2,1,0:T(8,128)(2,1)S(1)}, u32[]{:S(2)}, u32[]{:S(2)}) %collective-permute-start.12) | collective-permute-done | bytes 196640 | tf_op jit(solution)/shard_map/ppermute | solution.py:69
  56.6 1.4 collective-permute-start.18
  59.1 1.4 collective-permute-start.21
  60.5 2.8 collective-permute-start.19
  63.8 3.1 collective-permute-start.5
  67.8 5.3 %collective-permute-done.11 = bf16[4,48,2048]{2,1,0:T(8,128)(2,1)S(1)} collective-permute-done((bf16[4,48,2048]{2,1,0:T(8,128)(2,1)S(1)}, bf16[4,48,2048]{2,1,0:T(8,128)(2,1)S(1)}, u32[]{:S(2)}, u32[]{:S(2)}) %collective-permute-start.11) | collective-permute-done | bytes 786464 | tf_op jit(solution)/shard_map/ppermute | solution.py:66
  74.0 6.1 %collective-permute-start.17 = (bf16[4,64,768]{2,1,0:T(8,128)(2,1)S(1)}, bf16[4,64,768]{2,1,0:T(8,128)(2,1)S(1)}, u32[]{:S(2)}, u32[]{:S(2)}) collective-permute-start(bf16[4,64,768]{2,1,0:T(8,128)(2,1)S(1)} %pad_maximum_fusion.12), channel_id=1, source_target_pairs={{0,4},{1,5},{2,6},{3,7},{4,0},{5,1},{6,2},{7,3},{8,12},{9,13},{10,... | collective-permute-start | bytes 1179656 | tf_op jit(solution)/shard_map/ppermute | solution.py:66
  80.3 7.0 %collective-permute-start.22 = (bf16[8,96,768]{2,1,0:T(8,128)(2,1)S(1)}, bf16[8,96,768]{2,1,0:T(8,128)(2,1)S(1)}, u32[]{:S(2)}, u32[]{:S(2)}) collective-permute-start(bf16[8,96,768]{2,1,0:T(8,128)(2,1)S(1)} %pad_maximum_fusion.2.refs_5_), channel_id=1, source_target_pairs={{0,16},{16,0},{1,17},{17,1},{2,18},{18,2},{3,19},{19,3},{4,20},{20... | collective-permute-start | bytes 3538952 | tf_op jit(solution)/shard_map/ppermute | solution.py:73
  87.6 8.8 %collective-permute-start.23 = (bf16[8,96,768]{2,1,0:T(8,128)(2,1)S(1)}, bf16[8,96,768]{2,1,0:T(8,128)(2,1)S(1)}, u32[]{:S(2)}, u32[]{:S(2)}) collective-permute-start(bf16[8,96,768]{2,1,0:T(8,128)(2,1)S(1)} %collective-permute-done.18.refs_6_), channel_id=1, source_target_pairs={{0,16},{16,0},{1,17},{17,1},{2,18},{18,2},{3,19},{19,3},{4,20},{20... | collective-permute-start | bytes 3538952 | tf_op jit(solution)/shard_map/ppermute | solution.py:73
  97.6 6.4 %collective-permute-start.26 = (bf16[8,48,2048]{2,1,0:T(8,128)(2,1)S(1)}, bf16[8,48,2048]{2,1,0:T(8,128)(2,1)S(1)}, u32[]{:S(2)}, u32[]{:S(2)}) collective-permute-start(bf16[8,48,2048]{2,1,0:T(8,128)(2,1)S(1)} %pad_maximum_fusion.refs_3_), channel_id=1, source_target_pairs={{0,16},{16,0},{1,17},{17,1},{2,18},{18,2},{3,19},{19,3},{4,20},{20... | collective-permute-start | bytes 4718600 | tf_op jit(solution)/shard_map/ppermute | solution.py:73
  104.1 11.5 %shard_map.230 = (bf16[512,1536]{1,0:T(8,128)(2,1)}, bf16[512,2304]{1,0:T(8,128)(2,1)}, bf16[2,12,256,256]{3,2,1,0:T(8,128)(2,1)}, f32[512,128]{1,0:T(8,128)}, b...) custom-call(s32[4]{0:T(128)S(1)} %pad_add_fusion.info, ...), custom_call_target="tpu_custom_call" | custom-call | flops 1 | bytes 1 | tf_op jit(solution)/shard_map/pallas_call | solution.py:136
  115.6 1.5 collective-permute-start.29
  117.0 1.4 collective-permute-start.25
  118.6 1.3 pad_maximum_fusion.1.refs_3_
  119.9 1.2 collective-permute-start.38
  121.8 9.3 %shard_map.231 = (f32[512,768]{1,0:T(8,128)S(1)}, f32[512,128]{1,0:T(8,128)}, bf16[512,3072]{1,0:T(8,128)(2,1)S(1)}, bf16[512,2048]{1,0:T(8,128)(2,1)}, bf16[512...) custom-call(s32[4]{0:T(128)S(1)} %pad_add_fusion.info, ...), custom_call_target="tpu_custom_call" | custom-call | flops 1 | bytes 1 | tf_op jit(solution)/shard_map/pallas_call | solution.py:136
  131.6 1.9 collective-permute-done.30.refs_7_
  133.9 3.0 shard_map.232
  136.9 11.4 %shard_map.233 = (bf16[512,1536]{1,0:T(8,128)(2,1)S(1)}, bf16[512,2304]{1,0:T(8,128)(2,1)}, bf16[2,12,256,256]{3,2,1,0:T(8,128)(2,1)}, f32[512,128]{1,0:T(8,128)...) custom-call(s32[4]{0:T(128)S(1)} %pad_add_fusion.info, ...), custom_call_target="tpu_custom_call" | custom-call | flops 1 | bytes 1 | tf_op jit(solution)/shard_map/pallas_call | solution.py:136
  149.5 1.6 collective-permute-done.33.refs_9_
  152.5 1.8 broadcast_select_fusion.refs_0_.refs_2_.refs_3_
  155.3 1.3 copy-done.9
  156.6 11.2 %shard_map.234 = (f32[512,768]{1,0:T(8,128)S(1)}, f32[512,128]{1,0:T(8,128)}, bf16[512,3072]{1,0:T(8,128)(2,1)S(1)}, bf16[512,2048]{1,0:T(8,128)(2,1)}, bf16[512...) custom-call(s32[4]{0:T(128)S(1)} %pad_add_fusion.info, ...), custom_call_target="tpu_custom_call" | custom-call | flops 1 | bytes 1 | tf_op jit(solution)/shard_map/pallas_call | solution.py:136
  167.8 14.9 %shard_map.235 = (bf16[512,2560]{1,0:T(8,128)(2,1)S(1)}, bf16[512,2560]{1,0:T(8,128)(2,1)S(1)}, f32[512,768]{1,0:T(8,128)S(1)}, bf16[512,768]{1,0:T(8,128)(2,1)S(1)}, bf16[16,2,64,768]{3,2,1,0:T(8,128)(2,1)}) custom-call(s32[4]{0:T(128)S(1)} %pad_add_fusion.info, bf16[1024,768]{1,0:T(8,128)(2,1)S(1)} %broadcast_select_fusion.refs_0_.refs_2_.refs_3_, ...), custom_call_target="tpu_custom_call" | custom-call | flops 1 | bytes 1 | tf_op jit(solution)/shard_map/pallas_call | solution.py:136
  183.1 13.9 %shard_map.236 = (bf16[512,768]{1,0:T(8,128)(2,1)S(1)}, bf16[512,1152]{1,0:T(8,128)(2,1)S(1)}, bf16[512,1920]{1,0:T(8,128)(2,1)S(1)}) custom-call(s32[4]{0:T(128)S(1)} %pad_add_fusion.info, bf16[512,768]{1,0:T(8,128)(2,1)S(1)} %get-tuple-element.617.gmix_ref, bf16[512,2304]{1,0:T(8,128)(2,1)} %get-tuple-element.618.qkv_ref, ...), custom_call_target="tpu_custom_call" | custom-call | flops 1 | bytes 1 | tf_op jit(solution)/shard_map/pallas_call | solution.py:136
  197.8 15.4 %shard_map.237 = (bf16[512,2560]{1,0:T(8,128)(2,1)S(1)}, bf16[512,2560]{1,0:T(8,128)(2,1)}, f32[512,768]{1,0:T(8,128)S(1)}, bf16[512,768]{1,0:T(8,128)(2,1)S(1)}) custom-call(s32[4]{0:T(128)S(1)} %pad_add_fusion.info, bf16[512,768]{1,0:T(8,128)(2,1)S(1)} %get-tuple-element.633.grad_ref.refs_8_, bf16[768,2048]{1,0:T(8,128)(2,1)} %bitcast.105, ...), custom_call_target="tpu_custom_call" | custom-call | flops 1 | bytes 1 | tf_op jit(solution)/shard_map/pallas_call | solution.py:136
  213.2 9.2 %shard_map.238 = (bf16[8,912,128]{2,1,0:T(8,128)(2,1)S(1)}, bf16[8,912,128]{2,1,0:T(8,128)(2,1)}) custom-call(s32[4]{0:T(128)S(1)} %pad_add_fusion.info, bf16[512,3072]{1,0:T(8,128)(2,1)S(1)} %get-tuple-element.630.refs_5_.refs_0_.low.high, bf16[512,3072]{1,0:T(8,128)(2,1)S(1)} %collective-permute-done.42.refs_1_, bf16[512,1536]{1,0:T(8,128)(2,1)S(1)} %copy-done.1, ...), custom_call_target="tpu_custom_call" | custom-call | flops 1 | bytes 1 | tf_op jit(solution)/shard_map/pallas_call | solution.py:136
  223.2 5.2 %shard_map.239 = (bf16[8,384,128]{2,1,0:T(8,128)(2,1)S(1)}, bf16[8,384,128]{2,1,0:T(8,128)(2,1)}) custom-call(s32[4]{0:T(128)S(1)} %pad_add_fusion.info, bf16[512,3072]{1,0:T(8,128)(2,1)S(1)} %get-tuple-element.630.refs_5_.refs_0_.low.high, bf16[512,3072]{1,0:T(8,128)(2,1)S(1)} %collective-permute-done.42.refs_1_, ...), custom_call_target="tpu_custom_call" | custom-call | flops 1 | bytes 1 | tf_op jit(solution)/shard_map/pallas_call | solution.py:136
  230.1 15.5 %shard_map.240 = (bf16[8,1296,128]{2,1,0:T(8,128)(2,1)S(1)}, bf16[8,1296,128]{2,1,0:T(8,128)(2,1)}) custom-call(s32[4]{0:T(128)S(1)} %pad_add_fusion.info, bf16[512,3072]{1,0:T(8,128)(2,1)S(1)} %get-tuple-element.663.refs_2_.refs_3_.normed_ref.refs_0_.refs_6_, bf16[512,3072]{1,0:T(8,128)(2,1)S(1)} %collective-permute-done.46.refs_1_.refs_7_, ...), custom_call_target="tpu_custom_call" | custom-call | flops 1 | bytes 1 | tf_op jit(solution)/shard_map/pallas_call | solution.py:136
  246.0 2.5 add_convert_fusion.1
  248.7 2.8 shard_map.241
  251.5 5.7 %shard_map.242 = (bf16[8,432,128]{2,1,0:T(8,128)(2,1)S(1)}, bf16[8,432,128]{2,1,0:T(8,128)(2,1)}) custom-call(s32[4]{0:T(128)S(1)} %pad_add_fusion.info, bf16[512,1536]{1,0:T(8,128)(2,1)S(1)} %copy-done.1, bf16[512,1536]{1,0:T(8,128)(2,1)S(1)} %collective-permute-done.34.refs_3_.oth_ref, bf16[512,1152]{1,0:T(8,128)(2,1)S(1)} %copy-done.28, ...), custom_call_target="tpu_custom_call" | custom-call | flops 1 | bytes 1 | tf_op jit(solution)/shard_map/pallas_call | solution.py:136
  257.3 15.2 %shard_map.243 = (bf16[512,768]{1,0:T(8,128)(2,1)S(1)}, bf16[512,1152]{1,0:T(8,128)(2,1)S(1)}, bf16[512,1920]{1,0:T(8,128)(2,1)}) custom-call(s32[4]{0:T(128)S(1)} %pad_add_fusion.info, bf16[512,768]{1,0:T(8,128)(2,1)S(1)} %copy-done.38, bf16[512,2304]{1,0:T(8,128)(2,1)} %get-tuple-element.700.qkv_ref, ...), custom_call_target="tpu_custom_call" | custom-call | flops 1 | bytes 1 | tf_op jit(solution)/shard_map/pallas_call | solution.py:136
  272.5 2.3 add_convert_fusion.3
  275.5 1.5 collective-permute-done.49
  277.0 1.6 add_convert_fusion
  279.2 1.2 collective-permute-start.50
  284.8 6.6 %shard_map.244 = (bf16[8,432,128]{2,1,0:T(8,128)(2,1)S(1)}, bf16[8,432,128]{2,1,0:T(8,128)(2,1)S(1)}) custom-call(s32[4]{0:T(128)S(1)} %pad_add_fusion.info, bf16[512,1536]{1,0:T(8,128)(2,1)} %get-tuple-element.613.refs_1_.refs_2_.normed_ref.own_ref, bf16[512,1536]{1,0:T(8,128)(2,1)} %collective-permute-done.40.refs_3_.oth_ref, ...), custom_call_target="tpu_custom_call" | custom-call | flops 1 | bytes 1 | tf_op jit(solution)/shard_map/pallas_call | solution.py:136
  291.4 13.2 %collective-permute-done.50 = bf16[8,384,128]{2,1,0:T(8,128)(2,1)} collective-permute-done((bf16[8,384,128]{2,1,0:T(8,128)(2,1)}, bf16[8,384,128]{2,1,0:T(8,128)(2,1)}, u32[]{:S(2)}, u32[]{:S(2)}) %collective-permute-start.50) | collective-permute-done | bytes 786464 | tf_op jit(solution)/shard_map/ppermute | solution.py:69
  307.6 2.5 collective-permute-start.51
  310.9 1.4 add_convert_fusion.2
  312.3 3.1 collective-permute-done.52
  316.4 2.6 collective-permute-done.55
  320.3 3.4 collective-permute-done.57
  325.2 3.4 collective-permute-start.61
  330.0 8.3 %collective-permute-done.56 = bf16[2,1296,128]{2,1,0:T(8,128)(2,1)S(1)} collective-permute-done((bf16[2,1296,128]{2,1,0:T(8,128)(2,1)S(1)}, bf16[2,1296,128]{2,1,0:T(8,128)(2,1)S(1)}, u32[]{:S(2)}, u32[]{:S(2)}) %collective-permute-start.56) | collective-permute-done | bytes 663584 | tf_op jit(solution)/shard_map/ppermute | solution.py:66
  341.7 2.1 collective-permute-start.59
  343.9 2.3 collective-permute-start.64
  346.2 12.6 %collective-permute-done.59 = bf16[1,1296,128]{2,1,0:T(8,128)(2,1)S(1)} collective-permute-done((bf16[1,1296,128]{2,1,0:T(8,128)(2,1)S(1)}, bf16[1,1296,128]{2,1,0:T(8,128)(2,1)S(1)}, u32[]{:S(2)}, u32[]{:S(2)}) %collective-permute-start.59) | collective-permute-done | bytes 331808 | tf_op jit(solution)/shard_map/ppermute | solution.py:66
  363.2 2.4 collective-permute-start.66
  365.5 4.0 %collective-permute-start.69 = (f32[1296,128]{1,0:T(8,128)S(1)}, f32[1296,128]{1,0:T(8,128)S(1)}, u32[]{:S(2)}, u32[]{:S(2)}) collective-permute-start(f32[1296,128]{1,0:T(8,128)S(1)} %get-tuple-element.822), channel_id=1, source_target_pairs={{0,16},{16,0},{1,17},{17,1},{2,18},{18,2},{3,19},{19,3},{4,20},{20... | collective-permute-start | bytes 1990664 | tf_op jit(solution)/shard_map/ppermute | solution.py:73
  371.8 5.3 %collective-permute-start.68 = (f32[432,128]{1,0:T(8,128)S(1)}, f32[432,128]{1,0:T(8,128)S(1)}, u32[]{:S(2)}, u32[]{:S(2)}) collective-permute-start(f32[432,128]{1,0:T(8,128)S(1)} %get-tuple-element.821), channel_id=1, source_target_pairs={{0,16},{16,0},{1,17},{17,1},{2,18},{18,2},{3,19},{19,3},{4,20},{20... | collective-permute-start | bytes 663560 | tf_op jit(solution)/shard_map/ppermute | solution.py:73
  377.1 2.1 maximum_select_fusion
  379.3 2.1 shard_map.246
  382.1 1.7 shard_map.245
  (267 shorter events, 55.8 us)
Async XLA Ops:
  3.1 7.9 %collective-permute-start.1 = (bf16[48,2048]{1,0:T(8,128)(2,1)S(1)}, bf16[48,2048]{1,0:T(8,128)(2,1)S(1)}, u32[]{:S(2)}, u32[]{:S(2)}) collective-permute-start(bf16[48,2048]{1,0:T(8,128)(2,1)S(1)} %broadcast_select_fusion.4), channel_id=1, source_target_pairs={{0,16},{16,0},{1,17},{17,1},{2,18},{18,2},{3,19},{19,3},{4,20},{20... | collective-permute-start | bytes 589832 | tf_op jit(solution)/shard_map/ppermute | solution.py:73
  11.2 14.8 %collective-permute-start.4 = (bf16[1,96,768]{2,1,0:T(8,128)(2,1)S(1)}, bf16[1,96,768]{2,1,0:T(8,128)(2,1)S(1)}, u32[]{:S(2)}, u32[]{:S(2)}) collective-permute-start(bf16[1,96,768]{2,1,0:T(8,128)(2,1)S(1)} %get-tuple-element.430), channel_id=1, source_target_pairs={{0,8},{1,9},{2,10},{3,11},{4,12},{5,13},{6,14},{7,15},{8,0},{9,1},... | collective-permute-start | bytes 442376 | tf_op jit(solution)/shard_map/ppermute | solution.py:66
  14.7 11.3 %collective-permute-start.2 = (bf16[1,64,768]{2,1,0:T(8,128)(2,1)S(1)}, bf16[1,64,768]{2,1,0:T(8,128)(2,1)S(1)}, u32[]{:S(2)}, u32[]{:S(2)}) collective-permute-start(bf16[1,64,768]{2,1,0:T(8,128)(2,1)S(1)} %get-tuple-element.427), channel_id=1, source_target_pairs={{0,2},{1,3},{2,0},{3,1},{4,6},{5,7},{6,4},{7,5},{8,10},{9,11},{10,... | collective-permute-start | bytes 294920 | tf_op jit(solution)/shard_map/ppermute | solution.py:69
  15.9 14.3 %collective-permute-start.6 = (bf16[1,48,2048]{2,1,0:T(8,128)(2,1)S(1)}, bf16[1,48,2048]{2,1,0:T(8,128)(2,1)S(1)}, u32[]{:S(2)}, u32[]{:S(2)}) collective-permute-start(bf16[1,48,2048]{2,1,0:T(8,128)(2,1)S(1)} %get-tuple-element.439), channel_id=1, source_target_pairs={{0,8},{1,9},{2,10},{3,11},{4,12},{5,13},{6,14},{7,15},{8,0},{9,1},... | collective-permute-start | bytes 589832 | tf_op jit(solution)/shard_map/ppermute | solution.py:66
  26.1 10.5 %collective-permute-start.10 = (bf16[1,96,768]{2,1,0:T(8,128)(2,1)S(1)}, bf16[1,96,768]{2,1,0:T(8,128)(2,1)S(1)}, u32[]{:S(2)}, u32[]{:S(2)}) collective-permute-start(bf16[1,96,768]{2,1,0:T(8,128)(2,1)S(1)} %get-tuple-element.446), channel_id=1, source_target_pairs={{0,8},{1,9},{2,10},{3,11},{4,12},{5,13},{6,14},{7,15},{8,0},{9,1},... | collective-permute-start | bytes 442376 | tf_op jit(solution)/shard_map/ppermute | solution.py:66
  26.1 14.3 %collective-permute-start.9 = (bf16[2,96,768]{2,1,0:T(8,128)(2,1)S(1)}, bf16[2,96,768]{2,1,0:T(8,128)(2,1)S(1)}, u32[]{:S(2)}, u32[]{:S(2)}) collective-permute-start(bf16[2,96,768]{2,1,0:T(8,128)(2,1)S(1)} %pad_maximum_fusion.14), channel_id=1, source_target_pairs={{0,4},{1,5},{2,6},{3,7},{4,0},{5,1},{6,2},{7,3},{8,12},{9,13},{10,... | collective-permute-start | bytes 884744 | tf_op jit(solution)/shard_map/ppermute | solution.py:66
  30.3 12.6 %collective-permute-start.7 = (bf16[2,48,2048]{2,1,0:T(8,128)(2,1)S(1)}, bf16[2,48,2048]{2,1,0:T(8,128)(2,1)S(1)}, u32[]{:S(2)}, u32[]{:S(2)}) collective-permute-start(bf16[2,48,2048]{2,1,0:T(8,128)(2,1)S(1)} %pad_maximum_fusion.10), channel_id=1, source_target_pairs={{0,1},{1,0},{2,3},{3,2},{4,5},{5,4},{6,7},{7,6},{8,9},{9,8},{10,11... | collective-permute-start | bytes 1179656 | tf_op jit(solution)/shard_map/ppermute | solution.py:69
  31.4 9.0 %collective-permute-start.8 = (bf16[1,64,768]{2,1,0:T(8,128)(2,1)S(1)}, bf16[1,64,768]{2,1,0:T(8,128)(2,1)S(1)}, u32[]{:S(2)}, u32[]{:S(2)}) collective-permute-start(bf16[1,64,768]{2,1,0:T(8,128)(2,1)S(1)} %get-tuple-element.444), channel_id=1, source_target_pairs={{0,8},{1,9},{2,10},{3,11},{4,12},{5,13},{6,14},{7,15},{8,0},{9,1},... | collective-permute-start | bytes 294920 | tf_op jit(solution)/shard_map/ppermute | solution.py:66
  36.6 11.2 %collective-permute-start.13 = (bf16[2,96,768]{2,1,0:T(8,128)(2,1)S(1)}, bf16[2,96,768]{2,1,0:T(8,128)(2,1)S(1)}, u32[]{:S(2)}, u32[]{:S(2)}) collective-permute-start(bf16[2,96,768]{2,1,0:T(8,128)(2,1)S(1)} %pad_maximum_fusion.15), channel_id=1, source_target_pairs={{0,4},{1,5},{2,6},{3,7},{4,0},{5,1},{6,2},{7,3},{8,12},{9,13},{10,... | collective-permute-start | bytes 884744 | tf_op jit(solution)/shard_map/ppermute | solution.py:66
  40.5 16.0 %collective-permute-start.16 = (bf16[4,96,768]{2,1,0:T(8,128)(2,1)S(1)}, bf16[4,96,768]{2,1,0:T(8,128)(2,1)S(1)}, u32[]{:S(2)}, u32[]{:S(2)}) collective-permute-start(bf16[4,96,768]{2,1,0:T(8,128)(2,1)S(1)} %pad_maximum_fusion.8), channel_id=1, source_target_pairs={{0,2},{1,3},{2,0},{3,1},{4,6},{5,7},{6,4},{7,5},{8,10},{9,11},{10,... | collective-permute-start | bytes 1769480 | tf_op jit(solution)/shard_map/ppermute | solution.py:69
  47.8 11.2 %collective-permute-start.15 = (bf16[4,96,768]{2,1,0:T(8,128)(2,1)S(1)}, bf16[4,96,768]{2,1,0:T(8,128)(2,1)S(1)}, u32[]{:S(2)}, u32[]{:S(2)}) collective-permute-start(bf16[4,96,768]{2,1,0:T(8,128)(2,1)S(1)} %pad_maximum_fusion.9), channel_id=1, source_target_pairs={{0,2},{1,3},{2,0},{3,1},{4,6},{5,7},{6,4},{7,5},{8,10},{9,11},{10,... | collective-permute-start | bytes 1769480 | tf_op jit(solution)/shard_map/ppermute | solution.py:69
  50.4 22.8 %collective-permute-start.11 = (bf16[4,48,2048]{2,1,0:T(8,128)(2,1)S(1)}, bf16[4,48,2048]{2,1,0:T(8,128)(2,1)S(1)}, u32[]{:S(2)}, u32[]{:S(2)}) collective-permute-start(bf16[4,48,2048]{2,1,0:T(8,128)(2,1)S(1)} %pad_maximum_fusion.4), channel_id=1, source_target_pairs={{0,4},{1,5},{2,6},{3,7},{4,0},{5,1},{6,2},{7,3},{8,12},{9,13},{10,... | collective-permute-start | bytes 2359304 | tf_op jit(solution)/shard_map/ppermute | solution.py:66
  56.2 7.6 %collective-permute-start.14 = (bf16[4,64,768]{2,1,0:T(8,128)(2,1)S(1)}, bf16[4,64,768]{2,1,0:T(8,128)(2,1)S(1)}, u32[]{:S(2)}, u32[]{:S(2)}) collective-permute-start(bf16[4,64,768]{2,1,0:T(8,128)(2,1)S(1)} %pad_maximum_fusion.11), channel_id=1, source_target_pairs={{0,2},{1,3},{2,0},{3,1},{4,6},{5,7},{6,4},{7,5},{8,10},{9,11},{10,... | collective-permute-start | bytes 1179656 | tf_op jit(solution)/shard_map/ppermute | solution.py:69
  56.6 23.7 %collective-permute-start.18 = (bf16[8,96,768]{2,1,0:T(8,128)(2,1)S(1)}, bf16[8,96,768]{2,1,0:T(8,128)(2,1)S(1)}, u32[]{:S(2)}, u32[]{:S(2)}) collective-permute-start(bf16[8,96,768]{2,1,0:T(8,128)(2,1)S(1)} %pad_maximum_fusion.2.refs_5_), channel_id=1, source_target_pairs={{0,1},{1,0},{2,3},{3,2},{4,5},{5,4},{6,7},{7,6},{8,9},{9,8},{10,11... | collective-permute-start | bytes 3538952 | tf_op jit(solution)/shard_map/ppermute | solution.py:69
  59.1 37.3 %collective-permute-start.21 = (bf16[8,96,768]{2,1,0:T(8,128)(2,1)S(1)}, bf16[8,96,768]{2,1,0:T(8,128)(2,1)S(1)}, u32[]{:S(2)}, u32[]{:S(2)}) collective-permute-start(bf16[8,96,768]{2,1,0:T(8,128)(2,1)S(1)} %pad_maximum_fusion.3.refs_5_), channel_id=1, source_target_pairs={{0,1},{1,0},{2,3},{3,2},{4,5},{5,4},{6,7},{7,6},{8,9},{9,8},{10,11... | collective-permute-start | bytes 3538952 | tf_op jit(solution)/shard_map/ppermute | solution.py:69
  60.5 13.5 %collective-permute-start.19 = (bf16[1,48,2048]{2,1,0:T(8,128)(2,1)S(1)}, bf16[1,48,2048]{2,1,0:T(8,128)(2,1)S(1)}, u32[]{:S(2)}, u32[]{:S(2)}) collective-permute-start(bf16[1,48,2048]{2,1,0:T(8,128)(2,1)S(1)} %get-tuple-element.488), channel_id=1, source_target_pairs={{0,8},{1,9},{2,10},{3,11},{4,12},{5,13},{6,14},{7,15},{8,0},{9,1},... | collective-permute-start | bytes 589832 | tf_op jit(solution)/shard_map/ppermute | solution.py:66
  63.8 10.1 %collective-permute-start.5 = (bf16[2,64,768]{2,1,0:T(8,128)(2,1)S(1)}, bf16[2,64,768]{2,1,0:T(8,128)(2,1)S(1)}, u32[]{:S(2)}, u32[]{:S(2)}) collective-permute-start(bf16[2,64,768]{2,1,0:T(8,128)(2,1)S(1)} %pad_maximum_fusion.16), channel_id=1, source_target_pairs={{0,8},{1,9},{2,10},{3,11},{4,12},{5,13},{6,14},{7,15},{8,0},{9,1},... | collective-permute-start | bytes 589832 | tf_op jit(solution)/shard_map/ppermute | solution.py:66
  74.0 41.6 %collective-permute-start.27 = (bf16[8,48,2048]{2,1,0:T(8,128)(2,1)S(1)}, bf16[8,48,2048]{2,1,0:T(8,128)(2,1)S(1)}, u32[]{:S(2)}, u32[]{:S(2)}) collective-permute-start(bf16[8,48,2048]{2,1,0:T(8,128)(2,1)S(1)} %pad_maximum_fusion.refs_3_), channel_id=1, source_target_pairs={{0,2},{1,3},{2,0},{3,1},{4,6},{5,7},{6,4},{7,5},{8,10},{9,11},{10,... | collective-permute-start | bytes 4718600 | tf_op jit(solution)/shard_map/ppermute | solution.py:69
  74.0 13.5 %collective-permute-start.17 = (bf16[4,64,768]{2,1,0:T(8,128)(2,1)S(1)}, bf16[4,64,768]{2,1,0:T(8,128)(2,1)S(1)}, u32[]{:S(2)}, u32[]{:S(2)}) collective-permute-start(bf16[4,64,768]{2,1,0:T(8,128)(2,1)S(1)} %pad_maximum_fusion.12), channel_id=1, source_target_pairs={{0,4},{1,5},{2,6},{3,7},{4,0},{5,1},{6,2},{7,3},{8,12},{9,13},{10,... | collective-permute-start | bytes 1179656 | tf_op jit(solution)/shard_map/ppermute | solution.py:66
  80.2 16.3 %collective-permute-start.20 = (bf16[2,48,2048]{2,1,0:T(8,128)(2,1)S(1)}, bf16[2,48,2048]{2,1,0:T(8,128)(2,1)S(1)}, u32[]{:S(2)}, u32[]{:S(2)}) collective-permute-start(bf16[2,48,2048]{2,1,0:T(8,128)(2,1)S(1)} %pad_maximum_fusion.13), channel_id=1, source_target_pairs={{0,4},{1,5},{2,6},{3,7},{4,0},{5,1},{6,2},{7,3},{8,12},{9,13},{10,... | collective-permute-start | bytes 1179656 | tf_op jit(solution)/shard_map/ppermute | solution.py:66
  80.3 23.7 %collective-permute-start.22 = (bf16[8,96,768]{2,1,0:T(8,128)(2,1)S(1)}, bf16[8,96,768]{2,1,0:T(8,128)(2,1)S(1)}, u32[]{:S(2)}, u32[]{:S(2)}) collective-permute-start(bf16[8,96,768]{2,1,0:T(8,128)(2,1)S(1)} %pad_maximum_fusion.2.refs_5_), channel_id=1, source_target_pairs={{0,16},{16,0},{1,17},{17,1},{2,18},{18,2},{3,19},{19,3},{4,20},{20... | collective-permute-start | bytes 3538952 | tf_op jit(solution)/shard_map/ppermute | solution.py:73
  87.6 16.5 %collective-permute-start.23 = (bf16[8,96,768]{2,1,0:T(8,128)(2,1)S(1)}, bf16[8,96,768]{2,1,0:T(8,128)(2,1)S(1)}, u32[]{:S(2)}, u32[]{:S(2)}) collective-permute-start(bf16[8,96,768]{2,1,0:T(8,128)(2,1)S(1)} %collective-permute-done.18.refs_6_), channel_id=1, source_target_pairs={{0,16},{16,0},{1,17},{17,1},{2,18},{18,2},{3,19},{19,3},{4,20},{20... | collective-permute-start | bytes 3538952 | tf_op jit(solution)/shard_map/ppermute | solution.py:73
  96.6 19.0 %collective-permute-start.28 = (bf16[4,48,2048]{2,1,0:T(8,128)(2,1)S(1)}, bf16[4,48,2048]{2,1,0:T(8,128)(2,1)S(1)}, u32[]{:S(2)}, u32[]{:S(2)}) collective-permute-start(bf16[4,48,2048]{2,1,0:T(8,128)(2,1)S(1)} %pad_maximum_fusion.7), channel_id=1, source_target_pairs={{0,2},{1,3},{2,0},{3,1},{4,6},{5,7},{6,4},{7,5},{8,10},{9,11},{10,... | collective-permute-start | bytes 2359304 | tf_op jit(solution)/shard_map/ppermute | solution.py:69
  97.6 23.6 %collective-permute-start.26 = (bf16[8,48,2048]{2,1,0:T(8,128)(2,1)S(1)}, bf16[8,48,2048]{2,1,0:T(8,128)(2,1)S(1)}, u32[]{:S(2)}, u32[]{:S(2)}) collective-permute-start(bf16[8,48,2048]{2,1,0:T(8,128)(2,1)S(1)} %pad_maximum_fusion.refs_3_), channel_id=1, source_target_pairs={{0,16},{16,0},{1,17},{17,1},{2,18},{18,2},{3,19},{19,3},{4,20},{20... | collective-permute-start | bytes 4718600 | tf_op jit(solution)/shard_map/ppermute | solution.py:73
  117.0 14.0 %collective-permute-start.25 = (bf16[8,64,768]{2,1,0:T(8,128)(2,1)S(1)}, bf16[8,64,768]{2,1,0:T(8,128)(2,1)S(1)}, u32[]{:S(2)}, u32[]{:S(2)}) collective-permute-start(bf16[8,64,768]{2,1,0:T(8,128)(2,1)S(1)} %pad_maximum_fusion.6.refs_4_), channel_id=1, source_target_pairs={{0,1},{1,0},{2,3},{3,2},{4,5},{5,4},{6,7},{7,6},{8,9},{9,8},{10,11... | collective-permute-start | bytes 2359304 | tf_op jit(solution)/shard_map/ppermute | solution.py:69
  118.4 13.2 %collective-permute-start.24 = (bf16[8,64,768]{2,1,0:T(8,128)(2,1)S(1)}, bf16[8,64,768]{2,1,0:T(8,128)(2,1)S(1)}, u32[]{:S(2)}, u32[]{:S(2)}) collective-permute-start(bf16[8,64,768]{2,1,0:T(8,128)(2,1)S(1)} %pad_maximum_fusion.6.refs_4_), channel_id=1, source_target_pairs={{0,16},{16,0},{1,17},{17,1},{2,18},{18,2},{3,19},{19,3},{4,20},{20... | collective-permute-start | bytes 2359304 | tf_op jit(solution)/shard_map/ppermute | solution.py:73
  119.9 31.1 %collective-permute-start.38 = (bf16[8,48,2048]{2,1,0:T(8,128)(2,1)}, bf16[8,48,2048]{2,1,0:T(8,128)(2,1)}, u32[]{:S(2)}, u32[]{:S(2)}) collective-permute-start(bf16[8,48,2048]{2,1,0:T(8,128)(2,1)} %pad_maximum_fusion.1.refs_3_), channel_id=1, source_target_pairs={{0,1},{1,0},{2,3},{3,2},{4,5},{5,4},{6,7},{7,6},{8,9},{9,8},{10,11... | collective-permute-start | bytes 4718600 | tf_op jit(solution)/shard_map/ppermute | solution.py:69
  121.2 15.7 %collective-permute-start.31 = (bf16[8,96,768]{2,1,0:T(8,128)(2,1)S(1)}, bf16[8,96,768]{2,1,0:T(8,128)(2,1)S(1)}, u32[]{:S(2)}, u32[]{:S(2)}) collective-permute-start(bf16[8,96,768]{2,1,0:T(8,128)(2,1)S(1)} %pad_maximum_fusion.3.refs_5_), channel_id=1, source_target_pairs={{0,16},{16,0},{1,17},{17,1},{2,18},{18,2},{3,19},{19,3},{4,20},{20... | collective-permute-start | bytes 3538952 | tf_op jit(solution)/shard_map/ppermute | solution.py:73
  121.7 15.2 %collective-permute-start.32 = (bf16[8,96,768]{2,1,0:T(8,128)(2,1)S(1)}, bf16[8,96,768]{2,1,0:T(8,128)(2,1)S(1)}, u32[]{:S(2)}, u32[]{:S(2)}) collective-permute-start(bf16[8,96,768]{2,1,0:T(8,128)(2,1)S(1)} %collective-permute-done.21.refs_6_), channel_id=1, source_target_pairs={{0,16},{16,0},{1,17},{17,1},{2,18},{18,2},{3,19},{19,3},{4,20},{20... | collective-permute-start | bytes 3538952 | tf_op jit(solution)/shard_map/ppermute | solution.py:73
  131.6 19.4 %collective-permute-start.33 = (bf16[8,64,768]{2,1,0:T(8,128)(2,1)}, bf16[8,64,768]{2,1,0:T(8,128)(2,1)}, u32[]{:S(2)}, u32[]{:S(2)}) collective-permute-start(bf16[8,64,768]{2,1,0:T(8,128)(2,1)} %pad_maximum_fusion.5.refs_8_), channel_id=1, source_target_pairs={{0,4},{1,5},{2,6},{3,7},{4,0},{5,1},{6,2},{7,3},{8,12},{9,13},{10,... | collective-permute-start | bytes 2359304 | tf_op jit(solution)/shard_map/ppermute | solution.py:66
  133.5 20.8 %collective-permute-start.37 = (bf16[8,48,2048]{2,1,0:T(8,128)(2,1)}, bf16[8,48,2048]{2,1,0:T(8,128)(2,1)}, u32[]{:S(2)}, u32[]{:S(2)}) collective-permute-start(bf16[8,48,2048]{2,1,0:T(8,128)(2,1)} %pad_maximum_fusion.1.refs_3_), channel_id=1, source_target_pairs={{0,16},{16,0},{1,17},{17,1},{2,18},{18,2},{3,19},{19,3},{4,20},{20... | collective-permute-start | bytes 4718600 | tf_op jit(solution)/shard_map/ppermute | solution.py:73
  151.9 31.2 %collective-permute-start.40 = (bf16[512,1536]{1,0:T(8,128)(2,1)}, bf16[512,1536]{1,0:T(8,128)(2,1)}, u32[]{:S(2)}, u32[]{:S(2)}) collective-permute-start(bf16[512,1536]{1,0:T(8,128)(2,1)} %get-tuple-element.613.refs_1_.refs_2_.normed_ref.own_ref), channel_id=1, source_target_pairs={{0,16},{16,0},{1,17},{17,1},{2,18},{18,2},{3,19},{19,3},{4,20},{20... | collective-permute-start | bytes 4718600 | tf_op jit(solution)/shard_map/ppermute | solution.py:73
  151.9 15.8 %collective-permute-start.35 = (bf16[8,64,768]{2,1,0:T(8,128)(2,1)}, bf16[8,64,768]{2,1,0:T(8,128)(2,1)}, u32[]{:S(2)}, u32[]{:S(2)}) collective-permute-start(bf16[8,64,768]{2,1,0:T(8,128)(2,1)} %pad_maximum_fusion.5.refs_8_), channel_id=1, source_target_pairs={{0,16},{16,0},{1,17},{17,1},{2,18},{18,2},{3,19},{19,3},{4,20},{20... | collective-permute-start | bytes 2359304 | tf_op jit(solution)/shard_map/ppermute | solution.py:73
  152.4 15.3 %collective-permute-start.36 = (bf16[8,64,768]{2,1,0:T(8,128)(2,1)}, bf16[8,64,768]{2,1,0:T(8,128)(2,1)}, u32[]{:S(2)}, u32[]{:S(2)}) collective-permute-start(bf16[8,64,768]{2,1,0:T(8,128)(2,1)} %collective-permute-done.33.refs_9_), channel_id=1, source_target_pairs={{0,16},{16,0},{1,17},{17,1},{2,18},{18,2},{3,19},{19,3},{4,20},{20... | collective-permute-start | bytes 2359304 | tf_op jit(solution)/shard_map/ppermute | solution.py:73
  182.7 30.6 %collective-permute-start.42 = (bf16[512,3072]{1,0:T(8,128)(2,1)S(1)}, bf16[512,3072]{1,0:T(8,128)(2,1)S(1)}, u32[]{:S(2)}, u32[]{:S(2)}) collective-permute-start(bf16[512,3072]{1,0:T(8,128)(2,1)S(1)} %get-tuple-element.630.refs_5_.refs_0_.low.high), channel_id=1, source_target_pairs={{0,16},{16,0},{1,17},{17,1},{2,18},{18,2},{3,19},{19,3},{4,20},{20... | collective-permute-start | bytes 9437192 | tf_op jit(solution)/shard_map/ppermute | solution.py:73
  197.1 16.2 %collective-permute-start.41 = (bf16[512,2560]{1,0:T(8,128)(2,1)S(1)}, bf16[512,2560]{1,0:T(8,128)(2,1)S(1)}, u32[]{:S(2)}, u32[]{:S(2)}) collective-permute-start(bf16[512,2560]{1,0:T(8,128)(2,1)S(1)} %get-tuple-element.629), channel_id=1, source_target_pairs={{0,16},{16,0},{1,17},{17,1},{2,18},{18,2},{3,19},{19,3},{4,20},{20... | collective-permute-start | bytes 7864328 | tf_op jit(solution)/shard_map/ppermute | solution.py:73
  197.3 16.0 %collective-permute-start.34 = (bf16[512,1536]{1,0:T(8,128)(2,1)S(1)}, bf16[512,1536]{1,0:T(8,128)(2,1)S(1)}, u32[]{:S(2)}, u32[]{:S(2)}) collective-permute-start(bf16[512,1536]{1,0:T(8,128)(2,1)S(1)} %copy-done.1), channel_id=1, source_target_pairs={{0,16},{16,0},{1,17},{17,1},{2,18},{18,2},{3,19},{19,3},{4,20},{20... | collective-permute-start | bytes 4718600 | tf_op jit(solution)/shard_map/ppermute | solution.py:73
  197.6 31.6 %collective-permute-start.46 = (bf16[512,3072]{1,0:T(8,128)(2,1)S(1)}, bf16[512,3072]{1,0:T(8,128)(2,1)S(1)}, u32[]{:S(2)}, u32[]{:S(2)}) collective-permute-start(bf16[512,3072]{1,0:T(8,128)(2,1)S(1)} %get-tuple-element.663.refs_2_.refs_3_.normed_ref.refs_0_.refs_6_), channel_id=1, source_target_pairs={{0,16},{16,0},{1,17},{17,1},{2,18},{18,2},{3,19},{19,3},{4,20},{20... | collective-permute-start | bytes 9437192 | tf_op jit(solution)/shard_map/ppermute | solution.py:73
  222.4 7.3 %collective-permute-start.45 = (bf16[512,2560]{1,0:T(8,128)(2,1)}, bf16[512,2560]{1,0:T(8,128)(2,1)S(1)}, u32[]{:S(2)}, u32[]{:S(2)}) collective-permute-start(bf16[512,2560]{1,0:T(8,128)(2,1)} %get-tuple-element.662), channel_id=1, source_target_pairs={{0,16},{16,0},{1,17},{17,1},{2,18},{18,2},{3,19},{19,3},{4,20},{20... | collective-permute-start | bytes 7864328 | tf_op jit(solution)/shard_map/ppermute | solution.py:73
  222.8 7.4 %collective-permute-start.44 = (bf16[512,1920]{1,0:T(8,128)(2,1)S(1)}, bf16[512,1920]{1,0:T(8,128)(2,1)S(1)}, u32[]{:S(2)}, u32[]{:S(2)}) collective-permute-start(bf16[512,1920]{1,0:T(8,128)(2,1)S(1)} %get-tuple-element.658), channel_id=1, source_target_pairs={{0,16},{16,0},{1,17},{17,1},{2,18},{18,2},{3,19},{19,3},{4,20},{20... | collective-permute-start | bytes 5898248 | tf_op jit(solution)/shard_map/ppermute | solution.py:73
  222.9 23.1 %collective-permute-start.43 = (bf16[8,912,128]{2,1,0:T(8,128)(2,1)}, bf16[8,912,128]{2,1,0:T(8,128)(2,1)}, u32[]{:S(2)}, u32[]{:S(2)}) collective-permute-start(bf16[8,912,128]{2,1,0:T(8,128)(2,1)} %get-tuple-element.657), channel_id=1, source_target_pairs={{0,2},{1,3},{2,0},{3,1},{4,6},{5,7},{6,4},{7,5},{8,10},{9,11},{10,... | collective-permute-start | bytes 5603336 | tf_op jit(solution)/shard_map/ppermute | solution.py:69
  245.7 31.4 %collective-permute-start.49 = (bf16[8,1296,128]{2,1,0:T(8,128)(2,1)}, bf16[8,1296,128]{2,1,0:T(8,128)(2,1)S(1)}, u32[]{:S(2)}, u32[]{:S(2)}) collective-permute-start(bf16[8,1296,128]{2,1,0:T(8,128)(2,1)} %get-tuple-element.720), channel_id=1, source_target_pairs={{0,2},{1,3},{2,0},{3,1},{4,6},{5,7},{6,4},{7,5},{8,10},{9,11},{10,... | collective-permute-start | bytes 7962632 | tf_op jit(solution)/shard_map/ppermute | solution.py:69
  248.6 24.0 %collective-permute-start.47 = (bf16[4,912,128]{2,1,0:T(8,128)(2,1)S(1)}, bf16[4,912,128]{2,1,0:T(8,128)(2,1)S(1)}, u32[]{:S(2)}, u32[]{:S(2)}) collective-permute-start(bf16[4,912,128]{2,1,0:T(8,128)(2,1)S(1)} %add_convert_fusion.1), channel_id=1, source_target_pairs={{0,4},{1,5},{2,6},{3,7},{4,0},{5,1},{6,2},{7,3},{8,12},{9,13},{10,... | collective-permute-start | bytes 2801672 | tf_op jit(solution)/shard_map/ppermute | solution.py:66
  274.9 9.9 %collective-permute-start.48 = (bf16[512,1920]{1,0:T(8,128)(2,1)}, bf16[512,1920]{1,0:T(8,128)(2,1)S(1)}, u32[]{:S(2)}, u32[]{:S(2)}) collective-permute-start(bf16[512,1920]{1,0:T(8,128)(2,1)} %get-tuple-element.718), channel_id=1, source_target_pairs={{0,16},{16,0},{1,17},{17,1},{2,18},{18,2},{3,19},{19,3},{4,20},{20... | collective-permute-start | bytes 5898248 | tf_op jit(solution)/shard_map/ppermute | solution.py:73
  278.9 31.1 %collective-permute-start.53 = (bf16[4,1296,128]{2,1,0:T(8,128)(2,1)}, bf16[4,1296,128]{2,1,0:T(8,128)(2,1)}, u32[]{:S(2)}, u32[]{:S(2)}) collective-permute-start(bf16[4,1296,128]{2,1,0:T(8,128)(2,1)} %add_convert_fusion), channel_id=1, source_target_pairs={{0,1},{1,0},{2,3},{3,2},{4,5},{5,4},{6,7},{7,6},{8,9},{9,8},{10,11... | collective-permute-start | bytes 3981320 | tf_op jit(solution)/shard_map/ppermute | solution.py:69
  279.2 25.5 %collective-permute-start.50 = (bf16[8,384,128]{2,1,0:T(8,128)(2,1)}, bf16[8,384,128]{2,1,0:T(8,128)(2,1)}, u32[]{:S(2)}, u32[]{:S(2)}) collective-permute-start(bf16[8,384,128]{2,1,0:T(8,128)(2,1)} %get-tuple-element.733), channel_id=1, source_target_pairs={{0,1},{1,0},{2,3},{3,2},{4,5},{5,4},{6,7},{7,6},{8,9},{9,8},{10,11... | collective-permute-start | bytes 2359304 | tf_op jit(solution)/shard_map/ppermute | solution.py:69
  280.4 25.3 %collective-permute-start.54 = (bf16[8,432,128]{2,1,0:T(8,128)(2,1)}, bf16[8,432,128]{2,1,0:T(8,128)(2,1)}, u32[]{:S(2)}, u32[]{:S(2)}) collective-permute-start(bf16[8,432,128]{2,1,0:T(8,128)(2,1)} %get-tuple-element.743), channel_id=1, source_target_pairs={{0,4},{1,5},{2,6},{3,7},{4,0},{5,1},{6,2},{7,3},{8,12},{9,13},{10,... | collective-permute-start | bytes 2654216 | tf_op jit(solution)/shard_map/ppermute | solution.py:66
  284.2 34.9 %collective-permute-start.58 = (bf16[2,912,128]{2,1,0:T(8,128)(2,1)S(1)}, bf16[2,912,128]{2,1,0:T(8,128)(2,1)S(1)}, u32[]{:S(2)}, u32[]{:S(2)}) collective-permute-start(bf16[2,912,128]{2,1,0:T(8,128)(2,1)S(1)} %copy-done.49), channel_id=1, source_target_pairs={{0,1},{1,0},{2,3},{3,2},{4,5},{5,4},{6,7},{7,6},{8,9},{9,8},{10,11... | collective-permute-start | bytes 1400840 | tf_op jit(solution)/shard_map/ppermute | solution.py:69
  305.8 13.2 %collective-permute-start.55 = (bf16[8,432,128]{2,1,0:T(8,128)(2,1)S(1)}, bf16[8,432,128]{2,1,0:T(8,128)(2,1)S(1)}, u32[]{:S(2)}, u32[]{:S(2)}) collective-permute-start(bf16[8,432,128]{2,1,0:T(8,128)(2,1)S(1)} %get-tuple-element.756), channel_id=1, source_target_pairs={{0,1},{1,0},{2,3},{3,2},{4,5},{5,4},{6,7},{7,6},{8,9},{9,8},{10,11... | collective-permute-start | bytes 2654216 | tf_op jit(solution)/shard_map/ppermute | solution.py:69
  307.2 8.1 %collective-permute-start.52 = (bf16[4,384,128]{2,1,0:T(8,128)(2,1)S(1)}, bf16[4,384,128]{2,1,0:T(8,128)(2,1)S(1)}, u32[]{:S(2)}, u32[]{:S(2)}) collective-permute-start(bf16[4,384,128]{2,1,0:T(8,128)(2,1)S(1)} %add_convert_fusion.6), channel_id=1, source_target_pairs={{0,4},{1,5},{2,6},{3,7},{4,0},{5,1},{6,2},{7,3},{8,12},{9,13},{10,... | collective-permute-start | bytes 1179656 | tf_op jit(solution)/shard_map/ppermute | solution.py:66
  307.6 8.8 %collective-permute-start.51 = (bf16[512,768]{1,0:T(8,128)(2,1)S(1)}, bf16[512,768]{1,0:T(8,128)(2,1)S(1)}, u32[]{:S(2)}, u32[]{:S(2)}) collective-permute-start(bf16[512,768]{1,0:T(8,128)(2,1)S(1)} %get-tuple-element.739), channel_id=1, source_target_pairs={{0,16},{16,0},{1,17},{17,1},{2,18},{18,2},{3,19},{19,3},{4,20},{20... | collective-permute-start | bytes 2359304 | tf_op jit(solution)/shard_map/ppermute | solution.py:73
  310.1 13.7 %collective-permute-start.57 = (bf16[4,432,128]{2,1,0:T(8,128)(2,1)S(1)}, bf16[4,432,128]{2,1,0:T(8,128)(2,1)S(1)}, u32[]{:S(2)}, u32[]{:S(2)}) collective-permute-start(bf16[4,432,128]{2,1,0:T(8,128)(2,1)S(1)} %add_convert_fusion.5), channel_id=1, source_target_pairs={{0,1},{1,0},{2,3},{3,2},{4,5},{5,4},{6,7},{7,6},{8,9},{9,8},{10,11... | collective-permute-start | bytes 1327112 | tf_op jit(solution)/shard_map/ppermute | solution.py:69
  319.0 19.3 %collective-permute-start.56 = (bf16[2,1296,128]{2,1,0:T(8,128)(2,1)S(1)}, bf16[2,1296,128]{2,1,0:T(8,128)(2,1)S(1)}, u32[]{:S(2)}, u32[]{:S(2)}) collective-permute-start(bf16[2,1296,128]{2,1,0:T(8,128)(2,1)S(1)} %add_convert_fusion.2), channel_id=1, source_target_pairs={{0,4},{1,5},{2,6},{3,7},{4,0},{5,1},{6,2},{7,3},{8,12},{9,13},{10,... | collective-permute-start | bytes 1990664 | tf_op jit(solution)/shard_map/ppermute | solution.py:66
  324.8 14.7 %collective-permute-start.62 = (bf16[2,384,128]{2,1,0:T(8,128)(2,1)S(1)}, bf16[2,384,128]{2,1,0:T(8,128)(2,1)S(1)}, u32[]{:S(2)}, u32[]{:S(2)}) collective-permute-start(bf16[2,384,128]{2,1,0:T(8,128)(2,1)S(1)} %add_convert_fusion.11), channel_id=1, source_target_pairs={{0,2},{1,3},{2,0},{3,1},{4,6},{5,7},{6,4},{7,5},{8,10},{9,11},{10,... | collective-permute-start | bytes 589832 | tf_op jit(solution)/shard_map/ppermute | solution.py:69
  325.2 15.3 %collective-permute-start.61 = (bf16[1,912,128]{2,1,0:T(8,128)(2,1)S(1)}, bf16[1,912,128]{2,1,0:T(8,128)(2,1)S(1)}, u32[]{:S(2)}, u32[]{:S(2)}) collective-permute-start(bf16[1,912,128]{2,1,0:T(8,128)(2,1)S(1)} %add_convert_fusion.8), channel_id=1, source_target_pairs={{0,8},{1,9},{2,10},{3,11},{4,12},{5,13},{6,14},{7,15},{8,0},{9,1},... | collective-permute-start | bytes 700424 | tf_op jit(solution)/shard_map/ppermute | solution.py:66
  328.5 13.1 %collective-permute-start.60 = (bf16[4,432,128]{2,1,0:T(8,128)(2,1)S(1)}, bf16[4,432,128]{2,1,0:T(8,128)(2,1)S(1)}, u32[]{:S(2)}, u32[]{:S(2)}) collective-permute-start(bf16[4,432,128]{2,1,0:T(8,128)(2,1)S(1)} %add_convert_fusion.4), channel_id=1, source_target_pairs={{0,2},{1,3},{2,0},{3,1},{4,6},{5,7},{6,4},{7,5},{8,10},{9,11},{10,... | collective-permute-start | bytes 1327112 | tf_op jit(solution)/shard_map/ppermute | solution.py:69
  329.6 30.4 %collective-permute-start.65 = (bf16[2,432,128]{2,1,0:T(8,128)(2,1)S(1)}, bf16[2,432,128]{2,1,0:T(8,128)(2,1)S(1)}, u32[]{:S(2)}, u32[]{:S(2)}) collective-permute-start(bf16[2,432,128]{2,1,0:T(8,128)(2,1)S(1)} %add_convert_fusion.10), channel_id=1, source_target_pairs={{0,2},{1,3},{2,0},{3,1},{4,6},{5,7},{6,4},{7,5},{8,10},{9,11},{10,... | collective-permute-start | bytes 663560 | tf_op jit(solution)/shard_map/ppermute | solution.py:69
  341.7 17.2 %collective-permute-start.59 = (bf16[1,1296,128]{2,1,0:T(8,128)(2,1)S(1)}, bf16[1,1296,128]{2,1,0:T(8,128)(2,1)S(1)}, u32[]{:S(2)}, u32[]{:S(2)}) collective-permute-start(bf16[1,1296,128]{2,1,0:T(8,128)(2,1)S(1)} %add_convert_fusion.7), channel_id=1, source_target_pairs={{0,8},{1,9},{2,10},{3,11},{4,12},{5,13},{6,14},{7,15},{8,0},{9,1},... | collective-permute-start | bytes 995336 | tf_op jit(solution)/shard_map/ppermute | solution.py:66
  343.9 17.2 %collective-permute-start.64 = (bf16[2,432,128]{2,1,0:T(8,128)(2,1)S(1)}, bf16[2,432,128]{2,1,0:T(8,128)(2,1)S(1)}, u32[]{:S(2)}, u32[]{:S(2)}) collective-permute-start(bf16[2,432,128]{2,1,0:T(8,128)(2,1)S(1)} %add_convert_fusion.9), channel_id=1, source_target_pairs={{0,4},{1,5},{2,6},{3,7},{4,0},{5,1},{6,2},{7,3},{8,12},{9,13},{10,... | collective-permute-start | bytes 663560 | tf_op jit(solution)/shard_map/ppermute | solution.py:66
  346.1 15.9 %collective-permute-start.63 = (bf16[1,384,128]{2,1,0:T(8,128)(2,1)S(1)}, bf16[1,384,128]{2,1,0:T(8,128)(2,1)S(1)}, u32[]{:S(2)}, u32[]{:S(2)}) collective-permute-start(bf16[1,384,128]{2,1,0:T(8,128)(2,1)S(1)} %add_convert_fusion.14), channel_id=1, source_target_pairs={{0,8},{1,9},{2,10},{3,11},{4,12},{5,13},{6,14},{7,15},{8,0},{9,1},... | collective-permute-start | bytes 294920 | tf_op jit(solution)/shard_map/ppermute | solution.py:66
  363.1 7.6 %collective-permute-start.67 = (bf16[1,432,128]{2,1,0:T(8,128)(2,1)S(1)}, bf16[1,432,128]{2,1,0:T(8,128)(2,1)S(1)}, u32[]{:S(2)}, u32[]{:S(2)}) collective-permute-start(bf16[1,432,128]{2,1,0:T(8,128)(2,1)S(1)} %add_convert_fusion.13), channel_id=1, source_target_pairs={{0,8},{1,9},{2,10},{3,11},{4,12},{5,13},{6,14},{7,15},{8,0},{9,1},... | collective-permute-start | bytes 331784 | tf_op jit(solution)/shard_map/ppermute | solution.py:66
  363.2 8.5 %collective-permute-start.66 = (bf16[1,432,128]{2,1,0:T(8,128)(2,1)S(1)}, bf16[1,432,128]{2,1,0:T(8,128)(2,1)S(1)}, u32[]{:S(2)}, u32[]{:S(2)}) collective-permute-start(bf16[1,432,128]{2,1,0:T(8,128)(2,1)S(1)} %add_convert_fusion.12), channel_id=1, source_target_pairs={{0,8},{1,9},{2,10},{3,11},{4,12},{5,13},{6,14},{7,15},{8,0},{9,1},... | collective-permute-start | bytes 331784 | tf_op jit(solution)/shard_map/ppermute | solution.py:66
  365.5 13.7 %collective-permute-start.69 = (f32[1296,128]{1,0:T(8,128)S(1)}, f32[1296,128]{1,0:T(8,128)S(1)}, u32[]{:S(2)}, u32[]{:S(2)}) collective-permute-start(f32[1296,128]{1,0:T(8,128)S(1)} %get-tuple-element.822), channel_id=1, source_target_pairs={{0,16},{16,0},{1,17},{17,1},{2,18},{18,2},{3,19},{19,3},{4,20},{20... | collective-permute-start | bytes 1990664 | tf_op jit(solution)/shard_map/ppermute | solution.py:73
  371.8 10.2 %collective-permute-start.68 = (f32[432,128]{1,0:T(8,128)S(1)}, f32[432,128]{1,0:T(8,128)S(1)}, u32[]{:S(2)}, u32[]{:S(2)}) collective-permute-start(f32[432,128]{1,0:T(8,128)S(1)} %get-tuple-element.821), channel_id=1, source_target_pairs={{0,16},{16,0},{1,17},{17,1},{2,18},{18,2},{3,19},{19,3},{4,20},{20... | collective-permute-start | bytes 663560 | tf_op jit(solution)/shard_map/ppermute | solution.py:73
  (60 other events, 608.0 us)
